TPU v7x, 32 devices: a whole 2x2x4 slice. The times are simulated.
32 devices in a mesh: dp: 8 (over z, x), tensor: 4 (over y, core).
Axes of the slice: x: 2, y: 2, z: 4, core: 2. Of those that a mesh axis runs over, the one named last changes fastest.
Arguments:
- tokens: bfloat16 [256, 128, 512], P('dp', 'tensor'), may hold values from -6 to 6
- memory: bfloat16 [256, 512, 512], P('dp', 'tensor'), may hold values from -6 to 6
- cotangent: bfloat16 [256, 128, 512], P('dp', 'tensor'), may hold values from -27 to 27
- buckets: int32 [256, 128, 128], P('dp'), may hold values from 0 to 31, as said below
- key_mask: int32 [256, 128, 128], P('dp'), may hold values from 0 to 1, as said below
- task_groups: int32 [256], P('dp'), may hold values from 0 to 3
- weights_in: float32 [6, 512, 512], P(None, 'dp', 'tensor'), may hold values from -0.25 to 0.25
- weights_out: float32 [2, 512, 512], P(None, 'tensor', 'dp'), may hold values from -0.75 to 0.75
- weights_up: float32 [512, 2048], P('dp', 'tensor'), may hold values from -0.25 to 0.25
- weights_down: float32 [2048, 512], P('tensor', 'dp'), may hold values from -0.1875 to 0.1875
- gains: float32 [3, 512], replicated, may hold values from 0.25 to 2.7
- position_bias: float32 [32, 8], P(None, 'tensor'), may hold values from -3 to 3
- momentum_in: float32 [6, 512, 512], P(None, 'dp', 'tensor'), may hold values from -0.005859375 to 0.005859375
- average_in: float32 [6, 512, 512], P(None, 'dp', 'tensor'), may hold values from -0.25 to 0.25
- momentum_out: float32 [2, 512, 512], P(None, 'tensor', 'dp'), may hold values from -0.005859375 to 0.005859375
- average_out: float32 [2, 512, 512], P(None, 'tensor', 'dp'), may hold values from -0.75 to 0.75
- momentum_up: float32 [512, 2048], P('dp', 'tensor'), may hold values from -0.005859375 to 0.005859375
- average_up: float32 [512, 2048], P('dp', 'tensor'), may hold values from -0.25 to 0.25
- momentum_down: float32 [2048, 512], P('tensor', 'dp'), may hold values from -0.005859375 to 0.005859375
- average_down: float32 [2048, 512], P('tensor', 'dp'), may hold values from -0.1875 to 0.1875
- momentum_gain: float32 [3, 512], P(None, 'tensor'), may hold values from -0.0234375 to 0.0234375
- average_gain: float32 [3, 512], P(None, 'tensor'), may hold values from 0.5 to 1.5
- momentum_bias: float32 [32, 8], P(None, 'tensor'), may hold values from -0.0234375 to 0.0234375
- average_bias: float32 [32, 8], P(None, 'tensor'), may hold values from -3 to 3
Outputs:
- output: bfloat16 [256, 128, 512], P('dp', 'tensor')
- tokens_grad: float32 [256, 128, 512], P('dp', 'tensor')
- memory_grad: float32 [256, 512, 512], P('dp', 'tensor')
- example_norms: float32 [256], P('dp')
- velocity_in: float32 [6, 512, 512], P(None, 'dp', 'tensor')
- averaged_in: float32 [6, 512, 512], P(None, 'dp', 'tensor')
- updated_in: float32 [6, 512, 512], P(None, 'dp', 'tensor')
- velocity_out: float32 [2, 512, 512], P(None, 'tensor', 'dp')
- averaged_out: float32 [2, 512, 512], P(None, 'tensor', 'dp')
- updated_out: float32 [2, 512, 512], P(None, 'tensor', 'dp')
- velocity_up: float32 [512, 2048], P('dp', 'tensor')
- averaged_up: float32 [512, 2048], P('dp', 'tensor')
- updated_up: float32 [512, 2048], P('dp', 'tensor')
- velocity_down: float32 [2048, 512], P('tensor', 'dp')
- averaged_down: float32 [2048, 512], P('tensor', 'dp')
- updated_down: float32 [2048, 512], P('tensor', 'dp')
- velocity_gain: float32 [3, 512], P(None, 'tensor')
- averaged_gain: float32 [3, 512], P(None, 'tensor')
- updated_gain: float32 [3, 512], P(None, 'tensor')
- velocity_bias: float32 [32, 8], P(None, 'tensor')
- averaged_bias: float32 [32, 8], P(None, 'tensor')
- updated_bias: float32 [32, 8], P(None, 'tensor')
Inputs may be any that keep to these rules, and one draw needn't show every extreme that they name: buckets[e, i, j] is the bucket of the distance from key j's position back to query i's, the same for all heads. key_mask is 0 above the diagonal and 1 on it.
All inputs are finite; a program needn't handle non-finite values.
Results may differ from a plain program's by a relative error of at most 0.023.
The roundings to bfloat16 on the way count: a program that leaves them out, or rounds other values in their place, can miss the bound.
Values may be sent and summed in bfloat16 or wider, within the bound.
No kernel may reach another device: no remote copies, remote signals or barrier semaphores. Data moves between devices by JAX's collectives and lax.ppermute only.
A program may use at most 512 MiB of HBM per device.

v0:
```python
import math

import jax
import jax.numpy as jnp
from jax import lax
from jax.sharding import PartitionSpec as P

epsilon = 1e-06
momentum_decay = 0.9
average_decay = 0.7
matrix_rate = 10.0
output_rate = 40.0
small_rate = 50.0
group_limits = (0.6, 0.85, 1.2, 1.7)


def lookup(bucket_ids, bias_table):
    onehot = (bucket_ids[..., None] == jnp.arange(bias_table.shape[0], dtype=jnp.int32)).astype(
        jnp.float32
    )
    return (
        onehot,
        jnp.einsum("estb,bh->ehst", onehot, bias_table, precision=lax.Precision.HIGHEST),
    )


def scores_of(queries, key_rows, bias_add, keep):
    scaling = 1.0 / math.sqrt(queries.shape[-1])
    scores = (
        jnp.einsum("eshd,ethd->ehst", queries, key_rows, preferred_element_type=jnp.float32)
        * scaling
    )
    if bias_add is not None:
        scores = jnp.where(keep[:, None], scores + bias_add, -1000000000.0)
    return scores


def attend(queries, key_rows, value_rows, bias_add, keep):
    scores = scores_of(queries, key_rows, bias_add, keep)
    row_peak = jnp.max(scores, -1, keepdims=True)
    row_total = row_peak + jnp.log(jnp.sum(jnp.exp(scores - row_peak), -1, keepdims=True))
    soft_weights = jnp.exp(scores - row_total).astype(jnp.bfloat16)
    mixture = jnp.einsum(
        "ehst,ethd->eshd", soft_weights, value_rows, preferred_element_type=jnp.float32
    )
    return (mixture.astype(jnp.bfloat16), row_total)


def attend_back(queries, key_rows, value_rows, d_mixture, row_total, bias_add, keep):
    scaling = 1.0 / math.sqrt(queries.shape[-1])
    soft_weights = jnp.exp(scores_of(queries, key_rows, bias_add, keep) - row_total)
    d_weights = jnp.einsum(
        "eshd,ethd->ehst", d_mixture, value_rows, preferred_element_type=jnp.float32
    )
    row_inner = jnp.sum(soft_weights * d_weights, -1, keepdims=True)
    d_scores = (soft_weights * (d_weights - row_inner)).astype(jnp.bfloat16)
    d_queries = (
        jnp.einsum("ehst,ethd->eshd", d_scores, key_rows, preferred_element_type=jnp.float32)
        * scaling
    ).astype(jnp.bfloat16)
    d_keys = (
        jnp.einsum("ehst,eshd->ethd", d_scores, queries, preferred_element_type=jnp.float32)
        * scaling
    ).astype(jnp.bfloat16)
    d_values = jnp.einsum(
        "ehst,eshd->ethd",
        soft_weights.astype(jnp.bfloat16),
        d_mixture,
        preferred_element_type=jnp.float32,
    ).astype(jnp.bfloat16)
    return (d_queries, d_keys, d_values, d_scores)


def stepper(parameter, gradient, momentum, average, step_rate):
    velocity = momentum_decay * momentum + gradient
    updated = parameter - step_rate * (gradient + momentum_decay * velocity)
    averaged = average_decay * average + (1.0 - average_decay) * updated
    return (velocity, averaged, updated)


def on_device(
    tokens,
    memory,
    cotangent,
    buckets,
    key_mask,
    task_groups,
    weights_in,
    weights_out,
    weights_up,
    weights_down,
    gains,
    position_bias,
    momentum_in,
    average_in,
    momentum_out,
    average_out,
    momentum_up,
    average_up,
    momentum_down,
    average_down,
    momentum_gain,
    average_gain,
    momentum_bias,
    average_bias,
):
    wide = jnp.float32
    narrow = jnp.bfloat16
    highest = lax.Precision.HIGHEST
    example_count = tokens.shape[0]
    seq_full = buckets.shape[1]
    gain_width = momentum_gain.shape[1]
    heads_local = position_bias.shape[1]
    inner_local = weights_in.shape[2]
    head_shape = (heads_local, inner_local // heads_local)
    bundle = math.gcd(example_count, max(1, 512 // seq_full))

    def blocked(operand):
        return operand.reshape((example_count // bundle, bundle) + operand.shape[1:])

    def split_heads(operand):
        return operand.reshape(operand.shape[:2] + head_shape)

    def product(form, left, right):
        return jnp.einsum(form, left, right, preferred_element_type=wide)

    proj_in, proj_out, proj_up, proj_down = (
        lax.all_gather(weights_in.astype(narrow), "dp", axis=1, tiled=True),
        lax.all_gather(weights_out.astype(narrow), "dp", axis=2, tiled=True),
        lax.all_gather(weights_up.astype(narrow), "dp", axis=0, tiled=True),
        lax.all_gather(weights_down.astype(narrow), "dp", axis=1, tiled=True),
    )
    memory_full = lax.all_gather(memory, "tensor", axis=1, tiled=True)
    memory_len = memory_full.shape[1]
    keep_rows = key_mask > 0

    def block_input(residual, which):
        gathered = lax.all_gather(residual.astype(narrow), "tensor", axis=1, tiled=True)
        rows_in = gathered.astype(wide)
        scaling = lax.rsqrt(jnp.mean(rows_in * rows_in, -1, keepdims=True) + epsilon)
        return (rows_in, scaling, (rows_in * scaling * gains[which]).astype(narrow))

    def block_output(partial_value):
        return lax.psum_scatter(partial_value, "tensor", scatter_dimension=1, tiled=True)

    def output_grad(gradient):
        return lax.all_gather(gradient.astype(narrow), "tensor", axis=1, tiled=True)

    def norm_back(rows_in, scaling, which, d_normed):
        weighted = d_normed * gains[which]
        cubed = scaling * scaling * scaling
        d_rows = scaling * weighted - rows_in * cubed * jnp.mean(
            rows_in * weighted, -1, keepdims=True
        )
        return (d_rows, jnp.sum(d_normed * rows_in * scaling, 1))

    def input_grads(rows_in, scaling, which, d_normed):
        d_rows, d_gain = norm_back(rows_in, scaling, which, d_normed)
        return (
            lax.psum_scatter(
                d_rows.astype(jnp.bfloat16), "tensor", scatter_dimension=1, tiled=True
            ).astype(jnp.float32),
            lax.psum_scatter(
                d_gain.astype(jnp.bfloat16), "tensor", scatter_dimension=1, tiled=True
            ).astype(jnp.float32),
        )

    residual_in = tokens.astype(wide)
    rows_a, scale_a, normed_a = block_input(residual_in, 0)
    self_qkv = product("esd,kdf->kesf", normed_a, proj_in[:3]).astype(narrow)
    self_query = split_heads(self_qkv[0])
    self_keys = split_heads(self_qkv[1])
    self_values = split_heads(self_qkv[2])

    def self_forward(items):
        queries, key_rows, value_rows, bucket_ids, keep = items
        onehot, bias_add = lookup(bucket_ids, position_bias)
        return attend(queries, key_rows, value_rows, bias_add, keep)

    self_mix, self_total = lax.map(
        self_forward,
        (
            blocked(self_query),
            blocked(self_keys),
            blocked(self_values),
            blocked(buckets),
            blocked(keep_rows),
        ),
    )
    self_mix = self_mix.reshape(example_count, seq_full, inner_local)
    residual_mid = residual_in + block_output(product("esf,fd->esd", self_mix, proj_out[0]))
    rows_b, scale_b, normed_b = block_input(residual_mid, 1)
    cross_query = split_heads(product("esd,df->esf", normed_b, proj_in[3]).astype(narrow))
    cross_kv = product("emd,kdf->kemf", memory_full, proj_in[4:6]).astype(narrow)
    cross_keys = split_heads(cross_kv[0])
    cross_values = split_heads(cross_kv[1])

    def cross_forward(items):
        queries, key_rows, value_rows = items
        return attend(queries, key_rows, value_rows, None, None)

    cross_mix, cross_total = lax.map(
        cross_forward, (blocked(cross_query), blocked(cross_keys), blocked(cross_values))
    )
    cross_mix = cross_mix.reshape(example_count, seq_full, inner_local)
    residual_late = residual_mid + block_output(product("esf,fd->esd", cross_mix, proj_out[1]))
    rows_c, scale_c, normed_c = block_input(residual_late, 2)
    hidden = product("esd,df->esf", normed_c, proj_up)
    active = jax.nn.gelu(hidden).astype(narrow)
    output = (residual_late + block_output(product("esf,fd->esd", active, proj_down))).astype(
        narrow
    )
    d_late = cotangent.astype(wide)
    d_top = output_grad(d_late)
    d_active = product("esd,fd->esf", d_top, proj_down)
    d_hidden = jax.vjp(jax.nn.gelu, hidden)[1](d_active)[0].astype(narrow)
    grad_down = product("esf,esd->efd", active, d_top)
    grad_up = product("esd,esf->edf", normed_c, d_hidden)
    d_rows_c, grad_gain_c = input_grads(
        rows_c, scale_c, 2, product("esf,df->esd", d_hidden, proj_up)
    )
    d_mid = d_late + d_rows_c
    d_cross_top = output_grad(d_mid)
    d_cross_mix = product("esd,fd->esf", d_cross_top, proj_out[1]).astype(narrow)
    grad_out_cross = product("esf,esd->efd", cross_mix, d_cross_top)

    def cross_backward(items):
        queries, key_rows, value_rows, d_mixture, row_total = items
        d_queries, d_keys, d_values, d_scores = attend_back(
            queries, key_rows, value_rows, d_mixture, row_total, None, None
        )
        return (d_queries, d_keys, d_values)

    back_query, back_keys, back_values = lax.map(
        cross_backward,
        (
            blocked(cross_query),
            blocked(cross_keys),
            blocked(cross_values),
            blocked(split_heads(d_cross_mix)),
            cross_total,
        ),
    )
    d_query_cross = back_query.reshape(example_count, seq_full, inner_local)
    d_keys_cross = back_keys.reshape(example_count, memory_len, inner_local)
    d_values_cross = back_values.reshape(example_count, memory_len, inner_local)
    grad_cross = jnp.stack(
        [
            product("esd,esf->edf", normed_b, d_query_cross),
            product("emd,emf->edf", memory_full, d_keys_cross),
            product("emd,emf->edf", memory_full, d_values_cross),
        ],
        1,
    )
    d_normed_b = product("esf,df->esd", d_query_cross, proj_in[3])
    memory_part = product("emf,df->emd", d_keys_cross, proj_in[4]) + product(
        "emf,df->emd", d_values_cross, proj_in[5]
    )
    d_rows_full, d_gain_full = norm_back(rows_b, scale_b, 1, d_normed_b)
    d_rows_b, grad_gain_b, memory_grad = (
        lax.psum_scatter(
            d_rows_full.astype(jnp.bfloat16), "tensor", scatter_dimension=1, tiled=True
        ).astype(jnp.float32),
        lax.psum_scatter(
            d_gain_full.astype(jnp.bfloat16), "tensor", scatter_dimension=1, tiled=True
        ).astype(jnp.float32),
        lax.psum_scatter(
            memory_part.astype(jnp.bfloat16), "tensor", scatter_dimension=1, tiled=True
        ).astype(jnp.float32),
    )
    d_early = d_mid + d_rows_b
    d_self_top = output_grad(d_early)
    d_self_mix = product("esd,fd->esf", d_self_top, proj_out[0]).astype(narrow)
    grad_out_self = product("esf,esd->efd", self_mix, d_self_top)

    def self_backward(items):
        queries, key_rows, value_rows, d_mixture, row_total, bucket_ids, keep = items
        onehot, bias_add = lookup(bucket_ids, position_bias)
        d_queries, d_keys, d_values, d_scores = attend_back(
            queries, key_rows, value_rows, d_mixture, row_total, bias_add, keep
        )
        d_table = jnp.einsum("ehst,estb->ebh", d_scores.astype(wide), onehot, precision=highest)
        return (d_queries, d_keys, d_values, d_table)

    back_query, back_keys, back_values, grad_bias = lax.map(
        self_backward,
        (
            blocked(self_query),
            blocked(self_keys),
            blocked(self_values),
            blocked(split_heads(d_self_mix)),
            self_total,
            blocked(buckets),
            blocked(keep_rows),
        ),
    )
    d_self_qkv = jnp.stack(
        [
            back_query.reshape(example_count, seq_full, inner_local),
            back_keys.reshape(example_count, seq_full, inner_local),
            back_values.reshape(example_count, seq_full, inner_local),
        ],
        0,
    )
    grad_self = product("esd,kesf->ekdf", normed_a, d_self_qkv)
    d_rows_a, grad_gain_a = input_grads(
        rows_a, scale_a, 0, product("kesf,kdf->esd", d_self_qkv, proj_in[:3])
    )
    tokens_grad = d_early + d_rows_a
    grad_in = jnp.concatenate([grad_self, grad_cross], 1)
    grad_out = jnp.stack([grad_out_self, grad_out_cross], 1)
    grad_gain = jnp.stack([grad_gain_a, grad_gain_b, grad_gain_c], 1)
    grad_bias = grad_bias.reshape(example_count, grad_bias.shape[2], heads_local)
    partial_value = jnp.sum(grad_in * grad_in, (1, 2, 3)) + jnp.sum(grad_out * grad_out, (1, 2, 3))
    partial_value = (
        partial_value + jnp.sum(grad_up * grad_up, (1, 2)) + jnp.sum(grad_down * grad_down, (1, 2))
    )
    partial_value = (
        partial_value
        + jnp.sum(grad_gain * grad_gain, (1, 2))
        + jnp.sum(grad_bias * grad_bias, (1, 2))
    )
    squares = lax.psum(partial_value, "tensor")
    example_norms = jnp.sqrt(squares + epsilon)
    norm_total = lax.psum(jnp.sum(example_norms), "dp")
    mean_norm = norm_total / (example_count * lax.axis_size("dp"))
    limits = jnp.sum(
        (task_groups[:, None] == jnp.arange(len(group_limits), dtype=jnp.int32))
        * jnp.asarray(group_limits, wide),
        1,
    )
    clip_weights = jnp.minimum(1.0 / mean_norm, limits / example_norms)
    sum_in = jnp.einsum("e,ekdf->kdf", clip_weights, grad_in, precision=highest)
    sum_out = jnp.einsum("e,ekfd->kfd", clip_weights, grad_out, precision=highest)
    sum_up = jnp.einsum("e,edf->df", clip_weights, grad_up, precision=highest)
    sum_down = jnp.einsum("e,efd->fd", clip_weights, grad_down, precision=highest)
    sum_gain = jnp.einsum("e,ekd->kd", clip_weights, grad_gain, precision=highest)
    sum_bias = jnp.einsum("e,ebh->bh", clip_weights, grad_bias, precision=highest)
    reduced_in, reduced_out, reduced_up, reduced_down = (
        lax.psum_scatter(sum_in.astype(jnp.bfloat16), "dp", scatter_dimension=1, tiled=True).astype(
            jnp.float32
        ),
        lax.psum_scatter(
            sum_out.astype(jnp.bfloat16), "dp", scatter_dimension=2, tiled=True
        ).astype(jnp.float32),
        lax.psum_scatter(sum_up.astype(jnp.bfloat16), "dp", scatter_dimension=0, tiled=True).astype(
            jnp.float32
        ),
        lax.psum_scatter(
            sum_down.astype(jnp.bfloat16), "dp", scatter_dimension=1, tiled=True
        ).astype(jnp.float32),
    )
    reduced_gain, reduced_bias = lax.psum((sum_gain, sum_bias), "dp")
    shrink = 1.0 / math.sqrt(example_count * lax.axis_size("dp"))
    gain_shard = lax.dynamic_slice_in_dim(
        gains, lax.axis_index("tensor") * gain_width, gain_width, 1
    )
    velocity_in, averaged_in, updated_in = stepper(
        weights_in, reduced_in * shrink, momentum_in, average_in, matrix_rate
    )
    velocity_out, averaged_out, updated_out = stepper(
        weights_out, reduced_out * shrink, momentum_out, average_out, output_rate
    )
    velocity_up, averaged_up, updated_up = stepper(
        weights_up, reduced_up * shrink, momentum_up, average_up, matrix_rate
    )
    velocity_down, averaged_down, updated_down = stepper(
        weights_down, reduced_down * shrink, momentum_down, average_down, matrix_rate
    )
    velocity_gain, averaged_gain, updated_gain = stepper(
        gain_shard, reduced_gain * shrink, momentum_gain, average_gain, small_rate
    )
    velocity_bias, averaged_bias, updated_bias = stepper(
        position_bias, reduced_bias * shrink, momentum_bias, average_bias, small_rate
    )
    return (
        output,
        tokens_grad,
        memory_grad,
        example_norms,
        velocity_in,
        averaged_in,
        updated_in,
        velocity_out,
        averaged_out,
        updated_out,
        velocity_up,
        averaged_up,
        updated_up,
        velocity_down,
        averaged_down,
        updated_down,
        velocity_gain,
        averaged_gain,
        updated_gain,
        velocity_bias,
        averaged_bias,
        updated_bias,
    )


def solution(mesh):
    return jax.shard_map(
        on_device,
        mesh=mesh,
        in_specs=(
            P("dp", "tensor", None),
            P("dp", "tensor", None),
            P("dp", "tensor", None),
            P("dp", None, None),
            P("dp", None, None),
            P("dp"),
            P(None, "dp", "tensor"),
            P(None, "tensor", "dp"),
            P("dp", "tensor"),
            P("tensor", "dp"),
            P(),
            P(None, "tensor"),
            P(None, "dp", "tensor"),
            P(None, "dp", "tensor"),
            P(None, "tensor", "dp"),
            P(None, "tensor", "dp"),
            P("dp", "tensor"),
            P("dp", "tensor"),
            P("tensor", "dp"),
            P("tensor", "dp"),
            P(None, "tensor"),
            P(None, "tensor"),
            P(None, "tensor"),
            P(None, "tensor"),
        ),
        out_specs=(
            P("dp", "tensor", None),
            P("dp", "tensor", None),
            P("dp", "tensor", None),
            P("dp"),
            P(None, "dp", "tensor"),
            P(None, "dp", "tensor"),
            P(None, "dp", "tensor"),
            P(None, "tensor", "dp"),
            P(None, "tensor", "dp"),
            P(None, "tensor", "dp"),
            P("dp", "tensor"),
            P("dp", "tensor"),
            P("dp", "tensor"),
            P("tensor", "dp"),
            P("tensor", "dp"),
            P("tensor", "dp"),
            P(None, "tensor"),
            P(None, "tensor"),
            P(None, "tensor"),
            P(None, "tensor"),
            P(None, "tensor"),
            P(None, "tensor"),
        ),
        check_vma=False,
    )
```

profile of v0, /device:TPU:0, one launch (start us, length us, event | category | flops | bytes accessed | tf_op | source)
XLA Modules:
  0.0 1659.9 jit_solution(10873623902681428442)
XLA Ops:
  9.8 32.5 %all_gather.35 = bf16[2,128,512]{1,0,2:T(2,128)(2,1)S(1)} all-gather(bf16[2,128,64]{1,0,2:T(2,128)(2,1)S(1)} %copy.223), channel_id=1, replica_groups=mesh['dp'=8,'tensor'=4] {'dp'}, dimensions={2}, use_global_device_ids=true | all-gather | bytes 294912 | tf_op jit(solution)/shard_map/all_gather | solution.py:129
  47.7 31.7 %all_gather.34 = bf16[6,512,128]{2,1,0:T(8,128)(2,1)S(1)} all-gather(bf16[6,64,128]{2,1,0:T(8,128)(2,1)S(1)} %convert_element_type.213), channel_id=1, replica_groups=mesh['dp'=8,'tensor'=4] {'dp'}, dimensions={1}, use_global_device_ids=true | all-gather | bytes 884736 | tf_op jit(solution)/shard_map/all_gather | solution.py:128
  79.5 3.4 fusion.114
  83.5 4.4 convert_bitcast_fusion.1
  89.7 57.1 %while.54 = (s32[]{:T(128)}, bf16[8,4,128,2,64]{2,4,3,1,0:T(8,128)(2,1)S(1)}, f32[8,4,2,128,1]{3,2,1,4,0:T(2,128)S(1)}, bf16[8,4,128,2,64]{2,4,3,1,0:T(8,128)(2,...) while((s32[]{:T(128)}, ...), condition=%wide.region_4.5_spmd, body=%wide.region_1.4_spmd.sunk | while | flops 87096320 | bytes 5212537 | solution.py:180
  147.8 4.7 fusion.174
  153.3 72.4 %reduce-scatter.21.cloned.1.call-done = f32[32,32,512]{2,1,0:T(8,128)} async-done(((f32[32,128,512]{2,1,0:T(8,128)}), f32[32,32,512]{2,1,0:T(8,128)}) %reduce-scatter.21.cloned.1.call-update) | async-done | bytes 2097168 | tf_op jit(solution)/shard_map/reduce_scatter | solution.py:144
  225.7 3.0 fusion.158
  229.2 104.2 %all-gather.10.cloned.1.call-done = bf16[32,512,512]{2,1,0:T(8,128)(2,1)} async-done(((bf16[32,128,512]{2,1,0:T(8,128)(2,1)}), bf16[32,512,512]{2,1,0:T(8,128)(2,1)}) %all-gather.10.cloned.1.call-update) | async-done | bytes 16777232 | tf_op jit(solution)/shard_map/all_gather | solution.py:133
  333.4 10.2 convert_bitcast_fusion
  343.6 6.3 fusion.200
  349.9 19.5 %all-gather.12.cloned.1.call-done = bf16[32,128,512]{2,1,0:T(8,128)(2,1)} async-done(((bf16[32,32,512]{2,1,0:T(8,128)(2,1)}), bf16[32,128,512]{2,1,0:T(8,128)(2,1)}) %all-gather.12.cloned.1.call-update) | async-done | bytes 4194320 | tf_op jit(solution)/shard_map/all_gather | solution.py:138
  369.4 3.1 fusion.123
  372.5 3.8 fusion.154
  376.5 31.4 %while.55 = (s32[]{:T(128)}, bf16[8,4,128,2,64]{2,4,3,1,0:T(8,128)(2,1)S(1)}, f32[8,4,2,128,1]{3,2,1,4,0:T(2,128)S(1)}, bf16[8,4,512,2,64]{2,4,3,1,0:T(8,128)(2,...) while((s32[]{:T(128)}, ...), condition=%wide.region_10.11_spmd, body=%wide.region_7.10_spmd.sunk | while | flops 138476544 | bytes 7637081 | solution.py:202
  409.3 6.0 fusion.171
  415.4 71.8 %reduce-scatter.23.cloned.1.call-done = f32[32,32,512]{2,1,0:T(8,128)} async-done(((f32[32,128,512]{2,1,0:T(8,128)}), f32[32,32,512]{2,1,0:T(8,128)}) %reduce-scatter.23.cloned.1.call-update) | async-done | bytes 2097168 | tf_op jit(solution)/shard_map/reduce_scatter | solution.py:144
  487.3 3.2 fusion.167
  493.1 31.4 %all_gather.40 = bf16[512,512]{0,1:T(8,128)(2,1)S(1)} all-gather(bf16[512,64]{0,1:T(8,128)(2,1)S(1)} %convert_element_type.228), channel_id=1, replica_groups=mesh['dp'=8,'tensor'=4] {'dp'}, dimensions={1}, use_global_device_ids=true | all-gather | bytes 589824 | tf_op jit(solution)/shard_map/all_gather | solution.py:131
  524.5 31.6 %all_gather.39 = bf16[512,512]{1,0:T(8,128)(2,1)S(1)} all-gather(bf16[64,512]{1,0:T(8,128)(2,1)S(1)} %convert_element_type.226), channel_id=1, replica_groups=mesh['dp'=8,'tensor'=4] {'dp'}, dimensions={0}, use_global_device_ids=true | all-gather | bytes 589824 | tf_op jit(solution)/shard_map/all_gather | solution.py:130
  556.1 3.1 fusion.132
  559.2 8.0 fusion.146
  567.2 9.8 fusion.113
  577.1 4.6 fusion.140
  581.7 3.7 fusion.137
  585.5 45.0 %reduce-scatter.27.cloned.1.call-done = bf16[32,32,512]{2,1,0:T(8,128)(2,1)} async-done(((bf16[32,128,512]{2,1,0:T(8,128)(2,1)}), bf16[32,32,512]{2,1,0:T(8,128)(2,1)}) %reduce-scatter.27.cloned.1.call-update) | async-done | bytes 1048592 | tf_op jit(solution)/shard_map/reduce_scatter | solution.py:160
  633.3 34.4 %all-gather.18.cloned.1.call-done = bf16[32,128,512]{2,1,0:T(8,128)(2,1)} async-done(((bf16[32,32,512]{2,1,0:T(8,128)(2,1)}), bf16[32,128,512]{2,1,0:T(8,128)(2,1)}) %all-gather.18.cloned.1.call-update) | async-done | bytes 4194320 | tf_op jit(solution)/shard_map/all_gather | solution.py:147
  667.7 3.7 convolution_convert_fusion.5
  671.7 67.0 %while.56 = (s32[]{:T(128)}, bf16[8,4,128,2,64]{2,4,3,1,0:T(8,128)(2,1)S(1)}, bf16[8,4,512,2,64]{2,4,3,1,0:T(8,128)(2,1)}, bf16[8,4,512,2,64]{2,4,3,1,0:T(8,128)...) while((s32[]{:T(128)}, ...), condition=%wide.region_18.19_spmd, body=%wide.region_16.18_spmd.sunk | while | flops 340655104 | bytes 19031152 | solution.py:234
  738.6 5.3 fusion.131
  744.0 3.8 fusion.128
  747.8 44.6 %reduce-scatter.29.cloned.1.call-done = bf16[32,32,512]{2,1,0:T(8,128)(2,1)} async-done(((bf16[32,128,512]{2,1,0:T(8,128)(2,1)}), bf16[32,32,512]{2,1,0:T(8,128)(2,1)}) %reduce-scatter.29.cloned.1.call-update) | async-done | bytes 1048592 | tf_op jit(solution)/shard_map/reduce_scatter | solution.py:261
  797.0 32.9 %all-gather.20.cloned.1.call-done = bf16[32,128,512]{2,1,0:T(8,128)(2,1)} async-done(((bf16[32,32,512]{2,1,0:T(8,128)(2,1)}), bf16[32,128,512]{2,1,0:T(8,128)(2,1)}) %all-gather.20.cloned.1.call-update) | async-done | bytes 4194320 | tf_op jit(solution)/shard_map/all_gather | solution.py:147
  829.9 3.7 convolution_convert_fusion.4
  837.3 111.8 %while.57 = (s32[]{:T(128)}, bf16[8,4,128,2,64]{2,4,3,1,0:T(8,128)(2,1)}, bf16[8,4,128,2,64]{2,4,3,1,0:T(8,128)(2,1)}, bf16[8,4,128,2,64]{2,4,3,1,0:T(8,128)(2,1...) while((s32[]{:T(128)}, ...), condition=%wide.region_23.24_spmd, body=%wide.region_21.23_spmd.sunk | while | flops 148438016 | bytes 9401757 | solution.py:285
  954.8 9.1 fusion.122
  964.7 9.7 fusion.162
  975.7 16.7 %multiply_reduce_fusion.5 = (f32[32]{0:T(128)}, f32[32,512,512]{2,1,0:T(8,128)}) fusion(bf16[32,128,512]{2,1,0:T(8,128)(2,1)} %copy-done.10, bf16[32,128,512]{2,1,0:T(8,128)(2,1)} %all-gather.14.cloned.1.call-done, f32[512]{0:T(512)S(1)} %bitcast.469, f32[32,128]{1,0:T(8,128)S(1)} %get-tuple-element.363), kind=kOutput, calls=%fused_computation.138 | convolution fusion | flops 2172649472 | bytes 41961600 | tf_op jit(solution)/shard_map/esd,esf->edf/dot_general | solution.py:125
  992.4 19.3 %multiply_reduce_fusion.4 = (f32[32]{0:T(128)}, f32[32,512,512]{2,1,0:T(8,128)}) fusion(bf16[32,128,512]{2,1,0:T(8,128)(2,1)S(1)} %copy-done.9, f32[32,128,512]{2,1,0:T(8,128)} %fusion.146), kind=kOutput, calls=%fused_computation.137 | convolution fusion | flops 2183135232 | bytes 46137472 | tf_op jit(solution)/shard_map/esf,esd->efd/dot_general | solution.py:125
  1012.6 7.2 convolution_bitcast_fusion.2
  1019.8 4.2 convolution_bitcast_fusion.1
  1024.1 14.3 convolution_bitcast_fusion.4
  1039.6 7.9 convolution_bitcast_fusion.5
  1049.3 14.8 convolution_bitcast_fusion
  1064.1 34.5 %pad_maximum_fusion = (f32[32,6,512,128]{2,3,1,0:T(8,128)}, f32[32]{0:T(128)S(1)}) fusion(f32[32,1,512,128]{2,3,1,0:T(8,128)} %convolution_bitcast_fusion.4, f32[32,1,512,128]{2,3,1,0:T(8,128)} %convolution_bitcast_fusion.5, f32[32,1,512,128]{2,3,1,0:T(8,128)} %convolution_bitcast_fusion.1, f32[32,3,512,128]{2,3,1,0:T(8,128)} %convolution_bitcast_fusion), kind=kLoop, calls=%fused_computation.131 | loop fusion | flops 62914528 | bytes 100663424 | tf_op jit(solution)/shard_map/concatenate | solution.py:310
  1098.6 49.7 %copy.187 = f32[32,6,512,128]{3,0,2,1:T(8,128)} copy(f32[32,6,512,128]{2,3,1,0:T(8,128)} %get-tuple-element.347) | data formatting | bytes 100663296 | tf_op jit(solution)/shard_map/concatenate | solution.py:310
  1148.4 3.4 convolution_bitcast_fusion.3
  1151.8 10.9 pad_maximum_fusion.1
  1163.7 6.4 psum.28
  1170.7 22.6 %psum.29 = f32[]{:T(128)} all-reduce(f32[]{:T(128)} %get-tuple-element.337), channel_id=1, replica_groups=mesh['dp'=8,'tensor'=4] {'dp'}, use_global_device_ids=true, to_apply=%region_41.42 | all-reduce | flops 1 | bytes 8 | tf_op jit(solution)/shard_map/psum | solution.py:325
  1194.0 22.4 %fusion.105 = bf16[1,2,128,512]{3,0,2,1:T(2,128)(2,1)S(1)} fusion(f32[32,2,128,512]{3,2,0,1:T(8,128)} %get-tuple-element.349, f32[32]{0:T(128)S(1)} %copy-done.43, f32[32]{0:T(128)S(1)} %get-tuple-element.338, f32[]{:T(128)S(6)} %div.34), kind=kOutput, calls=%fused_computation.143 | convolution fusion | flops 50331712 | bytes 17039620 | tf_op jit(solution)/shard_map/e,ekfd->kfd/dot_general | solution.py:334
  1217.5 43.2 %fusion.101 = bf16[1,512,512]{2,0,1:T(2,128)(2,1)S(1)} fusion(f32[32,512,512]{2,1,0:T(8,128)} %get-tuple-element.373, f32[32]{0:T(128)S(1)} %copy-done.43, f32[32]{0:T(128)S(1)} %get-tuple-element.338, f32[]{:T(128)S(6)} %div.34), kind=kOutput, calls=%fused_computation.135 | convolution fusion | flops 100663360 | bytes 34078980 | tf_op jit(solution)/shard_map/e,edf->df/dot_general | solution.py:335
  1261.7 43.5 %fusion.99 = bf16[1,512,512]{2,0,1:T(2,128)(2,1)S(1)} fusion(f32[32,512,512]{2,1,0:T(8,128)} %get-tuple-element.371, f32[32]{0:T(128)S(1)} %copy-done.43, f32[32]{0:T(128)S(1)} %get-tuple-element.338, f32[]{:T(128)S(6)} %div.34), kind=kOutput, calls=%fused_computation.133 | convolution fusion | flops 100663360 | bytes 34078980 | tf_op jit(solution)/shard_map/e,efd->fd/dot_general | solution.py:336
  1307.6 27.9 %fusion.184 = f32[1,6,512,128]{3,0,2,1:T(1,128)S(1)} fusion(f32[32,6,512,128]{3,0,2,1:T(8,128)} %copy.187, f32[32]{0:T(128)S(1)} %copy-done.43, f32[32]{0:T(128)S(1)} %get-tuple-element.338, f32[]{:T(128)S(6)} %div.34), kind=kOutput, calls=%fused_computation.291 | convolution fusion | flops 150995008 | bytes 51904772 | tf_op jit(solution)/shard_map/e,ekdf->kdf/dot_general | solution.py:333
  1336.6 7.0 fusion.119
  1343.7 18.1 %fusion.169 = f32[32,512,512]{2,1,0:T(8,128)} fusion(bf16[32,512,128]{1,2,0:T(8,128)(2,1)} %bitcast.437, bf16[6,512,128]{2,1,0:T(8,128)(2,1)} %copy-done.23), kind=kOutput, calls=%fused_computation.244 | convolution fusion | flops 2147483648 | bytes 37879808 | tf_op jit(solution)/shard_map/emf,df->emd/dot_general | solution.py:125
  1361.9 19.1 %add_convert_fusion = bf16[32,512,512]{2,1,0:T(8,128)(2,1)} fusion(f32[32,512,512]{2,1,0:T(8,128)} %fusion.169, bf16[32,512,128]{1,2,0:T(8,128)(2,1)S(1)} %bitcast.440, bf16[6,512,128]{2,1,0:T(8,128)(2,1)} %copy-done.23), kind=kOutput, calls=%fused_computation.139 | convolution fusion | flops 2164260864 | bytes 54657024 | tf_op jit(solution)/shard_map/emf,df->emd/dot_general | solution.py:125
  1382.6 4.4 add_convert_fusion.1
  1387.9 17.2 %all-reduce = (f32[3,128]{1,0:T(4,128)S(1)}, f32[32,2]{0,1:T(2,128)S(1)}) all-reduce(f32[3,128]{1,0:T(4,128)S(1)} %bitcast.487, f32[32,2]{0,1:T(2,128)S(1)} %bitcast.488), channel_id=1, replica_groups=mesh['dp'=8,'tensor'=4] {'dp'}, use_global_device_ids=true, to_apply=%region_47.48 | all-reduce | flops 448 | bytes 3584 | tf_op jit(solution)/shard_map/psum | solution.py:353
  1412.9 57.5 %reduce-scatter.35.cloned.1.call-done = bf16[6,64,128]{2,1,0:T(8,128)(2,1)} async-done(((bf16[6,512,128]{2,1,0:T(8,128)(2,1)}), bf16[6,64,128]{2,1,0:T(8,128)(2,1)}) %reduce-scatter.35.cloned.1.call-update) | async-done | bytes 98320 | tf_op jit(solution)/shard_map/reduce_scatter | solution.py:340
  1472.4 44.8 %reduce-scatter.31.cloned.1.call-done = bf16[32,32,512]{2,1,0:T(8,128)(2,1)} async-done(((bf16[32,128,512]{2,1,0:T(8,128)(2,1)}), bf16[32,32,512]{2,1,0:T(8,128)(2,1)}) %reduce-scatter.31.cloned.1.call-update) | async-done | bytes 1048592 | tf_op jit(solution)/shard_map/reduce_scatter | solution.py:160
  1517.2 3.8 convert_add_fusion
  1521.0 124.9 %reduce-scatter.33.cloned.1.call-done = bf16[32,128,512]{2,1,0:T(8,128)(2,1)} async-done(((bf16[32,512,512]{2,1,0:T(8,128)(2,1)}), bf16[32,128,512]{2,1,0:T(8,128)(2,1)}) %reduce-scatter.33.cloned.1.call-update) | async-done | bytes 4194320 | tf_op jit(solution)/shard_map/reduce_scatter | solution.py:267
  1645.9 6.7 convert_element_type.243
  (477 shorter events, 325.6 us)
Async XLA Ops:
  7.2 72.3 %all-gather.8.cloned.1.call-start = ((), (), s32[]{:S(2)}) async-start(), calls=%async_computation.14 | async-start | bytes 5242880 | tf_op jit(solution)/shard_map/all_gather | solution.py:138
  7.9 217.8 %reduce-scatter.21.cloned.1.call-start = ((), (), s32[]{:S(2)}) async-start(), calls=%async_computation.15 | async-start | bytes 10485760 | tf_op jit(solution)/shard_map/reduce_scatter | solution.py:144
  47.7 41.7 %copy-start.38 = (f32[1,512]{1,0:T(1,128)}, f32[1,512]{1,0:T(1,128)S(1)}, u32[]{:S(2)}) copy-start(f32[1,512]{1,0:T(1,128)S(1)} %get-tuple-element.366) | copy-start | bytes 6148
  79.5 9.9 copy-start.23
  83.5 6.2 copy-start.47
  152.5 73.3 %copy-start.8 = (bf16[32,32,512]{2,1,0:T(8,128)(2,1)S(1)}, bf16[32,32,512]{2,1,0:T(8,128)(2,1)}, u32[]{:S(2)}) copy-start(bf16[32,32,512]{2,1,0:T(8,128)(2,1)} %param.33) | copy-start | bytes 3145732
  152.5 76.5 %copy-start.25 = (bf16[1,128,512]{1,0,2:T(2,128)(2,1)S(1)}, bf16[1,128,512]{1,0,2:T(2,128)(2,1)}, u32[]{:S(2)}) copy-start(bf16[1,128,512]{1,0,2:T(2,128)(2,1)} %get-tuple-element.356) | copy-start | bytes 393220
  152.5 180.9 %copy-start.24 = (bf16[6,512,128]{2,1,0:T(8,128)(2,1)S(1)}, bf16[6,512,128]{2,1,0:T(8,128)(2,1)}, u32[]{:S(2)}) copy-start(bf16[6,512,128]{2,1,0:T(8,128)(2,1)} %copy-done.23) | copy-start | bytes 2359300
  152.5 180.8 %all-gather.10.cloned.1.call-start = ((), (), s32[]{:S(2)}) async-start(), calls=%async_computation.16 | async-start | bytes 20971520 | tf_op jit(solution)/shard_map/all_gather | solution.py:133
  153.3 216.1 %all-gather.12.cloned.1.call-start = ((), (), s32[]{:S(2)}) async-start(), calls=%async_computation.17 | async-start | bytes 5242880 | tf_op jit(solution)/shard_map/all_gather | solution.py:138
  228.7 258.5 %reduce-scatter.23.cloned.1.call-start = ((), (), s32[]{:S(2)}) async-start(), calls=%async_computation.18 | async-start | bytes 10485760 | tf_op jit(solution)/shard_map/reduce_scatter | solution.py:144
  409.3 77.9 %copy-start.4 = (f32[32,32,512]{2,1,0:T(8,128)S(1)}, f32[32,32,512]{2,1,0:T(8,128)}, u32[]{:S(2)}) copy-start(f32[32,32,512]{2,1,0:T(8,128)} %reduce-scatter.21.cloned.1.call-done) | copy-start | bytes 6291460
  415.4 140.7 %all-gather.14.cloned.1.call-start = ((), (), s32[]{:S(2)}) async-start(), calls=%async_computation.19 | async-start | bytes 5242880 | tf_op jit(solution)/shard_map/all_gather | solution.py:138
  490.5 76.8 %all-gather.16.cloned.1.call-start = ((), (), s32[]{:S(2)}) async-start(), calls=%async_computation.21 | async-start | bytes 5242880 | tf_op jit(solution)/shard_map/all_gather | solution.py:147
  491.2 139.2 %reduce-scatter.27.cloned.1.call-start = ((), (), s32[]{:S(2)}) async-start(), calls=%async_computation.22 | async-start | bytes 5242880 | tf_op jit(solution)/shard_map/reduce_scatter | solution.py:160
  524.5 42.8 %copy-start.27 = (bf16[512,512]{0,1:T(8,128)(2,1)}, bf16[512,512]{0,1:T(8,128)(2,1)S(1)}, u32[]{:S(2)}) copy-start(bf16[512,512]{0,1:T(8,128)(2,1)S(1)} %all_gather.40) | copy-start | bytes 1572868
  567.2 9.8 copy-start
  581.7 48.8 %copy-start.6 = (bf16[32,32,512]{2,1,0:T(8,128)(2,1)S(1)}, bf16[32,32,512]{2,1,0:T(8,128)(2,1)}, u32[]{:S(2)}) copy-start(bf16[32,32,512]{2,1,0:T(8,128)(2,1)} %param.35) | copy-start | bytes 3145732
  585.4 82.3 %all-gather.18.cloned.1.call-start = ((), (), s32[]{:S(2)}) async-start(), calls=%async_computation.23 | async-start | bytes 5242880 | tf_op jit(solution)/shard_map/all_gather | solution.py:147
  633.1 159.3 %reduce-scatter.29.cloned.1.call-start = ((), (), s32[]{:S(2)}) async-start(), calls=%async_computation.24 | async-start | bytes 5242880 | tf_op jit(solution)/shard_map/reduce_scatter | solution.py:261
  738.6 9.1 copy-start.16
  744.0 48.5 %copy-start.11 = (bf16[32,32,512]{2,1,0:T(8,128)(2,1)S(1)}, bf16[32,32,512]{2,1,0:T(8,128)(2,1)}, u32[]{:S(2)}) copy-start(bf16[32,32,512]{2,1,0:T(8,128)(2,1)} %reduce-scatter.27.cloned.1.call-done) | copy-start | bytes 3145732
  747.8 47.5 %copy-start.35 = (bf16[32,512]{1,0:T(8,128)(2,1)S(1)}, bf16[32,512]{1,0:T(8,128)(2,1)}, u32[]{:S(2)}) copy-start(bf16[32,512]{1,0:T(8,128)(2,1)} %get-tuple-element.237) | copy-start | bytes 98308
  747.8 82.1 %all-gather.20.cloned.1.call-start = ((), (), s32[]{:S(2)}) async-start(), calls=%async_computation.25 | async-start | bytes 5242880 | tf_op jit(solution)/shard_map/all_gather | solution.py:147
  795.2 216.5 %reduce-scatter.47.cloned.1.call-start = ((), (), s32[]{:S(2)}) async-start(), calls=%async_computation.34 | async-start | bytes 163840
  796.1 251.5 %reduce-scatter.45.cloned.1.call-start = ((), (), s32[]{:S(2)}) async-start(), calls=%async_computation.33 | async-start | bytes 163840
  796.9 365.8 %reduce-scatter.43.cloned.1.call-start = ((), (), s32[]{:S(2)}) async-start(), calls=%async_computation.32 | async-start | bytes 163840
  837.3 117.5 %copy-start.31 = (f32[32,128]{1,0:T(8,128)S(1)}, f32[32,128]{1,0:T(8,128)}, u32[]{:S(2)}) copy-start(f32[32,128]{1,0:T(8,128)} %copy-done.30) | copy-start | bytes 49156
  837.3 117.5 %copy-start.39 = (f32[1,512]{1,0:T(1,128)S(1)}, f32[1,512]{1,0:T(1,128)}, u32[]{:S(2)}) copy-start(f32[1,512]{1,0:T(1,128)} %copy-done.38) | copy-start | bytes 6148
  949.1 14.8 copy-start.48
  950.7 13.2 copy-start.18
  952.7 11.2 copy-start.20
  954.8 9.1 copy-start.21
  964.7 416.4 %reduce-scatter.25.cloned.1.call-start = ((), (), s32[]{:S(2)}) async-start(), calls=%async_computation.20 | async-start | bytes 10485760 | tf_op jit(solution)/shard_map/reduce_scatter | solution.py:144
  974.5 433.2 %reduce-scatter.37.cloned.1.call-start = ((), (), s32[]{:S(2)}) async-start(), calls=%async_computation.29 | async-start | bytes 294912 | tf_op jit(solution)/shard_map/reduce_scatter | solution.py:343
  975.7 16.7 %copy-start.9 = (bf16[32,128,512]{2,1,0:T(8,128)(2,1)S(1)}, bf16[32,128,512]{2,1,0:T(8,128)(2,1)}, u32[]{:S(2)}) copy-start(bf16[32,128,512]{2,1,0:T(8,128)(2,1)} %all-gather.16.cloned.1.call-done) | copy-start | bytes 12582916
  1011.7 8.1 copy-start.17
  1012.6 7.2 copy-start.2
  1024.0 14.4 slice-start
  1024.0 14.4 slice-start.1
  1024.0 14.3 slice-start.2
  1024.0 15.5 slice-start.3
  1039.6 9.8 copy-start.19
  1039.6 9.8 copy-start.40
  1048.3 115.2 %copy-start.36 = (bf16[32,128]{1,0:T(8,128)(2,1)}, bf16[32,128]{1,0:T(8,128)(2,1)S(1)}, u32[]{:S(2)}) copy-start(bf16[32,128]{1,0:T(8,128)(2,1)S(1)} %copy.204) | copy-start | bytes 24580
  1098.6 49.8 %copy-start.13 = (bf16[8,4,128,2,64]{2,4,3,1,0:T(8,128)(2,1)S(1)}, bf16[8,4,128,2,64]{2,4,3,1,0:T(8,128)(2,1)}, u32[]{:S(2)}) copy-start(bf16[8,4,128,2,64]{2,4,3,1,0:T(8,128)(2,1)} %copy-done.12) | copy-start | bytes 3145732
  1151.8 11.9 copy-start.45
  1151.8 11.9 copy-start.46
  1151.8 42.2 %copy-start.43 = (f32[32]{0:T(128)S(1)}, f32[32]{0:T(128)}, u32[]{:S(2)}) copy-start(f32[32]{0:T(128)} %select_reduce_fusion) | copy-start | bytes 388
  1163.6 30.4 %copy-start.37 = (bf16[32,128]{1,0:T(8,128)(2,1)}, bf16[32,128]{1,0:T(8,128)(2,1)S(1)}, u32[]{:S(2)}) copy-start(bf16[32,128]{1,0:T(8,128)(2,1)S(1)} %copy.202) | copy-start | bytes 24580
  1170.7 217.1 %copy-start.42 = (f32[32]{0:T(128)}, f32[32]{0:T(128)S(1)}, u32[]{:S(2)}) copy-start(f32[32]{0:T(128)S(1)} %get-tuple-element.338) | copy-start | bytes 388
  1217.4 191.9 %reduce-scatter.39.cloned.1.call-start = ((), (), s32[]{:S(2)}) async-start(), calls=%async_computation.30 | async-start | bytes 589824 | tf_op jit(solution)/shard_map/reduce_scatter | solution.py:346
  1261.7 149.4 %reduce-scatter.41.cloned.1.call-start = ((), (), s32[]{:S(2)}) async-start(), calls=%async_computation.31 | async-start | bytes 589824 | tf_op jit(solution)/shard_map/reduce_scatter | solution.py:349
  1307.6 29.0 %copy-start.41 = (f32[32,128]{1,0:T(8,128)S(1)}, f32[32,128]{1,0:T(8,128)}, u32[]{:S(2)}) copy-start(f32[32,128]{1,0:T(8,128)} %get-tuple-element.234) | copy-start | bytes 49156
  1307.6 29.0 %copy-start.32 = (f32[32,128]{1,0:T(8,128)S(1)}, f32[32,128]{1,0:T(8,128)}, u32[]{:S(2)}) copy-start(f32[32,128]{1,0:T(8,128)} %copy-done.30) | copy-start | bytes 49156
  1307.6 29.0 %copy-start.34 = (f32[32,128]{1,0:T(8,128)S(1)}, f32[32,128]{1,0:T(8,128)}, u32[]{:S(2)}) copy-start(f32[32,128]{1,0:T(8,128)} %get-tuple-element.358) | copy-start | bytes 49156
  1307.6 162.9 %reduce-scatter.35.cloned.1.call-start = ((), (), s32[]{:S(2)}) async-start(), calls=%async_computation.28 | async-start | bytes 884736 | tf_op jit(solution)/shard_map/reduce_scatter | solution.py:340
  1336.5 180.6 %reduce-scatter.31.cloned.1.call-start = ((), (), s32[]{:S(2)}) async-start(), calls=%async_computation.26 | async-start | bytes 5242880 | tf_op jit(solution)/shard_map/reduce_scatter | solution.py:160
  1343.7 302.2 %reduce-scatter.33.cloned.1.call-start = ((), (), s32[]{:S(2)}) async-start(), calls=%async_computation.27 | async-start | bytes 20971520 | tf_op jit(solution)/shard_map/reduce_scatter | solution.py:267
  1343.7 18.1 %copy-start.3 = (bf16[8,4,512,2,64]{2,4,3,1,0:T(8,128)(2,1)S(1)}, bf16[8,4,512,2,64]{2,4,3,1,0:T(8,128)(2,1)}, u32[]{:S(2)}) copy-start(bf16[8,4,512,2,64]{2,4,3,1,0:T(8,128)(2,1)} %get-tuple-element.231) | copy-start | bytes 12582916
  1381.0 26.7 %copy-start.29 = (f32[2,128,64]{1,2,0:T(8,128)S(1)}, f32[2,128,64]{1,2,0:T(8,128)}, u32[]{:S(2)}) copy-start(f32[2,128,64]{1,2,0:T(8,128)} %param.40) | copy-start | bytes 196612
  1381.0 28.3 %copy-start.28 = (f32[64,512]{1,0:T(8,128)S(1)}, f32[64,512]{1,0:T(8,128)}, u32[]{:S(2)}) copy-start(f32[64,512]{1,0:T(8,128)} %param.41) | copy-start | bytes 393220
  1381.0 89.5 %copy-start.26 = (f32[6,64,128]{2,1,0:T(8,128)S(1)}, f32[6,64,128]{2,1,0:T(8,128)}, u32[]{:S(2)}) copy-start(f32[6,64,128]{2,1,0:T(8,128)} %param.39) | copy-start | bytes 589828
  1381.0 136.1 %copy-start.7 = (bf16[32,32,512]{2,1,0:T(8,128)(2,1)S(1)}, bf16[32,32,512]{2,1,0:T(8,128)(2,1)}, u32[]{:S(2)}) copy-start(bf16[32,32,512]{2,1,0:T(8,128)(2,1)} %param.35) | copy-start | bytes 3145732
  (12 other events, 39.1 us)
Sparse Core Ops, SparseCore 0:
  9.6 37.1 all-gather.7
  152.6 73.0 reduce-scatter.20
  227.4 105.9 all-gather.9
  334.9 34.4 all-gather.11
  415.5 71.6 reduce-scatter.22
  490.6 34.4 all-gather.13
  526.7 34.4 all-gather.15
  585.5 44.8 reduce-scatter.26
  633.2 34.4 all-gather.17
  747.9 44.4 reduce-scatter.28
  795.3 34.4 all-gather.19
  832.7 19.6 reduce-scatter.46
  855.5 19.5 reduce-scatter.44
  964.8 19.5 reduce-scatter.42
  987.0 71.7 reduce-scatter.24
  1217.6 58.0 reduce-scatter.36
  1278.8 60.8 reduce-scatter.38
  1343.3 60.9 reduce-scatter.40
  1408.2 62.2 reduce-scatter.34
  1473.6 43.5 reduce-scatter.30
  1519.7 126.0 reduce-scatter.32
where the time goes:
time: 1670 us; the launch traced here: 1660 us
  waiting for transfers between devices  654 us (39%)
  matrix products  570 us (34%)
  blocking collectives  173 us (10%)
  other arithmetic  122 us (7%)
  local copies, waits for them, and re-layouts  120 us (7%)
    dot_general x23, matrix products, product(): return jnp.einsum(form, left, right, preferred_element_type=wide)  208 us
    reduce_scatter x3, waiting for transfers between devices, block_output(): lax.psum_scatter(partial_value, 'tensor', scatter_dimension=1, tiled=True)  144 us
    reduce_scatter x1, waiting for transfers between devices, on_device(): lax.psum_scatter(memory_part.astype(jnp.bfloat16), 'tensor', scatter_dime...  125 us
    all_gather x1, waiting for transfers between devices, on_device(): memory_full = lax.all_gather(memory, 'tensor', axis=1, tiled=True)  104 us
    reduce_scatter x2, waiting for transfers between devices, input_grads(): lax.psum_scatter(d_rows.astype(jnp.bfloat16), 'tensor', scatter_dimension...  89.7 us
    all_gather x3, waiting for transfers between devices, output_grad(): return lax.all_gather(gradient.astype(narrow), 'tensor', axis=1, tiled=True)  67.3 us
    reduce_scatter x1, waiting for transfers between devices, on_device(): lax.psum_scatter(sum_in.astype(jnp.bfloat16), 'dp', scatter_dimension=1,...  57.5 us
    concatenate x1, local copies, waits for them, and re-layouts, on_device(): grad_in = jnp.concatenate([grad_self, grad_cross], 1)  49.7 us
  transfers between devices with their start and end apart: 21, of which 11 were waited for; matrix products, arithmetic and copies ran while one was open for 35% of the time, Pallas kernels for 0%

commit v1 on v0

v1 whole, which is shorter than its diff:
```python
import functools
import math

import jax
import jax.numpy as jnp
from jax import lax
from jax.experimental import pallas as pl
from jax.experimental.pallas import tpu as pltpu
from jax.sharding import PartitionSpec as P

epsilon = 1e-06
momentum_decay = 0.9
average_decay = 0.7
matrix_rate = 10.0
output_rate = 40.0
small_rate = 50.0
group_limits = (0.6, 0.85, 1.2, 1.7)
head_dim = 64
quad = 4
quad_width = quad * head_dim
dp_slots = 8
tensor_slots = 4
wide = jnp.float32
narrow = jnp.bfloat16
vmem_bytes = 58 * 2**20

core = ("tensor", 1)
row = ("tensor", 2)
side = ("dp", 1)
near = ("dp", 2)
far = ("dp", 4)
gather_orders = ((row, near, far, side, core), (row, side, near, far, core))
reduce_orders = (
    (core, side, row, near, far),
    (core, row, side, near, far),
    (core, near, far, side, row),
    (core, side, near, far, row),
)


def dot_nn(left, right):
    return lax.dot_general(left, right, (((1,), (0,)), ((), ())), preferred_element_type=wide)


def dot_nt(left, right):
    return lax.dot_general(left, right, (((1,), (1,)), ((), ())), preferred_element_type=wide)


def dot_tn(left, right):
    return lax.dot_general(left, right, (((0,), (0,)), ((), ())), preferred_element_type=wide)


def head_masks(dtype):
    lanes = lax.broadcasted_iota(jnp.int32, (1, quad_width), 1) // head_dim
    return [(lanes == head).astype(wide).astype(dtype) for head in range(quad)]


def stack_heads(block, masks):
    return jnp.concatenate([block * mask for mask in masks], 0)


def unstack_heads(block, masks):
    rows = block.shape[0] // quad
    total = block[:rows] * masks[0]
    for head in range(1, quad):
        total = total + block[head * rows : (head + 1) * rows] * masks[head]
    return total


def norm_scale(rows):
    return lax.rsqrt(jnp.mean(rows * rows, -1, keepdims=True) + epsilon)


def norm_back(rows, gain, d_normed):
    scaling = norm_scale(rows)
    weighted = d_normed * gain
    cubed = scaling * scaling * scaling
    d_rows = scaling * weighted - rows * cubed * jnp.mean(rows * weighted, -1, keepdims=True)
    return d_rows, d_normed * rows * scaling


def softmax_keys(scores):
    peak = jnp.max(scores, 0, keepdims=True)
    weights = jnp.exp(scores - peak)
    return weights * (1.0 / jnp.sum(weights, 0, keepdims=True))


def gram_squares(left, right_grams):
    return jnp.sum(dot_nt(left, left) * right_grams, 0, keepdims=True)


def fold_lanes(row_sums):
    width = row_sums.shape[1]
    total = row_sums[:, :128]
    for start in range(128, width, 128):
        total = total + row_sums[:, start : start + 128]
    return total


def slot_places(order, first_is_high):
    places = []
    count = len(order)
    for slot in range(1 << count):
        index = {"dp": 0, "tensor": 0}
        for stage, (axis, bit) in enumerate(order):
            place = count - 1 - stage if first_is_high else stage
            if (slot >> place) & 1:
                index[axis] |= bit
        places.append((index["dp"], index["tensor"]))
    return places


def start_weights(info, pieces, plans, held, sems):
    me_dp, me_tensor = info[0], info[1]
    for piece, (first, count, places), sem in zip(pieces, plans, sems):
        for slot, (dp_index, tensor_index) in enumerate(places):
            high = pl.multiple_of((dp_index ^ me_dp) * 64, 64)
            left = pl.multiple_of((tensor_index ^ me_tensor) * 128, 128)
            pltpu.make_async_copy(
                piece.at[slot],
                held.at[pl.ds(first, count), pl.ds(high, 64), pl.ds(left, 128)],
                sem,
            ).start()


def wait_weights(plans, held, sems):
    for (first, count, places), sem in zip(plans, sems):
        whole = held.at[pl.ds(first, count)]
        pltpu.make_async_copy(whole, whole, sem).wait()


def place_rows(info, parts, held):
    rows = parts[0].shape[1]
    for index, part in enumerate(parts):
        start = pl.multiple_of((info[2] ^ index) * rows, rows)
        held[:, pl.ds(start, rows), :] = part[...]


def split_rows(info, held, parts):
    rows = parts[0].shape[1]
    for index, part in enumerate(parts):
        start = pl.multiple_of((info[2] ^ index) * rows, rows)
        part[...] = held[:, pl.ds(start, rows), :].astype(part.dtype)


def self_forward_kernel(shards, plans, heads_local, *refs):
    refs = list(refs)

    def take(count):
        taken = refs[:count]
        del refs[:count]
        return taken

    (info,) = take(1)
    parts = take(shards)
    buckets, key_mask, gains, table = take(4)
    pieces = take(len(plans))
    rows_out, normed_out, qkv_out, weights_out, mix_out, mid_out = take(6)
    held, sems, rows_held, mix_held = take(4)
    sem_list = [sems.at[index] for index in range(len(plans))]

    @pl.when(pl.program_id(0) == 0)
    def _():
        start_weights(info, pieces, plans, held, sem_list)
        wait_weights(plans, held, sem_list)

    masks = head_masks(narrow)
    masks_wide = head_masks(wide)
    place_rows(info, parts, rows_held)
    rows_out[...] = rows_held[...]
    bundle, seq, width = rows_held.shape
    flat = rows_held[...].reshape(bundle * seq, width).astype(wide)
    normed = (flat * norm_scale(flat) * gains[0:1, :]).astype(narrow)
    normed_out[...] = normed.reshape(bundle, seq, width)
    for index in range(3):
        value = dot_nn(normed, held[index]).astype(narrow)
        qkv_out[index] = value.reshape(bundle, seq, width)
    for example in range(bundle):
        code = jnp.where(key_mask[example] > 0, buckets[example], -1).T
        safe = jnp.maximum(code, 0)
        code_all = jnp.concatenate([code] * quad, 1)
        for group in range(width // quad_width):
            columns = slice(group * quad_width, (group + 1) * quad_width)
            bias = []
            for head in range(group * quad, (group + 1) * quad):
                spot = ((head // heads_local) ^ info[2]) * heads_local + head % heads_local
                line = jnp.broadcast_to(table[pl.ds(spot, 1), :], (seq, 128))
                bias.append(jnp.take_along_axis(line, safe, axis=1))
            queries = stack_heads(qkv_out[0, example, :, columns], masks)
            scores = dot_nt(qkv_out[1, example, :, columns], queries) * (
                1.0 / math.sqrt(head_dim)
            ) + jnp.concatenate(bias, 1)
            weights = softmax_keys(jnp.where(code_all >= 0, scores, -1000000000.0))
            weights_out[example, group] = weights
            mixture = dot_tn(weights.astype(narrow), qkv_out[2, example, :, columns])
            mix_held[example, :, columns] = unstack_heads(mixture, masks_wide).astype(narrow)
    mix_out[...] = mix_held[...]
    mix = mix_held[...].reshape(bundle * seq, width)
    mid_out[...] = (flat + dot_nt(mix, held[3])).reshape(bundle, seq, width)


def cross_kernel(shards, plans, *refs):
    refs = list(refs)

    def take(count):
        taken = refs[:count]
        del refs[:count]
        return taken

    (info,) = take(1)
    memory_parts = take(shards)
    cotangent_parts = take(shards)
    mid_in, gains = take(2)
    pieces = take(len(plans))
    output_parts = take(shards)
    memory_grads = take(shards)
    (
        early_out,
        normed_b_out,
        d_query_out,
        d_keys_out,
        d_values_out,
        mix_out,
        d_mid_out,
        normed_c_out,
        d_hidden_out,
        active_out,
        d_top_out,
        d_gain_b_out,
        d_gain_c_out,
        squares_out,
    ) = take(14)
    held, sems, memory_held, keys_held, values_held, weights_held, rows_held, query_held = take(8)
    sem_list = [sems.at[index] for index in range(len(plans))]

    @pl.when(pl.program_id(0) == 0)
    def _():
        start_weights(info, pieces, plans, held, sem_list)
        wait_weights(plans, held, sem_list)

    masks = head_masks(narrow)
    masks_wide = head_masks(wide)
    scaling = 1.0 / math.sqrt(head_dim)
    bundle, seq, width = mid_in.shape
    memory_rows = memory_parts[0].shape[1]
    memory_len = memory_held.shape[1]
    groups = width // quad_width

    def flatten(block):
        return block.reshape(block.shape[0] * block.shape[1], block.shape[2])

    def unflatten(block):
        return block.reshape(bundle, block.shape[0] // bundle, block.shape[1])

    for index, part in enumerate(memory_parts):
        memory_held[:, index * memory_rows : (index + 1) * memory_rows, :] = part[...]
    place_rows(info, cotangent_parts, d_top_out)
    mid = flatten(mid_in[...])
    rows_b = mid.astype(narrow).astype(wide)
    normed_b = (rows_b * norm_scale(rows_b) * gains[1:2, :]).astype(narrow)
    normed_b_out[...] = unflatten(normed_b)
    query_held[...] = unflatten(dot_nn(normed_b, held[0]).astype(narrow))
    memory_flat = flatten(memory_held[...])
    keys_held[...] = unflatten(dot_nn(memory_flat, held[1]).astype(narrow))
    values_held[...] = unflatten(dot_nn(memory_flat, held[2]).astype(narrow))
    for example in range(bundle):
        for group in range(groups):
            columns = slice(group * quad_width, (group + 1) * quad_width)
            queries = stack_heads(query_held[example, :, columns], masks)
            scores = dot_nt(keys_held[example, :, columns], queries) * scaling
            weights = softmax_keys(scores)
            weights_held[example, group] = weights
            mixture = dot_tn(weights.astype(narrow), values_held[example, :, columns])
            mix_out[example, :, columns] = unstack_heads(mixture, masks_wide).astype(narrow)
    late = mid + dot_nt(flatten(mix_out[...]), held[3])
    rows_c = late.astype(narrow).astype(wide)
    normed_c = (rows_c * norm_scale(rows_c) * gains[2:3, :]).astype(narrow)
    normed_c_out[...] = unflatten(normed_c)
    d_top = flatten(d_top_out[...])
    total = late
    d_normed = jnp.zeros((bundle * seq, width), wide)
    up_grams = [jnp.zeros((seq, seq), wide) for _ in range(bundle)]
    down_grams = [jnp.zeros((seq, seq), wide) for _ in range(bundle)]
    slope = math.sqrt(2.0 / math.pi)
    for index in range(4):
        hidden = dot_nn(normed_c, held[4 + index])
        square = hidden * hidden
        bend = jnp.tanh(slope * hidden * (1.0 + 0.044715 * square))
        half = 0.5 * (1.0 + bend)
        active = (hidden * half).astype(narrow)
        steep = half + 0.5 * hidden * (1.0 - bend * bend) * (
            slope * (1.0 + (3.0 * 0.044715) * square)
        )
        total = total + dot_nt(active, held[8 + index])
        d_hidden = (dot_nn(d_top, held[8 + index]) * steep).astype(narrow)
        d_normed = d_normed + dot_nt(d_hidden, held[4 + index])
        active_out[index] = unflatten(active)
        d_hidden_out[index] = unflatten(d_hidden)
        for example in range(bundle):
            span = slice(example * seq, (example + 1) * seq)
            up_grams[example] += dot_nt(d_hidden[span], d_hidden[span])
            down_grams[example] += dot_nt(active[span], active[span])
    rows_held[...] = unflatten(total)
    split_rows(info, rows_held, output_parts)
    d_rows, d_gain_rows = norm_back(rows_c, gains[2:3, :], d_normed)
    d_gain_c = jnp.sum(unflatten(d_gain_rows), 1, keepdims=True)
    d_gain_c_out[...] = d_gain_c
    d_mid = d_top.astype(wide) + d_rows
    d_mid_low = d_mid.astype(narrow)
    d_mid_out[...] = unflatten(d_mid_low)
    d_mix = dot_nn(d_mid_low, held[3]).astype(narrow)
    squares = []
    for example in range(bundle):
        span = slice(example * seq, (example + 1) * seq)
        for group in range(groups):
            columns = slice(group * quad_width, (group + 1) * quad_width)
            keys = keys_held[example, :, columns]
            queries = stack_heads(query_held[example, :, columns], masks)
            d_mixes = stack_heads(d_mix[span, columns], masks)
            weights = weights_held[example, group]
            d_weights = dot_nt(values_held[example, :, columns], d_mixes)
            inner = jnp.sum(weights * d_weights, 0, keepdims=True)
            d_scores = (weights * (d_weights - inner)).astype(narrow)
            d_query_out[example, :, columns] = (
                unstack_heads(dot_tn(d_scores, keys), masks_wide) * scaling
            ).astype(narrow)
            d_keys_out[example, :, columns] = (dot_nn(d_scores, queries) * scaling).astype(narrow)
            d_values_out[example, :, columns] = dot_nn(weights.astype(narrow), d_mixes).astype(
                narrow
            )
        memory_grad = dot_nt(d_keys_out[example], held[1]) + dot_nt(d_values_out[example], held[2])
        for index, part in enumerate(memory_grads):
            part[example] = memory_grad[
                index * memory_rows : (index + 1) * memory_rows
            ].astype(part.dtype)
        d_query = d_query_out[example]
        mix = mix_out[example]
        square_sum = gram_squares(normed_b[span], dot_nt(d_query, d_query))
        square_sum += gram_squares(mix, dot_nt(d_mid_low[span], d_mid_low[span]))
        square_sum += gram_squares(normed_c[span], up_grams[example])
        square_sum += gram_squares(d_top[span], down_grams[example])
        for block in (d_keys_out, d_values_out):
            product = dot_tn(memory_held[example], block[example])
            square_sum += fold_lanes(jnp.sum(product * product, 0, keepdims=True))
        square_sum += fold_lanes(d_gain_c[example] * d_gain_c[example])
        squares.append(square_sum)
    d_normed_b = dot_nt(flatten(d_query_out[...]), held[0])
    d_rows_b, d_gain_rows = norm_back(rows_b, gains[1:2, :], d_normed_b)
    d_gain_b = jnp.sum(unflatten(d_gain_rows), 1, keepdims=True)
    d_gain_b_out[...] = d_gain_b
    for example in range(bundle):
        squares_out[example] = squares[example] + fold_lanes(
            d_gain_b[example] * d_gain_b[example]
        )
    early_out[...] = unflatten(d_mid + d_rows_b)


def self_backward_kernel(shards, plans, *refs):
    refs = list(refs)

    def take(count):
        taken = refs[:count]
        del refs[:count]
        return taken

    info, early_in, rows_in, normed_in, qkv_in, weights_in, mix_in = take(7)
    squares_in, buckets, gains = take(3)
    pieces = take(len(plans))
    tokens_grads = take(shards)
    d_qkv_out, d_early_out, d_gain_out, d_bias_out, squares_out = take(5)
    held, sems, rows_held = take(3)
    sem_list = [sems.at[index] for index in range(len(plans))]

    @pl.when(pl.program_id(0) == 0)
    def _():
        start_weights(info, pieces, plans, held, sem_list)
        wait_weights(plans, held, sem_list)

    masks = head_masks(narrow)
    masks_wide = head_masks(wide)
    scaling = 1.0 / math.sqrt(head_dim)
    bundle, seq, width = early_in.shape
    groups = width // quad_width
    bucket_count = d_bias_out.shape[2]

    def flatten(block):
        return block.reshape(block.shape[0] * block.shape[1], block.shape[2])

    def unflatten(block):
        return block.reshape(bundle, block.shape[0] // bundle, block.shape[1])

    early = flatten(early_in[...])
    d_early = early.astype(narrow)
    d_early_out[...] = unflatten(d_early)
    d_mix = dot_nn(d_early, held[3]).astype(narrow)
    squares = []
    for example in range(bundle):
        span = slice(example * seq, (example + 1) * seq)
        code = buckets[example].T
        for group in range(groups):
            columns = slice(group * quad_width, (group + 1) * quad_width)
            keys = qkv_in[1, example, :, columns]
            queries = stack_heads(qkv_in[0, example, :, columns], masks)
            d_mixes = stack_heads(d_mix[span, columns], masks)
            weights = weights_in[example, group]
            d_weights = dot_nt(qkv_in[2, example, :, columns], d_mixes)
            inner = jnp.sum(weights * d_weights, 0, keepdims=True)
            d_scores = (weights * (d_weights - inner)).astype(narrow)
            d_qkv_out[0, example, :, columns] = (
                unstack_heads(dot_tn(d_scores, keys), masks_wide) * scaling
            ).astype(narrow)
            d_qkv_out[1, example, :, columns] = (dot_nn(d_scores, queries) * scaling).astype(
                narrow
            )
            d_qkv_out[2, example, :, columns] = dot_nn(weights.astype(narrow), d_mixes).astype(
                narrow
            )
            d_wide = d_scores.astype(wide)
            for bucket in range(bucket_count):
                chosen = code == bucket
                for head in range(quad):
                    picked = jnp.where(chosen, d_wide[:, head * seq : (head + 1) * seq], 0.0)
                    d_bias_out[example, group * quad + head, pl.ds(bucket, 1), :] = jnp.sum(
                        picked, 0, keepdims=True
                    )
        grams = jnp.zeros((seq, seq), wide)
        for index in range(3):
            block = d_qkv_out[index, example]
            grams = grams + dot_nt(block, block)
        square_sum = gram_squares(normed_in[example], grams)
        square_sum += gram_squares(mix_in[example], dot_nt(d_early[span], d_early[span]))
        squares.append(square_sum)
    d_normed = dot_nt(flatten(d_qkv_out[0]), held[0])
    d_normed = d_normed + dot_nt(flatten(d_qkv_out[1]), held[1])
    d_normed = d_normed + dot_nt(flatten(d_qkv_out[2]), held[2])
    d_rows, d_gain_rows = norm_back(flatten(rows_in[...]).astype(wide), gains[0:1, :], d_normed)
    d_gain = jnp.sum(unflatten(d_gain_rows), 1, keepdims=True)
    d_gain_out[...] = d_gain
    for example in range(bundle):
        squares_out[example] = (
            squares[example]
            + squares_in[example]
            + fold_lanes(d_gain[example] * d_gain[example])
        )
    rows_held[...] = unflatten(early + d_rows)
    split_rows(info, rows_held, tokens_grads)


def pair_gradient_kernel(layouts, places, bundle_sizes, *refs):
    refs = list(refs)

    def take(count):
        taken = refs[:count]
        del refs[:count]
        return taken

    info, clip = take(2)
    unit_refs = [(take(lefts), take(rights)) for lefts, rights in layouts]
    out, scaled, tile = refs
    me_dp, me_tensor = info[0], info[1]
    for unit, (lefts, rights) in enumerate(unit_refs):
        total = None
        example = 0
        for left, right in zip(lefts, rights):
            count = left.shape[0]
            for index in range(count):
                scaled[index] = (left[index].astype(wide) * clip[example + index]).astype(narrow)
            example += count
            block = dot_tn(
                scaled[0:count].reshape(count * left.shape[1], left.shape[2]),
                right[...].reshape(count * left.shape[1], right.shape[-1]),
            )
            total = block if total is None else total + block
        tile[...] = total.astype(narrow)
        for slot, (dp_index, tensor_index) in enumerate(places):
            high = pl.multiple_of((dp_index ^ me_dp) * 64, 64)
            left_edge = pl.multiple_of((tensor_index ^ me_tensor) * 128, 128)
            out[slot, unit] = tile[pl.ds(high, 64), pl.ds(left_edge, 128)]


def memory_gradient_kernel(shards, chunks, places, steps, *refs):
    refs = list(refs)

    def take(count):
        taken = refs[:count]
        del refs[:count]
        return taken

    info, clip = take(2)
    memory_parts = [take(shards) for _ in range(chunks)]
    d_keys = take(chunks)
    d_values = take(chunks)
    out, scaled, total, tile = refs
    me_dp, me_tensor = info[0], info[1]
    step = pl.program_id(0)

    @pl.when(step == 0)
    def _():
        total[...] = jnp.zeros_like(total)

    for chunk in range(chunks):

        @pl.when(step // steps == chunk)
        def _(chunk=chunk):
            factor = clip[step]
            for index, part in enumerate(memory_parts[chunk]):
                rows = part.shape[1]
                scaled[index * rows : (index + 1) * rows, :] = (
                    part[0].astype(wide) * factor
                ).astype(narrow)
            total[0] += dot_tn(scaled[...], d_keys[chunk][0])
            total[1] += dot_tn(scaled[...], d_values[chunk][0])

    @pl.when(step == steps * chunks - 1)
    def _():
        for unit in range(2):
            tile[...] = total[unit].astype(narrow)
            for slot, (dp_index, tensor_index) in enumerate(places):
                high = pl.multiple_of((dp_index ^ me_dp) * 64, 64)
                left_edge = pl.multiple_of((tensor_index ^ me_tensor) * 128, 128)
                out[slot, unit] = tile[pl.ds(high, 64), pl.ds(left_edge, 128)]


def swap(value, axis, bit):
    size = lax.axis_size(axis)
    return lax.ppermute(value, axis, [(index, index ^ bit) for index in range(size)])


def gather_slots(shard, order):
    gathered = shard[None]
    for axis, bit in order:
        gathered = jnp.concatenate([gathered, swap(gathered, axis, bit)], 0)
    return gathered


def reduce_slots(slots, order):
    for axis, bit in order:
        half = slots.shape[0] // 2
        arrived = swap(slots[half:], axis, bit)
        slots = (slots[:half].astype(wide) + arrived.astype(wide)).astype(narrow)
    return slots[0]


def sum_everywhere(value):
    for axis in ("tensor", "dp"):
        bit = 1
        while bit < lax.axis_size(axis):
            value = value + swap(value, axis, bit)
            bit *= 2
    return value


def stepper(parameter, gradient, momentum, average, step_rate):
    velocity = momentum_decay * momentum + gradient
    updated = parameter - step_rate * (gradient + momentum_decay * velocity)
    averaged = average_decay * average + (1.0 - average_decay) * updated
    return (velocity, averaged, updated)


def on_device(
    tokens,
    memory,
    cotangent,
    buckets,
    key_mask,
    task_groups,
    weights_in,
    weights_out,
    weights_up,
    weights_down,
    gains,
    position_bias,
    momentum_in,
    average_in,
    momentum_out,
    average_out,
    momentum_up,
    average_up,
    momentum_down,
    average_down,
    momentum_gain,
    average_gain,
    momentum_bias,
    average_bias,
):
    shards = lax.axis_size("tensor")
    replicas = lax.axis_size("dp")
    me_tensor = lax.axis_index("tensor")
    me_dp = lax.axis_index("dp")
    width = tokens.shape[2]
    seq = buckets.shape[1]
    seq_rows = tokens.shape[1]
    memory_rows = memory.shape[1]
    memory_len = memory_rows * shards
    group_count = tokens.shape[0]
    local = group_count // shards
    chunks = 2 if local % 2 == 0 else 1
    per_chunk = local // chunks
    bundle = 2 if per_chunk % 2 == 0 else 1
    steps = per_chunk // bundle
    bucket_count, heads_local = position_bias.shape
    heads = heads_local * shards
    gain_width = momentum_gain.shape[1]
    staged = shards == tensor_slots and replicas == dp_slots

    slot_base = [me_dp, me_tensor] if staged else [0 * me_dp, 0 * me_tensor]
    kernel_info = jnp.stack(slot_base + [me_tensor]).astype(jnp.int32)

    def square_shards():
        high, across = weights_in.shape[1], weights_in.shape[2]
        split = lambda block: block.reshape(high, -1, across).transpose(1, 0, 2)
        return (
            weights_in.astype(narrow),
            weights_out.astype(narrow).transpose(0, 2, 1),
            split(weights_up.astype(narrow)),
            split(weights_down.astype(narrow).T),
        )

    shard_in, shard_out, shard_up, shard_down = square_shards()

    def gather_group(blocks):
        count = blocks.shape[0]
        if staged:
            half = count // 2
            pieces = [
                gather_slots(blocks[:half], gather_orders[0]),
                gather_slots(blocks[half:], gather_orders[1]),
            ]
            plans = [
                (0, half, slot_places(gather_orders[0], False)),
                (half, count - half, slot_places(gather_orders[1], False)),
            ]
            return pieces, plans
        whole = lax.all_gather(blocks, "dp", axis=1, tiled=True)
        whole = lax.all_gather(whole, "tensor", axis=2, tiled=True)
        whole = whole.reshape(count, dp_slots, 64, tensor_slots, 128).transpose(1, 3, 0, 2, 4)
        whole = whole.reshape(dp_slots * tensor_slots, count, 64, 128)
        places = [(slot // tensor_slots, slot % tensor_slots) for slot in range(32)]
        return [whole], [(0, count, places)]

    def exchange(value, start, count):
        found = []
        for index in range(shards):
            first = (me_tensor ^ index) * local + start
            block = lax.dynamic_slice_in_dim(value, first, count, 0)
            found.append(swap(block, "tensor", index) if index else block)
        return found

    table = jnp.pad(position_bias.T, ((0, 0), (0, 128 - bucket_count)))
    table_all = jnp.concatenate(
        [swap(table, "tensor", index) if index else table for index in range(shards)], 0
    )
    self_pieces, self_plans = gather_group(jnp.concatenate([shard_in[:3], shard_out[:1]], 0))
    token_parts = exchange(tokens, 0, local)
    cross_pieces, cross_plans = gather_group(jnp.concatenate([shard_in[3:6], shard_out[1:2]], 0))
    inner_pieces, inner_plans = gather_group(jnp.concatenate([shard_up, shard_down], 0))
    cross_pieces = cross_pieces + inner_pieces
    cross_plans = cross_plans + [
        (first + 4, count, places) for first, count, places in inner_plans
    ]
    memory_parts = [exchange(memory, chunk * per_chunk, per_chunk) for chunk in range(chunks)]
    cotangent_parts = exchange(cotangent, 0, local)
    bucket_mine = lax.dynamic_slice_in_dim(buckets, me_tensor * local, local, 0)
    mask_mine = lax.dynamic_slice_in_dim(key_mask, me_tensor * local, local, 0)
    groups_mine = lax.dynamic_slice_in_dim(task_groups, me_tensor * local, local, 0)

    smem = pl.BlockSpec(memory_space=pltpu.SMEM)
    anywhere = pl.BlockSpec(memory_space=pl.ANY)
    params = pltpu.CompilerParams(
        vmem_limit_bytes=vmem_bytes, dimension_semantics=("arbitrary",)
    )

    def part_spec(shape, offset=0, lead=None):
        rest = tuple(shape)
        zeros = (0,) * len(rest)
        if lead is None:
            return pl.BlockSpec((bundle,) + rest, lambda step: (step + offset,) + zeros)
        return pl.BlockSpec((lead, bundle) + rest, lambda step: (0, step + offset) + zeros)

    def whole_spec(shape):
        return pl.BlockSpec(tuple(shape), lambda step: (0,) * len(shape))

    def shaped(shape, dtype, lead=None):
        front = (per_chunk,) if lead is None else (lead, per_chunk)
        return jax.ShapeDtypeStruct(front + tuple(shape), dtype)

    groups = width // quad_width
    row_block = (seq, width)

    def self_forward(chunk):
        offset = chunk * steps
        kernel = functools.partial(self_forward_kernel, shards, self_plans, heads_local)
        return pl.pallas_call(
            kernel,
            grid=(steps,),
            in_specs=[smem]
            + [part_spec((seq_rows, width), offset)] * shards
            + [part_spec((seq, seq), offset)] * 2
            + [whole_spec(gains.shape), whole_spec(table_all.shape)]
            + [anywhere] * len(self_pieces),
            out_specs=[
                part_spec(row_block),
                part_spec(row_block),
                part_spec(row_block, lead=3),
                part_spec((groups, seq, quad * seq)),
                part_spec(row_block),
                part_spec(row_block),
            ],
            out_shape=[
                shaped(row_block, narrow),
                shaped(row_block, narrow),
                shaped(row_block, narrow, 3),
                shaped((groups, seq, quad * seq), wide),
                shaped(row_block, narrow),
                shaped(row_block, wide),
            ],
            scratch_shapes=[
                pltpu.VMEM((4, width, width), narrow),
                pltpu.SemaphoreType.DMA((len(self_pieces),)),
                pltpu.VMEM((bundle,) + row_block, narrow),
                pltpu.VMEM((bundle,) + row_block, narrow),
            ],
            compiler_params=params,
            name="self_forward",
            cost_estimate=pl.CostEstimate(
                flops=per_chunk * 400_000_000, bytes_accessed=per_chunk * 2_000_000, transcendentals=0
            ),
        )(
            kernel_info,
            *token_parts,
            bucket_mine,
            mask_mine,
            gains,
            table_all,
            *self_pieces,
        )

    def cross(chunk, mid):
        offset = chunk * steps
        kernel = functools.partial(cross_kernel, shards, cross_plans)
        gain_block = (1, width)
        return pl.pallas_call(
            kernel,
            grid=(steps,),
            in_specs=[smem]
            + [part_spec((memory_rows, width))] * shards
            + [part_spec((seq_rows, width), offset)] * shards
            + [part_spec(row_block), whole_spec(gains.shape)]
            + [anywhere] * len(cross_pieces),
            out_specs=[part_spec((seq_rows, width))] * shards
            + [part_spec((memory_rows, width))] * shards
            + [
                part_spec(row_block),
                part_spec(row_block),
                part_spec(row_block),
                part_spec((memory_len, width)),
                part_spec((memory_len, width)),
                part_spec(row_block),
                part_spec(row_block),
                part_spec(row_block),
                part_spec(row_block, lead=4),
                part_spec(row_block, lead=4),
                part_spec(row_block),
                part_spec(gain_block),
                part_spec(gain_block),
                part_spec((1, 128)),
            ],
            out_shape=[shaped((seq_rows, width), narrow)] * shards
            + [shaped((memory_rows, width), narrow if index else wide) for index in range(shards)]
            + [
                shaped(row_block, wide),
                shaped(row_block, narrow),
                shaped(row_block, narrow),
                shaped((memory_len, width), narrow),
                shaped((memory_len, width), narrow),
                shaped(row_block, narrow),
                shaped(row_block, narrow),
                shaped(row_block, narrow),
                shaped(row_block, narrow, 4),
                shaped(row_block, narrow, 4),
                shaped(row_block, narrow),
                shaped(gain_block, wide),
                shaped(gain_block, wide),
                shaped((1, 128), wide),
            ],
            scratch_shapes=[
                pltpu.VMEM((12, width, width), narrow),
                pltpu.SemaphoreType.DMA((len(cross_pieces),)),
                pltpu.VMEM((bundle, memory_len, width), narrow),
                pltpu.VMEM((bundle, memory_len, width), narrow),
                pltpu.VMEM((bundle, memory_len, width), narrow),
                pltpu.VMEM((bundle, groups, memory_len, quad * seq), wide),
                pltpu.VMEM((bundle,) + row_block, wide),
                pltpu.VMEM((bundle,) + row_block, narrow),
            ],
            compiler_params=params,
            name="cross",
            cost_estimate=pl.CostEstimate(
                flops=per_chunk * 8_000_000_000, bytes_accessed=per_chunk * 6_000_000, transcendentals=0
            ),
        )(kernel_info, *memory_parts[chunk], *cotangent_parts, mid, gains, *cross_pieces)

    def self_backward(chunk, early, rows, normed, qkv, weights, mix, squares):
        offset = chunk * steps
        kernel = functools.partial(self_backward_kernel, shards, self_plans)
        return pl.pallas_call(
            kernel,
            grid=(steps,),
            in_specs=[
                smem,
                part_spec(row_block),
                part_spec(row_block),
                part_spec(row_block),
                part_spec(row_block, lead=3),
                part_spec((groups, seq, quad * seq)),
                part_spec(row_block),
                part_spec((1, 128)),
                part_spec((seq, seq), offset),
                whole_spec(gains.shape),
            ]
            + [anywhere] * len(self_pieces),
            out_specs=[part_spec((seq_rows, width))] * shards
            + [
                part_spec(row_block, lead=3),
                part_spec(row_block),
                part_spec((1, width)),
                part_spec((heads, bucket_count, 128)),
                part_spec((1, 128)),
            ],
            out_shape=[
                shaped((seq_rows, width), narrow if index else wide) for index in range(shards)
            ]
            + [
                shaped(row_block, narrow, 3),
                shaped(row_block, narrow),
                shaped((1, width), wide),
                shaped((heads, bucket_count, 128), wide),
                shaped((1, 128), wide),
            ],
            scratch_shapes=[
                pltpu.VMEM((4, width, width), narrow),
                pltpu.SemaphoreType.DMA((len(self_pieces),)),
                pltpu.VMEM((bundle,) + row_block, wide),
            ],
            compiler_params=params,
            name="self_backward",
            cost_estimate=pl.CostEstimate(
                flops=per_chunk * 1_500_000_000, bytes_accessed=per_chunk * 3_000_000, transcendentals=0
            ),
        )(
            kernel_info,
            early,
            rows,
            normed,
            qkv,
            weights,
            mix,
            squares,
            bucket_mine,
            gains,
            *self_pieces,
        )

    span = range(chunks)
    first = [self_forward(chunk) for chunk in span]
    second = [cross(chunk, first[chunk][5]) for chunk in span]
    third = []
    for chunk in span:
        rows, normed, qkv, weights, mix, mid = first[chunk]
        tail = second[chunk][2 * shards :]
        third.append(self_backward(chunk, tail[0], rows, normed, qkv, weights, mix, tail[13]))

    def give_back(blocks_of, dtype, rows):
        whole = jnp.zeros((group_count, rows, width), dtype)
        for chunk in span:
            for index, block in enumerate(blocks_of(chunk)):
                arrived = swap(block, "tensor", index) if index else block
                place = (me_tensor ^ index) * local + chunk * per_chunk
                whole = lax.dynamic_update_slice_in_dim(whole, arrived.astype(dtype), place, 0)
        return whole

    output = give_back(lambda chunk: second[chunk][:shards], narrow, seq_rows)
    memory_grad = give_back(lambda chunk: second[chunk][shards : 2 * shards], wide, memory_rows)
    tokens_grad = give_back(lambda chunk: third[chunk][:shards], wide, seq_rows)

    tails = [second[chunk][2 * shards :] for chunk in span]
    ends = [third[chunk][shards:] for chunk in span]

    def joined(pieces):
        return jnp.concatenate(pieces, 0)

    grad_bias = jnp.sum(joined([end[3] for end in ends]), -1)
    squares = jnp.sum(joined([end[4] for end in ends]), (1, 2)) + jnp.sum(
        grad_bias * grad_bias, (1, 2)
    )
    norms_mine = jnp.sqrt(squares + epsilon)
    norm_total = sum_everywhere(jnp.full((8, 128), jnp.sum(norms_mine)))[0, 0]
    mean_norm = norm_total / (group_count * replicas)
    norm_parts = jnp.zeros((group_count,), wide)
    padded = jnp.broadcast_to(norms_mine[:, None], (local, 128))
    for index in range(shards):
        arrived = swap(padded, "tensor", index) if index else padded
        norm_parts = lax.dynamic_update_slice_in_dim(
            norm_parts, arrived[:, 0], (me_tensor ^ index) * local, 0
        )
    example_norms = norm_parts
    limits = jnp.sum(
        (groups_mine[:, None] == jnp.arange(len(group_limits), dtype=jnp.int32))
        * jnp.asarray(group_limits, wide),
        1,
    )
    clip_weights = jnp.minimum(1.0 / mean_norm, limits / norms_mine)

    grad_gain = jnp.concatenate(
        [
            joined([end[2] for end in ends]),
            joined([tail[11] for tail in tails]),
            joined([tail[12] for tail in tails]),
        ],
        1,
    )
    sum_gain = jnp.sum(clip_weights[:, None, None] * grad_gain, 0)
    sum_bias = jnp.sum(clip_weights[:, None, None] * grad_bias, 0)
    small = jnp.concatenate([sum_gain.reshape(-1), sum_bias.reshape(-1)])
    small = lax.psum(small.reshape(-1, 128), ("dp", "tensor")).reshape(-1)
    gain_total = small[: 3 * width].reshape(3, width)
    bias_total = small[3 * width :].reshape(heads, bucket_count).T

    slot_count = dp_slots * tensor_slots

    def places_of(order):
        if staged:
            return slot_places(order, True)
        return [(slot // tensor_slots, slot % tensor_slots) for slot in range(slot_count)]

    def pair_gradient(order, units):
        layouts = [(len(lefts), len(rights)) for lefts, rights, lead in units]
        operands, specs = [], []
        for lefts, rights, lead in units:
            for block in lefts:
                operands.append(block)
                specs.append(pl.BlockSpec(memory_space=pltpu.VMEM))
            for block in rights:
                operands.append(block)
                if lead is None:
                    specs.append(pl.BlockSpec(memory_space=pltpu.VMEM))
                else:
                    specs.append(
                        pl.BlockSpec(
                            (None,) + block.shape[1:], lambda step, lead=lead: (lead, 0, 0, 0)
                        )
                    )
        specs = [
            whole_spec(block.shape) if spec.memory_space is pltpu.VMEM else spec
            for block, spec in zip(operands, specs)
        ]
        return pl.pallas_call(
            functools.partial(pair_gradient_kernel, layouts, places_of(order), per_chunk),
            grid=(1,),
            in_specs=[smem, smem] + specs,
            out_specs=whole_spec((slot_count, 2, 64, 128)),
            out_shape=jax.ShapeDtypeStruct((slot_count, 2, 64, 128), narrow),
            scratch_shapes=[
                pltpu.VMEM((per_chunk, seq, width), narrow),
                pltpu.VMEM((width, width), narrow),
            ],
            compiler_params=params,
            name="pair_gradient",
            cost_estimate=pl.CostEstimate(
                flops=2_000_000_000, bytes_accessed=5_000_000, transcendentals=0
            ),
        )(kernel_info, clip_weights, *operands)

    def memory_gradient(order):
        def example_spec(rows, chunk):
            return pl.BlockSpec(
                (1, rows, width),
                lambda step: (jnp.clip(step - chunk * per_chunk, 0, per_chunk - 1), 0, 0),
            )

        operands, specs = [], []
        for chunk in span:
            for block in memory_parts[chunk]:
                operands.append(block)
                specs.append(example_spec(memory_rows, chunk))
        for place in (3, 4):
            for chunk in span:
                operands.append(tails[chunk][place])
                specs.append(example_spec(memory_len, chunk))
        return pl.pallas_call(
            functools.partial(
                memory_gradient_kernel, shards, chunks, places_of(order), per_chunk
            ),
            grid=(local,),
            in_specs=[smem, smem] + specs,
            out_specs=whole_spec((slot_count, 2, 64, 128)),
            out_shape=jax.ShapeDtypeStruct((slot_count, 2, 64, 128), narrow),
            scratch_shapes=[
                pltpu.VMEM((memory_len, width), narrow),
                pltpu.VMEM((2, width, width), wide),
                pltpu.VMEM((width, width), narrow),
            ],
            compiler_params=params,
            name="memory_gradient",
            cost_estimate=pl.CostEstimate(
                flops=5_000_000_000, bytes_accessed=12_000_000, transcendentals=0
            ),
        )(kernel_info, clip_weights, *operands)

    normed_a = [first[chunk][1] for chunk in span]
    mix_a = [first[chunk][4] for chunk in span]
    d_qkv = [end[0] for end in ends]
    d_early = [end[1] for end in ends]
    normed_b = [tail[1] for tail in tails]
    d_query_b = [tail[2] for tail in tails]
    mix_b = [tail[5] for tail in tails]
    d_mid = [tail[6] for tail in tails]
    normed_c = [tail[7] for tail in tails]
    d_hidden = [tail[8] for tail in tails]
    active = [tail[9] for tail in tails]
    d_top = [tail[10] for tail in tails]
    jobs = []
    for index in range(2):
        jobs.append(
            [(normed_c, d_hidden, 2 * index), (normed_c, d_hidden, 2 * index + 1)]
        )
    for index in range(2):
        jobs.append([(d_top, active, 2 * index), (d_top, active, 2 * index + 1)])
    jobs.append([(normed_a, d_qkv, 0), (normed_a, d_qkv, 1)])
    jobs.append([(normed_a, d_qkv, 2), (d_early, mix_a, None)])
    jobs.append([(normed_b, d_query_b, None), (d_mid, mix_b, None)])
    orders = [reduce_orders[index % 4] for index in range(8)]
    slots = [pair_gradient(orders[index], job) for index, job in enumerate(jobs)]
    slots.append(memory_gradient(orders[7]))

    shrink = 1.0 / math.sqrt(group_count * replicas)
    if staged:
        reduced = [reduce_slots(block, order) for block, order in zip(slots, orders)]
    else:
        reduced = []
        for block in slots:
            whole = block.reshape(dp_slots, tensor_slots, 2, 64, 128).transpose(2, 0, 3, 1, 4)
            whole = whole.reshape(2, width, width)
            whole = lax.psum_scatter(whole, "dp", scatter_dimension=1, tiled=True)
            reduced.append(lax.psum_scatter(whole, "tensor", scatter_dimension=2, tiled=True))
    reduced = [block.astype(wide) * shrink for block in reduced]

    def merge(pieces):
        blocks = jnp.concatenate(pieces, 0)
        count, high, across = blocks.shape
        return blocks.transpose(1, 0, 2).reshape(high, count * across)

    grad_in = jnp.stack(
        [
            reduced[4][0],
            reduced[4][1],
            reduced[5][0],
            reduced[6][0],
            reduced[7][0],
            reduced[7][1],
        ],
        0,
    )
    grad_out = jnp.stack([reduced[5][1].T, reduced[6][1].T], 0)
    grad_up = merge(reduced[:2])
    grad_down = merge(reduced[2:4]).T

    gain_start = me_tensor * gain_width
    gain_shard = lax.dynamic_slice_in_dim(gains, gain_start, gain_width, 1)
    gain_grad = lax.dynamic_slice_in_dim(gain_total, gain_start, gain_width, 1) * shrink
    bias_grad = (
        lax.dynamic_slice_in_dim(bias_total, me_tensor * heads_local, heads_local, 1) * shrink
    )
    velocity_in, averaged_in, updated_in = stepper(
        weights_in, grad_in, momentum_in, average_in, matrix_rate
    )
    velocity_out, averaged_out, updated_out = stepper(
        weights_out, grad_out, momentum_out, average_out, output_rate
    )
    velocity_up, averaged_up, updated_up = stepper(
        weights_up, grad_up, momentum_up, average_up, matrix_rate
    )
    velocity_down, averaged_down, updated_down = stepper(
        weights_down, grad_down, momentum_down, average_down, matrix_rate
    )
    velocity_gain, averaged_gain, updated_gain = stepper(
        gain_shard, gain_grad, momentum_gain, average_gain, small_rate
    )
    velocity_bias, averaged_bias, updated_bias = stepper(
        position_bias, bias_grad, momentum_bias, average_bias, small_rate
    )
    return (
        output,
        tokens_grad,
        memory_grad,
        example_norms,
        velocity_in,
        averaged_in,
        updated_in,
        velocity_out,
        averaged_out,
        updated_out,
        velocity_up,
        averaged_up,
        updated_up,
        velocity_down,
        averaged_down,
        updated_down,
        velocity_gain,
        averaged_gain,
        updated_gain,
        velocity_bias,
        averaged_bias,
        updated_bias,
    )


def solution(mesh):
    return jax.shard_map(
        on_device,
        mesh=mesh,
        in_specs=(
            P("dp", "tensor", None),
            P("dp", "tensor", None),
            P("dp", "tensor", None),
            P("dp", None, None),
            P("dp", None, None),
            P("dp"),
            P(None, "dp", "tensor"),
            P(None, "tensor", "dp"),
            P("dp", "tensor"),
            P("tensor", "dp"),
            P(),
            P(None, "tensor"),
            P(None, "dp", "tensor"),
            P(None, "dp", "tensor"),
            P(None, "tensor", "dp"),
            P(None, "tensor", "dp"),
            P("dp", "tensor"),
            P("dp", "tensor"),
            P("tensor", "dp"),
            P("tensor", "dp"),
            P(None, "tensor"),
            P(None, "tensor"),
            P(None, "tensor"),
            P(None, "tensor"),
        ),
        out_specs=(
            P("dp", "tensor", None),
            P("dp", "tensor", None),
            P("dp", "tensor", None),
            P("dp"),
            P(None, "dp", "tensor"),
            P(None, "dp", "tensor"),
            P(None, "dp", "tensor"),
            P(None, "tensor", "dp"),
            P(None, "tensor", "dp"),
            P(None, "tensor", "dp"),
            P("dp", "tensor"),
            P("dp", "tensor"),
            P("dp", "tensor"),
            P("tensor", "dp"),
            P("tensor", "dp"),
            P("tensor", "dp"),
            P(None, "tensor"),
            P(None, "tensor"),
            P(None, "tensor"),
            P(None, "tensor"),
            P(None, "tensor"),
            P(None, "tensor"),
        ),
        check_vma=False,
    )
```

time: 1670 us -> 537 us (0.32)
  matrix products: 570 us -> 0 us
  waiting for transfers between devices: 654 us -> 120 us
  Pallas kernels: 0 us -> 168 us
  blocking collectives: 173 us -> 38.1 us
  starting transfers between devices: 1.66 us -> 103 us
  other arithmetic: 122 us -> 36.7 us
  local copies, waits for them, and re-layouts: 120 us -> 61.6 us
    dot_general x165 -> x0, matrix products: 570 us -> none  [the longest x23 208 us: product(): return jnp.einsum(form, left, right, preferred_element_type=wide)]
    reduce_scatter x11 -> x0, waiting for transfers between devices: 461 us -> none  [the longest x3 144 us: block_output(): lax.psum_scatter(partial_value, 'tensor', scatter_dimension=1, tiled=True)]
    all_gather x7 -> x0, waiting for transfers between devices: 191 us -> none  [the longest x1 104 us: on_device(): memory_full = lax.all_gather(memory, 'tensor', axis=1, tiled=True)]
    pallas_call x0 -> x14, Pallas kernels: none -> 168 us  [the longest x2 72 us: cross(): pl.pallas_call(kernel, grid=(steps,), in_specs=[smem] + [part_spec((memor...]
    all_gather x4 -> x0, blocking collectives: 127 us -> none  [the longest x1 32.5 us: on_device(): lax.all_gather(weights_out.astype(narrow), 'dp', axis=2, tiled=True)]
    ppermute x0 -> x111, waiting for transfers between devices: none -> 120 us  [swap(): lax.ppermute(value, axis, [(index, index ^ bit) for index in range(size)])]
    ppermute x0 -> x111, starting transfers between devices: none -> 103 us  [swap(): lax.ppermute(value, axis, [(index, index ^ bit) for index in range(size)])]
    concatenate x1 -> x12, local copies, waits for them, and re-layouts: 49.7 us -> 6.26 us  [gather_slots(): gathered = jnp.concatenate([gathered, swap(gathered, axis, bit)], 0)]
  transfers between devices with their start and end apart: 21 -> 111, of which waited for: 11 -> 30; matrix products, arithmetic and copies ran while one was open for 35% -> 17% of each run, Pallas kernels for 0% -> 22%
where the time goes in v1:
time: 537 us; the launch traced here: 531 us
  Pallas kernels  168 us (31%)
  waiting for transfers between devices  120 us (22%)
  starting transfers between devices  103 us (19%)
  local copies, waits for them, and re-layouts  61.6 us (11%)
  blocking collectives  38.1 us (7%)
  other arithmetic  36.7 us (7%)
    ppermute x111, waiting for transfers between devices, swap(): lax.ppermute(value, axis, [(index, index ^ bit) for index in range(size)])  120 us
    ppermute x111, starting transfers between devices, swap(): lax.ppermute(value, axis, [(index, index ^ bit) for index in range(size)])  103 us
    pallas_call x2, Pallas kernels, cross(): pl.pallas_call(kernel, grid=(steps,), in_specs=[smem] + [part_spec((memor...  72 us
    psum x1, blocking collectives, on_device(): small = lax.psum(small.reshape(-1, 128), ('dp', 'tensor')).reshape(-1)  38.1 us
    pallas_call x2, Pallas kernels, self_backward(): pl.pallas_call(kernel, grid=(steps,), in_specs=[smem, part_spec(row_block...  33.9 us
    pallas_call x7, Pallas kernels, pair_gradient(): pl.pallas_call(functools.partial(pair_gradient_kernel, layouts, places_of...  32.2 us
    pallas_call x2, Pallas kernels, self_forward(): pl.pallas_call(kernel, grid=(steps,), in_specs=[smem] + [part_spec((seq_r...  18 us
    unnamed x205, local copies, waits for them, and re-layouts  17.8 us
  transfers between devices with their start and end apart: 111, of which 30 were waited for; matrix products, arithmetic and copies ran while one was open for 17% of the time, Pallas kernels for 22%

profile of v1, /device:TPU:0, one launch (start us, length us, event | category | flops | bytes accessed | tf_op | source)
XLA Modules:
  0.0 531.1 jit_solution(4730364081945880900)
XLA Ops:
  1.5 3.0 collective-permute-start.10
  7.1 2.0 collective-permute-start.17
  17.8 2.3 constant_dynamic-slice_fusion.7
  20.2 4.0 constant_dynamic-slice_fusion.3
  24.8 2.0 collective-permute-start.12
  26.8 2.0 collective-permute-start.37
  29.5 2.0 collective-permute-start.18
  36.4 2.0 collective-permute-start.38
  41.8 2.7 collective-permute-start.14
  50.6 2.1 collective-permute-done.19
  52.7 6.1 %collective-permute-start.34 = (bf16[4,4,64,128]{3,2,1,0:T(8,128)(2,1)S(1)}, bf16[4,4,64,128]{3,2,1,0:T(8,128)(2,1)S(1)}, u32[]{:S(2)}, u32[]{:S(2)}) collective-permute-start(bf16[4,4,64,128]{3,2,1,0:T(8,128)(2,1)S(1)} %pad_maximum_fusion.6), channel_id=1, source_target_pairs={{0,16},{4,20},{8,24},{12,28},{16,0},{20,4},{24,8},{28,12},{1,17},{... | collective-permute-start | bytes 786440 | tf_op jit(solution)/shard_map/ppermute | solution.py:526
  61.4 1.9 collective-permute-start.30
  66.8 26.2 %collective-permute-done.34 = bf16[4,4,64,128]{3,2,1,0:T(8,128)(2,1)S(1)} collective-permute-done((bf16[4,4,64,128]{3,2,1,0:T(8,128)(2,1)S(1)}, bf16[4,4,64,128]{3,2,1,0:T(8,128)(2,1)S(1)}, u32[]{:S(2)}, u32[]{:S(2)}) %collective-permute-start.34) | collective-permute-done | bytes 262176 | tf_op jit(solution)/shard_map/ppermute | solution.py:526
  95.4 3.3 collective-permute-done.20
  100.6 3.7 collective-permute-done.30
  104.8 6.5 %collective-permute-done.40 = bf16[8,4,64,128]{3,2,1,0:T(8,128)(2,1)S(1)} collective-permute-done((bf16[8,4,64,128]{3,2,1,0:T(8,128)(2,1)S(1)}, bf16[8,4,64,128]{3,2,1,0:T(8,128)(2,1)S(1)}, u32[]{:S(2)}, u32[]{:S(2)}) %collective-permute-start.40) | collective-permute-done | bytes 524320 | tf_op jit(solution)/shard_map/ppermute | solution.py:526
  120.7 6.4 %collective-permute-done.8.refs_4_ = bf16[8,32,512]{2,1,0:T(8,128)(2,1)S(1)} collective-permute-done((bf16[8,32,512]{2,1,0:T(8,128)(2,1)S(1)}, bf16[8,32,512]{2,1,0:T(8,128)(2,1)S(1)}, u32[]{:S(2)}, u32[]{:S(2)}) %collective-permute-start.8) | collective-permute-done | bytes 262176 | tf_op jit(solution)/shard_map/ppermute | solution.py:526
  127.8 9.2 %self_forward.3 = (bf16[4,128,512]{2,1,0:T(8,128)(2,1)}, bf16[4,128,512]{2,1,0:T(8,128)(2,1)}, bf16[3,4,128,512]{3,2,1,0:T(8,128)(2,1)}, f32[4,2,128,512]{3,2,1,...) custom-call(s32[3]{0:T(128)} %pad_add_fusion.refs_0_, bf16[8,32,512]{2,1,0:T(8,128)(2,1)} %get-tuple-element.204.refs_1_, ...), custom_call_target="tpu_custom_call" | custom-call | flops 1600000000 | bytes 8000000 | tf_op jit(solution)/shard_map/self_forward/pallas_call | solution.py:693
  139.5 8.9 %self_forward.2 = (bf16[4,128,512]{2,1,0:T(8,128)(2,1)}, bf16[4,128,512]{2,1,0:T(8,128)(2,1)}, bf16[3,4,128,512]{3,2,1,0:T(8,128)(2,1)}, f32[4,2,128,512]{3,2,1,...) custom-call(s32[3]{0:T(128)} %pad_add_fusion.refs_0_, bf16[8,32,512]{2,1,0:T(8,128)(2,1)} %get-tuple-element.204.refs_1_, ...), custom_call_target="tpu_custom_call" | custom-call | flops 1600000000 | bytes 8000000 | tf_op jit(solution)/shard_map/self_forward/pallas_call | solution.py:693
  151.7 17.0 %collective-permute-done.4.refs_7_ = bf16[8,32,512]{2,1,0:T(8,128)(2,1)S(1)} collective-permute-done((bf16[8,32,512]{2,1,0:T(8,128)(2,1)S(1)}, bf16[8,32,512]{2,1,0:T(8,128)(2,1)S(1)}, u32[]{:S(2)}, u32[]{:S(2)}) %collective-permute-start.4) | collective-permute-done | bytes 262176 | tf_op jit(solution)/shard_map/ppermute | solution.py:526
  168.7 3.9 collective-permute-done.5.refs_8_
  174.7 36.1 %cross.3 = (bf16[4,32,512]{2,1,0:T(8,128)(2,1)}, bf16[4,32,512]{2,1,0:T(8,128)(2,1)}, bf16[4,32,512]{2,1,0:T(8,128)(2,1)}, bf16[4,32,512]{2,1,0:T(8,128)(2,1)}, ...) custom-call(s32[3]{0:T(128)} %pad_add_fusion.refs_0_, ...), custom_call_target="tpu_custom_call" | custom-call | flops 32000000000 | bytes 24000000 | tf_op jit(solution)/shard_map/cross/pallas_call | solution.py:742
  210.9 16.9 %self_backward.3 = (f32[4,32,512]{2,1,0:T(8,128)}, bf16[4,32,512]{2,1,0:T(8,128)(2,1)}, bf16[4,32,512]{2,1,0:T(8,128)(2,1)}, bf16[4,32,512]{2,1,0:T(8,128)(2,1)}...) custom-call(s32[3]{0:T(128)} %pad_add_fusion.refs_0_, ...), custom_call_target="tpu_custom_call" | custom-call | flops 6000000000 | bytes 12000000 | tf_op jit(solution)/shard_map/self_backward/pallas_call | solution.py:806
  229.0 35.9 %cross.2 = (bf16[4,32,512]{2,1,0:T(8,128)(2,1)}, bf16[4,32,512]{2,1,0:T(8,128)(2,1)}, bf16[4,32,512]{2,1,0:T(8,128)(2,1)}, bf16[4,32,512]{2,1,0:T(8,128)(2,1)}, ...) custom-call(s32[3]{0:T(128)} %pad_add_fusion.refs_0_, ...), custom_call_target="tpu_custom_call" | custom-call | flops 32000000000 | bytes 24000000 | tf_op jit(solution)/shard_map/cross/pallas_call | solution.py:742
  264.9 17.0 %self_backward.2 = (f32[4,32,512]{2,1,0:T(8,128)}, bf16[4,32,512]{2,1,0:T(8,128)(2,1)}, bf16[4,32,512]{2,1,0:T(8,128)(2,1)}, bf16[4,32,512]{2,1,0:T(8,128)(2,1)}...) custom-call(s32[3]{0:T(128)} %pad_add_fusion.refs_0_, ...), custom_call_target="tpu_custom_call" | custom-call | flops 6000000000 | bytes 12000000 | tf_op jit(solution)/shard_map/self_backward/pallas_call | solution.py:806
  288.0 4.5 broadcast_in_dim.52
  303.1 3.0 collective-permute-done.68
  306.3 3.5 collective-permute-done.69
  310.5 3.9 collective-permute-done.70
  317.3 4.6 pair_gradient.12
  321.9 4.6 pair_gradient.13
  326.5 4.6 pair_gradient.10
  331.1 4.7 pair_gradient.11
  336.1 38.1 %psum.7 = f32[14,128]{1,0:T(8,128)S(1)} all-reduce(f32[14,128]{1,0:T(8,128)S(1)} %maximum_bitcast_fusion.2), channel_id=1, replica_groups=mesh['dp'=8,'tensor'=4] {'dp','tensor'}, use_global_device_ids=true, to_apply=%region_7.8 | all-reduce | flops 1792 | bytes 14336 | tf_op jit(solution)/shard_map/psum | solution.py:925
  374.3 1.9 slice.487
  378.7 4.6 pair_gradient.7
  383.3 4.6 pair_gradient.8
  387.9 1.9 slice.433
  389.7 4.6 pair_gradient.9
  394.4 1.9 slice.444
  397.2 12.1 %memory_gradient.1 = bf16[32,2,64,128]{3,2,1,0:T(8,128)(2,1)} custom-call(s32[3]{0:T(128)} %pad_add_fusion.refs_0_, f32[8]{0:T(128)} %get-tuple-element.277.refs_1_, bf16[4,128,512]{2,1,0:T(8,128)(2,1)} %get-tuple-element.200.refs_1_.refs_2_, bf16[4,128,512]{2,1,0:T(8,128)(2,1)} %copy-done.70, bf16[4,128,512]{2,1,0:T(8,128)(2,1)} %copy-done.71, ...), custom_call_target="tpu_custom_call" | custom-call | flops 5000000000 | bytes 12000000 | tf_op jit(solution)/shard_map/memory_gradient/pallas_call | solution.py:990
  413.3 2.5 collective-permute-start.54
  417.5 1.7 collective-permute-start.55
  421.4 2.1 collective-permute-done.55
  426.1 3.5 collective-permute-done.43
  434.8 2.3 collective-permute-done.49
  440.1 2.5 collective-permute-done.56
  444.6 2.1 convert_dynamic-update-slice_fusion.5
  447.7 2.1 convert_dynamic-update-slice_fusion.4
  449.9 2.2 convert_dynamic-update-slice_fusion.3
  454.7 2.7 collective-permute-done.61
  458.5 7.8 %collective-permute-done.62 = bf16[4,128,512]{2,1,0:T(8,128)(2,1)S(1)} collective-permute-done((bf16[4,128,512]{2,1,0:T(8,128)(2,1)S(1)}, bf16[4,128,512]{2,1,0:T(8,128)(2,1)S(1)}, u32[]{:S(2)}, u32[]{:S(2)}) %collective-permute-start.62) | collective-permute-done | bytes 524320 | tf_op jit(solution)/shard_map/ppermute | solution.py:526
  469.8 1.8 collective-permute-start.102
  478.6 1.7 collective-permute-start.82
  482.2 4.5 collective-permute-done.92
  488.8 1.9 collective-permute-start.108
  493.4 4.5 collective-permute-done.87
  501.4 2.1 collective-permute-start.88
  505.1 3.1 collective-permute-done.83
  508.3 2.1 collective-permute-start.99
  511.4 2.1 collective-permute-start.74
  513.7 1.8 collective-permute-start.105
  515.6 1.8 collective-permute-start.110
  522.1 1.8 collective-permute-start.85
  (569 shorter events, 141.0 us)
Async XLA Ops:
  1.5 23.3 %collective-permute-start.10 = (f32[2,128]{1,0:T(2,128)S(1)}, f32[2,128]{1,0:T(2,128)S(1)}, u32[]{:S(2)}, u32[]{:S(2)}) collective-permute-start(f32[2,128]{1,0:T(2,128)S(1)} %pad.4), channel_id=1, source_target_pairs={{0,2},{1,3},{2,0},{3,1},{4,6},{5,7},{6,4},{7,5},{8,10},{9,11},{10,... | collective-permute-start | bytes 3080 | tf_op jit(solution)/shard_map/ppermute | solution.py:526
  4.4 22.3 %collective-permute-start.11 = (f32[2,128]{1,0:T(2,128)S(1)}, f32[2,128]{1,0:T(2,128)S(1)}, u32[]{:S(2)}, u32[]{:S(2)}) collective-permute-start(f32[2,128]{1,0:T(2,128)S(1)} %pad.4), channel_id=1, source_target_pairs={{0,3},{1,2},{2,1},{3,0},{4,7},{5,6},{6,5},{7,4},{8,11},{9,10},{10,... | collective-permute-start | bytes 3080 | tf_op jit(solution)/shard_map/ppermute | solution.py:526
  4.4 22.4 %collective-permute-start.9 = (f32[2,128]{1,0:T(2,128)S(1)}, f32[2,128]{1,0:T(2,128)S(1)}, u32[]{:S(2)}, u32[]{:S(2)}) collective-permute-start(f32[2,128]{1,0:T(2,128)S(1)} %pad.4), channel_id=1, source_target_pairs={{0,1},{1,0},{2,3},{3,2},{4,5},{5,4},{6,7},{7,6},{8,9},{9,8},{10,11... | collective-permute-start | bytes 3080 | tf_op jit(solution)/shard_map/ppermute | solution.py:526
  7.1 22.3 %collective-permute-start.17 = (bf16[1,2,64,128]{3,2,1,0:T(8,128)(2,1)S(1)}, bf16[1,2,64,128]{3,2,1,0:T(8,128)(2,1)S(1)}, u32[]{:S(2)}, u32[]{:S(2)}) collective-permute-start(bf16[1,2,64,128]{3,2,1,0:T(8,128)(2,1)S(1)} %get-tuple-element.193), channel_id=1, source_target_pairs={{0,2},{1,3},{2,0},{3,1},{4,6},{5,7},{6,4},{7,5},{8,10},{9,11},{10,... | collective-permute-start | bytes 98312 | tf_op jit(solution)/shard_map/ppermute | solution.py:526
  9.7 21.8 %collective-permute-start.27 = (bf16[1,2,64,128]{3,2,1,0:T(8,128)(2,1)S(1)}, bf16[1,2,64,128]{3,2,1,0:T(8,128)(2,1)S(1)}, u32[]{:S(2)}, u32[]{:S(2)}) collective-permute-start(bf16[1,2,64,128]{3,2,1,0:T(8,128)(2,1)S(1)} %get-tuple-element.191), channel_id=1, source_target_pairs={{0,2},{1,3},{2,0},{3,1},{4,6},{5,7},{6,4},{7,5},{8,10},{9,11},{10,... | collective-permute-start | bytes 98312 | tf_op jit(solution)/shard_map/ppermute | solution.py:526
  26.8 9.5 %collective-permute-start.37 = (bf16[1,4,64,128]{3,2,1,0:T(8,128)(2,1)S(1)}, bf16[1,4,64,128]{3,2,1,0:T(8,128)(2,1)S(1)}, u32[]{:S(2)}, u32[]{:S(2)}) collective-permute-start(bf16[1,4,64,128]{3,2,1,0:T(8,128)(2,1)S(1)} %bitcast_bitcast_fusion.1), channel_id=1, source_target_pairs={{0,2},{1,3},{2,0},{3,1},{4,6},{5,7},{6,4},{7,5},{8,10},{9,11},{10,... | collective-permute-start | bytes 196616 | tf_op jit(solution)/shard_map/ppermute | solution.py:526
  29.5 10.2 %collective-permute-start.18 = (bf16[2,2,64,128]{3,2,1,0:T(8,128)(2,1)S(1)}, bf16[2,2,64,128]{3,2,1,0:T(8,128)(2,1)S(1)}, u32[]{:S(2)}, u32[]{:S(2)}) collective-permute-start(bf16[2,2,64,128]{3,2,1,0:T(8,128)(2,1)S(1)} %pad_maximum_fusion.16), channel_id=1, source_target_pairs={{0,4},{4,0},{8,12},{12,8},{16,20},{20,16},{24,28},{28,24},{1,5},{5... | collective-permute-start | bytes 196616 | tf_op jit(solution)/shard_map/ppermute | solution.py:526
  31.5 9.8 %collective-permute-start.13 = (bf16[2,2,64,128]{3,2,1,0:T(8,128)(2,1)S(1)}, bf16[2,2,64,128]{3,2,1,0:T(8,128)(2,1)S(1)}, u32[]{:S(2)}, u32[]{:S(2)}) collective-permute-start(bf16[2,2,64,128]{3,2,1,0:T(8,128)(2,1)S(1)} %pad_maximum_fusion.15), channel_id=1, source_target_pairs={{0,8},{4,12},{8,0},{12,4},{16,24},{20,28},{24,16},{28,20},{1,9},{5... | collective-permute-start | bytes 196616 | tf_op jit(solution)/shard_map/ppermute | solution.py:526
  36.4 11.8 %collective-permute-start.38 = (bf16[2,4,64,128]{3,2,1,0:T(8,128)(2,1)S(1)}, bf16[2,4,64,128]{3,2,1,0:T(8,128)(2,1)S(1)}, u32[]{:S(2)}, u32[]{:S(2)}) collective-permute-start(bf16[2,4,64,128]{3,2,1,0:T(8,128)(2,1)S(1)} %pad_maximum_fusion.14), channel_id=1, source_target_pairs={{0,4},{4,0},{8,12},{12,8},{16,20},{20,16},{24,28},{28,24},{1,5},{5... | collective-permute-start | bytes 393224 | tf_op jit(solution)/shard_map/ppermute | solution.py:526
  39.7 8.9 %collective-permute-start.33 = (bf16[2,4,64,128]{3,2,1,0:T(8,128)(2,1)S(1)}, bf16[2,4,64,128]{3,2,1,0:T(8,128)(2,1)S(1)}, u32[]{:S(2)}, u32[]{:S(2)}) collective-permute-start(bf16[2,4,64,128]{3,2,1,0:T(8,128)(2,1)S(1)} %pad_maximum_fusion.13), channel_id=1, source_target_pairs={{0,8},{4,12},{8,0},{12,4},{16,24},{20,28},{24,16},{28,20},{1,9},{5... | collective-permute-start | bytes 393224 | tf_op jit(solution)/shard_map/ppermute | solution.py:526
  41.3 11.4 %collective-permute-start.19 = (bf16[4,2,64,128]{3,2,1,0:T(8,128)(2,1)S(1)}, bf16[4,2,64,128]{3,2,1,0:T(8,128)(2,1)S(1)}, u32[]{:S(2)}, u32[]{:S(2)}) collective-permute-start(bf16[4,2,64,128]{3,2,1,0:T(8,128)(2,1)S(1)} %pad_maximum_fusion.10), channel_id=1, source_target_pairs={{0,8},{4,12},{8,0},{12,4},{16,24},{20,28},{24,16},{28,20},{1,9},{5... | collective-permute-start | bytes 393224 | tf_op jit(solution)/shard_map/ppermute | solution.py:526
  41.8 17.0 %collective-permute-start.14 = (bf16[4,2,64,128]{3,2,1,0:T(8,128)(2,1)S(1)}, bf16[4,2,64,128]{3,2,1,0:T(8,128)(2,1)S(1)}, u32[]{:S(2)}, u32[]{:S(2)}) collective-permute-start(bf16[4,2,64,128]{3,2,1,0:T(8,128)(2,1)S(1)} %pad_maximum_fusion.9), channel_id=1, source_target_pairs={{0,16},{4,20},{8,24},{12,28},{16,0},{20,4},{24,8},{28,12},{1,17},{... | collective-permute-start | bytes 393224 | tf_op jit(solution)/shard_map/ppermute | solution.py:526
  44.5 15.3 %collective-permute-start.29 = (bf16[4,2,64,128]{3,2,1,0:T(8,128)(2,1)S(1)}, bf16[4,2,64,128]{3,2,1,0:T(8,128)(2,1)S(1)}, u32[]{:S(2)}, u32[]{:S(2)}) collective-permute-start(bf16[4,2,64,128]{3,2,1,0:T(8,128)(2,1)S(1)} %pad_maximum_fusion.12), channel_id=1, source_target_pairs={{0,8},{4,12},{8,0},{12,4},{16,24},{20,28},{24,16},{28,20},{1,9},{5... | collective-permute-start | bytes 393224 | tf_op jit(solution)/shard_map/ppermute | solution.py:526
  48.2 13.2 %collective-permute-start.24 = (bf16[4,2,64,128]{3,2,1,0:T(8,128)(2,1)S(1)}, bf16[4,2,64,128]{3,2,1,0:T(8,128)(2,1)S(1)}, u32[]{:S(2)}, u32[]{:S(2)}) collective-permute-start(bf16[4,2,64,128]{3,2,1,0:T(8,128)(2,1)S(1)} %pad_maximum_fusion.11), channel_id=1, source_target_pairs={{0,16},{4,20},{8,24},{12,28},{16,0},{20,4},{24,8},{28,12},{1,17},{... | collective-permute-start | bytes 393224 | tf_op jit(solution)/shard_map/ppermute | solution.py:526
  48.6 17.5 %collective-permute-start.39 = (bf16[4,4,64,128]{3,2,1,0:T(8,128)(2,1)S(1)}, bf16[4,4,64,128]{3,2,1,0:T(8,128)(2,1)S(1)}, u32[]{:S(2)}, u32[]{:S(2)}) collective-permute-start(bf16[4,4,64,128]{3,2,1,0:T(8,128)(2,1)S(1)} %pad_maximum_fusion.7), channel_id=1, source_target_pairs={{0,8},{4,12},{8,0},{12,4},{16,24},{20,28},{24,16},{28,20},{1,9},{5... | collective-permute-start | bytes 786440 | tf_op jit(solution)/shard_map/ppermute | solution.py:526
  52.7 40.4 %collective-permute-start.34 = (bf16[4,4,64,128]{3,2,1,0:T(8,128)(2,1)S(1)}, bf16[4,4,64,128]{3,2,1,0:T(8,128)(2,1)S(1)}, u32[]{:S(2)}, u32[]{:S(2)}) collective-permute-start(bf16[4,4,64,128]{3,2,1,0:T(8,128)(2,1)S(1)} %pad_maximum_fusion.6), channel_id=1, source_target_pairs={{0,16},{4,20},{8,24},{12,28},{16,0},{20,4},{24,8},{28,12},{1,17},{... | collective-permute-start | bytes 786440 | tf_op jit(solution)/shard_map/ppermute | solution.py:526
  58.8 39.9 %collective-permute-start.20 = (bf16[8,2,64,128]{3,2,1,0:T(8,128)(2,1)S(1)}, bf16[8,2,64,128]{3,2,1,0:T(8,128)(2,1)S(1)}, u32[]{:S(2)}, u32[]{:S(2)}) collective-permute-start(bf16[8,2,64,128]{3,2,1,0:T(8,128)(2,1)S(1)} %pad_maximum_fusion.3), channel_id=1, source_target_pairs={{0,16},{4,20},{8,24},{12,28},{16,0},{20,4},{24,8},{28,12},{1,17},{... | collective-permute-start | bytes 786440 | tf_op jit(solution)/shard_map/ppermute | solution.py:526
  59.9 39.0 %collective-permute-start.15 = (bf16[8,2,64,128]{3,2,1,0:T(8,128)(2,1)S(1)}, bf16[8,2,64,128]{3,2,1,0:T(8,128)(2,1)S(1)}, u32[]{:S(2)}, u32[]{:S(2)}) collective-permute-start(bf16[8,2,64,128]{3,2,1,0:T(8,128)(2,1)S(1)} %pad_maximum_fusion.2), channel_id=1, source_target_pairs={{0,4},{4,0},{8,12},{12,8},{16,20},{20,16},{24,28},{28,24},{1,5},{5... | collective-permute-start | bytes 786440 | tf_op jit(solution)/shard_map/ppermute | solution.py:526
  61.4 42.9 %collective-permute-start.30 = (bf16[8,2,64,128]{3,2,1,0:T(8,128)(2,1)S(1)}, bf16[8,2,64,128]{3,2,1,0:T(8,128)(2,1)S(1)}, u32[]{:S(2)}, u32[]{:S(2)}) collective-permute-start(bf16[8,2,64,128]{3,2,1,0:T(8,128)(2,1)S(1)} %pad_maximum_fusion.5), channel_id=1, source_target_pairs={{0,16},{4,20},{8,24},{12,28},{16,0},{20,4},{24,8},{28,12},{1,17},{... | collective-permute-start | bytes 786440 | tf_op jit(solution)/shard_map/ppermute | solution.py:526
  66.2 45.2 %collective-permute-start.40 = (bf16[8,4,64,128]{3,2,1,0:T(8,128)(2,1)S(1)}, bf16[8,4,64,128]{3,2,1,0:T(8,128)(2,1)S(1)}, u32[]{:S(2)}, u32[]{:S(2)}) collective-permute-start(bf16[8,4,64,128]{3,2,1,0:T(8,128)(2,1)S(1)} %pad_maximum_fusion.1), channel_id=1, source_target_pairs={{0,16},{4,20},{8,24},{12,28},{16,0},{20,4},{24,8},{28,12},{1,17},{... | collective-permute-start | bytes 1572872 | tf_op jit(solution)/shard_map/ppermute | solution.py:526
  93.1 18.2 %collective-permute-start.35 = (bf16[8,4,64,128]{3,2,1,0:T(8,128)(2,1)S(1)}, bf16[8,4,64,128]{3,2,1,0:T(8,128)(2,1)S(1)}, u32[]{:S(2)}, u32[]{:S(2)}) collective-permute-start(bf16[8,4,64,128]{3,2,1,0:T(8,128)(2,1)S(1)} %pad_maximum_fusion), channel_id=1, source_target_pairs={{0,4},{4,0},{8,12},{12,8},{16,20},{20,16},{24,28},{28,24},{1,5},{5... | collective-permute-start | bytes 1572872 | tf_op jit(solution)/shard_map/ppermute | solution.py:526
  98.7 15.7 %collective-permute-start.6 = (bf16[8,32,512]{2,1,0:T(8,128)(2,1)S(1)}, bf16[8,32,512]{2,1,0:T(8,128)(2,1)S(1)}, u32[]{:S(2)}, u32[]{:S(2)}) collective-permute-start(bf16[8,32,512]{2,1,0:T(8,128)(2,1)S(1)} %copy-done.30), channel_id=1, source_target_pairs={{0,1},{1,0},{2,3},{3,2},{4,5},{5,4},{6,7},{7,6},{8,9},{9,8},{10,11... | collective-permute-start | bytes 786440 | tf_op jit(solution)/shard_map/ppermute | solution.py:526
  98.9 16.3 %collective-permute-start.7 = (bf16[8,32,512]{2,1,0:T(8,128)(2,1)S(1)}, bf16[8,32,512]{2,1,0:T(8,128)(2,1)S(1)}, u32[]{:S(2)}, u32[]{:S(2)}) collective-permute-start(bf16[8,32,512]{2,1,0:T(8,128)(2,1)S(1)} %copy-done.29), channel_id=1, source_target_pairs={{0,2},{1,3},{2,0},{3,1},{4,6},{5,7},{6,4},{7,5},{8,10},{9,11},{10,... | collective-permute-start | bytes 786440 | tf_op jit(solution)/shard_map/ppermute | solution.py:526
  104.3 11.4 %collective-permute-start.25 = (bf16[8,2,64,128]{3,2,1,0:T(8,128)(2,1)S(1)}, bf16[8,2,64,128]{3,2,1,0:T(8,128)(2,1)S(1)}, u32[]{:S(2)}, u32[]{:S(2)}) collective-permute-start(bf16[8,2,64,128]{3,2,1,0:T(8,128)(2,1)S(1)} %pad_maximum_fusion.4), channel_id=1, source_target_pairs={{0,4},{4,0},{8,12},{12,8},{16,20},{20,16},{24,28},{28,24},{1,5},{5... | collective-permute-start | bytes 786440 | tf_op jit(solution)/shard_map/ppermute | solution.py:526
  115.1 33.3 %collective-permute-start.41 = (bf16[16,4,64,128]{3,2,1,0:T(8,128)(2,1)}, bf16[16,4,64,128]{3,2,1,0:T(8,128)(2,1)S(1)}, u32[]{:S(2)}, u32[]{:S(2)}) collective-permute-start(bf16[16,4,64,128]{3,2,1,0:T(8,128)(2,1)} %get-tuple-element.210), channel_id=1, source_target_pairs={{0,1},{1,0},{2,3},{3,2},{4,5},{5,4},{6,7},{7,6},{8,9},{9,8},{10,11... | collective-permute-start | bytes 3145736 | tf_op jit(solution)/shard_map/ppermute | solution.py:526
  115.8 34.1 %collective-permute-start.36 = (bf16[16,4,64,128]{3,2,1,0:T(8,128)(2,1)}, bf16[16,4,64,128]{3,2,1,0:T(8,128)(2,1)S(1)}, u32[]{:S(2)}, u32[]{:S(2)}) collective-permute-start(bf16[16,4,64,128]{3,2,1,0:T(8,128)(2,1)} %get-tuple-element.212), channel_id=1, source_target_pairs={{0,1},{1,0},{2,3},{3,2},{4,5},{5,4},{6,7},{7,6},{8,9},{9,8},{10,11... | collective-permute-start | bytes 3145736 | tf_op jit(solution)/shard_map/ppermute | solution.py:526
  119.8 18.8 %collective-permute-start.26 = (bf16[16,2,64,128]{3,2,1,0:T(8,128)(2,1)}, bf16[16,2,64,128]{3,2,1,0:T(8,128)(2,1)S(1)}, u32[]{:S(2)}, u32[]{:S(2)}) collective-permute-start(bf16[16,2,64,128]{3,2,1,0:T(8,128)(2,1)} %get-tuple-element.220), channel_id=1, source_target_pairs={{0,1},{1,0},{2,3},{3,2},{4,5},{5,4},{6,7},{7,6},{8,9},{9,8},{10,11... | collective-permute-start | bytes 1572872 | tf_op jit(solution)/shard_map/ppermute | solution.py:526
  120.6 16.4 %collective-permute-start.3 = (bf16[8,32,512]{2,1,0:T(8,128)(2,1)S(1)}, bf16[8,32,512]{2,1,0:T(8,128)(2,1)S(1)}, u32[]{:S(2)}, u32[]{:S(2)}) collective-permute-start(bf16[8,32,512]{2,1,0:T(8,128)(2,1)S(1)} %copy-done.27), channel_id=1, source_target_pairs={{0,1},{1,0},{2,3},{3,2},{4,5},{5,4},{6,7},{7,6},{8,9},{9,8},{10,11... | collective-permute-start | bytes 786440 | tf_op jit(solution)/shard_map/ppermute | solution.py:526
  127.1 47.1 %collective-permute-start.45 = (bf16[4,128,512]{2,1,0:T(8,128)(2,1)S(1)}, bf16[4,128,512]{2,1,0:T(8,128)(2,1)}, u32[]{:S(2)}, u32[]{:S(2)}) collective-permute-start(bf16[4,128,512]{2,1,0:T(8,128)(2,1)S(1)} %copy-done.25), channel_id=1, source_target_pairs={{0,1},{1,0},{2,3},{3,2},{4,5},{5,4},{6,7},{7,6},{8,9},{9,8},{10,11... | collective-permute-start | bytes 1572872 | tf_op jit(solution)/shard_map/ppermute | solution.py:526
  137.0 37.7 %collective-permute-start.46 = (bf16[4,128,512]{2,1,0:T(8,128)(2,1)S(1)}, bf16[4,128,512]{2,1,0:T(8,128)(2,1)}, u32[]{:S(2)}, u32[]{:S(2)}) collective-permute-start(bf16[4,128,512]{2,1,0:T(8,128)(2,1)S(1)} %copy-done.24), channel_id=1, source_target_pairs={{0,2},{1,3},{2,0},{3,1},{4,6},{5,7},{6,4},{7,5},{8,10},{9,11},{10,... | collective-permute-start | bytes 1572872 | tf_op jit(solution)/shard_map/ppermute | solution.py:526
  138.7 36.0 %collective-permute-start.47 = (bf16[4,128,512]{2,1,0:T(8,128)(2,1)S(1)}, bf16[4,128,512]{2,1,0:T(8,128)(2,1)}, u32[]{:S(2)}, u32[]{:S(2)}) collective-permute-start(bf16[4,128,512]{2,1,0:T(8,128)(2,1)S(1)} %copy-done.23), channel_id=1, source_target_pairs={{0,3},{1,2},{2,1},{3,0},{4,7},{5,6},{6,5},{7,4},{8,11},{9,10},{10,... | collective-permute-start | bytes 1572872 | tf_op jit(solution)/shard_map/ppermute | solution.py:526
  148.4 20.3 %collective-permute-start.4 = (bf16[8,32,512]{2,1,0:T(8,128)(2,1)S(1)}, bf16[8,32,512]{2,1,0:T(8,128)(2,1)S(1)}, u32[]{:S(2)}, u32[]{:S(2)}) collective-permute-start(bf16[8,32,512]{2,1,0:T(8,128)(2,1)S(1)} %copy-done.26), channel_id=1, source_target_pairs={{0,2},{1,3},{2,0},{3,1},{4,6},{5,7},{6,4},{7,5},{8,10},{9,11},{10,... | collective-permute-start | bytes 786440 | tf_op jit(solution)/shard_map/ppermute | solution.py:526
  149.9 22.7 %collective-permute-start.5 = (bf16[8,32,512]{2,1,0:T(8,128)(2,1)S(1)}, bf16[8,32,512]{2,1,0:T(8,128)(2,1)S(1)}, u32[]{:S(2)}, u32[]{:S(2)}) collective-permute-start(bf16[8,32,512]{2,1,0:T(8,128)(2,1)S(1)} %get-tuple-element.206), channel_id=1, source_target_pairs={{0,3},{1,2},{2,1},{3,0},{4,7},{5,6},{6,5},{7,4},{8,11},{9,10},{10,... | collective-permute-start | bytes 786440 | tf_op jit(solution)/shard_map/ppermute | solution.py:526
  168.7 59.1 %collective-permute-start = (bf16[4,128,512]{2,1,0:T(8,128)(2,1)S(1)}, bf16[4,128,512]{2,1,0:T(8,128)(2,1)S(1)}, u32[]{:S(2)}, u32[]{:S(2)}) collective-permute-start(bf16[4,128,512]{2,1,0:T(8,128)(2,1)S(1)} %copy-done.22), channel_id=1, source_target_pairs={{0,1},{1,0},{2,3},{3,2},{4,5},{5,4},{6,7},{7,6},{8,9},{9,8},{10,11... | collective-permute-start | bytes 1572872 | tf_op jit(solution)/shard_map/ppermute | solution.py:526
  172.7 55.1 %collective-permute-start.1 = (bf16[4,128,512]{2,1,0:T(8,128)(2,1)S(1)}, bf16[4,128,512]{2,1,0:T(8,128)(2,1)S(1)}, u32[]{:S(2)}, u32[]{:S(2)}) collective-permute-start(bf16[4,128,512]{2,1,0:T(8,128)(2,1)S(1)} %copy-done.21), channel_id=1, source_target_pairs={{0,2},{1,3},{2,0},{3,1},{4,6},{5,7},{6,4},{7,5},{8,10},{9,11},{10,... | collective-permute-start | bytes 1572872 | tf_op jit(solution)/shard_map/ppermute | solution.py:526
  174.2 53.6 %collective-permute-start.2 = (bf16[4,128,512]{2,1,0:T(8,128)(2,1)S(1)}, bf16[4,128,512]{2,1,0:T(8,128)(2,1)S(1)}, u32[]{:S(2)}, u32[]{:S(2)}) collective-permute-start(bf16[4,128,512]{2,1,0:T(8,128)(2,1)S(1)} %get-tuple-element.197), channel_id=1, source_target_pairs={{0,3},{1,2},{2,1},{3,0},{4,7},{5,6},{6,5},{7,4},{8,11},{9,10},{10,... | collective-permute-start | bytes 1572872 | tf_op jit(solution)/shard_map/ppermute | solution.py:526
  284.9 17.5 %collective-permute-start.63 = (f32[8,128]{0,1:T(8,128)S(1)}, f32[8,128]{0,1:T(8,128)S(1)}, u32[]{:S(2)}, u32[]{:S(2)}) collective-permute-start(f32[8,128]{0,1:T(8,128)S(1)} %broadcast_in_dim.54), channel_id=1, source_target_pairs={{0,1},{1,0},{2,3},{3,2},{4,5},{5,4},{6,7},{7,6},{8,9},{9,8},{10,11... | collective-permute-start | bytes 12296 | tf_op jit(solution)/shard_map/ppermute | solution.py:526
  285.1 21.0 %collective-permute-start.64 = (f32[8,128]{0,1:T(8,128)S(1)}, f32[8,128]{0,1:T(8,128)S(1)}, u32[]{:S(2)}, u32[]{:S(2)}) collective-permute-start(f32[8,128]{0,1:T(8,128)S(1)} %broadcast_in_dim.54), channel_id=1, source_target_pairs={{0,2},{1,3},{2,0},{3,1},{4,6},{5,7},{6,4},{7,5},{8,10},{9,11},{10,... | collective-permute-start | bytes 12296 | tf_op jit(solution)/shard_map/ppermute | solution.py:526
  286.6 23.1 %collective-permute-start.65 = (f32[8,128]{0,1:T(8,128)S(1)}, f32[8,128]{0,1:T(8,128)S(1)}, u32[]{:S(2)}, u32[]{:S(2)}) collective-permute-start(f32[8,128]{0,1:T(8,128)S(1)} %broadcast_in_dim.54), channel_id=1, source_target_pairs={{0,3},{1,2},{2,1},{3,0},{4,7},{5,6},{6,5},{7,4},{8,11},{9,10},{10,... | collective-permute-start | bytes 12296 | tf_op jit(solution)/shard_map/ppermute | solution.py:526
  287.9 155.8 %collective-permute-start.57 = (bf16[4,128,512]{2,1,0:T(8,128)(2,1)}, bf16[4,128,512]{2,1,0:T(8,128)(2,1)}, u32[]{:S(2)}, u32[]{:S(2)}) collective-permute-start(bf16[4,128,512]{2,1,0:T(8,128)(2,1)} %get-tuple-element.129), channel_id=1, source_target_pairs={{0,1},{1,0},{2,3},{3,2},{4,5},{5,4},{6,7},{7,6},{8,9},{9,8},{10,11... | collective-permute-start | bytes 1572872 | tf_op jit(solution)/shard_map/ppermute | solution.py:526
  300.2 146.6 %collective-permute-start.58 = (bf16[4,128,512]{2,1,0:T(8,128)(2,1)}, bf16[4,128,512]{2,1,0:T(8,128)(2,1)}, u32[]{:S(2)}, u32[]{:S(2)}) collective-permute-start(bf16[4,128,512]{2,1,0:T(8,128)(2,1)} %get-tuple-element.130), channel_id=1, source_target_pairs={{0,2},{1,3},{2,0},{3,1},{4,6},{5,7},{6,4},{7,5},{8,10},{9,11},{10,... | collective-permute-start | bytes 1572872 | tf_op jit(solution)/shard_map/ppermute | solution.py:526
  306.1 143.8 %collective-permute-start.59 = (bf16[4,128,512]{2,1,0:T(8,128)(2,1)}, bf16[4,128,512]{2,1,0:T(8,128)(2,1)}, u32[]{:S(2)}, u32[]{:S(2)}) collective-permute-start(bf16[4,128,512]{2,1,0:T(8,128)(2,1)} %get-tuple-element.131), channel_id=1, source_target_pairs={{0,3},{1,2},{2,1},{3,0},{4,7},{5,6},{6,5},{7,4},{8,11},{9,10},{10,... | collective-permute-start | bytes 1572872 | tf_op jit(solution)/shard_map/ppermute | solution.py:526
  309.7 102.7 %collective-permute-start.51 = (bf16[4,32,512]{2,1,0:T(8,128)(2,1)}, bf16[4,32,512]{2,1,0:T(8,128)(2,1)S(1)}, u32[]{:S(2)}, u32[]{:S(2)}) collective-permute-start(bf16[4,32,512]{2,1,0:T(8,128)(2,1)} %get-tuple-element.114), channel_id=1, source_target_pairs={{0,1},{1,0},{2,3},{3,2},{4,5},{5,4},{6,7},{7,6},{8,9},{9,8},{10,11... | collective-permute-start | bytes 393224 | tf_op jit(solution)/shard_map/ppermute | solution.py:526
  314.3 99.0 %collective-permute-start.52 = (bf16[4,32,512]{2,1,0:T(8,128)(2,1)}, bf16[4,32,512]{2,1,0:T(8,128)(2,1)}, u32[]{:S(2)}, u32[]{:S(2)}) collective-permute-start(bf16[4,32,512]{2,1,0:T(8,128)(2,1)} %get-tuple-element.115), channel_id=1, source_target_pairs={{0,2},{1,3},{2,0},{3,1},{4,6},{5,7},{6,4},{7,5},{8,10},{9,11},{10,... | collective-permute-start | bytes 393224 | tf_op jit(solution)/shard_map/ppermute | solution.py:526
  439.3 13.8 %collective-permute-start.60 = (bf16[4,128,512]{2,1,0:T(8,128)(2,1)S(1)}, bf16[4,128,512]{2,1,0:T(8,128)(2,1)S(1)}, u32[]{:S(2)}, u32[]{:S(2)}) collective-permute-start(bf16[4,128,512]{2,1,0:T(8,128)(2,1)S(1)} %copy-done.69), channel_id=1, source_target_pairs={{0,1},{1,0},{2,3},{3,2},{4,5},{5,4},{6,7},{7,6},{8,9},{9,8},{10,11... | collective-permute-start | bytes 1572872 | tf_op jit(solution)/shard_map/ppermute | solution.py:526
  442.6 14.8 %collective-permute-start.61 = (bf16[4,128,512]{2,1,0:T(8,128)(2,1)S(1)}, bf16[4,128,512]{2,1,0:T(8,128)(2,1)S(1)}, u32[]{:S(2)}, u32[]{:S(2)}) collective-permute-start(bf16[4,128,512]{2,1,0:T(8,128)(2,1)S(1)} %copy-done.68), channel_id=1, source_target_pairs={{0,2},{1,3},{2,0},{3,1},{4,6},{5,7},{6,4},{7,5},{8,10},{9,11},{10,... | collective-permute-start | bytes 1572872 | tf_op jit(solution)/shard_map/ppermute | solution.py:526
  443.8 22.6 %collective-permute-start.62 = (bf16[4,128,512]{2,1,0:T(8,128)(2,1)S(1)}, bf16[4,128,512]{2,1,0:T(8,128)(2,1)S(1)}, u32[]{:S(2)}, u32[]{:S(2)}) collective-permute-start(bf16[4,128,512]{2,1,0:T(8,128)(2,1)S(1)} %copy-done.67), channel_id=1, source_target_pairs={{0,3},{1,2},{2,1},{3,0},{4,7},{5,6},{6,5},{7,4},{8,11},{9,10},{10,... | collective-permute-start | bytes 1572872 | tf_op jit(solution)/shard_map/ppermute | solution.py:526
  446.7 21.7 %collective-permute-start.101 = (bf16[16,2,64,128]{3,2,1,0:T(8,128)(2,1)}, bf16[16,2,64,128]{3,2,1,0:T(8,128)(2,1)S(1)}, u32[]{:S(2)}, u32[]{:S(2)}) collective-permute-start(bf16[16,2,64,128]{3,2,1,0:T(8,128)(2,1)} %slice.487), channel_id=1, source_target_pairs={{0,1},{1,0},{2,3},{3,2},{4,5},{5,4},{6,7},{7,6},{8,9},{9,8},{10,11... | collective-permute-start | bytes 1572872 | tf_op jit(solution)/shard_map/ppermute | solution.py:526
  449.9 18.8 %collective-permute-start.106 = (bf16[16,2,64,128]{3,2,1,0:T(8,128)(2,1)}, bf16[16,2,64,128]{3,2,1,0:T(8,128)(2,1)S(1)}, u32[]{:S(2)}, u32[]{:S(2)}) collective-permute-start(bf16[16,2,64,128]{3,2,1,0:T(8,128)(2,1)} %slice.497), channel_id=1, source_target_pairs={{0,1},{1,0},{2,3},{3,2},{4,5},{5,4},{6,7},{7,6},{8,9},{9,8},{10,11... | collective-permute-start | bytes 1572872 | tf_op jit(solution)/shard_map/ppermute | solution.py:526
  453.1 16.4 %collective-permute-start.91 = (bf16[16,2,64,128]{3,2,1,0:T(8,128)(2,1)S(1)}, bf16[16,2,64,128]{3,2,1,0:T(8,128)(2,1)S(1)}, u32[]{:S(2)}, u32[]{:S(2)}) collective-permute-start(bf16[16,2,64,128]{3,2,1,0:T(8,128)(2,1)S(1)} %copy-done.19), channel_id=1, source_target_pairs={{0,1},{1,0},{2,3},{3,2},{4,5},{5,4},{6,7},{7,6},{8,9},{9,8},{10,11... | collective-permute-start | bytes 1572872 | tf_op jit(solution)/shard_map/ppermute | solution.py:526
  457.4 12.4 %collective-permute-start.96 = (bf16[16,2,64,128]{3,2,1,0:T(8,128)(2,1)S(1)}, bf16[16,2,64,128]{3,2,1,0:T(8,128)(2,1)S(1)}, u32[]{:S(2)}, u32[]{:S(2)}) collective-permute-start(bf16[16,2,64,128]{3,2,1,0:T(8,128)(2,1)S(1)} %copy-done.18), channel_id=1, source_target_pairs={{0,1},{1,0},{2,3},{3,2},{4,5},{5,4},{6,7},{7,6},{8,9},{9,8},{10,11... | collective-permute-start | bytes 1572872 | tf_op jit(solution)/shard_map/ppermute | solution.py:526
  471.9 9.2 %collective-permute-start.107 = (bf16[8,2,64,128]{3,2,1,0:T(8,128)(2,1)S(1)}, bf16[8,2,64,128]{3,2,1,0:T(8,128)(2,1)S(1)}, u32[]{:S(2)}, u32[]{:S(2)}) collective-permute-start(bf16[8,2,64,128]{3,2,1,0:T(8,128)(2,1)S(1)} %slice.499), channel_id=1, source_target_pairs={{0,4},{4,0},{8,12},{12,8},{16,20},{20,16},{24,28},{28,24},{1,5},{5... | collective-permute-start | bytes 786440 | tf_op jit(solution)/shard_map/ppermute | solution.py:526
  473.2 13.5 %collective-permute-start.92 = (bf16[8,2,64,128]{3,2,1,0:T(8,128)(2,1)S(1)}, bf16[8,2,64,128]{3,2,1,0:T(8,128)(2,1)S(1)}, u32[]{:S(2)}, u32[]{:S(2)}) collective-permute-start(bf16[8,2,64,128]{3,2,1,0:T(8,128)(2,1)S(1)} %slice.469), channel_id=1, source_target_pairs={{0,4},{4,0},{8,12},{12,8},{16,20},{20,16},{24,28},{28,24},{1,5},{5... | collective-permute-start | bytes 786440 | tf_op jit(solution)/shard_map/ppermute | solution.py:526
  474.5 13.3 %collective-permute-start.97 = (bf16[8,2,64,128]{3,2,1,0:T(8,128)(2,1)S(1)}, bf16[8,2,64,128]{3,2,1,0:T(8,128)(2,1)S(1)}, u32[]{:S(2)}, u32[]{:S(2)}) collective-permute-start(bf16[8,2,64,128]{3,2,1,0:T(8,128)(2,1)S(1)} %slice.479), channel_id=1, source_target_pairs={{0,2},{1,3},{2,0},{3,1},{4,6},{5,7},{6,4},{7,5},{8,10},{9,11},{10,... | collective-permute-start | bytes 786440 | tf_op jit(solution)/shard_map/ppermute | solution.py:526
  475.5 13.2 %collective-permute-start.77 = (bf16[8,2,64,128]{3,2,1,0:T(8,128)(2,1)S(1)}, bf16[8,2,64,128]{3,2,1,0:T(8,128)(2,1)S(1)}, u32[]{:S(2)}, u32[]{:S(2)}) collective-permute-start(bf16[8,2,64,128]{3,2,1,0:T(8,128)(2,1)S(1)} %slice.435), channel_id=1, source_target_pairs={{0,2},{1,3},{2,0},{3,1},{4,6},{5,7},{6,4},{7,5},{8,10},{9,11},{10,... | collective-permute-start | bytes 786440 | tf_op jit(solution)/shard_map/ppermute | solution.py:526
  478.6 12.1 %collective-permute-start.82 = (bf16[8,2,64,128]{3,2,1,0:T(8,128)(2,1)S(1)}, bf16[8,2,64,128]{3,2,1,0:T(8,128)(2,1)S(1)}, u32[]{:S(2)}, u32[]{:S(2)}) collective-permute-start(bf16[8,2,64,128]{3,2,1,0:T(8,128)(2,1)S(1)} %slice.446), channel_id=1, source_target_pairs={{0,8},{4,12},{8,0},{12,4},{16,24},{20,28},{24,16},{28,20},{1,9},{5... | collective-permute-start | bytes 786440 | tf_op jit(solution)/shard_map/ppermute | solution.py:526
  481.1 11.4 %collective-permute-start.72 = (bf16[8,2,64,128]{3,2,1,0:T(8,128)(2,1)S(1)}, bf16[8,2,64,128]{3,2,1,0:T(8,128)(2,1)S(1)}, u32[]{:S(2)}, u32[]{:S(2)}) collective-permute-start(bf16[8,2,64,128]{3,2,1,0:T(8,128)(2,1)S(1)} %slice.425), channel_id=1, source_target_pairs={{0,4},{4,0},{8,12},{12,8},{16,20},{20,16},{24,28},{28,24},{1,5},{5... | collective-permute-start | bytes 786440 | tf_op jit(solution)/shard_map/ppermute | solution.py:526
  486.7 11.2 %collective-permute-start.87 = (bf16[8,2,64,128]{3,2,1,0:T(8,128)(2,1)S(1)}, bf16[8,2,64,128]{3,2,1,0:T(8,128)(2,1)S(1)}, u32[]{:S(2)}, u32[]{:S(2)}) collective-permute-start(bf16[8,2,64,128]{3,2,1,0:T(8,128)(2,1)S(1)} %slice.457), channel_id=1, source_target_pairs={{0,4},{4,0},{8,12},{12,8},{16,20},{20,16},{24,28},{28,24},{1,5},{5... | collective-permute-start | bytes 786440 | tf_op jit(solution)/shard_map/ppermute | solution.py:526
  487.8 11.2 %collective-permute-start.103 = (bf16[4,2,64,128]{3,2,1,0:T(8,128)(2,1)S(1)}, bf16[4,2,64,128]{3,2,1,0:T(8,128)(2,1)S(1)}, u32[]{:S(2)}, u32[]{:S(2)}) collective-permute-start(bf16[4,2,64,128]{3,2,1,0:T(8,128)(2,1)S(1)} %slice.491), channel_id=1, source_target_pairs={{0,16},{4,20},{8,24},{12,28},{16,0},{20,4},{24,8},{28,12},{1,17},{... | collective-permute-start | bytes 393224 | tf_op jit(solution)/shard_map/ppermute | solution.py:526
  488.8 11.2 %collective-permute-start.108 = (bf16[4,2,64,128]{3,2,1,0:T(8,128)(2,1)S(1)}, bf16[4,2,64,128]{3,2,1,0:T(8,128)(2,1)S(1)}, u32[]{:S(2)}, u32[]{:S(2)}) collective-permute-start(bf16[4,2,64,128]{3,2,1,0:T(8,128)(2,1)S(1)} %slice.501), channel_id=1, source_target_pairs={{0,8},{4,12},{8,0},{12,4},{16,24},{20,28},{24,16},{28,20},{1,9},{5... | collective-permute-start | bytes 393224 | tf_op jit(solution)/shard_map/ppermute | solution.py:526
  490.7 10.7 %collective-permute-start.93 = (bf16[4,2,64,128]{3,2,1,0:T(8,128)(2,1)S(1)}, bf16[4,2,64,128]{3,2,1,0:T(8,128)(2,1)S(1)}, u32[]{:S(2)}, u32[]{:S(2)}) collective-permute-start(bf16[4,2,64,128]{3,2,1,0:T(8,128)(2,1)S(1)} %slice.471), channel_id=1, source_target_pairs={{0,2},{1,3},{2,0},{3,1},{4,6},{5,7},{6,4},{7,5},{8,10},{9,11},{10,... | collective-permute-start | bytes 393224 | tf_op jit(solution)/shard_map/ppermute | solution.py:526
  492.5 11.1 %collective-permute-start.98 = (bf16[4,2,64,128]{3,2,1,0:T(8,128)(2,1)S(1)}, bf16[4,2,64,128]{3,2,1,0:T(8,128)(2,1)S(1)}, u32[]{:S(2)}, u32[]{:S(2)}) collective-permute-start(bf16[4,2,64,128]{3,2,1,0:T(8,128)(2,1)S(1)} %slice.481), channel_id=1, source_target_pairs={{0,4},{4,0},{8,12},{12,8},{16,20},{20,16},{24,28},{28,24},{1,5},{5... | collective-permute-start | bytes 393224 | tf_op jit(solution)/shard_map/ppermute | solution.py:526
  499.1 9.1 %collective-permute-start.83 = (bf16[4,2,64,128]{3,2,1,0:T(8,128)(2,1)S(1)}, bf16[4,2,64,128]{3,2,1,0:T(8,128)(2,1)S(1)}, u32[]{:S(2)}, u32[]{:S(2)}) collective-permute-start(bf16[4,2,64,128]{3,2,1,0:T(8,128)(2,1)S(1)} %slice.448), channel_id=1, source_target_pairs={{0,16},{4,20},{8,24},{12,28},{16,0},{20,4},{24,8},{28,12},{1,17},{... | collective-permute-start | bytes 393224 | tf_op jit(solution)/shard_map/ppermute | solution.py:526
  501.4 9.0 %collective-permute-start.88 = (bf16[4,2,64,128]{3,2,1,0:T(8,128)(2,1)S(1)}, bf16[4,2,64,128]{3,2,1,0:T(8,128)(2,1)S(1)}, u32[]{:S(2)}, u32[]{:S(2)}) collective-permute-start(bf16[4,2,64,128]{3,2,1,0:T(8,128)(2,1)S(1)} %slice.459), channel_id=1, source_target_pairs={{0,8},{4,12},{8,0},{12,4},{16,24},{20,28},{24,16},{28,20},{1,9},{5... | collective-permute-start | bytes 393224 | tf_op jit(solution)/shard_map/ppermute | solution.py:526
  (139 other events, 1635.0 us)

commit v2 on v1

v2 whole, which is shorter than its diff:
```python
import functools
import math

import jax
import jax.numpy as jnp
from jax import lax
from jax.experimental import pallas as pl
from jax.experimental.pallas import tpu as pltpu
from jax.sharding import PartitionSpec as P

epsilon = 1e-06
momentum_decay = 0.9
average_decay = 0.7
matrix_rate = 10.0
output_rate = 40.0
small_rate = 50.0
group_limits = (0.6, 0.85, 1.2, 1.7)
head_dim = 64
quad = 4
quad_width = quad * head_dim
dp_slots = 8
tensor_slots = 4
wide = jnp.float32
narrow = jnp.bfloat16
vmem_bytes = 58 * 2**20
cost_scale = 1.0

core = ("tensor", 1)
row = ("tensor", 2)
side = ("dp", 1)
near = ("dp", 2)
far = ("dp", 4)
gather_order = (far, near, row, side, core)
reduce_orders = (
    (core, side, row, near, far),
    (core, row, near, far, side),
    (core, row, side, near, far),
    (core, near, far, side, row),
)
reduce_counts = (5, 3, 3, 5)


def dot_nn(left, right):
    return lax.dot_general(left, right, (((1,), (0,)), ((), ())), preferred_element_type=wide)


def dot_nt(left, right):
    return lax.dot_general(left, right, (((1,), (1,)), ((), ())), preferred_element_type=wide)


def dot_tn(left, right):
    return lax.dot_general(left, right, (((0,), (0,)), ((), ())), preferred_element_type=wide)


def head_masks(dtype):
    lanes = lax.broadcasted_iota(jnp.int32, (1, quad_width), 1) // head_dim
    return [(lanes == head).astype(wide).astype(dtype) for head in range(quad)]


def stack_heads(block, masks):
    return jnp.concatenate([block * mask for mask in masks], 0)


def unstack_heads(block, masks):
    rows = block.shape[0] // quad
    total = block[:rows] * masks[0]
    for head in range(1, quad):
        total = total + block[head * rows : (head + 1) * rows] * masks[head]
    return total


def norm_scale(rows):
    return lax.rsqrt(jnp.mean(rows * rows, -1, keepdims=True) + epsilon)


def norm_back(rows, gain, d_normed):
    scaling = norm_scale(rows)
    weighted = d_normed * gain
    cubed = scaling * scaling * scaling
    d_rows = scaling * weighted - rows * cubed * jnp.mean(rows * weighted, -1, keepdims=True)
    return d_rows, d_normed * rows * scaling


def softmax_keys(scores):
    peak = jnp.max(scores, 0, keepdims=True)
    weights = jnp.exp(scores - peak)
    return weights * (1.0 / jnp.sum(weights, 0, keepdims=True))


def gram_squares(left, right_grams):
    return jnp.sum(dot_nt(left, left) * right_grams, 0, keepdims=True)


def fold_lanes(row_sums):
    width = row_sums.shape[1]
    total = row_sums[:, :128]
    for start in range(128, width, 128):
        total = total + row_sums[:, start : start + 128]
    return total


def slot_places(order, first_is_high):
    places = []
    count = len(order)
    for slot in range(1 << count):
        index = {"dp": 0, "tensor": 0}
        for stage, (axis, bit) in enumerate(order):
            place = count - 1 - stage if first_is_high else stage
            if (slot >> place) & 1:
                index[axis] |= bit
        places.append((index["dp"], index["tensor"]))
    return places


def start_weights(info, pieces, plans, held, sems):
    for piece, (first, count, places, relative), sem in zip(pieces, plans, sems):
        for slot, (dp_index, tensor_index) in enumerate(places):
            if relative:
                high = pl.multiple_of((dp_index ^ info[0]) * 64, 64)
                left = pl.multiple_of((tensor_index ^ info[1]) * 128, 128)
            else:
                high, left = dp_index * 64, tensor_index * 128
            pltpu.make_async_copy(
                piece.at[slot],
                held.at[pl.ds(first, count), pl.ds(high, 64), pl.ds(left, 128)],
                sem,
            ).start()


def wait_weights(plans, held, sems):
    for (first, count, places, relative), sem in zip(plans, sems):
        share = 512 * len(places) // (dp_slots * tensor_slots)
        whole = held.at[pl.ds(first, count), pl.ds(0, share)]
        pltpu.make_async_copy(whole, whole, sem).wait()


def place_rows(info, parts, held, first=0):
    rows = held.shape[1] // len(parts)
    for index, part in enumerate(parts):
        start = pl.multiple_of((info[2] ^ index) * rows, rows)
        held[:, pl.ds(start, rows), :] = part[:, first : first + rows, :]


def split_rows(info, held, parts, first=0):
    rows = held.shape[1] // len(parts)
    for index, part in enumerate(parts):
        start = pl.multiple_of((info[2] ^ index) * rows, rows)
        part[:, first : first + rows, :] = held[:, pl.ds(start, rows), :].astype(part.dtype)


def self_forward_kernel(shards, plans, heads_local, *refs):
    refs = list(refs)

    def take(count):
        taken = refs[:count]
        del refs[:count]
        return taken

    (info,) = take(1)
    parts = take(shards)
    buckets, key_mask, gains, table = take(4)
    pieces = take(len(plans))
    normed_out, rows_out, qkv_out, weights_out, mix_out, mid_out = take(6)
    held, sems, rows_held, mix_held = take(4)
    sem_list = [sems.at[index] for index in range(len(plans))]

    @pl.when(pl.program_id(0) == 0)
    def _():
        start_weights(info, pieces, plans, held, sem_list)
        wait_weights(plans, held, sem_list)

    masks = head_masks(narrow)
    masks_wide = head_masks(wide)
    place_rows(info, parts, rows_held)
    rows_out[...] = rows_held[...]
    bundle, seq, width = rows_held.shape
    flat = rows_held[...].reshape(bundle * seq, width).astype(wide)
    normed = (flat * norm_scale(flat) * gains[0:1, :]).astype(narrow)
    normed_out[...] = normed.reshape(bundle, seq, width)
    for index in range(3):
        value = dot_nn(normed, held[index]).astype(narrow)
        qkv_out[index] = value.reshape(bundle, seq, width)
    for example in range(bundle):
        code = jnp.where(key_mask[example] > 0, buckets[example], -1).T
        safe = jnp.maximum(code, 0)
        code_all = jnp.concatenate([code] * quad, 1)
        for group in range(width // quad_width):
            columns = slice(group * quad_width, (group + 1) * quad_width)
            bias = []
            for head in range(group * quad, (group + 1) * quad):
                spot = ((head // heads_local) ^ info[2]) * heads_local + head % heads_local
                line = jnp.broadcast_to(table[pl.ds(spot, 1), :], (seq, 128))
                bias.append(jnp.take_along_axis(line, safe, axis=1))
            queries = stack_heads(qkv_out[0, example, :, columns], masks)
            scores = dot_nt(qkv_out[1, example, :, columns], queries) * (
                1.0 / math.sqrt(head_dim)
            ) + jnp.concatenate(bias, 1)
            weights = softmax_keys(jnp.where(code_all >= 0, scores, -1000000000.0))
            weights_out[example, group] = weights
            mixture = dot_tn(weights.astype(narrow), qkv_out[2, example, :, columns])
            mix_held[example, :, columns] = unstack_heads(mixture, masks_wide).astype(narrow)
    mix_out[...] = mix_held[...]
    mix = mix_held[...].reshape(bundle * seq, width)
    mid_out[...] = (flat + dot_nt(mix, held[3])).reshape(bundle, seq, width)


def cross_kernel(shards, plans, aliased, *refs):
    refs = list(refs)

    def take(count):
        taken = refs[:count]
        del refs[:count]
        return taken

    (info,) = take(1)
    memory_parts = take(shards)
    mid_in, gains = take(2)
    pieces = take(len(plans))
    take(aliased)
    own_output, own_grad = take(2)
    sent_parts = take(shards - 1)
    (
        early_out,
        normed_b_out,
        d_query_out,
        d_pair_out,
        mix_out,
        d_mid_out,
        normed_c_out,
        d_hidden_out,
        active_out,
        d_top_out,
        d_gain_b_out,
        d_gain_c_out,
        squares_out,
    ) = take(13)
    d_keys_out, d_values_out = d_pair_out.at[0], d_pair_out.at[1]
    held, sems, memory_held, keys_held, values_held, weights_held, rows_held, query_held = take(8)
    sem_list = [sems.at[index] for index in range(len(plans))]

    @pl.when(pl.program_id(0) == 0)
    def _():
        start_weights(info, pieces, plans, held, sem_list)
        wait_weights(plans, held, sem_list)

    masks = head_masks(narrow)
    masks_wide = head_masks(wide)
    scaling = 1.0 / math.sqrt(head_dim)
    bundle, seq, width = mid_in.shape
    memory_len = memory_held.shape[1]
    memory_rows = memory_len // shards
    groups = width // quad_width

    def flatten(block):
        return block.reshape(block.shape[0] * block.shape[1], block.shape[2])

    def unflatten(block):
        return block.reshape(bundle, block.shape[0] // bundle, block.shape[1])

    for index, part in enumerate(memory_parts):
        memory_held[:, index * memory_rows : (index + 1) * memory_rows, :] = part[
            :, :memory_rows, :
        ]
    place_rows(info, memory_parts, d_top_out, memory_rows)
    mid = flatten(mid_in[...])
    rows_b = mid.astype(narrow).astype(wide)
    normed_b = (rows_b * norm_scale(rows_b) * gains[1:2, :]).astype(narrow)
    normed_b_out[...] = unflatten(normed_b)
    query_held[...] = unflatten(dot_nn(normed_b, held[0]).astype(narrow))
    memory_flat = flatten(memory_held[...])
    keys_held[...] = unflatten(dot_nn(memory_flat, held[1]).astype(narrow))
    values_held[...] = unflatten(dot_nn(memory_flat, held[2]).astype(narrow))
    for example in range(bundle):
        for group in range(groups):
            columns = slice(group * quad_width, (group + 1) * quad_width)
            queries = stack_heads(query_held[example, :, columns], masks)
            scores = dot_nt(keys_held[example, :, columns], queries) * scaling
            weights = softmax_keys(scores)
            weights_held[example, group] = weights
            mixture = dot_tn(weights.astype(narrow), values_held[example, :, columns])
            mix_out[example, :, columns] = unstack_heads(mixture, masks_wide).astype(narrow)
    late = mid + dot_nt(flatten(mix_out[...]), held[3])
    rows_c = late.astype(narrow).astype(wide)
    normed_c = (rows_c * norm_scale(rows_c) * gains[2:3, :]).astype(narrow)
    normed_c_out[...] = unflatten(normed_c)
    d_top = flatten(d_top_out[...])
    total = late
    d_normed = jnp.zeros((bundle * seq, width), wide)
    up_grams = [jnp.zeros((seq, seq), wide) for _ in range(bundle)]
    down_grams = [jnp.zeros((seq, seq), wide) for _ in range(bundle)]
    slope = math.sqrt(2.0 / math.pi)
    for index in range(4):
        hidden = dot_nn(normed_c, held[4 + index])
        square = hidden * hidden
        bend = jnp.tanh(slope * hidden * (1.0 + 0.044715 * square))
        half = 0.5 * (1.0 + bend)
        active = (hidden * half).astype(narrow)
        steep = half + 0.5 * hidden * (1.0 - bend * bend) * (
            slope * (1.0 + (3.0 * 0.044715) * square)
        )
        total = total + dot_nt(active, held[8 + index])
        d_hidden = (dot_nn(d_top, held[8 + index]) * steep).astype(narrow)
        d_normed = d_normed + dot_nt(d_hidden, held[4 + index])
        active_out[index] = unflatten(active)
        d_hidden_out[index] = unflatten(d_hidden)
        for example in range(bundle):
            span = slice(example * seq, (example + 1) * seq)
            up_grams[example] += dot_nt(d_hidden[span], d_hidden[span])
            down_grams[example] += dot_nt(active[span], active[span])
    rows_held[...] = unflatten(total)
    for index in range(shards):
        start = pl.multiple_of((info[2] ^ index) * (seq // shards), seq // shards)
        block = rows_held[:, pl.ds(start, seq // shards), :].astype(narrow)
        if index:
            sent_parts[index - 1][:, memory_rows:, :] = block
        else:
            own_output[...] = block
    d_rows, d_gain_rows = norm_back(rows_c, gains[2:3, :], d_normed)
    d_gain_c = jnp.sum(unflatten(d_gain_rows), 1, keepdims=True)
    d_gain_c_out[...] = d_gain_c
    d_mid = d_top.astype(wide) + d_rows
    d_mid_low = d_mid.astype(narrow)
    d_mid_out[...] = unflatten(d_mid_low)
    d_mix = dot_nn(d_mid_low, held[3]).astype(narrow)
    squares = []
    for example in range(bundle):
        span = slice(example * seq, (example + 1) * seq)
        for group in range(groups):
            columns = slice(group * quad_width, (group + 1) * quad_width)
            keys = keys_held[example, :, columns]
            queries = stack_heads(query_held[example, :, columns], masks)
            d_mixes = stack_heads(d_mix[span, columns], masks)
            weights = weights_held[example, group]
            d_weights = dot_nt(values_held[example, :, columns], d_mixes)
            inner = jnp.sum(weights * d_weights, 0, keepdims=True)
            d_scores = (weights * (d_weights - inner)).astype(narrow)
            d_query_out[example, :, columns] = (
                unstack_heads(dot_tn(d_scores, keys), masks_wide) * scaling
            ).astype(narrow)
            d_keys_out[example, :, columns] = (dot_nn(d_scores, queries) * scaling).astype(narrow)
            d_values_out[example, :, columns] = dot_nn(weights.astype(narrow), d_mixes).astype(
                narrow
            )
        memory_grad = dot_nt(d_keys_out[example], held[1]) + dot_nt(d_values_out[example], held[2])
        own_grad[example] = memory_grad[:memory_rows]
        for index, part in enumerate(sent_parts):
            part[example, :memory_rows, :] = memory_grad[
                (index + 1) * memory_rows : (index + 2) * memory_rows
            ].astype(narrow)
        d_query = d_query_out[example]
        mix = mix_out[example]
        square_sum = gram_squares(normed_b[span], dot_nt(d_query, d_query))
        square_sum += gram_squares(mix, dot_nt(d_mid_low[span], d_mid_low[span]))
        square_sum += gram_squares(normed_c[span], up_grams[example])
        square_sum += gram_squares(d_top[span], down_grams[example])
        for block in (d_keys_out, d_values_out):
            product = dot_tn(memory_held[example], block[example])
            square_sum += fold_lanes(jnp.sum(product * product, 0, keepdims=True))
        square_sum += fold_lanes(d_gain_c[example] * d_gain_c[example])
        squares.append(square_sum)
    d_normed_b = dot_nt(flatten(d_query_out[...]), held[0])
    d_rows_b, d_gain_rows = norm_back(rows_b, gains[1:2, :], d_normed_b)
    d_gain_b = jnp.sum(unflatten(d_gain_rows), 1, keepdims=True)
    d_gain_b_out[...] = d_gain_b
    for example in range(bundle):
        squares_out[example] = squares[example] + fold_lanes(
            d_gain_b[example] * d_gain_b[example]
        )
    early_out[...] = unflatten(d_mid + d_rows_b)


def self_backward_kernel(shards, plans, *refs):
    refs = list(refs)

    def take(count):
        taken = refs[:count]
        del refs[:count]
        return taken

    info, early_in, rows_in, normed_in, qkv_in, weights_in, mix_in = take(7)
    squares_in, d_gain_b, d_gain_c, buckets, gains = take(5)
    pieces = take(len(plans))
    tokens_grads = take(shards)
    d_qkv_out, d_early_out, small_out, norms_out = take(4)
    held, sems, rows_held, bias_held = take(4)
    sem_list = [sems.at[index] for index in range(len(plans))]

    @pl.when(pl.program_id(0) == 0)
    def _():
        start_weights(info, pieces, plans, held, sem_list)
        wait_weights(plans, held, sem_list)

    masks = head_masks(narrow)
    masks_wide = head_masks(wide)
    scaling = 1.0 / math.sqrt(head_dim)
    bundle, seq, width = early_in.shape
    groups = width // quad_width
    bucket_count = bias_held.shape[0] // (groups * quad)

    def flatten(block):
        return block.reshape(block.shape[0] * block.shape[1], block.shape[2])

    def unflatten(block):
        return block.reshape(bundle, block.shape[0] // bundle, block.shape[1])

    early = flatten(early_in[...])
    d_early = early.astype(narrow)
    d_early_out[...] = unflatten(d_early)
    d_mix = dot_nn(d_early, held[3]).astype(narrow)
    squares = []
    for example in range(bundle):
        span = slice(example * seq, (example + 1) * seq)
        code = buckets[example].T
        for group in range(groups):
            columns = slice(group * quad_width, (group + 1) * quad_width)
            keys = qkv_in[1, example, :, columns]
            queries = stack_heads(qkv_in[0, example, :, columns], masks)
            d_mixes = stack_heads(d_mix[span, columns], masks)
            weights = weights_in[example, group]
            d_weights = dot_nt(qkv_in[2, example, :, columns], d_mixes)
            inner = jnp.sum(weights * d_weights, 0, keepdims=True)
            d_scores = (weights * (d_weights - inner)).astype(narrow)
            d_qkv_out[0, example, :, columns] = (
                unstack_heads(dot_tn(d_scores, keys), masks_wide) * scaling
            ).astype(narrow)
            d_qkv_out[1, example, :, columns] = (dot_nn(d_scores, queries) * scaling).astype(
                narrow
            )
            d_qkv_out[2, example, :, columns] = dot_nn(weights.astype(narrow), d_mixes).astype(
                narrow
            )
            d_wide = d_scores.astype(wide)
            for bucket in range(bucket_count):
                chosen = code == bucket
                for head in range(quad):
                    picked = jnp.where(chosen, d_wide[:, head * seq : (head + 1) * seq], 0.0)
                    spot = (group * quad + head) * bucket_count + bucket
                    bias_held[spot : spot + 1, :] = jnp.sum(picked, 0, keepdims=True)
        d_bias = lax.dot_general(
            jnp.ones((8, 128), wide),
            bias_held[...],
            (((1,), (1,)), ((), ())),
            precision=lax.Precision.HIGHEST,
            preferred_element_type=wide,
        )[:1]
        small_out[example, :, 3 * width :] = d_bias
        grams = jnp.zeros((seq, seq), wide)
        for index in range(3):
            block = d_qkv_out[index, example]
            grams = grams + dot_nt(block, block)
        square_sum = gram_squares(normed_in[example], grams)
        square_sum += gram_squares(mix_in[example], dot_nt(d_early[span], d_early[span]))
        square_sum += fold_lanes(d_bias * d_bias)
        squares.append(square_sum)
    d_normed = dot_nt(flatten(d_qkv_out[0]), held[0])
    d_normed = d_normed + dot_nt(flatten(d_qkv_out[1]), held[1])
    d_normed = d_normed + dot_nt(flatten(d_qkv_out[2]), held[2])
    d_rows, d_gain_rows = norm_back(flatten(rows_in[...]).astype(wide), gains[0:1, :], d_normed)
    d_gain = jnp.sum(unflatten(d_gain_rows), 1, keepdims=True)
    small_out[:, :, :width] = d_gain
    small_out[:, :, width : 2 * width] = d_gain_b[...]
    small_out[:, :, 2 * width : 3 * width] = d_gain_c[...]
    for example in range(bundle):
        square_sum = (
            squares[example]
            + squares_in[example]
            + fold_lanes(d_gain[example] * d_gain[example])
        )
        total = jnp.sum(square_sum, -1, keepdims=True) + epsilon
        norms_out[example] = jnp.broadcast_to(jnp.sqrt(total), (1, 128))
    rows_held[...] = unflatten(early + d_rows)
    split_rows(info, rows_held, tokens_grads)


class Gradients:
    def __init__(self, info, clip, loads, load_sems, scaled, tile, held, store_sems):
        self.info, self.clip, self.scaled = info, clip, scaled
        self.tile, self.held, self.store_sems = tile, held, store_sems
        self.copies = [
            pltpu.make_async_copy(source, target, load_sems.at[index])
            for index, (source, target) in enumerate(loads)
        ]
        self.targets = [target for source, target in loads]
        self.stores = []
        for copy in self.copies:
            copy.start()

    def read(self, index):
        self.copies[index].wait()
        return self.targets[index]

    def scale(self, index):
        block = self.read(index)
        count, rows, width = block.shape
        for example in range(count):
            self.scaled[example * rows : (example + 1) * rows, :] = (
                block[example].astype(wide) * self.clip[example]
            ).astype(narrow)

    def product(self, index):
        block = self.read(index)
        return dot_tn(self.scaled[...], block[...].reshape(self.scaled.shape[0], block.shape[-1]))

    def write(self, value, outs, unit, places):
        number = len(self.stores) // 2
        tile = self.tile.at[number % 2]
        tile[...] = value.astype(narrow)
        halves = self.held.at[number]
        count = len(places) // 2
        for slot, (dp_index, tensor_index) in enumerate(places):
            high = pl.multiple_of((dp_index ^ self.info[0]) * 64, 64)
            left = pl.multiple_of((tensor_index ^ self.info[1]) * 128, 128)
            halves[slot // count, slot % count] = tile[pl.ds(high, 64), pl.ds(left, 128)]
        for half, out in enumerate(outs):
            copy = pltpu.make_async_copy(
                halves.at[half], out.at[:, unit], self.store_sems.at[len(self.stores)]
            )
            copy.start()
            self.stores.append(copy)

    def finish(self):
        for copy in self.stores:
            copy.wait()


def inner_gradient_kernel(places, info, clip, normed, d_hidden, d_top, active, *refs):
    outs = (refs[:2], refs[2:4])
    rows_held, blocks_held, load_sems, scaled, tile, held, store_sems = refs[4:]
    loads = []
    for piece, (left, right) in enumerate(((normed, d_hidden), (d_top, active))):
        loads.append((left, rows_held.at[piece]))
        loads += [(right.at[unit], blocks_held.at[4 * piece + unit]) for unit in range(4)]
    work = Gradients(info, clip, loads, load_sems, scaled, tile, held, store_sems)
    for piece in range(2):
        work.scale(5 * piece)
        for unit in range(4):
            spot = 4 * piece + unit
            out = int(spot >= reduce_counts[0])
            spot -= out * reduce_counts[0]
            work.write(work.product(5 * piece + 1 + unit), outs[out], spot, places[out])
    work.finish()


def attention_gradient_kernel(shards, chunks, places, info, clip, *refs):
    normed_a, d_qkv, d_early, mix_a, normed_b, d_query, d_mid, mix_b = refs[:8]
    parts = refs[8 : 8 + shards * chunks]
    refs = refs[8 + shards * chunks :]
    d_pair = refs[0]
    self_out, cross_out = refs[1:3], refs[3:5]
    rows_held, parts_held, pairs_held, memory_held = refs[5:9]
    load_sems, scaled, tile, held, store_sems = refs[9:]
    count, memory_len = d_pair.shape[1:3]
    part_len = memory_len // shards
    group = count // chunks
    sources = [normed_a, d_qkv.at[0], d_qkv.at[1], d_qkv.at[2], d_early, mix_a]
    sources += [normed_b, d_query, d_mid, mix_b]
    loads = [(source, rows_held.at[index]) for index, source in enumerate(sources)]
    first = len(loads)
    for chunk in range(chunks):
        for index in range(shards):
            place = chunk * shards + index
            loads.append((parts[place].at[:, pl.ds(0, part_len)], parts_held.at[place]))
        for unit in range(2):
            loads.append(
                (d_pair.at[unit, pl.ds(chunk * group, group)], pairs_held.at[2 * chunk + unit])
            )
    work = Gradients(info, clip, loads, load_sems, scaled, tile, held, store_sems)
    work.scale(0)
    for unit in range(3):
        work.write(work.product(1 + unit), self_out, unit, places[0])
    work.scale(4)
    work.write(work.product(5), cross_out, 0, places[1])
    work.scale(6)
    work.write(work.product(7), cross_out, 1, places[1])
    work.scale(8)
    work.write(work.product(9), cross_out, 2, places[1])
    totals = [None, None]
    for chunk in range(chunks):
        start = first + chunk * (shards + 2)
        for index in range(shards):
            block = work.read(start + index)
            for example in range(group):
                top = (example * shards + index) * part_len
                memory_held[chunk, top : top + part_len, :] = (
                    block[example].astype(wide) * clip[chunk * group + example]
                ).astype(narrow)
        for unit in range(2):
            pair = work.read(start + shards + unit)
            product = dot_tn(
                memory_held[chunk], pair[...].reshape(group * memory_len, pair.shape[-1])
            )
            totals[unit] = product if chunk == 0 else totals[unit] + product
    for unit in range(2):
        work.write(totals[unit], cross_out, 3 + unit, places[1])
    work.finish()


def stepper(parameter, gradient, momentum, average, step_rate):
    velocity = momentum_decay * momentum + gradient
    updated = parameter - step_rate * (gradient + momentum_decay * velocity)
    averaged = average_decay * average + (1.0 - average_decay) * updated
    return (velocity, averaged, updated)


def update_kernel(shrink, *refs):
    sums = refs[:8]
    params, outs = refs[8:20], refs[20:]

    def gradient(piece, unit):
        total = sums[2 * piece][unit].astype(wide) + sums[2 * piece + 1][unit].astype(wide)
        return total * shrink

    def step(group, spot, value, rate):
        weight, momentum, average = params[3 * group : 3 * group + 3]
        stepped = stepper(weight[spot], value, momentum[spot], average[spot], rate)
        for out, block in zip(outs[3 * group : 3 * group + 3], stepped):
            out[spot] = block

    inside = ((2, 0), (2, 1), (2, 2), (3, 1), (3, 3), (3, 4))
    for index, (piece, unit) in enumerate(inside):
        step(0, index, gradient(piece, unit), matrix_rate)
    for index, unit in enumerate((0, 2)):
        step(1, index, gradient(3, unit), output_rate)
    for index in range(4):
        spot = (slice(None), slice(128 * index, 128 * (index + 1)))
        step(2, spot, gradient(0, index), matrix_rate)
        piece, unit = (1, index - 1) if index else (0, 4)
        step(3, spot, gradient(piece, unit), matrix_rate)


def assemble_kernel(shards, chunks, *refs):
    refs = list(refs[1:])

    def take(count):
        taken = refs[:count]
        del refs[:count]
        return taken

    arrived = [take(shards - 1) for _ in range(chunks)]
    tokens_parts = take(shards - 1)
    take(3)
    output, tokens_grad, memory_grad = refs
    rows = memory_grad.shape[1]
    for index in range(shards - 1):
        for chunk in range(chunks):

            @pl.when((pl.program_id(0) == index) & (pl.program_id(1) == chunk))
            def _(index=index, chunk=chunk):
                tokens_grad[...] = tokens_parts[index][...].astype(wide)
                block = arrived[chunk][index]
                output[...] = block[:, rows:, :]
                memory_grad[...] = block[:, :rows, :].astype(wide)


def swap(value, axis, bit):
    size = lax.axis_size(axis)
    return lax.ppermute(value, axis, [(index, index ^ bit) for index in range(size)])


def after(value, *earlier):
    return lax.optimization_barrier((value,) + earlier)[0]


def gather_slots(shard):
    gathered = shard[None]
    for axis, bit in gather_order[:3]:
        gathered = jnp.concatenate([gathered, swap(gathered, axis, bit)], 0)
    beside = swap(gathered, *gather_order[3])
    pieces = [gathered, beside, swap(gathered, *gather_order[4]), swap(beside, *gather_order[4])]
    places = slot_places(gather_order, False)
    count = len(places) // 4
    return [
        (piece, places[index * count : (index + 1) * count]) for index, piece in enumerate(pieces)
    ]


def add_stage(kept, arrived):
    half = kept.shape[0] // 2

    def added(start, stop):
        total = kept[start:stop].astype(wide) + arrived[start:stop].astype(wide)
        return total.astype(narrow)

    if not half:
        return added(0, 1)[0], None
    return added(0, half), added(half, 2 * half)


def on_device(
    tokens,
    memory,
    cotangent,
    buckets,
    key_mask,
    task_groups,
    weights_in,
    weights_out,
    weights_up,
    weights_down,
    gains,
    position_bias,
    momentum_in,
    average_in,
    momentum_out,
    average_out,
    momentum_up,
    average_up,
    momentum_down,
    average_down,
    momentum_gain,
    average_gain,
    momentum_bias,
    average_bias,
):
    shards = lax.axis_size("tensor")
    replicas = lax.axis_size("dp")
    me_tensor = lax.axis_index("tensor")
    me_dp = lax.axis_index("dp")
    width = tokens.shape[2]
    seq = buckets.shape[1]
    seq_rows = tokens.shape[1]
    memory_rows = memory.shape[1]
    memory_len = memory_rows * shards
    group_count = tokens.shape[0]
    local = group_count // shards
    chunks = 2 if local % 2 == 0 else 1
    per_chunk = local // chunks
    bundle = 2 if per_chunk % 2 == 0 else 1
    steps = per_chunk // bundle
    bucket_count, heads_local = position_bias.shape
    heads = heads_local * shards
    gain_width = momentum_gain.shape[1]
    staged = shards == tensor_slots and replicas == dp_slots

    slot_base = [me_dp, me_tensor] if staged else [0 * me_dp, 0 * me_tensor]
    kernel_info = jnp.stack(slot_base + [me_tensor]).astype(jnp.int32)

    def square_shards():
        high, across = weights_in.shape[1], weights_in.shape[2]
        split = lambda block: block.reshape(high, -1, across).transpose(1, 0, 2)
        return (
            weights_in.astype(narrow),
            weights_out.astype(narrow).transpose(0, 2, 1),
            split(weights_up.astype(narrow)),
            split(weights_down.astype(narrow).T),
        )

    shard_in, shard_out, shard_up, shard_down = square_shards()
    slot_count = dp_slots * tensor_slots
    plain_places = [(slot // tensor_slots, slot % tensor_slots) for slot in range(slot_count)]

    def gather_late(blocks):
        count = blocks.shape[0]
        if staged:
            whole = lax.all_gather(blocks, ("dp", "tensor"), axis=0)
        else:
            whole = lax.all_gather(blocks, "dp", axis=1, tiled=True)
            whole = lax.all_gather(whole, "tensor", axis=2, tiled=True)
            whole = whole.reshape(count, dp_slots, 64, tensor_slots, 128).transpose(1, 3, 0, 2, 4)
            whole = whole.reshape(slot_count, count, 64, 128)
        return [whole], [(0, count, plain_places, False)]

    def gather_soon(blocks):
        if not staged:
            return gather_late(blocks)
        pieces, plans = [], []
        for piece, places in gather_slots(blocks):
            pieces.append(piece)
            plans.append((0, blocks.shape[0], places, True))
        return pieces, plans

    def exchange(values, start, count):
        found = []
        for index in range(shards):
            first = (me_tensor ^ index) * local + start
            blocks = [lax.dynamic_slice_in_dim(value, first, count, 0) for value in values]
            block = jnp.concatenate(blocks, 1) if len(blocks) > 1 else blocks[0]
            found.append(swap(block, "tensor", index) if index else block)
        return found

    late_pieces, late_plans = gather_late(
        jnp.concatenate([shard_in[3:6], shard_out[1:2], shard_up, shard_down], 0)
    )
    token_parts = exchange([tokens], 0, local)
    self_pieces, self_plans = gather_soon(jnp.concatenate([shard_in[:3], shard_out[:1]], 0))
    table = jnp.pad(position_bias.T, ((0, 0), (0, 128 - bucket_count)))
    table_all = jnp.concatenate(
        [swap(table, "tensor", index) if index else table for index in range(shards)], 0
    )
    memory_parts = []
    earlier = token_parts
    for chunk in range(chunks):
        source, _ = lax.optimization_barrier((memory, earlier[-1]))
        earlier = exchange([source, cotangent], chunk * per_chunk, per_chunk)
        memory_parts.append(earlier)
    bucket_mine = lax.dynamic_slice_in_dim(buckets, me_tensor * local, local, 0)
    mask_mine = lax.dynamic_slice_in_dim(key_mask, me_tensor * local, local, 0)
    groups_mine = lax.dynamic_slice_in_dim(task_groups, me_tensor * local, local, 0)

    smem = pl.BlockSpec(memory_space=pltpu.SMEM)
    anywhere = pl.BlockSpec(memory_space=pl.ANY)
    params = pltpu.CompilerParams(
        vmem_limit_bytes=vmem_bytes, dimension_semantics=("arbitrary",)
    )

    def part_spec(shape, offset=0, lead=None):
        zeros = (0,) * len(shape)
        if lead is None:
            return pl.BlockSpec(
                (bundle,) + tuple(shape), lambda step, *_: (step + offset,) + zeros
            )
        return pl.BlockSpec(
            (lead, bundle) + tuple(shape), lambda step, *_: (0, step + offset) + zeros
        )

    def own_spec(shape, offset=0):
        zeros = (0,) * len(shape)
        return pl.BlockSpec(
            (bundle,) + tuple(shape),
            lambda step, info: (info[2] * (local // bundle) + step + offset,) + zeros,
        )

    def whole_spec(shape):
        return pl.BlockSpec(tuple(shape), lambda step, *_: (0,) * len(shape))

    def shaped(shape, dtype, lead=None, count=local):
        front = (count,) if lead is None else (lead, count)
        return jax.ShapeDtypeStruct(front + tuple(shape), dtype)

    def cost(flops, moved):
        return pl.CostEstimate(
            flops=int(flops * cost_scale), bytes_accessed=int(moved * cost_scale), transcendentals=0
        )

    groups = width // quad_width
    row_block = (seq, width)
    part_rows = memory_rows + seq_rows

    normed_a, rows_a, qkv_a, weights_a, mix_a, mid = pl.pallas_call(
        functools.partial(self_forward_kernel, shards, self_plans, heads_local),
        grid=(local // bundle,),
        in_specs=[smem]
        + [part_spec((seq_rows, width))] * shards
        + [part_spec((seq, seq))] * 2
        + [whole_spec(gains.shape), whole_spec(table_all.shape)]
        + [anywhere] * len(self_pieces),
        out_specs=[
            part_spec(row_block),
            part_spec(row_block),
            part_spec(row_block, lead=3),
            part_spec((groups, seq, quad * seq)),
            part_spec(row_block),
            part_spec(row_block),
        ],
        out_shape=[
            shaped(row_block, narrow),
            shaped(row_block, narrow),
            shaped(row_block, narrow, 3),
            shaped((groups, seq, quad * seq), wide),
            shaped(row_block, narrow),
            shaped(row_block, wide),
        ],
        scratch_shapes=[
            pltpu.VMEM((4, width, width), narrow),
            pltpu.SemaphoreType.DMA((len(self_pieces),)),
            pltpu.VMEM((bundle,) + row_block, narrow),
            pltpu.VMEM((bundle,) + row_block, narrow),
        ],
        compiler_params=params,
        name="self_forward",
        cost_estimate=cost(local * 2e9, local * 2e6),
    )(
        kernel_info,
        *token_parts,
        bucket_mine,
        mask_mine,
        gains,
        table_all,
        *self_pieces,
    )

    def cross(chunk, filled):
        offset = chunk * steps
        gain_block = (1, width)
        kept_specs = [
            part_spec(row_block, offset),
            part_spec(row_block, offset),
            part_spec(row_block, offset),
            part_spec((memory_len, width), offset, 2),
            part_spec(row_block, offset),
            part_spec(row_block, offset),
            part_spec(row_block, offset),
            part_spec(row_block, offset, 4),
            part_spec(row_block, offset, 4),
            part_spec(row_block, offset),
            part_spec(gain_block, offset),
            part_spec(gain_block, offset),
            part_spec((1, 128), offset),
        ]
        kept_shapes = [
            shaped(row_block, wide),
            shaped(row_block, narrow),
            shaped(row_block, narrow),
            shaped((memory_len, width), narrow, 2),
            shaped(row_block, narrow),
            shaped(row_block, narrow),
            shaped(row_block, narrow),
            shaped(row_block, narrow, 4),
            shaped(row_block, narrow, 4),
            shaped(row_block, narrow),
            shaped(gain_block, wide),
            shaped(gain_block, wide),
            shaped((1, 128), wide),
        ]
        own_specs = [own_spec((seq_rows, width), offset), own_spec((memory_rows, width), offset)]
        own_shapes = [
            shaped((seq_rows, width), narrow, count=group_count),
            shaped((memory_rows, width), wide, count=group_count),
        ]
        operands = [kernel_info, *memory_parts[chunk], mid, gains, *late_pieces]
        aliases = {}
        for index, block in enumerate(filled):
            aliases[len(operands) + index] = index if index < 2 else index + shards - 1
        return pl.pallas_call(
            functools.partial(cross_kernel, shards, late_plans, len(filled)),
            grid_spec=pltpu.PrefetchScalarGridSpec(
                num_scalar_prefetch=1,
                grid=(steps,),
                in_specs=[part_spec((part_rows, width))] * shards
                + [part_spec(row_block, offset), whole_spec(gains.shape)]
                + [anywhere] * (len(late_pieces) + len(filled)),
                out_specs=own_specs + [part_spec((part_rows, width))] * (shards - 1) + kept_specs,
                scratch_shapes=[
                    pltpu.VMEM((12, width, width), narrow),
                    pltpu.SemaphoreType.DMA((len(late_pieces),)),
                    pltpu.VMEM((bundle, memory_len, width), narrow),
                    pltpu.VMEM((bundle, memory_len, width), narrow),
                    pltpu.VMEM((bundle, memory_len, width), narrow),
                    pltpu.VMEM((bundle, groups, memory_len, quad * seq), wide),
                    pltpu.VMEM((bundle,) + row_block, wide),
                    pltpu.VMEM((bundle,) + row_block, narrow),
                ],
            ),
            out_shape=own_shapes
            + [shaped((part_rows, width), narrow, count=per_chunk)] * (shards - 1)
            + kept_shapes,
            input_output_aliases=aliases,
            compiler_params=params,
            name="cross",
            cost_estimate=cost(per_chunk * 8e9, per_chunk * 6e6),
        )(*operands, *filled)

    filled, sent = [], []
    for chunk in range(chunks):
        found = cross(chunk, filled)
        sent.append(found[2 : shards + 1])
        filled = list(found[:2]) + list(found[shards + 1 :])
    own_output, own_memory = filled[:2]
    (
        early,
        normed_b,
        d_query_b,
        d_pair,
        mix_b,
        d_mid,
        normed_c,
        d_hidden,
        active,
        d_top,
        d_gain_b,
        d_gain_c,
        squares,
    ) = filled[2:]
    arrived = [
        [swap(block, "tensor", index + 1) for index, block in enumerate(blocks)] for blocks in sent
    ]
    soon = [block for blocks in arrived[:-1] for block in blocks]

    found = pl.pallas_call(
        functools.partial(self_backward_kernel, shards, self_plans),
        grid_spec=pltpu.PrefetchScalarGridSpec(
            num_scalar_prefetch=1,
            grid=(local // bundle,),
            in_specs=[
            part_spec(row_block),
            part_spec(row_block),
            part_spec(row_block),
            part_spec(row_block, lead=3),
            part_spec((groups, seq, quad * seq)),
            part_spec(row_block),
            part_spec((1, 128)),
            part_spec((1, width)),
            part_spec((1, width)),
            part_spec((seq, seq)),
            whole_spec(gains.shape),
        ]
        + [anywhere] * len(self_pieces),
        out_specs=[own_spec((seq_rows, width))]
        + [part_spec((seq_rows, width))] * (shards - 1)
        + [
            part_spec(row_block, lead=3),
            part_spec(row_block),
            part_spec((1, 3 * width + heads * bucket_count)),
            part_spec((1, 128)),
        ],
        scratch_shapes=[
            pltpu.VMEM((4, width, width), narrow),
            pltpu.SemaphoreType.DMA((len(self_pieces),)),
            pltpu.VMEM((bundle,) + row_block, wide),
            pltpu.VMEM((heads * bucket_count, 128), wide),
        ],
        ),
        out_shape=[shaped((seq_rows, width), wide, count=group_count)]
        + [shaped((seq_rows, width), narrow)] * (shards - 1)
        + [
            shaped(row_block, narrow, 3),
            shaped(row_block, narrow),
            shaped((1, 3 * width + heads * bucket_count), wide),
            shaped((1, 128), wide),
        ],
        compiler_params=params,
        name="self_backward",
        cost_estimate=cost(local * 3e9, local * 3e6),
    )(
        after(kernel_info, *soon),
        early,
        rows_a,
        normed_a,
        qkv_a,
        weights_a,
        mix_a,
        squares,
        d_gain_b,
        d_gain_c,
        bucket_mine,
        gains,
        *self_pieces,
    )
    own_tokens, tokens_sent = found[0], found[1:shards]
    d_qkv, d_early, small, norms = found[shards:]

    norms = after(norms.reshape(local, 128), *arrived[-1])
    norm_slots = norms
    bit = 1
    while bit < shards:
        norm_slots = jnp.concatenate([norm_slots, swap(norm_slots, "tensor", bit)], 0)
        bit *= 2
    total = jnp.broadcast_to(jnp.sum(norm_slots, 0, keepdims=True), (8, 128))
    bit = 1
    while bit < replicas:
        total = total + swap(total, "dp", bit)
        bit *= 2
    order = jnp.arange(shards, dtype=jnp.int32) ^ me_tensor
    example_norms = norm_slots[:, 0].reshape(shards, local)[order].reshape(group_count)
    mean_norm = total[0, 0] / (group_count * replicas)
    limits = jnp.sum(
        (groups_mine[:, None] == jnp.arange(len(group_limits), dtype=jnp.int32))
        * jnp.asarray(group_limits, wide),
        1,
    )
    clip_weights = jnp.minimum(1.0 / mean_norm, limits / norms[:, 0])
    small = jnp.sum(clip_weights[:, None, None] * small, 0).reshape(-1, 128)

    def places_of(index):
        return slot_places(reduce_orders[index], True) if staged else plain_places

    out_shapes = [
        jax.ShapeDtypeStruct((slot_count // 2, count, 64, 128), narrow) for count in reduce_counts
    ]

    def gradient_call(kernel, clip, operands, outs, loads, extra, name, work):
        return pl.pallas_call(
            kernel,
            in_specs=[smem, smem] + [anywhere] * len(operands),
            out_specs=[anywhere] * 4,
            out_shape=[shape for shape in outs for _ in range(2)],
            scratch_shapes=extra
            + [
                pltpu.SemaphoreType.DMA((loads,)),
                pltpu.VMEM((local * seq, width), narrow),
                pltpu.VMEM((2, width, width), narrow),
                pltpu.VMEM((8, 2, slot_count // 2, 64, 128), narrow),
                pltpu.SemaphoreType.DMA((16,)),
            ],
            compiler_params=pltpu.CompilerParams(vmem_limit_bytes=vmem_bytes),
            name=name,
            cost_estimate=work,
        )(kernel_info, clip, *operands)

    def inner_gradients(clip):
        kernel = functools.partial(inner_gradient_kernel, (places_of(0), places_of(1)))
        extra = [
            pltpu.VMEM((2, local, seq, width), narrow),
            pltpu.VMEM((8, local, seq, width), narrow),
        ]
        operands = [normed_c, d_hidden, d_top, active]
        return gradient_call(
            kernel, clip, operands, out_shapes[:2], 10, extra, "inner_gradients", cost(9e9, 14e6)
        )

    def attention_gradients(clip):
        kernel = functools.partial(
            attention_gradient_kernel, shards, chunks, (places_of(2), places_of(3))
        )
        extra = [
            pltpu.VMEM((10, local, seq, width), narrow),
            pltpu.VMEM((chunks * shards, per_chunk, memory_rows, width), narrow),
            pltpu.VMEM((2 * chunks, per_chunk, memory_len, width), narrow),
            pltpu.VMEM((chunks, per_chunk * memory_len, width), narrow),
        ]
        operands = [normed_a, d_qkv, d_early, mix_a, normed_b, d_query_b, d_mid, mix_b]
        operands += [block for blocks in memory_parts for block in blocks] + [d_pair]
        return gradient_call(
            kernel,
            clip,
            operands,
            out_shapes[2:],
            10 + chunks * (shards + 2),
            extra,
            "attention_gradients",
            cost(14e9, 30e6),
        )

    tokens_arrived = [swap(block, "tensor", index + 1) for index, block in enumerate(tokens_sent)]

    def by_place(shape, index, chunk=None):
        def spot(place, step, info):
            if chunk is not None:
                return (0, 0, 0)
            return (jnp.where(place == index, step, jnp.where(place < index, 0, chunks - 1)), 0, 0)

        return pl.BlockSpec((per_chunk,) + shape, spot)

    def to_place(shape):
        return pl.BlockSpec(
            (per_chunk,) + shape,
            lambda place, step, info: ((info[2] ^ (place + 1)) * chunks + step, 0, 0),
        )

    small_rows, large_rows = (seq_rows, width), (memory_rows, width)
    operands = [block for blocks in arrived for block in blocks] + tokens_arrived
    assemble = pl.pallas_call(
        functools.partial(assemble_kernel, shards, chunks),
        grid_spec=pltpu.PrefetchScalarGridSpec(
            num_scalar_prefetch=1,
            grid=(shards - 1, chunks),
            in_specs=[
                by_place((part_rows, width), index, chunk)
                for chunk in range(chunks)
                for index in range(shards - 1)
            ]
            + [by_place(small_rows, index) for index in range(shards - 1)]
            + [anywhere] * 3,
            out_specs=[to_place(small_rows), to_place(small_rows), to_place(large_rows)],
        ),
        out_shape=[
            jax.ShapeDtypeStruct((group_count,) + small_rows, narrow),
            jax.ShapeDtypeStruct((group_count,) + small_rows, wide),
            jax.ShapeDtypeStruct((group_count,) + large_rows, wide),
        ],
        input_output_aliases={len(operands) + 1 + index: index for index in range(3)},
        compiler_params=pltpu.CompilerParams(
            vmem_limit_bytes=vmem_bytes, dimension_semantics=("arbitrary", "arbitrary")
        ),
        name="assemble",
        cost_estimate=cost(1e6, 20e6),
    )
    returned = operands + [own_output, own_tokens, own_memory]

    pairs = [None] * 4

    def travel(index, stage):
        kept, sent = pairs[index]
        pairs[index] = add_stage(kept, swap(sent, *reduce_orders[index][stage]))

    last_stage = len(reduce_orders[0]) - 1
    done = [0] * 4

    def travel(*indices):
        for index in indices:
            if staged and done[index] <= last_stage:
                kept, sent = pairs[index]
                order = reduce_orders[index][done[index]]
                pairs[index] = add_stage(kept, swap(sent, *order))
                done[index] += 1

    def there(*indices):
        return [block for index in indices for block in pairs[index] if block is not None]

    found = inner_gradients(clip_weights)
    pairs[:2] = [tuple(found[:2]), tuple(found[2:])]
    found = attention_gradients(after(clip_weights, *there(0, 1), *tokens_arrived))
    pairs[2:] = [tuple(found[:2]), tuple(found[2:])]
    travel(0, 1)
    travel(2, 3)
    travel(0, 1, 2, 3)
    output, tokens_grad, memory_grad = assemble(after(kernel_info, *there(0)), *returned)

    def together(*extra):
        held = lax.optimization_barrier((pairs, extra))
        pairs[:] = held[0]
        return held[1]

    shrink = 1.0 / math.sqrt(group_count * replicas)
    if staged:
        small = small + swap(small, *core)
        small = after(small, *there(2, 3))
        small = small + swap(small, *side)
        small, output = together(small, output)
        small = small + swap(small, *row)
        travel(0, 1, 2, 3)
        (small,) = together(small)
        small = small + swap(small, *near)
        travel(0, 1, 2, 3)
        (small,) = together(small)
        small = small + swap(small, *far)
        last = [swap(sent, *order[-1]) for (kept, sent), order in zip(pairs, reduce_orders)]
        last = [block[0] for pair, came in zip(pairs, last) for block in (pair[0], came)]
    else:
        reduced = []
        for kept, sent in pairs:
            whole = jnp.concatenate([kept, sent], 0)
            count = whole.shape[1]
            whole = whole.reshape(dp_slots, tensor_slots, count, 64, 128).transpose(2, 0, 3, 1, 4)
            whole = whole.reshape(count, width, width)
            whole = lax.psum_scatter(whole, "dp", scatter_dimension=1, tiled=True)
            reduced.append(lax.psum_scatter(whole, "tensor", scatter_dimension=2, tiled=True))
        small = lax.psum(small, ("dp", "tensor"))
    small = small.reshape(-1)
    gain_total = small[: 3 * width].reshape(3, width)
    bias_total = small[3 * width :].reshape(heads, bucket_count).T

    large = [
        (weights_in, momentum_in, average_in, matrix_rate),
        (weights_out, momentum_out, average_out, output_rate),
        (weights_up, momentum_up, average_up, matrix_rate),
        (weights_down, momentum_down, average_down, matrix_rate),
    ]
    if staged:
        turns = ((0, 1, 2), (0, 2, 1), (0, 1), (1, 0))
        turned = [
            block.transpose(turn) for group, turn in zip(large, turns) for block in group[:3]
        ]
        operands = last + turned
        stepped = pl.pallas_call(
            functools.partial(update_kernel, shrink),
            out_shape=[
                jax.ShapeDtypeStruct(block.shape, wide) for block in turned
            ],
            compiler_params=pltpu.CompilerParams(vmem_limit_bytes=vmem_bytes),
            name="update",
            cost_estimate=cost(1e6, 4e6),
        )(*operands)
        stepped = [block.transpose(turns[index // 3]) for index, block in enumerate(stepped)]
    else:
        reduced = [block.astype(wide) * shrink for block in reduced]

        def merge(blocks):
            count, high, across = blocks.shape
            return blocks.transpose(1, 0, 2).reshape(high, count * across)

        inside = jnp.concatenate([reduced[2], reduced[3][1:2], reduced[3][3:]], 0)
        outward = jnp.stack([reduced[3][0].T, reduced[3][2].T], 0)
        down = jnp.concatenate([reduced[0][4:], reduced[1]], 0)
        gradients = [inside, outward, merge(reduced[0][:4]), merge(down).T]
        stepped = []
        for (weight, momentum, average, rate), gradient in zip(large, gradients):
            stepped += stepper(weight, gradient, momentum, average, rate)
    (
        velocity_in,
        averaged_in,
        updated_in,
        velocity_out,
        averaged_out,
        updated_out,
        velocity_up,
        averaged_up,
        updated_up,
        velocity_down,
        averaged_down,
        updated_down,
    ) = stepped

    gain_start = me_tensor * gain_width
    gain_shard = lax.dynamic_slice_in_dim(gains, gain_start, gain_width, 1)
    gain_grad = lax.dynamic_slice_in_dim(gain_total, gain_start, gain_width, 1) * shrink
    bias_grad = (
        lax.dynamic_slice_in_dim(bias_total, me_tensor * heads_local, heads_local, 1) * shrink
    )
    velocity_gain, averaged_gain, updated_gain = stepper(
        gain_shard, gain_grad, momentum_gain, average_gain, small_rate
    )
    velocity_bias, averaged_bias, updated_bias = stepper(
        position_bias, bias_grad, momentum_bias, average_bias, small_rate
    )
    return (
        output,
        tokens_grad,
        memory_grad,
        example_norms,
        velocity_in,
        averaged_in,
        updated_in,
        velocity_out,
        averaged_out,
        updated_out,
        velocity_up,
        averaged_up,
        updated_up,
        velocity_down,
        averaged_down,
        updated_down,
        velocity_gain,
        averaged_gain,
        updated_gain,
        velocity_bias,
        averaged_bias,
        updated_bias,
    )


def solution(mesh):
    return jax.shard_map(
        on_device,
        mesh=mesh,
        in_specs=(
            P("dp", "tensor", None),
            P("dp", "tensor", None),
            P("dp", "tensor", None),
            P("dp", None, None),
            P("dp", None, None),
            P("dp"),
            P(None, "dp", "tensor"),
            P(None, "tensor", "dp"),
            P("dp", "tensor"),
            P("tensor", "dp"),
            P(),
            P(None, "tensor"),
            P(None, "dp", "tensor"),
            P(None, "dp", "tensor"),
            P(None, "tensor", "dp"),
            P(None, "tensor", "dp"),
            P("dp", "tensor"),
            P("dp", "tensor"),
            P("tensor", "dp"),
            P("tensor", "dp"),
            P(None, "tensor"),
            P(None, "tensor"),
            P(None, "tensor"),
            P(None, "tensor"),
        ),
        out_specs=(
            P("dp", "tensor", None),
            P("dp", "tensor", None),
            P("dp", "tensor", None),
            P("dp"),
            P(None, "dp", "tensor"),
            P(None, "dp", "tensor"),
            P(None, "dp", "tensor"),
            P(None, "tensor", "dp"),
            P(None, "tensor", "dp"),
            P(None, "tensor", "dp"),
            P("dp", "tensor"),
            P("dp", "tensor"),
            P("dp", "tensor"),
            P("tensor", "dp"),
            P("tensor", "dp"),
            P("tensor", "dp"),
            P(None, "tensor"),
            P(None, "tensor"),
            P(None, "tensor"),
            P(None, "tensor"),
            P(None, "tensor"),
            P(None, "tensor"),
        ),
        check_vma=False,
    )
```

time: 537 us -> 352 us (0.66)
  local copies, waits for them, and re-layouts: 61.6 us -> 12.9 us
  starting transfers between devices: 103 us -> 54.7 us
  blocking collectives: 38.1 us -> 0 us
  waiting for transfers between devices: 120 us -> 90.2 us
  other arithmetic: 36.7 us -> 18.4 us
  Pallas kernels: 168 us -> 154 us
  between operations: 3.52 us -> 15.8 us
    ppermute x111 -> x57, starting transfers between devices: 103 us -> 54.6 us  [swap(): lax.ppermute(value, axis, [(index, index ^ bit) for index in range(size)])]
    ppermute x111 -> x57, waiting for transfers between devices: 120 us -> 78.3 us  [swap(): lax.ppermute(value, axis, [(index, index ^ bit) for index in range(size)])]
    psum x1 -> x0, blocking collectives: 38.1 us -> none  [on_device(): small = lax.psum(small.reshape(-1, 128), ('dp', 'tensor')).reshape(-1)]
    unnamed x205 -> x84, local copies, waits for them, and re-layouts: 17.8 us -> 2.47 us
    dynamic_update_slice x12 -> x0, other arithmetic: 15.1 us -> none  [give_back(): lax.dynamic_update_slice_in_dim(whole, arrived.astype(dtype), place, 0)]
    pallas_call x14 -> x8, Pallas kernels: 168 us -> 154 us  [the longest x2 71.9 us: cross(): pl.pallas_call(functools.partial(cross_kernel, shards, late_plans, len(fi...]
    all_gather x0 -> x1, waiting for transfers between devices: none -> 11.9 us  [gather_late(): whole = lax.all_gather(blocks, ('dp', 'tensor'), axis=0)]
    slice x41 -> x2, local copies, waits for them, and re-layouts: 11 us -> 1.32 us  [the longest x1 0.8 us: on_device(): clip_weights = jnp.minimum(1.0 / mean_norm, limits / norms[:, 0])]
  transfers between devices with their start and end apart: 111 -> 58, of which waited for: 30 -> 20; matrix products, arithmetic and copies ran while one was open for 17% -> 6% of each run, Pallas kernels for 22% -> 44%
where the time goes in v2:
time: 352 us; the launch traced here: 346 us
  Pallas kernels  154 us (44%)
  waiting for transfers between devices  90.2 us (26%)
  starting transfers between devices  54.7 us (16%)
  other arithmetic  18.4 us (5%)
  between operations  15.8 us (4%)
  local copies, waits for them, and re-layouts  12.9 us (4%)
    ppermute x57, waiting for transfers between devices, swap(): lax.ppermute(value, axis, [(index, index ^ bit) for index in range(size)])  78.3 us
    pallas_call x2, Pallas kernels, cross(): pl.pallas_call(functools.partial(cross_kernel, shards, late_plans, len(fi...  71.9 us
    ppermute x57, starting transfers between devices, swap(): lax.ppermute(value, axis, [(index, index ^ bit) for index in range(size)])  54.6 us
    pallas_call x1, Pallas kernels, on_device(): pl.pallas_call(functools.partial(self_backward_kernel, shards, self_plans...  32.7 us
    pallas_call x2, Pallas kernels, gradient_call(): pl.pallas_call(kernel, in_specs=[smem, smem] + [anywhere] * len(operands)...  25.3 us
    pallas_call x1, Pallas kernels, on_device(): pl.pallas_call(functools.partial(self_forward_kernel, shards, self_plans,...  14 us
    all_gather x1, waiting for transfers between devices, gather_late(): whole = lax.all_gather(blocks, ('dp', 'tensor'), axis=0)  11.9 us
    pallas_call x1, Pallas kernels, on_device(): assemble(after(kernel_info, *there(0)), *returned)  7.69 us
  transfers between devices with their start and end apart: 58, of which 20 were waited for; matrix products, arithmetic and copies ran while one was open for 6% of the time, Pallas kernels for 44%

profile of v2, /device:TPU:0, one launch (start us, length us, event | category | flops | bytes accessed | tf_op | source)
XLA Modules:
  0.0 346.4 jit_solution(4967480823664209377)
XLA Ops:
  7.3 1.0 convert_bitcast_fusion.1
  8.3 1.0 convert_element_type.303
  9.3 0.9 convert_bitcast_fusion
  10.3 0.9 convert_element_type.305
  12.3 2.5 collective-permute-start.8
  15.4 1.0 constant_dynamic-slice_fusion.13
  16.4 1.5 collective-permute-start
  17.9 2.7 collective-permute-start.9
  20.5 1.4 constant_dynamic-slice_fusion.3
  21.9 2.8 collective-permute-done.9
  26.3 1.9 constant_dynamic-slice_fusion.11.refs_6_
  28.2 2.8 collective-permute-done.10
  31.1 1.7 constant_dynamic-slice_fusion.17
  33.3 7.0 %collective-permute-done.11 = bf16[4,4,64,128]{3,2,1,0:T(8,128)(2,1)S(1)} collective-permute-done((bf16[4,4,64,128]{3,2,1,0:T(8,128)(2,1)S(1)}, bf16[4,4,64,128]{3,2,1,0:T(8,128)(2,1)S(1)}, u32[]{:S(2)}, u32[]{:S(2)}) %collective-permute-start.11) | collective-permute-done | bytes 262176 | tf_op jit(solution)/shard_map/ppermute | solution.py:657
  40.3 1.6 collective-permute-start.12
  43.8 0.9 pad_maximum_fusion.refs_1_.refs_8_
  44.7 9.5 %collective-permute-done.3.refs_4_.refs_11_ = bf16[4,160,512]{2,1,0:T(8,128)(2,1)S(1)} collective-permute-done((bf16[4,160,512]{2,1,0:T(8,128)(2,1)S(1)}, bf16[4,160,512]{2,1,0:T(8,128)(2,1)S(1)}, u32[]{:S(2)}, u32[]{:S(2)}) %collective-permute-start.3) | collective-permute-done | bytes 655392 | tf_op jit(solution)/shard_map/ppermute | solution.py:657
  54.2 3.1 collective-permute-start.13
  58.3 0.9 pad_maximum_fusion.4.refs_1_.refs_12_
  59.2 0.9 pad_maximum_fusion.5
  60.1 0.9 pad_maximum_fusion.7
  61.8 1.7 collective-permute-start.19
  64.3 14.0 %self_forward.1 = (bf16[8,128,512]{2,1,0:T(8,128)(2,1)}, bf16[8,128,512]{2,1,0:T(8,128)(2,1)}, bf16[3,8,128,512]{3,2,1,0:T(8,128)(2,1)}, f32[8,2,128,512]{3,2,1,...) custom-call(s32[3]{0:T(128)} %pad_add_fusion.refs_0_.info, ...), custom_call_target="tpu_custom_call" | custom-call | flops 16000000000 | bytes 16000000 | tf_op jit(solution)/shard_map/self_forward/pallas_call | solution.py:839
  78.3 11.1 %collective-permute-done.2.refs_3_.refs_10_ = bf16[4,160,512]{2,1,0:T(8,128)(2,1)} collective-permute-done((bf16[4,160,512]{2,1,0:T(8,128)(2,1)S(1)}, bf16[4,160,512]{2,1,0:T(8,128)(2,1)}, u32[]{:S(2)}, u32[]{:S(2)}) %collective-permute-start.2) | collective-permute-done | bytes 655392 | tf_op jit(solution)/shard_map/ppermute | solution.py:657
  89.4 11.9 %all-gather.3.cloned.1.call-done = bf16[384,64,128]{2,1,0:T(8,128)(2,1)} async-done(((bf16[12,64,128]{2,1,0:T(8,128)(2,1)}), bf16[384,64,128]{2,1,0:T(8,128)(2,1)}) %all-gather.3.cloned.1.call-update) | async-done | bytes 6291472 | tf_op jit(solution)/shard_map/all_gather | solution.py:755
  101.3 35.8 %cross.2 = (bf16[32,32,512]{2,1,0:T(8,128)(2,1)}, f32[32,128,512]{2,1,0:T(8,128)}, bf16[4,160,512]{2,1,0:T(8,128)(2,1)}, bf16[4,160,512]{2,1,0:T(8,128)(2,1)}, b...) custom-call(s32[3]{0:T(128)} %pad_add_fusion.refs_0_.info, ...), custom_call_target="tpu_custom_call" | custom-call | flops 32000000000 | bytes 24000000 | tf_op jit(solution)/shard_map/cross/pallas_call | solution.py:924
  138.0 1.0 collective-permute-start.17
  139.8 36.2 %cross.3 = (bf16[32,32,512]{2,1,0:T(8,128)(2,1)}, f32[32,128,512]{2,1,0:T(8,128)}, bf16[4,160,512]{2,1,0:T(8,128)(2,1)}, bf16[4,160,512]{2,1,0:T(8,128)(2,1)}, b...) custom-call(s32[3]{0:T(128)} %pad_add_fusion.refs_0_.info, ...), custom_call_target="tpu_custom_call", output_to_operand_aliasing={{0}: (8, {}), {1}: (9, {}), {5}: (10, {}), {6}: (11, {}), {... | custom-call | flops 32000000000 | bytes 24000000 | tf_op jit(solution)/shard_map/cross/pallas_call | solution.py:924
  177.2 0.9 collective-permute-start.23
  178.1 32.7 %self_backward.1 = (f32[32,32,512]{2,1,0:T(8,128)}, bf16[8,32,512]{2,1,0:T(8,128)(2,1)}, bf16[8,32,512]{2,1,0:T(8,128)(2,1)}, bf16[8,32,512]{2,1,0:T(8,128)(2,1)...) custom-call(s32[3]{0:T(128)} %pad_add_fusion.refs_0_.info, ...), custom_call_target="tpu_custom_call" | custom-call | flops 24000000000 | bytes 24000000 | tf_op jit(solution)/shard_map/self_backward/pallas_call | solution.py:979
  211.7 1.0 collective-permute-done.24
  214.7 2.4 collective-permute-done.25
  217.1 1.5 collective-permute-start.26
  218.7 2.1 collective-permute-done.26
  220.8 1.6 collective-permute-start.27
  222.5 1.9 collective-permute-done.27
  224.4 2.0 collective-permute-start.28
  227.8 1.2 collective-permute-start.35
  230.8 10.1 %inner_gradients.1 = (bf16[16,5,64,128]{3,2,1,0:T(8,128)(2,1)}, bf16[16,5,64,128]{3,2,1,0:T(8,128)(2,1)}, bf16[16,3,64,128]{3,2,1,0:T(8,128)(2,1)}, bf16[16,3,64,128]{3,2,1,0:T(8,128)(2,1)}) custom-call(s32[3]{0:T(128)} %pad_add_fusion.refs_0_.info, f32[8]{0:T(128)} %divide_minimum_fusion.clip, bf16[8,128,512]{2,1,0:T(8,128)(2,1)} %get-tuple-element.166.normed, ...), custom_call_target="tpu_custom_call" | custom-call | flops 8999999488 | bytes 14000000 | tf_op jit(solution)/shard_map/inner_gradients/pallas_call | solution.py:1072
  241.4 15.2 %attention_gradients.1 = (bf16[16,3,64,128]{3,2,1,0:T(8,128)(2,1)}, bf16[16,3,64,128]{3,2,1,0:T(8,128)(2,1)}, bf16[16,5,64,128]{3,2,1,0:T(8,128)(2,1)}, bf16[16,5,64,128]{3,2,1,0:T(8,128)(2,1)}) custom-call(s32[3]{0:T(128)} %pad_add_fusion.refs_0_.info, f32[8]{0:T(128)} %divide_minimum_fusion.clip, bf16[8,128,512]{2,1,0:T(8,128)(2,1)} %get-tuple-element.154.refs_3_.refs_0_, ...), custom_call_target="tpu_custom_call" | custom-call | flops 14000000000 | bytes 30000000 | tf_op jit(solution)/shard_map/attention_gradients/pallas_call | solution.py:1072
  257.9 4.8 %collective-permute-done.40 = f32[14,128]{1,0:T(8,128)S(1)} collective-permute-done((f32[14,128]{1,0:T(8,128)S(1)}, f32[14,128]{1,0:T(8,128)S(1)}, u32[]{:S(2)}, u32[]{:S(2)}) %collective-permute-start.40) | collective-permute-done | bytes 7200 | tf_op jit(solution)/shard_map/ppermute | solution.py:657
  264.0 1.5 collective-permute-start.37
  266.1 1.3 collective-permute-start.39
  267.9 1.5 collective-permute-start.30
  269.4 5.7 %collective-permute-done.32 = bf16[8,3,64,128]{3,2,1,0:T(8,128)(2,1)S(1)} collective-permute-done((bf16[8,3,64,128]{3,2,1,0:T(8,128)(2,1)S(1)}, bf16[8,3,64,128]{3,2,1,0:T(8,128)(2,1)S(1)}, u32[]{:S(2)}, u32[]{:S(2)}) %collective-permute-start.32) | collective-permute-done | bytes 393248 | tf_op jit(solution)/shard_map/ppermute | solution.py:657
  275.2 7.5 %collective-permute-done.37 = bf16[8,3,64,128]{3,2,1,0:T(8,128)(2,1)S(1)} collective-permute-done((bf16[8,3,64,128]{3,2,1,0:T(8,128)(2,1)S(1)}, bf16[8,3,64,128]{3,2,1,0:T(8,128)(2,1)S(1)}, u32[]{:S(2)}, u32[]{:S(2)}) %collective-permute-start.37) | collective-permute-done | bytes 393248 | tf_op jit(solution)/shard_map/ppermute | solution.py:657
  283.1 1.5 collective-permute-start.41
  284.9 7.7 %assemble.1 = (bf16[32,32,512]{2,1,0:T(8,128)(2,1)}, f32[32,32,512]{2,1,0:T(8,128)}, f32[32,128,512]{2,1,0:T(8,128)}) custom-call(s32[3]{0:T(128)} %pad_add_fusion.refs_0_.info, bf16[4,160,512]{2,1,0:T(8,128)(2,1)} %copy-done.8, bf16[4,160,512]{2,1,0:T(8,128)(2,1)} %copy-done.9, ...), custom_call_target="tpu_custom_call", output_to_operand_aliasing={{0}: (10, {}), {1}: (11, {}), {2}: (12, {})} | custom-call | flops 1000000 | bytes 20000000 | tf_op jit(solution)/shard_map/assemble/pallas_call | solution.py:1197
  292.6 1.5 collective-permute-start.43
  294.7 1.5 collective-permute-start.42
  296.7 1.2 collective-permute-start.45
  297.9 1.6 collective-permute-done.43
  299.5 2.3 collective-permute-done.44
  301.9 1.2 collective-permute-done.42
  303.2 9.1 %collective-permute-done.45 = bf16[4,5,64,128]{3,2,1,0:T(8,128)(2,1)S(1)} collective-permute-done((bf16[4,5,64,128]{3,2,1,0:T(8,128)(2,1)S(1)}, bf16[4,5,64,128]{3,2,1,0:T(8,128)(2,1)S(1)}, u32[]{:S(2)}, u32[]{:S(2)}) %collective-permute-start.45) | collective-permute-done | bytes 327712 | tf_op jit(solution)/shard_map/ppermute | solution.py:657
  312.5 2.4 collective-permute-start.51
  315.0 2.0 collective-permute-start.49
  316.9 1.5 collective-permute-start.50
  319.3 3.4 collective-permute-done.49
  326.6 2.4 collective-permute-start.52
  328.9 1.9 collective-permute-start.53
  331.9 1.3 multiply_add_fusion
  333.8 2.0 collective-permute-done.54
  336.5 2.8 update.1
  (225 shorter events, 30.3 us)
Async XLA Ops:
  7.2 94.1 %all-gather.3.cloned.1.call-start = ((), (), s32[]{:S(2)}) async-start(), calls=%async_computation | async-start | bytes 6488064 | tf_op jit(solution)/shard_map/all_gather | solution.py:755
  12.3 30.3 %collective-permute-start.8 = (f32[2,128]{1,0:T(2,128)S(1)}, f32[2,128]{1,0:T(2,128)S(1)}, u32[]{:S(2)}, u32[]{:S(2)}) collective-permute-start(f32[2,128]{1,0:T(2,128)S(1)} %pad.4), channel_id=1, source_target_pairs={{0,3},{1,2},{2,1},{3,0},{4,7},{5,6},{6,5},{7,4},{8,11},{9,10},{10,... | collective-permute-start | bytes 3080 | tf_op jit(solution)/shard_map/ppermute | solution.py:657
  14.7 27.8 %collective-permute-start.7 = (f32[2,128]{1,0:T(2,128)S(1)}, f32[2,128]{1,0:T(2,128)S(1)}, u32[]{:S(2)}, u32[]{:S(2)}) collective-permute-start(f32[2,128]{1,0:T(2,128)S(1)} %pad.4), channel_id=1, source_target_pairs={{0,2},{1,3},{2,0},{3,1},{4,6},{5,7},{6,4},{7,5},{8,10},{9,11},{10,... | collective-permute-start | bytes 3080 | tf_op jit(solution)/shard_map/ppermute | solution.py:657
  15.4 27.3 %collective-permute-start.6 = (f32[2,128]{1,0:T(2,128)S(1)}, f32[2,128]{1,0:T(2,128)S(1)}, u32[]{:S(2)}, u32[]{:S(2)}) collective-permute-start(f32[2,128]{1,0:T(2,128)S(1)} %pad.4), channel_id=1, source_target_pairs={{0,1},{1,0},{2,3},{3,2},{4,5},{5,4},{6,7},{7,6},{8,9},{9,8},{10,11... | collective-permute-start | bytes 3080 | tf_op jit(solution)/shard_map/ppermute | solution.py:657
  16.4 14.7 %collective-permute-start = (bf16[8,32,512]{2,1,0:T(8,128)(2,1)}, bf16[8,32,512]{2,1,0:T(8,128)(2,1)}, u32[]{:S(2)}, u32[]{:S(2)}) collective-permute-start(bf16[8,32,512]{2,1,0:T(8,128)(2,1)} %get-tuple-element.274), channel_id=1, source_target_pairs={{0,3},{1,2},{2,1},{3,0},{4,7},{5,6},{6,5},{7,4},{8,11},{9,10},{10,... | collective-permute-start | bytes 786440 | tf_op jit(solution)/shard_map/ppermute | solution.py:657
  17.9 6.8 %collective-permute-start.9 = (bf16[1,4,64,128]{3,2,1,0:T(8,128)(2,1)S(1)}, bf16[1,4,64,128]{3,2,1,0:T(8,128)(2,1)S(1)}, u32[]{:S(2)}, u32[]{:S(2)}) collective-permute-start(bf16[1,4,64,128]{3,2,1,0:T(8,128)(2,1)S(1)} %maximum_bitcast_fusion), channel_id=1, source_target_pairs={{0,16},{4,20},{8,24},{12,28},{16,0},{20,4},{24,8},{28,12},{1,17},{... | collective-permute-start | bytes 196616 | tf_op jit(solution)/shard_map/ppermute | solution.py:657
  24.7 6.2 %collective-permute-start.10 = (bf16[2,4,64,128]{3,2,1,0:T(8,128)(2,1)S(1)}, bf16[2,4,64,128]{3,2,1,0:T(8,128)(2,1)S(1)}, u32[]{:S(2)}, u32[]{:S(2)}) collective-permute-start(bf16[2,4,64,128]{3,2,1,0:T(8,128)(2,1)S(1)} %pad_maximum_fusion.11), channel_id=1, source_target_pairs={{0,8},{4,12},{8,0},{12,4},{16,24},{20,28},{24,16},{28,20},{1,9},{5... | collective-permute-start | bytes 393224 | tf_op jit(solution)/shard_map/ppermute | solution.py:657
  31.0 9.3 %collective-permute-start.11 = (bf16[4,4,64,128]{3,2,1,0:T(8,128)(2,1)S(1)}, bf16[4,4,64,128]{3,2,1,0:T(8,128)(2,1)S(1)}, u32[]{:S(2)}, u32[]{:S(2)}) collective-permute-start(bf16[4,4,64,128]{3,2,1,0:T(8,128)(2,1)S(1)} %pad_maximum_fusion.9), channel_id=1, source_target_pairs={{0,2},{1,3},{2,0},{3,1},{4,6},{5,7},{6,4},{7,5},{8,10},{9,11},{10,... | collective-permute-start | bytes 786440 | tf_op jit(solution)/shard_map/ppermute | solution.py:657
  32.9 21.4 %collective-permute-start.3 = (bf16[4,160,512]{2,1,0:T(8,128)(2,1)S(1)}, bf16[4,160,512]{2,1,0:T(8,128)(2,1)S(1)}, u32[]{:S(2)}, u32[]{:S(2)}) collective-permute-start(bf16[4,160,512]{2,1,0:T(8,128)(2,1)S(1)} %pad_maximum_fusion.3), channel_id=1, source_target_pairs={{0,3},{1,2},{2,1},{3,0},{4,7},{5,6},{6,5},{7,4},{8,11},{9,10},{10,... | collective-permute-start | bytes 1966088 | tf_op jit(solution)/shard_map/ppermute | solution.py:657
  40.3 17.0 %collective-permute-start.12 = (bf16[8,4,64,128]{3,2,1,0:T(8,128)(2,1)S(1)}, bf16[8,4,64,128]{3,2,1,0:T(8,128)(2,1)S(1)}, u32[]{:S(2)}, u32[]{:S(2)}) collective-permute-start(bf16[8,4,64,128]{3,2,1,0:T(8,128)(2,1)S(1)} %pad_maximum_fusion.8.refs_9_.refs_12_), channel_id=1, source_target_pairs={{0,4},{4,0},{8,12},{12,8},{16,20},{20,16},{24,28},{28,24},{1,5},{5... | collective-permute-start | bytes 1572872 | tf_op jit(solution)/shard_map/ppermute | solution.py:657
  42.5 18.5 %collective-permute-start.4 = (bf16[8,32,512]{2,1,0:T(8,128)(2,1)S(1)}, bf16[8,32,512]{2,1,0:T(8,128)(2,1)S(1)}, u32[]{:S(2)}, u32[]{:S(2)}) collective-permute-start(bf16[8,32,512]{2,1,0:T(8,128)(2,1)S(1)} %copy-done.18), channel_id=1, source_target_pairs={{0,1},{1,0},{2,3},{3,2},{4,5},{5,4},{6,7},{7,6},{8,9},{9,8},{10,11... | collective-permute-start | bytes 786440 | tf_op jit(solution)/shard_map/ppermute | solution.py:657
  42.6 18.5 %collective-permute-start.5 = (bf16[8,32,512]{2,1,0:T(8,128)(2,1)S(1)}, bf16[8,32,512]{2,1,0:T(8,128)(2,1)S(1)}, u32[]{:S(2)}, u32[]{:S(2)}) collective-permute-start(bf16[8,32,512]{2,1,0:T(8,128)(2,1)S(1)} %copy-done.17), channel_id=1, source_target_pairs={{0,2},{1,3},{2,0},{3,1},{4,6},{5,7},{6,4},{7,5},{8,10},{9,11},{10,... | collective-permute-start | bytes 786440 | tf_op jit(solution)/shard_map/ppermute | solution.py:657
  43.3 35.0 %collective-permute-start.1 = (bf16[4,160,512]{2,1,0:T(8,128)(2,1)S(1)}, bf16[4,160,512]{2,1,0:T(8,128)(2,1)}, u32[]{:S(2)}, u32[]{:S(2)}) collective-permute-start(bf16[4,160,512]{2,1,0:T(8,128)(2,1)S(1)} %pad_maximum_fusion.1), channel_id=1, source_target_pairs={{0,1},{1,0},{2,3},{3,2},{4,5},{5,4},{6,7},{7,6},{8,9},{9,8},{10,11... | collective-permute-start | bytes 1966088 | tf_op jit(solution)/shard_map/ppermute | solution.py:657
  54.2 7.6 %collective-permute-start.13 = (bf16[8,4,64,128]{3,2,1,0:T(8,128)(2,1)S(1)}, bf16[8,4,64,128]{3,2,1,0:T(8,128)(2,1)S(1)}, u32[]{:S(2)}, u32[]{:S(2)}) collective-permute-start(bf16[8,4,64,128]{3,2,1,0:T(8,128)(2,1)S(1)} %pad_maximum_fusion.8.refs_9_.refs_12_), channel_id=1, source_target_pairs={{0,1},{1,0},{2,3},{3,2},{4,5},{5,4},{6,7},{7,6},{8,9},{9,8},{10,11... | collective-permute-start | bytes 1572872 | tf_op jit(solution)/shard_map/ppermute | solution.py:657
  57.3 6.1 %collective-permute-start.14 = (bf16[8,4,64,128]{3,2,1,0:T(8,128)(2,1)S(1)}, bf16[8,4,64,128]{3,2,1,0:T(8,128)(2,1)S(1)}, u32[]{:S(2)}, u32[]{:S(2)}) collective-permute-start(bf16[8,4,64,128]{3,2,1,0:T(8,128)(2,1)S(1)} %collective-permute-done.12.refs_10_.refs_13_), channel_id=1, source_target_pairs={{0,1},{1,0},{2,3},{3,2},{4,5},{5,4},{6,7},{7,6},{8,9},{9,8},{10,11... | collective-permute-start | bytes 1572872 | tf_op jit(solution)/shard_map/ppermute | solution.py:657
  61.0 28.4 %collective-permute-start.2 = (bf16[4,160,512]{2,1,0:T(8,128)(2,1)S(1)}, bf16[4,160,512]{2,1,0:T(8,128)(2,1)}, u32[]{:S(2)}, u32[]{:S(2)}) collective-permute-start(bf16[4,160,512]{2,1,0:T(8,128)(2,1)S(1)} %pad_maximum_fusion.2), channel_id=1, source_target_pairs={{0,2},{1,3},{2,0},{3,1},{4,6},{5,7},{6,4},{7,5},{8,10},{9,11},{10,... | collective-permute-start | bytes 1966088 | tf_op jit(solution)/shard_map/ppermute | solution.py:657
  61.1 76.9 %collective-permute-start.18 = (bf16[4,160,512]{2,1,0:T(8,128)(2,1)}, bf16[4,160,512]{2,1,0:T(8,128)(2,1)}, u32[]{:S(2)}, u32[]{:S(2)}) collective-permute-start(bf16[4,160,512]{2,1,0:T(8,128)(2,1)} %pad_maximum_fusion.5), channel_id=1, source_target_pairs={{0,1},{1,0},{2,3},{3,2},{4,5},{5,4},{6,7},{7,6},{8,9},{9,8},{10,11... | collective-permute-start | bytes 1966088 | tf_op jit(solution)/shard_map/ppermute | solution.py:657
  61.8 77.2 %collective-permute-start.19 = (bf16[4,160,512]{2,1,0:T(8,128)(2,1)S(1)}, bf16[4,160,512]{2,1,0:T(8,128)(2,1)S(1)}, u32[]{:S(2)}, u32[]{:S(2)}) collective-permute-start(bf16[4,160,512]{2,1,0:T(8,128)(2,1)S(1)} %pad_maximum_fusion.6), channel_id=1, source_target_pairs={{0,2},{1,3},{2,0},{3,1},{4,6},{5,7},{6,4},{7,5},{8,10},{9,11},{10,... | collective-permute-start | bytes 1966088 | tf_op jit(solution)/shard_map/ppermute | solution.py:657
  64.3 74.8 %collective-permute-start.20 = (bf16[4,160,512]{2,1,0:T(8,128)(2,1)}, bf16[4,160,512]{2,1,0:T(8,128)(2,1)}, u32[]{:S(2)}, u32[]{:S(2)}) collective-permute-start(bf16[4,160,512]{2,1,0:T(8,128)(2,1)} %pad_maximum_fusion.7), channel_id=1, source_target_pairs={{0,3},{1,2},{2,1},{3,0},{4,7},{5,6},{6,5},{7,4},{8,11},{9,10},{10,... | collective-permute-start | bytes 1966088 | tf_op jit(solution)/shard_map/ppermute | solution.py:657
  137.1 40.1 %collective-permute-start.15 = (bf16[4,160,512]{2,1,0:T(8,128)(2,1)}, bf16[4,160,512]{2,1,0:T(8,128)(2,1)S(1)}, u32[]{:S(2)}, u32[]{:S(2)}) collective-permute-start(bf16[4,160,512]{2,1,0:T(8,128)(2,1)} %get-tuple-element.132), channel_id=1, source_target_pairs={{0,1},{1,0},{2,3},{3,2},{4,5},{5,4},{6,7},{7,6},{8,9},{9,8},{10,11... | collective-permute-start | bytes 1966088 | tf_op jit(solution)/shard_map/ppermute | solution.py:657
  137.4 40.7 %collective-permute-start.16 = (bf16[4,160,512]{2,1,0:T(8,128)(2,1)}, bf16[4,160,512]{2,1,0:T(8,128)(2,1)S(1)}, u32[]{:S(2)}, u32[]{:S(2)}) collective-permute-start(bf16[4,160,512]{2,1,0:T(8,128)(2,1)} %get-tuple-element.133), channel_id=1, source_target_pairs={{0,2},{1,3},{2,0},{3,1},{4,6},{5,7},{6,4},{7,5},{8,10},{9,11},{10,... | collective-permute-start | bytes 1966088 | tf_op jit(solution)/shard_map/ppermute | solution.py:657
  138.0 40.1 %collective-permute-start.17 = (bf16[4,160,512]{2,1,0:T(8,128)(2,1)}, bf16[4,160,512]{2,1,0:T(8,128)(2,1)S(1)}, u32[]{:S(2)}, u32[]{:S(2)}) collective-permute-start(bf16[4,160,512]{2,1,0:T(8,128)(2,1)} %get-tuple-element.134), channel_id=1, source_target_pairs={{0,3},{1,2},{2,1},{3,0},{4,7},{5,6},{6,5},{7,4},{8,11},{9,10},{10,... | collective-permute-start | bytes 1966088 | tf_op jit(solution)/shard_map/ppermute | solution.py:657
  176.0 34.8 %collective-permute-start.21 = (bf16[4,160,512]{2,1,0:T(8,128)(2,1)}, bf16[4,160,512]{2,1,0:T(8,128)(2,1)S(1)}, u32[]{:S(2)}, u32[]{:S(2)}) collective-permute-start(bf16[4,160,512]{2,1,0:T(8,128)(2,1)} %get-tuple-element.162), channel_id=1, source_target_pairs={{0,1},{1,0},{2,3},{3,2},{4,5},{5,4},{6,7},{7,6},{8,9},{9,8},{10,11... | collective-permute-start | bytes 1966088 | tf_op jit(solution)/shard_map/ppermute | solution.py:657
  176.6 34.2 %collective-permute-start.22 = (bf16[4,160,512]{2,1,0:T(8,128)(2,1)}, bf16[4,160,512]{2,1,0:T(8,128)(2,1)S(1)}, u32[]{:S(2)}, u32[]{:S(2)}) collective-permute-start(bf16[4,160,512]{2,1,0:T(8,128)(2,1)} %get-tuple-element.163), channel_id=1, source_target_pairs={{0,2},{1,3},{2,0},{3,1},{4,6},{5,7},{6,4},{7,5},{8,10},{9,11},{10,... | collective-permute-start | bytes 1966088 | tf_op jit(solution)/shard_map/ppermute | solution.py:657
  177.2 33.6 %copy-start.8 = (bf16[4,160,512]{2,1,0:T(8,128)(2,1)}, bf16[4,160,512]{2,1,0:T(8,128)(2,1)S(1)}, u32[]{:S(2)}) copy-start(bf16[4,160,512]{2,1,0:T(8,128)(2,1)S(1)} %collective-permute-done.15.refs_1_) | copy-start | bytes 1966084
  177.2 33.7 %collective-permute-start.23 = (bf16[4,160,512]{2,1,0:T(8,128)(2,1)}, bf16[4,160,512]{2,1,0:T(8,128)(2,1)}, u32[]{:S(2)}, u32[]{:S(2)}) collective-permute-start(bf16[4,160,512]{2,1,0:T(8,128)(2,1)} %get-tuple-element.164), channel_id=1, source_target_pairs={{0,3},{1,2},{2,1},{3,0},{4,7},{5,6},{6,5},{7,4},{8,11},{9,10},{10,... | collective-permute-start | bytes 1966088 | tf_op jit(solution)/shard_map/ppermute | solution.py:657
  178.1 32.8 %copy-start.9 = (bf16[4,160,512]{2,1,0:T(8,128)(2,1)}, bf16[4,160,512]{2,1,0:T(8,128)(2,1)S(1)}, u32[]{:S(2)}) copy-start(bf16[4,160,512]{2,1,0:T(8,128)(2,1)S(1)} %collective-permute-done.16.refs_2_) | copy-start | bytes 1966084
  178.1 32.8 %copy-start.10 = (bf16[4,160,512]{2,1,0:T(8,128)(2,1)}, bf16[4,160,512]{2,1,0:T(8,128)(2,1)S(1)}, u32[]{:S(2)}) copy-start(bf16[4,160,512]{2,1,0:T(8,128)(2,1)S(1)} %collective-permute-done.17.refs_3_) | copy-start | bytes 1966084
  178.1 40.5 %copy-start.40 = (s32[32]{0:T(128)S(1)}, s32[32]{0:T(128)}, u32[]{:S(2)}) copy-start(s32[32]{0:T(128)} %param.30) | copy-start | bytes 388
  178.1 44.3 %copy-start.41 = (f32[4]{0:T(128)S(1)}, f32[4]{0:T(128)}, u32[]{:S(2)}) copy-start(f32[4]{0:T(128)} %constant.62.clone) | copy-start | bytes 52
  210.8 30.0 %copy-start.11 = (bf16[4,160,512]{2,1,0:T(8,128)(2,1)}, bf16[4,160,512]{2,1,0:T(8,128)(2,1)S(1)}, u32[]{:S(2)}) copy-start(bf16[4,160,512]{2,1,0:T(8,128)(2,1)S(1)} %collective-permute-done.21.refs_4_) | copy-start | bytes 1966084
  210.9 1.8 collective-permute-start.24
  213.4 3.7 %collective-permute-start.25 = (f32[16,128]{1,0:T(8,128)S(1)}, f32[16,128]{1,0:T(8,128)S(1)}, u32[]{:S(2)}, u32[]{:S(2)}) collective-permute-start(f32[16,128]{1,0:T(8,128)S(1)} %pad_maximum_fusion.14), channel_id=1, source_target_pairs={{0,2},{1,3},{2,0},{3,1},{4,6},{5,7},{6,4},{7,5},{8,10},{9,11},{10,... | collective-permute-start | bytes 24584 | tf_op jit(solution)/shard_map/ppermute | solution.py:657
  217.1 3.7 %collective-permute-start.26 = (f32[8,128]{1,0:T(8,128)S(1)}, f32[8,128]{1,0:T(8,128)S(1)}, u32[]{:S(2)}, u32[]{:S(2)}) collective-permute-start(f32[8,128]{1,0:T(8,128)S(1)} %broadcast_in_dim.5), channel_id=1, source_target_pairs={{0,4},{4,0},{8,12},{12,8},{16,20},{20,16},{24,28},{28,24},{1,5},{5... | collective-permute-start | bytes 12296 | tf_op jit(solution)/shard_map/ppermute | solution.py:657
  220.8 3.6 %collective-permute-start.27 = (f32[8,128]{1,0:T(8,128)S(1)}, f32[8,128]{1,0:T(8,128)S(1)}, u32[]{:S(2)}, u32[]{:S(2)}) collective-permute-start(f32[8,128]{1,0:T(8,128)S(1)} %broadcast_add_fusion), channel_id=1, source_target_pairs={{0,8},{4,12},{8,0},{12,4},{16,24},{20,28},{24,16},{28,20},{1,9},{5... | collective-permute-start | bytes 12296 | tf_op jit(solution)/shard_map/ppermute | solution.py:657
  224.4 4.7 %collective-permute-start.28 = (f32[8,128]{1,0:T(8,128)S(1)}, f32[8,128]{1,0:T(8,128)S(1)}, u32[]{:S(2)}, u32[]{:S(2)}) collective-permute-start(f32[8,128]{1,0:T(8,128)S(1)} %fusion.9), channel_id=1, source_target_pairs={{0,16},{4,20},{8,24},{12,28},{16,0},{20,4},{24,8},{28,12},{1,17},{... | collective-permute-start | bytes 12296 | tf_op jit(solution)/shard_map/ppermute | solution.py:657
  227.1 14.2 %collective-permute-start.33 = (bf16[8,32,512]{2,1,0:T(8,128)(2,1)}, bf16[8,32,512]{2,1,0:T(8,128)(2,1)S(1)}, u32[]{:S(2)}, u32[]{:S(2)}) collective-permute-start(bf16[8,32,512]{2,1,0:T(8,128)(2,1)} %get-tuple-element.174), channel_id=1, source_target_pairs={{0,1},{1,0},{2,3},{3,2},{4,5},{5,4},{6,7},{7,6},{8,9},{9,8},{10,11... | collective-permute-start | bytes 786440 | tf_op jit(solution)/shard_map/ppermute | solution.py:657
  227.2 14.1 %collective-permute-start.34 = (bf16[8,32,512]{2,1,0:T(8,128)(2,1)}, bf16[8,32,512]{2,1,0:T(8,128)(2,1)S(1)}, u32[]{:S(2)}, u32[]{:S(2)}) collective-permute-start(bf16[8,32,512]{2,1,0:T(8,128)(2,1)} %get-tuple-element.175), channel_id=1, source_target_pairs={{0,2},{1,3},{2,0},{3,1},{4,6},{5,7},{6,4},{7,5},{8,10},{9,11},{10,... | collective-permute-start | bytes 786440 | tf_op jit(solution)/shard_map/ppermute | solution.py:657
  227.8 13.5 %collective-permute-start.35 = (bf16[8,32,512]{2,1,0:T(8,128)(2,1)}, bf16[8,32,512]{2,1,0:T(8,128)(2,1)S(1)}, u32[]{:S(2)}, u32[]{:S(2)}) collective-permute-start(bf16[8,32,512]{2,1,0:T(8,128)(2,1)} %get-tuple-element.176), channel_id=1, source_target_pairs={{0,3},{1,2},{2,1},{3,0},{4,7},{5,6},{6,5},{7,4},{8,11},{9,10},{10,... | collective-permute-start | bytes 786440 | tf_op jit(solution)/shard_map/ppermute | solution.py:657
  240.9 21.9 %collective-permute-start.31 = (bf16[16,3,64,128]{3,2,1,0:T(8,128)(2,1)}, bf16[16,3,64,128]{3,2,1,0:T(8,128)(2,1)S(1)}, u32[]{:S(2)}, u32[]{:S(2)}) collective-permute-start(bf16[16,3,64,128]{3,2,1,0:T(8,128)(2,1)} %get-tuple-element.173), channel_id=1, source_target_pairs={{0,1},{1,0},{2,3},{3,2},{4,5},{5,4},{6,7},{7,6},{8,9},{9,8},{10,11... | collective-permute-start | bytes 2359304 | tf_op jit(solution)/shard_map/ppermute | solution.py:657
  256.6 8.8 %collective-permute-start.38 = (bf16[16,5,64,128]{3,2,1,0:T(8,128)(2,1)}, bf16[16,5,64,128]{3,2,1,0:T(8,128)(2,1)S(1)}, u32[]{:S(2)}, u32[]{:S(2)}) collective-permute-start(bf16[16,5,64,128]{3,2,1,0:T(8,128)(2,1)} %get-tuple-element.188), channel_id=1, source_target_pairs={{0,1},{1,0},{2,3},{3,2},{4,5},{5,4},{6,7},{7,6},{8,9},{9,8},{10,11... | collective-permute-start | bytes 3932168 | tf_op jit(solution)/shard_map/ppermute | solution.py:657
  256.9 6.8 %collective-permute-start.36 = (bf16[16,3,64,128]{3,2,1,0:T(8,128)(2,1)}, bf16[16,3,64,128]{3,2,1,0:T(8,128)(2,1)S(1)}, u32[]{:S(2)}, u32[]{:S(2)}) collective-permute-start(bf16[16,3,64,128]{3,2,1,0:T(8,128)(2,1)} %get-tuple-element.186), channel_id=1, source_target_pairs={{0,1},{1,0},{2,3},{3,2},{4,5},{5,4},{6,7},{7,6},{8,9},{9,8},{10,11... | collective-permute-start | bytes 2359304 | tf_op jit(solution)/shard_map/ppermute | solution.py:657
  257.2 10.2 %collective-permute-start.29 = (bf16[16,5,64,128]{3,2,1,0:T(8,128)(2,1)S(1)}, bf16[16,5,64,128]{3,2,1,0:T(8,128)(2,1)S(1)}, u32[]{:S(2)}, u32[]{:S(2)}) collective-permute-start(bf16[16,5,64,128]{3,2,1,0:T(8,128)(2,1)S(1)} %copy-done.32), channel_id=1, source_target_pairs={{0,1},{1,0},{2,3},{3,2},{4,5},{5,4},{6,7},{7,6},{8,9},{9,8},{10,11... | collective-permute-start | bytes 3932168 | tf_op jit(solution)/shard_map/ppermute | solution.py:657
  257.5 5.2 %collective-permute-start.40 = (f32[14,128]{1,0:T(8,128)S(1)}, f32[14,128]{1,0:T(8,128)S(1)}, u32[]{:S(2)}, u32[]{:S(2)}) collective-permute-start(f32[14,128]{1,0:T(8,128)S(1)} %bitcast.69), channel_id=1, source_target_pairs={{0,1},{1,0},{2,3},{3,2},{4,5},{5,4},{6,7},{7,6},{8,9},{9,8},{10,11... | collective-permute-start | bytes 21512 | tf_op jit(solution)/shard_map/ppermute | solution.py:657
  263.1 12.0 %collective-permute-start.32 = (bf16[8,3,64,128]{3,2,1,0:T(8,128)(2,1)S(1)}, bf16[8,3,64,128]{3,2,1,0:T(8,128)(2,1)S(1)}, u32[]{:S(2)}, u32[]{:S(2)}) collective-permute-start(bf16[8,3,64,128]{3,2,1,0:T(8,128)(2,1)S(1)} %get-tuple-element.259), channel_id=1, source_target_pairs={{0,2},{1,3},{2,0},{3,1},{4,6},{5,7},{6,4},{7,5},{8,10},{9,11},{10,... | collective-permute-start | bytes 1179656 | tf_op jit(solution)/shard_map/ppermute | solution.py:657
  264.0 18.8 %collective-permute-start.37 = (bf16[8,3,64,128]{3,2,1,0:T(8,128)(2,1)S(1)}, bf16[8,3,64,128]{3,2,1,0:T(8,128)(2,1)S(1)}, u32[]{:S(2)}, u32[]{:S(2)}) collective-permute-start(bf16[8,3,64,128]{3,2,1,0:T(8,128)(2,1)S(1)} %get-tuple-element.257), channel_id=1, source_target_pairs={{0,2},{1,3},{2,0},{3,1},{4,6},{5,7},{6,4},{7,5},{8,10},{9,11},{10,... | collective-permute-start | bytes 1179656 | tf_op jit(solution)/shard_map/ppermute | solution.py:657
  266.1 16.8 %collective-permute-start.39 = (bf16[8,5,64,128]{3,2,1,0:T(8,128)(2,1)S(1)}, bf16[8,5,64,128]{3,2,1,0:T(8,128)(2,1)S(1)}, u32[]{:S(2)}, u32[]{:S(2)}) collective-permute-start(bf16[8,5,64,128]{3,2,1,0:T(8,128)(2,1)S(1)} %get-tuple-element.253), channel_id=1, source_target_pairs={{0,8},{4,12},{8,0},{12,4},{16,24},{20,28},{24,16},{28,20},{1,9},{5... | collective-permute-start | bytes 1966088 | tf_op jit(solution)/shard_map/ppermute | solution.py:657
  267.9 16.8 %collective-permute-start.30 = (bf16[8,5,64,128]{3,2,1,0:T(8,128)(2,1)S(1)}, bf16[8,5,64,128]{3,2,1,0:T(8,128)(2,1)S(1)}, u32[]{:S(2)}, u32[]{:S(2)}) collective-permute-start(bf16[8,5,64,128]{3,2,1,0:T(8,128)(2,1)S(1)} %get-tuple-element.255), channel_id=1, source_target_pairs={{0,4},{4,0},{8,12},{12,8},{16,20},{20,16},{24,28},{28,24},{1,5},{5... | collective-permute-start | bytes 1966088 | tf_op jit(solution)/shard_map/ppermute | solution.py:657
  283.1 9.5 %collective-permute-start.41 = (f32[14,128]{1,0:T(8,128)S(1)}, f32[14,128]{1,0:T(8,128)S(1)}, u32[]{:S(2)}, u32[]{:S(2)}) collective-permute-start(f32[14,128]{1,0:T(8,128)S(1)} %bitcast_add_fusion), channel_id=1, source_target_pairs={{0,4},{4,0},{8,12},{12,8},{16,20},{20,16},{24,28},{28,24},{1,5},{5... | collective-permute-start | bytes 21512 | tf_op jit(solution)/shard_map/ppermute | solution.py:657
  292.6 6.9 %collective-permute-start.43 = (bf16[4,3,64,128]{3,2,1,0:T(8,128)(2,1)S(1)}, bf16[4,3,64,128]{3,2,1,0:T(8,128)(2,1)S(1)}, u32[]{:S(2)}, u32[]{:S(2)}) collective-permute-start(bf16[4,3,64,128]{3,2,1,0:T(8,128)(2,1)S(1)} %get-tuple-element.202), channel_id=1, source_target_pairs={{0,8},{4,12},{8,0},{12,4},{16,24},{20,28},{24,16},{28,20},{1,9},{5... | collective-permute-start | bytes 589832 | tf_op jit(solution)/shard_map/ppermute | solution.py:657
  294.1 3.8 %collective-permute-start.46 = (f32[14,128]{1,0:T(8,128)S(1)}, f32[14,128]{1,0:T(8,128)S(1)}, u32[]{:S(2)}, u32[]{:S(2)}) collective-permute-start(f32[14,128]{1,0:T(8,128)S(1)} %add.248), channel_id=1, source_target_pairs={{0,2},{1,3},{2,0},{3,1},{4,6},{5,7},{6,4},{7,5},{8,10},{9,11},{10,... | collective-permute-start | bytes 21512 | tf_op jit(solution)/shard_map/ppermute | solution.py:657
  294.7 8.4 %collective-permute-start.42 = (bf16[4,5,64,128]{3,2,1,0:T(8,128)(2,1)S(1)}, bf16[4,5,64,128]{3,2,1,0:T(8,128)(2,1)S(1)}, u32[]{:S(2)}, u32[]{:S(2)}) collective-permute-start(bf16[4,5,64,128]{3,2,1,0:T(8,128)(2,1)S(1)} %get-tuple-element.200), channel_id=1, source_target_pairs={{0,2},{1,3},{2,0},{3,1},{4,6},{5,7},{6,4},{7,5},{8,10},{9,11},{10,... | collective-permute-start | bytes 983048 | tf_op jit(solution)/shard_map/ppermute | solution.py:657
  296.1 5.7 %collective-permute-start.44 = (bf16[4,3,64,128]{3,2,1,0:T(8,128)(2,1)S(1)}, bf16[4,3,64,128]{3,2,1,0:T(8,128)(2,1)S(1)}, u32[]{:S(2)}, u32[]{:S(2)}) collective-permute-start(bf16[4,3,64,128]{3,2,1,0:T(8,128)(2,1)S(1)} %get-tuple-element.204), channel_id=1, source_target_pairs={{0,4},{4,0},{8,12},{12,8},{16,20},{20,16},{24,28},{28,24},{1,5},{5... | collective-permute-start | bytes 589832 | tf_op jit(solution)/shard_map/ppermute | solution.py:657
  296.7 15.6 %collective-permute-start.45 = (bf16[4,5,64,128]{3,2,1,0:T(8,128)(2,1)S(1)}, bf16[4,5,64,128]{3,2,1,0:T(8,128)(2,1)S(1)}, u32[]{:S(2)}, u32[]{:S(2)}) collective-permute-start(bf16[4,5,64,128]{3,2,1,0:T(8,128)(2,1)S(1)} %get-tuple-element.206), channel_id=1, source_target_pairs={{0,16},{4,20},{8,24},{12,28},{16,0},{20,4},{24,8},{28,12},{1,17},{... | collective-permute-start | bytes 983048 | tf_op jit(solution)/shard_map/ppermute | solution.py:657
  312.4 6.2 %collective-permute-start.48 = (bf16[2,3,64,128]{3,2,1,0:T(8,128)(2,1)S(1)}, bf16[2,3,64,128]{3,2,1,0:T(8,128)(2,1)S(1)}, u32[]{:S(2)}, u32[]{:S(2)}) collective-permute-start(bf16[2,3,64,128]{3,2,1,0:T(8,128)(2,1)S(1)} %get-tuple-element.211), channel_id=1, source_target_pairs={{0,16},{4,20},{8,24},{12,28},{16,0},{20,4},{24,8},{28,12},{1,17},{... | collective-permute-start | bytes 294920 | tf_op jit(solution)/shard_map/ppermute | solution.py:657
  312.5 5.9 %collective-permute-start.51 = (f32[14,128]{1,0:T(8,128)S(1)}, f32[14,128]{1,0:T(8,128)S(1)}, u32[]{:S(2)}, u32[]{:S(2)}) collective-permute-start(f32[14,128]{1,0:T(8,128)S(1)} %add.258), channel_id=1, source_target_pairs={{0,8},{4,12},{8,0},{12,4},{16,24},{20,28},{24,16},{28,20},{1,9},{5... | collective-permute-start | bytes 21512 | tf_op jit(solution)/shard_map/ppermute | solution.py:657
  314.9 8.4 %collective-permute-start.47 = (bf16[2,5,64,128]{3,2,1,0:T(8,128)(2,1)S(1)}, bf16[2,5,64,128]{3,2,1,0:T(8,128)(2,1)S(1)}, u32[]{:S(2)}, u32[]{:S(2)}) collective-permute-start(bf16[2,5,64,128]{3,2,1,0:T(8,128)(2,1)S(1)} %get-tuple-element.209), channel_id=1, source_target_pairs={{0,8},{4,12},{8,0},{12,4},{16,24},{20,28},{24,16},{28,20},{1,9},{5... | collective-permute-start | bytes 491528 | tf_op jit(solution)/shard_map/ppermute | solution.py:657
  315.0 7.7 %collective-permute-start.49 = (bf16[2,3,64,128]{3,2,1,0:T(8,128)(2,1)S(1)}, bf16[2,3,64,128]{3,2,1,0:T(8,128)(2,1)S(1)}, u32[]{:S(2)}, u32[]{:S(2)}) collective-permute-start(bf16[2,3,64,128]{3,2,1,0:T(8,128)(2,1)S(1)} %get-tuple-element.213), channel_id=1, source_target_pairs={{0,8},{4,12},{8,0},{12,4},{16,24},{20,28},{24,16},{28,20},{1,9},{5... | collective-permute-start | bytes 294920 | tf_op jit(solution)/shard_map/ppermute | solution.py:657
  316.9 7.0 %collective-permute-start.50 = (bf16[2,5,64,128]{3,2,1,0:T(8,128)(2,1)S(1)}, bf16[2,5,64,128]{3,2,1,0:T(8,128)(2,1)S(1)}, u32[]{:S(2)}, u32[]{:S(2)}) collective-permute-start(bf16[2,5,64,128]{3,2,1,0:T(8,128)(2,1)S(1)} %get-tuple-element.215), channel_id=1, source_target_pairs={{0,4},{4,0},{8,12},{12,8},{16,20},{20,16},{24,28},{28,24},{1,5},{5... | collective-permute-start | bytes 491528 | tf_op jit(solution)/shard_map/ppermute | solution.py:657
  324.6 7.2 %collective-permute-start.56 = (f32[14,128]{1,0:T(8,128)S(1)}, f32[14,128]{1,0:T(8,128)S(1)}, u32[]{:S(2)}, u32[]{:S(2)}) collective-permute-start(f32[14,128]{1,0:T(8,128)S(1)} %add.267), channel_id=1, source_target_pairs={{0,16},{4,20},{8,24},{12,28},{16,0},{20,4},{24,8},{28,12},{1,17},{... | collective-permute-start | bytes 21512 | tf_op jit(solution)/shard_map/ppermute | solution.py:657
  326.6 9.2 %collective-permute-start.52 = (bf16[1,5,64,128]{3,2,1,0:T(8,128)(2,1)S(1)}, bf16[1,5,64,128]{3,2,1,0:T(8,128)(2,1)S(1)}, u32[]{:S(2)}, u32[]{:S(2)}) collective-permute-start(bf16[1,5,64,128]{3,2,1,0:T(8,128)(2,1)S(1)} %get-tuple-element.218), channel_id=1, source_target_pairs={{0,16},{4,20},{8,24},{12,28},{16,0},{20,4},{24,8},{28,12},{1,17},{... | collective-permute-start | bytes 245768 | tf_op jit(solution)/shard_map/ppermute | solution.py:657
  328.9 4.9 %collective-permute-start.53 = (bf16[1,3,64,128]{3,2,1,0:T(8,128)(2,1)S(1)}, bf16[1,3,64,128]{3,2,1,0:T(8,128)(2,1)S(1)}, u32[]{:S(2)}, u32[]{:S(2)}) collective-permute-start(bf16[1,3,64,128]{3,2,1,0:T(8,128)(2,1)S(1)} %get-tuple-element.220), channel_id=1, source_target_pairs={{0,4},{4,0},{8,12},{12,8},{16,20},{20,16},{24,28},{28,24},{1,5},{5... | collective-permute-start | bytes 147464 | tf_op jit(solution)/shard_map/ppermute | solution.py:657
  330.8 5.0 %collective-permute-start.54 = (bf16[1,3,64,128]{3,2,1,0:T(8,128)(2,1)S(1)}, bf16[1,3,64,128]{3,2,1,0:T(8,128)(2,1)S(1)}, u32[]{:S(2)}, u32[]{:S(2)}) collective-permute-start(bf16[1,3,64,128]{3,2,1,0:T(8,128)(2,1)S(1)} %get-tuple-element.222), channel_id=1, source_target_pairs={{0,16},{4,20},{8,24},{12,28},{16,0},{20,4},{24,8},{28,12},{1,17},{... | collective-permute-start | bytes 147464 | tf_op jit(solution)/shard_map/ppermute | solution.py:657
  331.3 4.6 %collective-permute-start.55 = (bf16[1,5,64,128]{3,2,1,0:T(8,128)(2,1)S(1)}, bf16[1,5,64,128]{3,2,1,0:T(8,128)(2,1)S(1)}, u32[]{:S(2)}, u32[]{:S(2)}) collective-permute-start(bf16[1,5,64,128]{3,2,1,0:T(8,128)(2,1)S(1)} %get-tuple-element.224), channel_id=1, source_target_pairs={{0,2},{1,3},{2,0},{3,1},{4,6},{5,7},{6,4},{7,5},{8,10},{9,11},{10,... | collective-permute-start | bytes 245768 | tf_op jit(solution)/shard_map/ppermute | solution.py:657
  (36 other events, 442.5 us)
Sparse Core Ops, SparseCore 0:
  12.4 88.8 all-gather.2

commit v3 on v2

--- a/solution.py
+++ b/solution.py
@@ -89,6 +89,16 @@
 
 def gram_squares(left, right_grams):
     return jnp.sum(dot_nt(left, left) * right_grams, 0, keepdims=True)
+
+
+def fold_causal(block):
+    size = block.shape[0]
+    lanes = lax.broadcasted_iota(jnp.int32, (8, size), 1)
+    rows = [block[:8], block[size // 2 : size // 2 + 8]]
+    for start in range(8, size // 2, 8):
+        other = pltpu.roll(block[size - start : size - start + 8], start, 1)
+        rows.append(jnp.where(lanes >= start, block[start : start + 8], other))
+    return jnp.concatenate(rows, 0)
 
 
 def fold_lanes(row_sums):
@@ -204,7 +214,7 @@
     mid_out[...] = (flat + dot_nt(mix, held[3])).reshape(bundle, seq, width)
 
 
-def cross_kernel(shards, plans, aliased, *refs):
+def cross_kernel(shards, plans, soon, aliased, *refs):
     refs = list(refs)
 
     def take(count):
@@ -241,7 +251,7 @@
     @pl.when(pl.program_id(0) == 0)
     def _():
         start_weights(info, pieces, plans, held, sem_list)
-        wait_weights(plans, held, sem_list)
+        wait_weights(plans[:soon], held, sem_list[:soon])
 
     masks = head_masks(narrow)
     masks_wide = head_masks(wide)
@@ -280,6 +290,11 @@
             mixture = dot_tn(weights.astype(narrow), values_held[example, :, columns])
             mix_out[example, :, columns] = unstack_heads(mixture, masks_wide).astype(narrow)
     late = mid + dot_nt(flatten(mix_out[...]), held[3])
+
+    @pl.when(pl.program_id(0) == 0)
+    def _():
+        wait_weights(plans[soon:], held, sem_list[soon:])
+
     rows_c = late.astype(narrow).astype(wide)
     normed_c = (rows_c * norm_scale(rows_c) * gains[2:3, :]).astype(narrow)
     normed_c_out[...] = unflatten(normed_c)
@@ -382,7 +397,7 @@
     pieces = take(len(plans))
     tokens_grads = take(shards)
     d_qkv_out, d_early_out, small_out, norms_out = take(4)
-    held, sems, rows_held, bias_held = take(4)
+    held, sems, rows_held, bias_held, folded_held = take(5)
     sem_list = [sems.at[index] for index in range(len(plans))]
 
     @pl.when(pl.program_id(0) == 0)
@@ -430,12 +445,17 @@
                 narrow
             )
             d_wide = d_scores.astype(wide)
-            for bucket in range(bucket_count):
-                chosen = code == bucket
-                for head in range(quad):
-                    picked = jnp.where(chosen, d_wide[:, head * seq : (head + 1) * seq], 0.0)
-                    spot = (group * quad + head) * bucket_count + bucket
-                    bias_held[spot : spot + 1, :] = jnp.sum(picked, 0, keepdims=True)
+            for head in range(quad):
+                folded_held[group * quad + head] = fold_causal(
+                    d_wide[:, head * seq : (head + 1) * seq]
+                )
+        code = fold_causal(code)
+        for bucket in range(bucket_count):
+            chosen = code == bucket
+            for head in range(groups * quad):
+                picked = jnp.where(chosen, folded_held[head], 0.0)
+                spot = head * bucket_count + bucket
+                bias_held[spot : spot + 1, :] = jnp.sum(picked, 0, keepdims=True)
         d_bias = lax.dot_general(
             jnp.ones((8, 128), wide),
             bias_held[...],
@@ -778,11 +798,13 @@
             found.append(swap(block, "tensor", index) if index else block)
         return found
 
-    late_pieces, late_plans = gather_late(
-        jnp.concatenate([shard_in[3:6], shard_out[1:2], shard_up, shard_down], 0)
-    )
+    late_pieces, late_plans = gather_late(jnp.concatenate([shard_up, shard_down], 0))
     token_parts = exchange([tokens], 0, local)
     self_pieces, self_plans = gather_soon(jnp.concatenate([shard_in[:3], shard_out[:1]], 0))
+    cross_pieces, cross_plans = gather_soon(jnp.concatenate([shard_in[3:6], shard_out[1:2]], 0))
+    late_plans = cross_plans + [(4,) + plan[1:] for plan in late_plans]
+    late_pieces = cross_pieces + late_pieces
+    soon_count = len(cross_pieces)
     table = jnp.pad(position_bias.T, ((0, 0), (0, 128 - bucket_count)))
     table_all = jnp.concatenate(
         [swap(table, "tensor", index) if index else table for index in range(shards)], 0
@@ -922,7 +944,7 @@
         for index, block in enumerate(filled):
             aliases[len(operands) + index] = index if index < 2 else index + shards - 1
         return pl.pallas_call(
-            functools.partial(cross_kernel, shards, late_plans, len(filled)),
+            functools.partial(cross_kernel, shards, late_plans, soon_count, len(filled)),
             grid_spec=pltpu.PrefetchScalarGridSpec(
                 num_scalar_prefetch=1,
                 grid=(steps,),
@@ -1008,6 +1030,7 @@
             pltpu.SemaphoreType.DMA((len(self_pieces),)),
             pltpu.VMEM((bundle,) + row_block, wide),
             pltpu.VMEM((heads * bucket_count, 128), wide),
+            pltpu.VMEM((heads, seq // 2 + 8, seq), wide),
         ],
         ),
         out_shape=[shaped((seq_rows, width), wide, count=group_count)]

time: 352 us -> 344 us (0.977)
  Pallas kernels: 154 us -> 148 us
  starting transfers between devices: 54.7 us -> 59.9 us
    all_gather x1, waiting for transfers between devices: 11.9 us -> 0.01 us  [gather_late(): whole = lax.all_gather(blocks, ('dp', 'tensor'), axis=0)]
    ppermute x57 -> x63, waiting for transfers between devices: 78.3 us -> 89.1 us  [swap(): lax.ppermute(value, axis, [(index, index ^ bit) for index in range(size)])]
    pallas_call x1, Pallas kernels: 32.7 us -> 27.1 us  [on_device(): pl.pallas_call(functools.partial(self_backward_kernel, shards, self_plans...]
    ppermute x57 -> x63, starting transfers between devices: 54.6 us -> 59.8 us  [swap(): lax.ppermute(value, axis, [(index, index ^ bit) for index in range(size)])]
  transfers between devices with their start and end apart: 58 -> 64, of which waited for: 20 -> 22; matrix products, arithmetic and copies ran while one was open for 6% -> 5% of each run, Pallas kernels for 44% -> 43%
where the time goes in v3:
time: 344 us; the launch traced here: 339 us
  Pallas kernels  148 us (43%)
  waiting for transfers between devices  89.1 us (26%)
  starting transfers between devices  59.9 us (17%)
  between operations  15.9 us (5%)
  other arithmetic  15 us (4%)
  local copies, waits for them, and re-layouts  10.7 us (3%)
    ppermute x63, waiting for transfers between devices, swap(): lax.ppermute(value, axis, [(index, index ^ bit) for index in range(size)])  89.1 us
    pallas_call x2, Pallas kernels, cross(): pl.pallas_call(functools.partial(cross_kernel, shards, late_plans, soon_c...  71.7 us
    ppermute x63, starting transfers between devices, swap(): lax.ppermute(value, axis, [(index, index ^ bit) for index in range(size)])  59.8 us
    pallas_call x1, Pallas kernels, on_device(): pl.pallas_call(functools.partial(self_backward_kernel, shards, self_plans...  27.1 us
    pallas_call x2, Pallas kernels, gradient_call(): pl.pallas_call(kernel, in_specs=[smem, smem] + [anywhere] * len(operands)...  25.3 us
    pallas_call x1, Pallas kernels, on_device(): pl.pallas_call(functools.partial(self_forward_kernel, shards, self_plans,...  13.7 us
    pallas_call x1, Pallas kernels, on_device(): assemble(after(kernel_info, *there(0)), *returned)  7.69 us
  transfers between devices with their start and end apart: 64, of which 22 were waited for; matrix products, arithmetic and copies ran while one was open for 5% of the time, Pallas kernels for 43%

profile of v3, /device:TPU:0, one launch (start us, length us, event | category | flops | bytes accessed | tf_op | source)
XLA Modules:
  0.0 338.9 jit_solution(16985286945689840363)
XLA Ops:
  7.3 1.1 convert_bitcast_fusion
  8.4 0.9 convert_element_type.305
  10.1 2.5 collective-permute-start.8
  13.3 1.0 constant_dynamic-slice_fusion.13
  14.3 1.5 collective-permute-start
  15.9 2.7 collective-permute-start.9
  18.6 0.8 constant_dynamic-slice_fusion.12.refs_5_.refs_10_
  19.4 2.0 constant_dynamic-slice_fusion.11.refs_6_
  23.2 1.3 collective-permute-start.15
  24.5 2.8 collective-permute-start.10
  27.9 2.9 collective-permute-done.15
  31.0 2.1 collective-permute-done.10
  33.1 1.5 collective-permute-start.11
  34.9 7.5 %collective-permute-done.11 = bf16[4,4,64,128]{3,2,1,0:T(8,128)(2,1)S(1)} collective-permute-done((bf16[4,4,64,128]{3,2,1,0:T(8,128)(2,1)S(1)}, bf16[4,4,64,128]{3,2,1,0:T(8,128)(2,1)S(1)}, u32[]{:S(2)}, u32[]{:S(2)}) %collective-permute-start.11) | collective-permute-done | bytes 262176 | tf_op jit(solution)/shard_map/ppermute | solution.py:677
  42.4 1.5 collective-permute-start.12
  44.0 2.4 collective-permute-start.17
  46.4 0.9 pad_maximum_fusion.refs_1_.refs_8_
  47.4 15.2 %collective-permute-done.17 = bf16[4,4,64,128]{3,2,1,0:T(8,128)(2,1)S(1)} collective-permute-done((bf16[4,4,64,128]{3,2,1,0:T(8,128)(2,1)S(1)}, bf16[4,4,64,128]{3,2,1,0:T(8,128)(2,1)S(1)}, u32[]{:S(2)}, u32[]{:S(2)}) %collective-permute-start.17) | collective-permute-done | bytes 262176 | tf_op jit(solution)/shard_map/ppermute | solution.py:677
  62.7 2.2 collective-permute-start.18
  65.8 0.9 pad_maximum_fusion.4.refs_1_.refs_12_
  67.2 2.5 collective-permute-start.2
  69.7 11.6 %collective-permute-done.18.refs_8_ = bf16[8,4,64,128]{3,2,1,0:T(8,128)(2,1)} collective-permute-done((bf16[8,4,64,128]{3,2,1,0:T(8,128)(2,1)S(1)}, bf16[8,4,64,128]{3,2,1,0:T(8,128)(2,1)}, u32[]{:S(2)}, u32[]{:S(2)}) %collective-permute-start.18) | collective-permute-done | bytes 524320 | tf_op jit(solution)/shard_map/ppermute | solution.py:677
  82.2 13.7 %self_forward.1 = (bf16[8,128,512]{2,1,0:T(8,128)(2,1)}, bf16[8,128,512]{2,1,0:T(8,128)(2,1)}, bf16[3,8,128,512]{3,2,1,0:T(8,128)(2,1)}, f32[8,2,128,512]{3,2,1,...) custom-call(s32[3]{0:T(128)} %pad_add_fusion.refs_0_.info, ...), custom_call_target="tpu_custom_call" | custom-call | flops 16000000000 | bytes 16000000 | tf_op jit(solution)/shard_map/self_forward/pallas_call | solution.py:861
  95.9 1.6 collective-permute-start.25
  99.1 35.7 %cross.2 = (bf16[32,32,512]{2,1,0:T(8,128)(2,1)}, f32[32,128,512]{2,1,0:T(8,128)}, bf16[4,160,512]{2,1,0:T(8,128)(2,1)}, bf16[4,160,512]{2,1,0:T(8,128)(2,1)}, b...) custom-call(s32[3]{0:T(128)} %pad_add_fusion.refs_0_.info, ...), custom_call_target="tpu_custom_call" | custom-call | flops 32000000000 | bytes 24000000 | tf_op jit(solution)/shard_map/cross/pallas_call | solution.py:946
  135.0 1.2 collective-permute-start.22
  136.7 36.0 %cross.3 = (bf16[32,32,512]{2,1,0:T(8,128)(2,1)}, f32[32,128,512]{2,1,0:T(8,128)}, bf16[4,160,512]{2,1,0:T(8,128)(2,1)}, bf16[4,160,512]{2,1,0:T(8,128)(2,1)}, b...) custom-call(s32[3]{0:T(128)} %pad_add_fusion.refs_0_.info, ...), custom_call_target="tpu_custom_call", output_to_operand_aliasing={{0}: (12, {}), {1}: (13, {}), {5}: (14, {}), {6}: (15, {}),... | custom-call | flops 32000000000 | bytes 24000000 | tf_op jit(solution)/shard_map/cross/pallas_call | solution.py:946
  173.2 1.2 collective-permute-start.28
  174.7 27.1 %self_backward.1 = (f32[32,32,512]{2,1,0:T(8,128)}, bf16[8,32,512]{2,1,0:T(8,128)(2,1)}, bf16[8,32,512]{2,1,0:T(8,128)(2,1)}, bf16[8,32,512]{2,1,0:T(8,128)(2,1)...) custom-call(s32[3]{0:T(128)} %pad_add_fusion.refs_0_.info, ...), custom_call_target="tpu_custom_call" | custom-call | flops 24000000000 | bytes 24000000 | tf_op jit(solution)/shard_map/self_backward/pallas_call | solution.py:1001
  201.8 1.6 collective-permute-done.29.refs_6_
  204.1 1.0 collective-permute-done.30
  205.8 1.2 collective-permute-start.31
  207.7 1.8 collective-permute-done.31
  210.2 3.0 collective-permute-done.32
  213.2 1.5 collective-permute-start.33
  214.7 2.1 collective-permute-done.33
  216.8 2.4 collective-permute-start.34
  220.1 1.2 collective-permute-start.40
  223.7 10.1 %inner_gradients.1 = (bf16[16,5,64,128]{3,2,1,0:T(8,128)(2,1)}, bf16[16,5,64,128]{3,2,1,0:T(8,128)(2,1)}, bf16[16,3,64,128]{3,2,1,0:T(8,128)(2,1)}, bf16[16,3,64,128]{3,2,1,0:T(8,128)(2,1)}) custom-call(s32[3]{0:T(128)} %pad_add_fusion.refs_0_.info, f32[8]{0:T(128)} %divide_minimum_fusion.clip, bf16[8,128,512]{2,1,0:T(8,128)(2,1)} %get-tuple-element.166.normed, ...), custom_call_target="tpu_custom_call" | custom-call | flops 8999999488 | bytes 14000000 | tf_op jit(solution)/shard_map/inner_gradients/pallas_call | solution.py:1095
  234.3 15.2 %attention_gradients.1 = (bf16[16,3,64,128]{3,2,1,0:T(8,128)(2,1)}, bf16[16,3,64,128]{3,2,1,0:T(8,128)(2,1)}, bf16[16,5,64,128]{3,2,1,0:T(8,128)(2,1)}, bf16[16,5,64,128]{3,2,1,0:T(8,128)(2,1)}) custom-call(s32[3]{0:T(128)} %pad_add_fusion.refs_0_.info, f32[8]{0:T(128)} %divide_minimum_fusion.clip, bf16[8,128,512]{2,1,0:T(8,128)(2,1)} %get-tuple-element.154.refs_3_.refs_0_, ...), custom_call_target="tpu_custom_call" | custom-call | flops 14000000000 | bytes 30000000 | tf_op jit(solution)/shard_map/attention_gradients/pallas_call | solution.py:1095
  250.9 4.8 %collective-permute-done.46 = f32[14,128]{1,0:T(8,128)S(1)} collective-permute-done((f32[14,128]{1,0:T(8,128)S(1)}, f32[14,128]{1,0:T(8,128)S(1)}, u32[]{:S(2)}, u32[]{:S(2)}) %collective-permute-start.46) | collective-permute-done | bytes 7200 | tf_op jit(solution)/shard_map/ppermute | solution.py:677
  256.0 1.2 collective-permute-start.38
  257.5 1.0 collective-permute-start.43
  259.0 1.5 collective-permute-start.45
  261.7 6.3 %collective-permute-done.38 = bf16[8,3,64,128]{3,2,1,0:T(8,128)(2,1)S(1)} collective-permute-done((bf16[8,3,64,128]{3,2,1,0:T(8,128)(2,1)S(1)}, bf16[8,3,64,128]{3,2,1,0:T(8,128)(2,1)S(1)}, u32[]{:S(2)}, u32[]{:S(2)}) %collective-permute-start.38) | collective-permute-done | bytes 393248 | tf_op jit(solution)/shard_map/ppermute | solution.py:677
  268.1 7.5 %collective-permute-done.43 = bf16[8,3,64,128]{3,2,1,0:T(8,128)(2,1)S(1)} collective-permute-done((bf16[8,3,64,128]{3,2,1,0:T(8,128)(2,1)S(1)}, bf16[8,3,64,128]{3,2,1,0:T(8,128)(2,1)S(1)}, u32[]{:S(2)}, u32[]{:S(2)}) %collective-permute-start.43) | collective-permute-done | bytes 393248 | tf_op jit(solution)/shard_map/ppermute | solution.py:677
  277.4 7.7 %assemble.1 = (bf16[32,32,512]{2,1,0:T(8,128)(2,1)}, f32[32,32,512]{2,1,0:T(8,128)}, f32[32,128,512]{2,1,0:T(8,128)}) custom-call(s32[3]{0:T(128)} %pad_add_fusion.refs_0_.info, bf16[4,160,512]{2,1,0:T(8,128)(2,1)} %copy-done.10, bf16[4,160,512]{2,1,0:T(8,128)(2,1)} %copy-done.11, ...), custom_call_target="tpu_custom_call", output_to_operand_aliasing={{0}: (10, {}), {1}: (11, {}), {2}: (12, {})} | custom-call | flops 1000000 | bytes 20000000 | tf_op jit(solution)/shard_map/assemble/pallas_call | solution.py:1220
  285.1 1.1 collective-permute-start.49
  286.2 1.1 collective-permute-start.52
  287.3 0.9 collective-permute-start.48
  288.2 1.5 collective-permute-start.50
  289.7 1.8 collective-permute-start.51
  291.5 2.3 collective-permute-done.50
  294.0 1.5 collective-permute-done.48
  295.7 9.5 %collective-permute-done.51 = bf16[4,5,64,128]{3,2,1,0:T(8,128)(2,1)S(1)} collective-permute-done((bf16[4,5,64,128]{3,2,1,0:T(8,128)(2,1)S(1)}, bf16[4,5,64,128]{3,2,1,0:T(8,128)(2,1)S(1)}, u32[]{:S(2)}, u32[]{:S(2)}) %collective-permute-start.51) | collective-permute-done | bytes 327712 | tf_op jit(solution)/shard_map/ppermute | solution.py:677
  305.3 2.5 collective-permute-start.57
  307.9 2.0 collective-permute-start.55
  310.5 0.9 collective-permute-done.54
  312.1 4.0 %collective-permute-done.55 = bf16[2,3,64,128]{3,2,1,0:T(8,128)(2,1)S(1)} collective-permute-done((bf16[2,3,64,128]{3,2,1,0:T(8,128)(2,1)S(1)}, bf16[2,3,64,128]{3,2,1,0:T(8,128)(2,1)S(1)}, u32[]{:S(2)}, u32[]{:S(2)}) %collective-permute-start.55) | collective-permute-done | bytes 98336 | tf_op jit(solution)/shard_map/ppermute | solution.py:677
  319.6 2.7 collective-permute-start.58
  322.8 1.1 collective-permute-start.61
  324.0 1.3 multiply_add_fusion
  326.5 1.8 collective-permute-done.60
  328.9 2.8 update.1
  (251 shorter events, 29.2 us)
Async XLA Ops:
  7.2 91.8 %all-gather.3.cloned.1.call-start = ((), (), s32[]{:S(2)}) async-start(), calls=%async_computation | async-start | bytes 4325376 | tf_op jit(solution)/shard_map/all_gather | solution.py:775
  10.1 12.5 %collective-permute-start.8 = (f32[2,128]{1,0:T(2,128)S(1)}, f32[2,128]{1,0:T(2,128)S(1)}, u32[]{:S(2)}, u32[]{:S(2)}) collective-permute-start(f32[2,128]{1,0:T(2,128)S(1)} %pad.4), channel_id=1, source_target_pairs={{0,3},{1,2},{2,1},{3,0},{4,7},{5,6},{6,5},{7,4},{8,11},{9,10},{10,... | collective-permute-start | bytes 3080 | tf_op jit(solution)/shard_map/ppermute | solution.py:677
  12.6 10.6 %collective-permute-start.7 = (f32[2,128]{1,0:T(2,128)S(1)}, f32[2,128]{1,0:T(2,128)S(1)}, u32[]{:S(2)}, u32[]{:S(2)}) collective-permute-start(f32[2,128]{1,0:T(2,128)S(1)} %pad.4), channel_id=1, source_target_pairs={{0,2},{1,3},{2,0},{3,1},{4,6},{5,7},{6,4},{7,5},{8,10},{9,11},{10,... | collective-permute-start | bytes 3080 | tf_op jit(solution)/shard_map/ppermute | solution.py:677
  13.2 11.3 %collective-permute-start.6 = (f32[2,128]{1,0:T(2,128)S(1)}, f32[2,128]{1,0:T(2,128)S(1)}, u32[]{:S(2)}, u32[]{:S(2)}) collective-permute-start(f32[2,128]{1,0:T(2,128)S(1)} %pad.4), channel_id=1, source_target_pairs={{0,1},{1,0},{2,3},{3,2},{4,5},{5,4},{6,7},{7,6},{8,9},{9,8},{10,11... | collective-permute-start | bytes 3080 | tf_op jit(solution)/shard_map/ppermute | solution.py:677
  14.3 20.3 %collective-permute-start = (bf16[8,32,512]{2,1,0:T(8,128)(2,1)}, bf16[8,32,512]{2,1,0:T(8,128)(2,1)}, u32[]{:S(2)}, u32[]{:S(2)}) collective-permute-start(bf16[8,32,512]{2,1,0:T(8,128)(2,1)} %get-tuple-element.274), channel_id=1, source_target_pairs={{0,3},{1,2},{2,1},{3,0},{4,7},{5,6},{6,5},{7,4},{8,11},{9,10},{10,... | collective-permute-start | bytes 786440 | tf_op jit(solution)/shard_map/ppermute | solution.py:677
  15.9 6.8 %collective-permute-start.9 = (bf16[1,4,64,128]{3,2,1,0:T(8,128)(2,1)S(1)}, bf16[1,4,64,128]{3,2,1,0:T(8,128)(2,1)S(1)}, u32[]{:S(2)}, u32[]{:S(2)}) collective-permute-start(bf16[1,4,64,128]{3,2,1,0:T(8,128)(2,1)S(1)} %maximum_bitcast_fusion), channel_id=1, source_target_pairs={{0,16},{4,20},{8,24},{12,28},{16,0},{20,4},{24,8},{28,12},{1,17},{... | collective-permute-start | bytes 196616 | tf_op jit(solution)/shard_map/ppermute | solution.py:677
  22.7 44.2 %collective-permute-start.4 = (bf16[8,32,512]{2,1,0:T(8,128)(2,1)S(1)}, bf16[8,32,512]{2,1,0:T(8,128)(2,1)S(1)}, u32[]{:S(2)}, u32[]{:S(2)}) collective-permute-start(bf16[8,32,512]{2,1,0:T(8,128)(2,1)S(1)} %copy-done.21), channel_id=1, source_target_pairs={{0,1},{1,0},{2,3},{3,2},{4,5},{5,4},{6,7},{7,6},{8,9},{9,8},{10,11... | collective-permute-start | bytes 786440 | tf_op jit(solution)/shard_map/ppermute | solution.py:677
  22.7 44.5 %collective-permute-start.5 = (bf16[8,32,512]{2,1,0:T(8,128)(2,1)S(1)}, bf16[8,32,512]{2,1,0:T(8,128)(2,1)S(1)}, u32[]{:S(2)}, u32[]{:S(2)}) collective-permute-start(bf16[8,32,512]{2,1,0:T(8,128)(2,1)S(1)} %copy-done.20), channel_id=1, source_target_pairs={{0,2},{1,3},{2,0},{3,1},{4,6},{5,7},{6,4},{7,5},{8,10},{9,11},{10,... | collective-permute-start | bytes 786440 | tf_op jit(solution)/shard_map/ppermute | solution.py:677
  23.2 7.6 %collective-permute-start.15 = (bf16[1,4,64,128]{3,2,1,0:T(8,128)(2,1)S(1)}, bf16[1,4,64,128]{3,2,1,0:T(8,128)(2,1)S(1)}, u32[]{:S(2)}, u32[]{:S(2)}) collective-permute-start(bf16[1,4,64,128]{3,2,1,0:T(8,128)(2,1)S(1)} %maximum_bitcast_fusion.1), channel_id=1, source_target_pairs={{0,16},{4,20},{8,24},{12,28},{16,0},{20,4},{24,8},{28,12},{1,17},{... | collective-permute-start | bytes 196616 | tf_op jit(solution)/shard_map/ppermute | solution.py:677
  24.5 8.5 %collective-permute-start.10 = (bf16[2,4,64,128]{3,2,1,0:T(8,128)(2,1)S(1)}, bf16[2,4,64,128]{3,2,1,0:T(8,128)(2,1)S(1)}, u32[]{:S(2)}, u32[]{:S(2)}) collective-permute-start(bf16[2,4,64,128]{3,2,1,0:T(8,128)(2,1)S(1)} %pad_maximum_fusion.12), channel_id=1, source_target_pairs={{0,8},{4,12},{8,0},{12,4},{16,24},{20,28},{24,16},{28,20},{1,9},{5... | collective-permute-start | bytes 393224 | tf_op jit(solution)/shard_map/ppermute | solution.py:677
  30.9 13.0 %collective-permute-start.16 = (bf16[2,4,64,128]{3,2,1,0:T(8,128)(2,1)S(1)}, bf16[2,4,64,128]{3,2,1,0:T(8,128)(2,1)S(1)}, u32[]{:S(2)}, u32[]{:S(2)}) collective-permute-start(bf16[2,4,64,128]{3,2,1,0:T(8,128)(2,1)S(1)} %pad_maximum_fusion.13), channel_id=1, source_target_pairs={{0,8},{4,12},{8,0},{12,4},{16,24},{20,28},{24,16},{28,20},{1,9},{5... | collective-permute-start | bytes 393224 | tf_op jit(solution)/shard_map/ppermute | solution.py:677
  33.1 9.3 %collective-permute-start.11 = (bf16[4,4,64,128]{3,2,1,0:T(8,128)(2,1)S(1)}, bf16[4,4,64,128]{3,2,1,0:T(8,128)(2,1)S(1)}, u32[]{:S(2)}, u32[]{:S(2)}) collective-permute-start(bf16[4,4,64,128]{3,2,1,0:T(8,128)(2,1)S(1)} %pad_maximum_fusion.10), channel_id=1, source_target_pairs={{0,2},{1,3},{2,0},{3,1},{4,6},{5,7},{6,4},{7,5},{8,10},{9,11},{10,... | collective-permute-start | bytes 786440 | tf_op jit(solution)/shard_map/ppermute | solution.py:677
  34.8 27.9 %collective-permute-start.3 = (bf16[4,160,512]{2,1,0:T(8,128)(2,1)S(1)}, bf16[4,160,512]{2,1,0:T(8,128)(2,1)S(1)}, u32[]{:S(2)}, u32[]{:S(2)}) collective-permute-start(bf16[4,160,512]{2,1,0:T(8,128)(2,1)S(1)} %pad_maximum_fusion.3), channel_id=1, source_target_pairs={{0,3},{1,2},{2,1},{3,0},{4,7},{5,6},{6,5},{7,4},{8,11},{9,10},{10,... | collective-permute-start | bytes 1966088 | tf_op jit(solution)/shard_map/ppermute | solution.py:677
  42.4 22.5 %collective-permute-start.12 = (bf16[8,4,64,128]{3,2,1,0:T(8,128)(2,1)S(1)}, bf16[8,4,64,128]{3,2,1,0:T(8,128)(2,1)S(1)}, u32[]{:S(2)}, u32[]{:S(2)}) collective-permute-start(bf16[8,4,64,128]{3,2,1,0:T(8,128)(2,1)S(1)} %pad_maximum_fusion.8.refs_9_.refs_12_), channel_id=1, source_target_pairs={{0,4},{4,0},{8,12},{12,8},{16,20},{20,16},{24,28},{28,24},{1,5},{5... | collective-permute-start | bytes 1572872 | tf_op jit(solution)/shard_map/ppermute | solution.py:677
  44.0 18.6 %collective-permute-start.17 = (bf16[4,4,64,128]{3,2,1,0:T(8,128)(2,1)S(1)}, bf16[4,4,64,128]{3,2,1,0:T(8,128)(2,1)S(1)}, u32[]{:S(2)}, u32[]{:S(2)}) collective-permute-start(bf16[4,4,64,128]{3,2,1,0:T(8,128)(2,1)S(1)} %pad_maximum_fusion.11), channel_id=1, source_target_pairs={{0,2},{1,3},{2,0},{3,1},{4,6},{5,7},{6,4},{7,5},{8,10},{9,11},{10,... | collective-permute-start | bytes 786440 | tf_op jit(solution)/shard_map/ppermute | solution.py:677
  62.6 7.0 %collective-permute-start.13 = (bf16[8,4,64,128]{3,2,1,0:T(8,128)(2,1)S(1)}, bf16[8,4,64,128]{3,2,1,0:T(8,128)(2,1)S(1)}, u32[]{:S(2)}, u32[]{:S(2)}) collective-permute-start(bf16[8,4,64,128]{3,2,1,0:T(8,128)(2,1)S(1)} %pad_maximum_fusion.8.refs_9_.refs_12_), channel_id=1, source_target_pairs={{0,1},{1,0},{2,3},{3,2},{4,5},{5,4},{6,7},{7,6},{8,9},{9,8},{10,11... | collective-permute-start | bytes 1572872 | tf_op jit(solution)/shard_map/ppermute | solution.py:677
  62.7 18.6 %collective-permute-start.18 = (bf16[8,4,64,128]{3,2,1,0:T(8,128)(2,1)S(1)}, bf16[8,4,64,128]{3,2,1,0:T(8,128)(2,1)}, u32[]{:S(2)}, u32[]{:S(2)}) collective-permute-start(bf16[8,4,64,128]{3,2,1,0:T(8,128)(2,1)S(1)} %pad_maximum_fusion.9.refs_7_), channel_id=1, source_target_pairs={{0,4},{4,0},{8,12},{12,8},{16,20},{20,16},{24,28},{28,24},{1,5},{5... | collective-permute-start | bytes 1572872 | tf_op jit(solution)/shard_map/ppermute | solution.py:677
  64.9 16.4 %collective-permute-start.14 = (bf16[8,4,64,128]{3,2,1,0:T(8,128)(2,1)S(1)}, bf16[8,4,64,128]{3,2,1,0:T(8,128)(2,1)S(1)}, u32[]{:S(2)}, u32[]{:S(2)}) collective-permute-start(bf16[8,4,64,128]{3,2,1,0:T(8,128)(2,1)S(1)} %collective-permute-done.12.refs_10_.refs_13_), channel_id=1, source_target_pairs={{0,1},{1,0},{2,3},{3,2},{4,5},{5,4},{6,7},{7,6},{8,9},{9,8},{10,11... | collective-permute-start | bytes 1572872 | tf_op jit(solution)/shard_map/ppermute | solution.py:677
  66.8 29.0 %collective-permute-start.1 = (bf16[4,160,512]{2,1,0:T(8,128)(2,1)S(1)}, bf16[4,160,512]{2,1,0:T(8,128)(2,1)S(1)}, u32[]{:S(2)}, u32[]{:S(2)}) collective-permute-start(bf16[4,160,512]{2,1,0:T(8,128)(2,1)S(1)} %pad_maximum_fusion.1), channel_id=1, source_target_pairs={{0,1},{1,0},{2,3},{3,2},{4,5},{5,4},{6,7},{7,6},{8,9},{9,8},{10,11... | collective-permute-start | bytes 1966088 | tf_op jit(solution)/shard_map/ppermute | solution.py:677
  67.2 30.3 %collective-permute-start.2 = (bf16[4,160,512]{2,1,0:T(8,128)(2,1)S(1)}, bf16[4,160,512]{2,1,0:T(8,128)(2,1)S(1)}, u32[]{:S(2)}, u32[]{:S(2)}) collective-permute-start(bf16[4,160,512]{2,1,0:T(8,128)(2,1)S(1)} %pad_maximum_fusion.2), channel_id=1, source_target_pairs={{0,2},{1,3},{2,0},{3,1},{4,6},{5,7},{6,4},{7,5},{8,10},{9,11},{10,... | collective-permute-start | bytes 1966088 | tf_op jit(solution)/shard_map/ppermute | solution.py:677
  69.7 28.1 %collective-permute-start.19 = (bf16[8,4,64,128]{3,2,1,0:T(8,128)(2,1)S(1)}, bf16[8,4,64,128]{3,2,1,0:T(8,128)(2,1)S(1)}, u32[]{:S(2)}, u32[]{:S(2)}) collective-permute-start(bf16[8,4,64,128]{3,2,1,0:T(8,128)(2,1)S(1)} %pad_maximum_fusion.9.refs_7_), channel_id=1, source_target_pairs={{0,1},{1,0},{2,3},{3,2},{4,5},{5,4},{6,7},{7,6},{8,9},{9,8},{10,11... | collective-permute-start | bytes 1572872 | tf_op jit(solution)/shard_map/ppermute | solution.py:677
  81.3 54.9 %collective-permute-start.24 = (bf16[4,160,512]{2,1,0:T(8,128)(2,1)S(1)}, bf16[4,160,512]{2,1,0:T(8,128)(2,1)}, u32[]{:S(2)}, u32[]{:S(2)}) collective-permute-start(bf16[4,160,512]{2,1,0:T(8,128)(2,1)S(1)} %pad_maximum_fusion.5), channel_id=1, source_target_pairs={{0,1},{1,0},{2,3},{3,2},{4,5},{5,4},{6,7},{7,6},{8,9},{9,8},{10,11... | collective-permute-start | bytes 1966088 | tf_op jit(solution)/shard_map/ppermute | solution.py:677
  81.4 17.7 %collective-permute-start.20 = (bf16[8,4,64,128]{3,2,1,0:T(8,128)(2,1)}, bf16[8,4,64,128]{3,2,1,0:T(8,128)(2,1)}, u32[]{:S(2)}, u32[]{:S(2)}) collective-permute-start(bf16[8,4,64,128]{3,2,1,0:T(8,128)(2,1)} %collective-permute-done.18.refs_8_), channel_id=1, source_target_pairs={{0,1},{1,0},{2,3},{3,2},{4,5},{5,4},{6,7},{7,6},{8,9},{9,8},{10,11... | collective-permute-start | bytes 1572872 | tf_op jit(solution)/shard_map/ppermute | solution.py:677
  95.9 40.9 %collective-permute-start.25 = (bf16[4,160,512]{2,1,0:T(8,128)(2,1)S(1)}, bf16[4,160,512]{2,1,0:T(8,128)(2,1)}, u32[]{:S(2)}, u32[]{:S(2)}) collective-permute-start(bf16[4,160,512]{2,1,0:T(8,128)(2,1)S(1)} %pad_maximum_fusion.6), channel_id=1, source_target_pairs={{0,2},{1,3},{2,0},{3,1},{4,6},{5,7},{6,4},{7,5},{8,10},{9,11},{10,... | collective-permute-start | bytes 1966088 | tf_op jit(solution)/shard_map/ppermute | solution.py:677
  97.4 39.3 %collective-permute-start.26 = (bf16[4,160,512]{2,1,0:T(8,128)(2,1)S(1)}, bf16[4,160,512]{2,1,0:T(8,128)(2,1)}, u32[]{:S(2)}, u32[]{:S(2)}) collective-permute-start(bf16[4,160,512]{2,1,0:T(8,128)(2,1)S(1)} %pad_maximum_fusion.7), channel_id=1, source_target_pairs={{0,3},{1,2},{2,1},{3,0},{4,7},{5,6},{6,5},{7,4},{8,11},{9,10},{10,... | collective-permute-start | bytes 1966088 | tf_op jit(solution)/shard_map/ppermute | solution.py:677
  134.8 39.6 %collective-permute-start.21 = (bf16[4,160,512]{2,1,0:T(8,128)(2,1)}, bf16[4,160,512]{2,1,0:T(8,128)(2,1)S(1)}, u32[]{:S(2)}, u32[]{:S(2)}) collective-permute-start(bf16[4,160,512]{2,1,0:T(8,128)(2,1)} %get-tuple-element.132), channel_id=1, source_target_pairs={{0,1},{1,0},{2,3},{3,2},{4,5},{5,4},{6,7},{7,6},{8,9},{9,8},{10,11... | collective-permute-start | bytes 1966088 | tf_op jit(solution)/shard_map/ppermute | solution.py:677
  135.0 39.6 %collective-permute-start.22 = (bf16[4,160,512]{2,1,0:T(8,128)(2,1)}, bf16[4,160,512]{2,1,0:T(8,128)(2,1)S(1)}, u32[]{:S(2)}, u32[]{:S(2)}) collective-permute-start(bf16[4,160,512]{2,1,0:T(8,128)(2,1)} %get-tuple-element.133), channel_id=1, source_target_pairs={{0,2},{1,3},{2,0},{3,1},{4,6},{5,7},{6,4},{7,5},{8,10},{9,11},{10,... | collective-permute-start | bytes 1966088 | tf_op jit(solution)/shard_map/ppermute | solution.py:677
  136.2 38.5 %collective-permute-start.23 = (bf16[4,160,512]{2,1,0:T(8,128)(2,1)}, bf16[4,160,512]{2,1,0:T(8,128)(2,1)S(1)}, u32[]{:S(2)}, u32[]{:S(2)}) collective-permute-start(bf16[4,160,512]{2,1,0:T(8,128)(2,1)} %get-tuple-element.134), channel_id=1, source_target_pairs={{0,3},{1,2},{2,1},{3,0},{4,7},{5,6},{6,5},{7,4},{8,11},{9,10},{10,... | collective-permute-start | bytes 1966088 | tf_op jit(solution)/shard_map/ppermute | solution.py:677
  172.7 29.1 %collective-permute-start.27 = (bf16[4,160,512]{2,1,0:T(8,128)(2,1)}, bf16[4,160,512]{2,1,0:T(8,128)(2,1)S(1)}, u32[]{:S(2)}, u32[]{:S(2)}) collective-permute-start(bf16[4,160,512]{2,1,0:T(8,128)(2,1)} %get-tuple-element.162), channel_id=1, source_target_pairs={{0,1},{1,0},{2,3},{3,2},{4,5},{5,4},{6,7},{7,6},{8,9},{9,8},{10,11... | collective-permute-start | bytes 1966088 | tf_op jit(solution)/shard_map/ppermute | solution.py:677
  173.2 28.6 %collective-permute-start.28 = (bf16[4,160,512]{2,1,0:T(8,128)(2,1)}, bf16[4,160,512]{2,1,0:T(8,128)(2,1)S(1)}, u32[]{:S(2)}, u32[]{:S(2)}) collective-permute-start(bf16[4,160,512]{2,1,0:T(8,128)(2,1)} %get-tuple-element.163), channel_id=1, source_target_pairs={{0,2},{1,3},{2,0},{3,1},{4,6},{5,7},{6,4},{7,5},{8,10},{9,11},{10,... | collective-permute-start | bytes 1966088 | tf_op jit(solution)/shard_map/ppermute | solution.py:677
  174.4 29.0 %collective-permute-start.29 = (bf16[4,160,512]{2,1,0:T(8,128)(2,1)}, bf16[4,160,512]{2,1,0:T(8,128)(2,1)}, u32[]{:S(2)}, u32[]{:S(2)}) collective-permute-start(bf16[4,160,512]{2,1,0:T(8,128)(2,1)} %get-tuple-element.164), channel_id=1, source_target_pairs={{0,3},{1,2},{2,1},{3,0},{4,7},{5,6},{6,5},{7,4},{8,11},{9,10},{10,... | collective-permute-start | bytes 1966088 | tf_op jit(solution)/shard_map/ppermute | solution.py:677
  203.4 1.7 collective-permute-start.30
  205.8 3.7 %collective-permute-start.31 = (f32[16,128]{1,0:T(8,128)S(1)}, f32[16,128]{1,0:T(8,128)S(1)}, u32[]{:S(2)}, u32[]{:S(2)}) collective-permute-start(f32[16,128]{1,0:T(8,128)S(1)} %pad_maximum_fusion.17), channel_id=1, source_target_pairs={{0,2},{1,3},{2,0},{3,1},{4,6},{5,7},{6,4},{7,5},{8,10},{9,11},{10,... | collective-permute-start | bytes 24584 | tf_op jit(solution)/shard_map/ppermute | solution.py:677
  209.5 3.7 %collective-permute-start.32 = (f32[8,128]{1,0:T(8,128)S(1)}, f32[8,128]{1,0:T(8,128)S(1)}, u32[]{:S(2)}, u32[]{:S(2)}) collective-permute-start(f32[8,128]{1,0:T(8,128)S(1)} %broadcast_in_dim.8), channel_id=1, source_target_pairs={{0,4},{4,0},{8,12},{12,8},{16,20},{20,16},{24,28},{28,24},{1,5},{5... | collective-permute-start | bytes 12296 | tf_op jit(solution)/shard_map/ppermute | solution.py:677
  213.2 3.6 %collective-permute-start.33 = (f32[8,128]{1,0:T(8,128)S(1)}, f32[8,128]{1,0:T(8,128)S(1)}, u32[]{:S(2)}, u32[]{:S(2)}) collective-permute-start(f32[8,128]{1,0:T(8,128)S(1)} %broadcast_add_fusion), channel_id=1, source_target_pairs={{0,8},{4,12},{8,0},{12,4},{16,24},{20,28},{24,16},{28,20},{1,9},{5... | collective-permute-start | bytes 12296 | tf_op jit(solution)/shard_map/ppermute | solution.py:677
  216.8 5.1 %collective-permute-start.34 = (f32[8,128]{1,0:T(8,128)S(1)}, f32[8,128]{1,0:T(8,128)S(1)}, u32[]{:S(2)}, u32[]{:S(2)}) collective-permute-start(f32[8,128]{1,0:T(8,128)S(1)} %fusion.9), channel_id=1, source_target_pairs={{0,16},{4,20},{8,24},{12,28},{16,0},{20,4},{24,8},{28,12},{1,17},{... | collective-permute-start | bytes 12296 | tf_op jit(solution)/shard_map/ppermute | solution.py:677
  220.0 14.2 %collective-permute-start.39 = (bf16[8,32,512]{2,1,0:T(8,128)(2,1)}, bf16[8,32,512]{2,1,0:T(8,128)(2,1)S(1)}, u32[]{:S(2)}, u32[]{:S(2)}) collective-permute-start(bf16[8,32,512]{2,1,0:T(8,128)(2,1)} %get-tuple-element.174), channel_id=1, source_target_pairs={{0,1},{1,0},{2,3},{3,2},{4,5},{5,4},{6,7},{7,6},{8,9},{9,8},{10,11... | collective-permute-start | bytes 786440 | tf_op jit(solution)/shard_map/ppermute | solution.py:677
  220.1 14.2 %collective-permute-start.40 = (bf16[8,32,512]{2,1,0:T(8,128)(2,1)}, bf16[8,32,512]{2,1,0:T(8,128)(2,1)S(1)}, u32[]{:S(2)}, u32[]{:S(2)}) collective-permute-start(bf16[8,32,512]{2,1,0:T(8,128)(2,1)} %get-tuple-element.175), channel_id=1, source_target_pairs={{0,2},{1,3},{2,0},{3,1},{4,6},{5,7},{6,4},{7,5},{8,10},{9,11},{10,... | collective-permute-start | bytes 786440 | tf_op jit(solution)/shard_map/ppermute | solution.py:677
  221.3 13.0 %collective-permute-start.41 = (bf16[8,32,512]{2,1,0:T(8,128)(2,1)}, bf16[8,32,512]{2,1,0:T(8,128)(2,1)S(1)}, u32[]{:S(2)}, u32[]{:S(2)}) collective-permute-start(bf16[8,32,512]{2,1,0:T(8,128)(2,1)} %get-tuple-element.176), channel_id=1, source_target_pairs={{0,3},{1,2},{2,1},{3,0},{4,7},{5,6},{6,5},{7,4},{8,11},{9,10},{10,... | collective-permute-start | bytes 786440 | tf_op jit(solution)/shard_map/ppermute | solution.py:677
  233.8 21.9 %collective-permute-start.37 = (bf16[16,3,64,128]{3,2,1,0:T(8,128)(2,1)}, bf16[16,3,64,128]{3,2,1,0:T(8,128)(2,1)S(1)}, u32[]{:S(2)}, u32[]{:S(2)}) collective-permute-start(bf16[16,3,64,128]{3,2,1,0:T(8,128)(2,1)} %get-tuple-element.173), channel_id=1, source_target_pairs={{0,1},{1,0},{2,3},{3,2},{4,5},{5,4},{6,7},{7,6},{8,9},{9,8},{10,11... | collective-permute-start | bytes 2359304 | tf_op jit(solution)/shard_map/ppermute | solution.py:677
  249.6 8.9 %collective-permute-start.44 = (bf16[16,5,64,128]{3,2,1,0:T(8,128)(2,1)}, bf16[16,5,64,128]{3,2,1,0:T(8,128)(2,1)S(1)}, u32[]{:S(2)}, u32[]{:S(2)}) collective-permute-start(bf16[16,5,64,128]{3,2,1,0:T(8,128)(2,1)} %get-tuple-element.188), channel_id=1, source_target_pairs={{0,1},{1,0},{2,3},{3,2},{4,5},{5,4},{6,7},{7,6},{8,9},{9,8},{10,11... | collective-permute-start | bytes 3932168 | tf_op jit(solution)/shard_map/ppermute | solution.py:677
  249.8 7.4 %collective-permute-start.42 = (bf16[16,3,64,128]{3,2,1,0:T(8,128)(2,1)}, bf16[16,3,64,128]{3,2,1,0:T(8,128)(2,1)S(1)}, u32[]{:S(2)}, u32[]{:S(2)}) collective-permute-start(bf16[16,3,64,128]{3,2,1,0:T(8,128)(2,1)} %get-tuple-element.186), channel_id=1, source_target_pairs={{0,1},{1,0},{2,3},{3,2},{4,5},{5,4},{6,7},{7,6},{8,9},{9,8},{10,11... | collective-permute-start | bytes 2359304 | tf_op jit(solution)/shard_map/ppermute | solution.py:677
  250.1 10.4 %collective-permute-start.35 = (bf16[16,5,64,128]{3,2,1,0:T(8,128)(2,1)S(1)}, bf16[16,5,64,128]{3,2,1,0:T(8,128)(2,1)S(1)}, u32[]{:S(2)}, u32[]{:S(2)}) collective-permute-start(bf16[16,5,64,128]{3,2,1,0:T(8,128)(2,1)S(1)} %copy-done.36), channel_id=1, source_target_pairs={{0,1},{1,0},{2,3},{3,2},{4,5},{5,4},{6,7},{7,6},{8,9},{9,8},{10,11... | collective-permute-start | bytes 3932168 | tf_op jit(solution)/shard_map/ppermute | solution.py:677
  250.4 5.2 %collective-permute-start.46 = (f32[14,128]{1,0:T(8,128)S(1)}, f32[14,128]{1,0:T(8,128)S(1)}, u32[]{:S(2)}, u32[]{:S(2)}) collective-permute-start(f32[14,128]{1,0:T(8,128)S(1)} %bitcast.71), channel_id=1, source_target_pairs={{0,1},{1,0},{2,3},{3,2},{4,5},{5,4},{6,7},{7,6},{8,9},{9,8},{10,11... | collective-permute-start | bytes 21512 | tf_op jit(solution)/shard_map/ppermute | solution.py:677
  256.0 12.0 %collective-permute-start.38 = (bf16[8,3,64,128]{3,2,1,0:T(8,128)(2,1)S(1)}, bf16[8,3,64,128]{3,2,1,0:T(8,128)(2,1)S(1)}, u32[]{:S(2)}, u32[]{:S(2)}) collective-permute-start(bf16[8,3,64,128]{3,2,1,0:T(8,128)(2,1)S(1)} %get-tuple-element.259), channel_id=1, source_target_pairs={{0,2},{1,3},{2,0},{3,1},{4,6},{5,7},{6,4},{7,5},{8,10},{9,11},{10,... | collective-permute-start | bytes 1179656 | tf_op jit(solution)/shard_map/ppermute | solution.py:677
  257.5 18.2 %collective-permute-start.43 = (bf16[8,3,64,128]{3,2,1,0:T(8,128)(2,1)S(1)}, bf16[8,3,64,128]{3,2,1,0:T(8,128)(2,1)S(1)}, u32[]{:S(2)}, u32[]{:S(2)}) collective-permute-start(bf16[8,3,64,128]{3,2,1,0:T(8,128)(2,1)S(1)} %get-tuple-element.257), channel_id=1, source_target_pairs={{0,2},{1,3},{2,0},{3,1},{4,6},{5,7},{6,4},{7,5},{8,10},{9,11},{10,... | collective-permute-start | bytes 1179656 | tf_op jit(solution)/shard_map/ppermute | solution.py:677
  259.0 16.8 %collective-permute-start.45 = (bf16[8,5,64,128]{3,2,1,0:T(8,128)(2,1)S(1)}, bf16[8,5,64,128]{3,2,1,0:T(8,128)(2,1)S(1)}, u32[]{:S(2)}, u32[]{:S(2)}) collective-permute-start(bf16[8,5,64,128]{3,2,1,0:T(8,128)(2,1)S(1)} %get-tuple-element.253), channel_id=1, source_target_pairs={{0,8},{4,12},{8,0},{12,4},{16,24},{20,28},{24,16},{28,20},{1,9},{5... | collective-permute-start | bytes 1966088 | tf_op jit(solution)/shard_map/ppermute | solution.py:677
  261.1 16.0 %collective-permute-start.36 = (bf16[8,5,64,128]{3,2,1,0:T(8,128)(2,1)S(1)}, bf16[8,5,64,128]{3,2,1,0:T(8,128)(2,1)S(1)}, u32[]{:S(2)}, u32[]{:S(2)}) collective-permute-start(bf16[8,5,64,128]{3,2,1,0:T(8,128)(2,1)S(1)} %get-tuple-element.255), channel_id=1, source_target_pairs={{0,4},{4,0},{8,12},{12,8},{16,20},{20,16},{24,28},{28,24},{1,5},{5... | collective-permute-start | bytes 1966088 | tf_op jit(solution)/shard_map/ppermute | solution.py:677
  276.1 9.0 %collective-permute-start.47 = (f32[14,128]{1,0:T(8,128)S(1)}, f32[14,128]{1,0:T(8,128)S(1)}, u32[]{:S(2)}, u32[]{:S(2)}) collective-permute-start(f32[14,128]{1,0:T(8,128)S(1)} %bitcast_add_fusion), channel_id=1, source_target_pairs={{0,4},{4,0},{8,12},{12,8},{16,20},{20,16},{24,28},{28,24},{1,5},{5... | collective-permute-start | bytes 21512 | tf_op jit(solution)/shard_map/ppermute | solution.py:677
  285.1 6.4 %collective-permute-start.49 = (bf16[4,3,64,128]{3,2,1,0:T(8,128)(2,1)S(1)}, bf16[4,3,64,128]{3,2,1,0:T(8,128)(2,1)S(1)}, u32[]{:S(2)}, u32[]{:S(2)}) collective-permute-start(bf16[4,3,64,128]{3,2,1,0:T(8,128)(2,1)S(1)} %get-tuple-element.202), channel_id=1, source_target_pairs={{0,8},{4,12},{8,0},{12,4},{16,24},{20,28},{24,16},{28,20},{1,9},{5... | collective-permute-start | bytes 589832 | tf_op jit(solution)/shard_map/ppermute | solution.py:677
  286.2 5.3 %collective-permute-start.52 = (f32[14,128]{1,0:T(8,128)S(1)}, f32[14,128]{1,0:T(8,128)S(1)}, u32[]{:S(2)}, u32[]{:S(2)}) collective-permute-start(f32[14,128]{1,0:T(8,128)S(1)} %add.248), channel_id=1, source_target_pairs={{0,2},{1,3},{2,0},{3,1},{4,6},{5,7},{6,4},{7,5},{8,10},{9,11},{10,... | collective-permute-start | bytes 21512 | tf_op jit(solution)/shard_map/ppermute | solution.py:677
  287.3 8.2 %collective-permute-start.48 = (bf16[4,5,64,128]{3,2,1,0:T(8,128)(2,1)S(1)}, bf16[4,5,64,128]{3,2,1,0:T(8,128)(2,1)S(1)}, u32[]{:S(2)}, u32[]{:S(2)}) collective-permute-start(bf16[4,5,64,128]{3,2,1,0:T(8,128)(2,1)S(1)} %get-tuple-element.200), channel_id=1, source_target_pairs={{0,2},{1,3},{2,0},{3,1},{4,6},{5,7},{6,4},{7,5},{8,10},{9,11},{10,... | collective-permute-start | bytes 983048 | tf_op jit(solution)/shard_map/ppermute | solution.py:677
  288.2 5.7 %collective-permute-start.50 = (bf16[4,3,64,128]{3,2,1,0:T(8,128)(2,1)S(1)}, bf16[4,3,64,128]{3,2,1,0:T(8,128)(2,1)S(1)}, u32[]{:S(2)}, u32[]{:S(2)}) collective-permute-start(bf16[4,3,64,128]{3,2,1,0:T(8,128)(2,1)S(1)} %get-tuple-element.204), channel_id=1, source_target_pairs={{0,4},{4,0},{8,12},{12,8},{16,20},{20,16},{24,28},{28,24},{1,5},{5... | collective-permute-start | bytes 589832 | tf_op jit(solution)/shard_map/ppermute | solution.py:677
  289.7 15.5 %collective-permute-start.51 = (bf16[4,5,64,128]{3,2,1,0:T(8,128)(2,1)S(1)}, bf16[4,5,64,128]{3,2,1,0:T(8,128)(2,1)S(1)}, u32[]{:S(2)}, u32[]{:S(2)}) collective-permute-start(bf16[4,5,64,128]{3,2,1,0:T(8,128)(2,1)S(1)} %get-tuple-element.206), channel_id=1, source_target_pairs={{0,16},{4,20},{8,24},{12,28},{16,0},{20,4},{24,8},{28,12},{1,17},{... | collective-permute-start | bytes 983048 | tf_op jit(solution)/shard_map/ppermute | solution.py:677
  305.3 6.2 %collective-permute-start.54 = (bf16[2,3,64,128]{3,2,1,0:T(8,128)(2,1)S(1)}, bf16[2,3,64,128]{3,2,1,0:T(8,128)(2,1)S(1)}, u32[]{:S(2)}, u32[]{:S(2)}) collective-permute-start(bf16[2,3,64,128]{3,2,1,0:T(8,128)(2,1)S(1)} %get-tuple-element.211), channel_id=1, source_target_pairs={{0,16},{4,20},{8,24},{12,28},{16,0},{20,4},{24,8},{28,12},{1,17},{... | collective-permute-start | bytes 294920 | tf_op jit(solution)/shard_map/ppermute | solution.py:677
  305.3 5.2 %collective-permute-start.57 = (f32[14,128]{1,0:T(8,128)S(1)}, f32[14,128]{1,0:T(8,128)S(1)}, u32[]{:S(2)}, u32[]{:S(2)}) collective-permute-start(f32[14,128]{1,0:T(8,128)S(1)} %add.258), channel_id=1, source_target_pairs={{0,8},{4,12},{8,0},{12,4},{16,24},{20,28},{24,16},{28,20},{1,9},{5... | collective-permute-start | bytes 21512 | tf_op jit(solution)/shard_map/ppermute | solution.py:677
  307.9 8.8 %collective-permute-start.53 = (bf16[2,5,64,128]{3,2,1,0:T(8,128)(2,1)S(1)}, bf16[2,5,64,128]{3,2,1,0:T(8,128)(2,1)S(1)}, u32[]{:S(2)}, u32[]{:S(2)}) collective-permute-start(bf16[2,5,64,128]{3,2,1,0:T(8,128)(2,1)S(1)} %get-tuple-element.209), channel_id=1, source_target_pairs={{0,8},{4,12},{8,0},{12,4},{16,24},{20,28},{24,16},{28,20},{1,9},{5... | collective-permute-start | bytes 491528 | tf_op jit(solution)/shard_map/ppermute | solution.py:677
  307.9 8.1 %collective-permute-start.55 = (bf16[2,3,64,128]{3,2,1,0:T(8,128)(2,1)S(1)}, bf16[2,3,64,128]{3,2,1,0:T(8,128)(2,1)S(1)}, u32[]{:S(2)}, u32[]{:S(2)}) collective-permute-start(bf16[2,3,64,128]{3,2,1,0:T(8,128)(2,1)S(1)} %get-tuple-element.213), channel_id=1, source_target_pairs={{0,8},{4,12},{8,0},{12,4},{16,24},{20,28},{24,16},{28,20},{1,9},{5... | collective-permute-start | bytes 294920 | tf_op jit(solution)/shard_map/ppermute | solution.py:677
  309.9 7.5 %collective-permute-start.56 = (bf16[2,5,64,128]{3,2,1,0:T(8,128)(2,1)S(1)}, bf16[2,5,64,128]{3,2,1,0:T(8,128)(2,1)S(1)}, u32[]{:S(2)}, u32[]{:S(2)}) collective-permute-start(bf16[2,5,64,128]{3,2,1,0:T(8,128)(2,1)S(1)} %get-tuple-element.215), channel_id=1, source_target_pairs={{0,4},{4,0},{8,12},{12,8},{16,20},{20,16},{24,28},{28,24},{1,5},{5... | collective-permute-start | bytes 491528 | tf_op jit(solution)/shard_map/ppermute | solution.py:677
  318.1 5.8 %collective-permute-start.62 = (f32[14,128]{1,0:T(8,128)S(1)}, f32[14,128]{1,0:T(8,128)S(1)}, u32[]{:S(2)}, u32[]{:S(2)}) collective-permute-start(f32[14,128]{1,0:T(8,128)S(1)} %add.267), channel_id=1, source_target_pairs={{0,16},{4,20},{8,24},{12,28},{16,0},{20,4},{24,8},{28,12},{1,17},{... | collective-permute-start | bytes 21512 | tf_op jit(solution)/shard_map/ppermute | solution.py:677
  319.6 8.6 %collective-permute-start.58 = (bf16[1,5,64,128]{3,2,1,0:T(8,128)(2,1)S(1)}, bf16[1,5,64,128]{3,2,1,0:T(8,128)(2,1)S(1)}, u32[]{:S(2)}, u32[]{:S(2)}) collective-permute-start(bf16[1,5,64,128]{3,2,1,0:T(8,128)(2,1)S(1)} %get-tuple-element.218), channel_id=1, source_target_pairs={{0,16},{4,20},{8,24},{12,28},{16,0},{20,4},{24,8},{28,12},{1,17},{... | collective-permute-start | bytes 245768 | tf_op jit(solution)/shard_map/ppermute | solution.py:677
  322.4 4.1 %collective-permute-start.59 = (bf16[1,3,64,128]{3,2,1,0:T(8,128)(2,1)S(1)}, bf16[1,3,64,128]{3,2,1,0:T(8,128)(2,1)S(1)}, u32[]{:S(2)}, u32[]{:S(2)}) collective-permute-start(bf16[1,3,64,128]{3,2,1,0:T(8,128)(2,1)S(1)} %get-tuple-element.220), channel_id=1, source_target_pairs={{0,4},{4,0},{8,12},{12,8},{16,20},{20,16},{24,28},{28,24},{1,5},{5... | collective-permute-start | bytes 147464 | tf_op jit(solution)/shard_map/ppermute | solution.py:677
  322.4 5.9 %collective-permute-start.60 = (bf16[1,3,64,128]{3,2,1,0:T(8,128)(2,1)S(1)}, bf16[1,3,64,128]{3,2,1,0:T(8,128)(2,1)S(1)}, u32[]{:S(2)}, u32[]{:S(2)}) collective-permute-start(bf16[1,3,64,128]{3,2,1,0:T(8,128)(2,1)S(1)} %get-tuple-element.222), channel_id=1, source_target_pairs={{0,16},{4,20},{8,24},{12,28},{16,0},{20,4},{24,8},{28,12},{1,17},{... | collective-permute-start | bytes 147464 | tf_op jit(solution)/shard_map/ppermute | solution.py:677
  322.8 5.5 %collective-permute-start.61 = (bf16[1,5,64,128]{3,2,1,0:T(8,128)(2,1)S(1)}, bf16[1,5,64,128]{3,2,1,0:T(8,128)(2,1)S(1)}, u32[]{:S(2)}, u32[]{:S(2)}) collective-permute-start(bf16[1,5,64,128]{3,2,1,0:T(8,128)(2,1)S(1)} %get-tuple-element.224), channel_id=1, source_target_pairs={{0,2},{1,3},{2,0},{3,1},{4,6},{5,7},{6,4},{7,5},{8,10},{9,11},{10,... | collective-permute-start | bytes 245768 | tf_op jit(solution)/shard_map/ppermute | solution.py:677
  (48 other events, 674.7 us)
Sparse Core Ops, SparseCore 0:
  11.5 73.2 all-gather.2

commit v4 on v3

--- a/solution.py
+++ b/solution.py
@@ -32,12 +32,11 @@
 far = ("dp", 4)
 gather_order = (far, near, row, side, core)
 reduce_orders = (
+    (core, side, near, row, far),
+    (core, row, near, side, far),
+    (core, row, near, far, side),
     (core, side, row, near, far),
-    (core, row, near, far, side),
-    (core, row, side, near, far),
-    (core, near, far, side, row),
 )
-reduce_counts = (5, 3, 3, 5)
 
 
 def dot_nn(left, right):
@@ -543,37 +542,86 @@
             copy.wait()
 
 
-def inner_gradient_kernel(places, info, clip, normed, d_hidden, d_top, active, *refs):
-    outs = (refs[:2], refs[2:4])
-    rows_held, blocks_held, load_sems, scaled, tile, held, store_sems = refs[4:]
-    loads = []
-    for piece, (left, right) in enumerate(((normed, d_hidden), (d_top, active))):
-        loads.append((left, rows_held.at[piece]))
-        loads += [(right.at[unit], blocks_held.at[4 * piece + unit]) for unit in range(4)]
+class Carry:
+    def __init__(self, info, count, first, parts, cuts, outs, low, sems):
+        self.low, self.sems, self.cuts, self.outs = low, sems, cuts, outs
+        self.spots = [
+            (info[2] ^ (index + 1)) * count + first for index in range(len(parts))
+        ]
+        self.loads = [
+            pltpu.make_async_copy(part, low.at[index], sems.at[index])
+            for index, part in enumerate(parts)
+        ]
+        for load in self.loads:
+            load.start()
+
+    def pass_on(self, helds):
+        stores = []
+        size = self.low.shape[1]
+        for index, (load, spot) in enumerate(zip(self.loads, self.spots)):
+            load.wait()
+            for (start, stop), out, held in zip(self.cuts, self.outs, helds):
+                held[index] = self.low[index, :, start:stop, :].astype(held.dtype)
+                sem = self.sems.at[len(self.loads) + len(stores)]
+                store = pltpu.make_async_copy(held.at[index], out.at[pl.ds(spot, size)], sem)
+                store.start()
+                stores.append(store)
+        return stores
+
+
+def inner_gradient_kernel(places, shards, local, first, info, clip, left, right, *refs):
+    parts, refs = refs[: shards - 1], refs[shards + 1 :]
+    outs, carried = refs[:2], refs[2:4]
+    rows_held, low_held, output_held, grad_held, carry_sems = refs[4:9]
+    load_sems, scaled, tile, held, store_sems = refs[9:]
+    loads = [(left, rows_held.at[0])]
+    loads += [(right.at[unit], rows_held.at[1 + unit]) for unit in range(4)]
     work = Gradients(info, clip, loads, load_sems, scaled, tile, held, store_sems)
-    for piece in range(2):
-        work.scale(5 * piece)
-        for unit in range(4):
-            spot = 4 * piece + unit
-            out = int(spot >= reduce_counts[0])
-            spot -= out * reduce_counts[0]
-            work.write(work.product(5 * piece + 1 + unit), outs[out], spot, places[out])
+    rows = grad_held.shape[2]
+    cuts = ((rows, low_held.shape[2]), (0, rows))
+    carry = Carry(info, local, first, parts, cuts, carried, low_held, carry_sems)
+    work.scale(0)
+    for unit in range(4):
+        work.write(work.product(1 + unit), outs, unit, places)
+    stores = carry.pass_on((output_held, grad_held))
     work.finish()
-
-
-def attention_gradient_kernel(shards, chunks, places, info, clip, *refs):
-    normed_a, d_qkv, d_early, mix_a, normed_b, d_query, d_mid, mix_b = refs[:8]
-    parts = refs[8 : 8 + shards * chunks]
-    refs = refs[8 + shards * chunks :]
+    for store in stores:
+        store.wait()
+
+
+def self_gradient_kernel(places, shards, local, info, clip, normed, d_qkv, d_early, mix, *refs):
+    parts, refs = refs[: shards - 1], refs[shards:]
+    outs, carried = refs[:2], refs[2:3]
+    rows_held, low_held, grad_held, carry_sems = refs[3:7]
+    load_sems, scaled, tile, held, store_sems = refs[7:]
+    sources = [normed, d_qkv.at[0], d_qkv.at[1], d_qkv.at[2], d_early, mix]
+    loads = [(source, rows_held.at[index]) for index, source in enumerate(sources)]
+    work = Gradients(info, clip, loads, load_sems, scaled, tile, held, store_sems)
+    cuts = ((0, low_held.shape[2]),)
+    carry = Carry(info, local, 0, parts, cuts, carried, low_held, carry_sems)
+    work.scale(0)
+    for unit in range(3):
+        work.write(work.product(1 + unit), outs, unit, places)
+    work.scale(4)
+    work.write(work.product(5), outs, 3, places)
+    stores = carry.pass_on((grad_held,))
+    work.finish()
+    for store in stores:
+        store.wait()
+
+
+def cross_gradient_kernel(shards, chunks, places, info, clip, *refs):
+    normed, d_query, d_mid, mix = refs[:4]
+    parts = refs[4 : 4 + shards * chunks]
+    refs = refs[4 + shards * chunks :]
     d_pair = refs[0]
-    self_out, cross_out = refs[1:3], refs[3:5]
-    rows_held, parts_held, pairs_held, memory_held = refs[5:9]
-    load_sems, scaled, tile, held, store_sems = refs[9:]
+    outs = refs[1:3]
+    rows_held, parts_held, pairs_held, memory_held = refs[3:7]
+    load_sems, scaled, tile, held, store_sems = refs[7:]
     count, memory_len = d_pair.shape[1:3]
     part_len = memory_len // shards
     group = count // chunks
-    sources = [normed_a, d_qkv.at[0], d_qkv.at[1], d_qkv.at[2], d_early, mix_a]
-    sources += [normed_b, d_query, d_mid, mix_b]
+    sources = [normed, d_query, d_mid, mix]
     loads = [(source, rows_held.at[index]) for index, source in enumerate(sources)]
     first = len(loads)
     for chunk in range(chunks):
@@ -586,14 +634,9 @@
             )
     work = Gradients(info, clip, loads, load_sems, scaled, tile, held, store_sems)
     work.scale(0)
-    for unit in range(3):
-        work.write(work.product(1 + unit), self_out, unit, places[0])
-    work.scale(4)
-    work.write(work.product(5), cross_out, 0, places[1])
-    work.scale(6)
-    work.write(work.product(7), cross_out, 1, places[1])
-    work.scale(8)
-    work.write(work.product(9), cross_out, 2, places[1])
+    work.write(work.product(1), outs, 0, places)
+    work.scale(2)
+    work.write(work.product(3), outs, 1, places)
     totals = [None, None]
     for chunk in range(chunks):
         start = first + chunk * (shards + 2)
@@ -611,7 +654,7 @@
             )
             totals[unit] = product if chunk == 0 else totals[unit] + product
     for unit in range(2):
-        work.write(totals[unit], cross_out, 3 + unit, places[1])
+        work.write(totals[unit], outs, 2 + unit, places)
     work.finish()
 
 
@@ -636,40 +679,15 @@
         for out, block in zip(outs[3 * group : 3 * group + 3], stepped):
             out[spot] = block
 
-    inside = ((2, 0), (2, 1), (2, 2), (3, 1), (3, 3), (3, 4))
+    inside = ((2, 0), (2, 1), (2, 2), (3, 0), (3, 2), (3, 3))
     for index, (piece, unit) in enumerate(inside):
         step(0, index, gradient(piece, unit), matrix_rate)
-    for index, unit in enumerate((0, 2)):
-        step(1, index, gradient(3, unit), output_rate)
+    for index, (piece, unit) in enumerate(((2, 3), (3, 1))):
+        step(1, index, gradient(piece, unit), output_rate)
     for index in range(4):
         spot = (slice(None), slice(128 * index, 128 * (index + 1)))
         step(2, spot, gradient(0, index), matrix_rate)
-        piece, unit = (1, index - 1) if index else (0, 4)
-        step(3, spot, gradient(piece, unit), matrix_rate)
-
-
-def assemble_kernel(shards, chunks, *refs):
-    refs = list(refs[1:])
-
-    def take(count):
-        taken = refs[:count]
-        del refs[:count]
-        return taken
-
-    arrived = [take(shards - 1) for _ in range(chunks)]
-    tokens_parts = take(shards - 1)
-    take(3)
-    output, tokens_grad, memory_grad = refs
-    rows = memory_grad.shape[1]
-    for index in range(shards - 1):
-        for chunk in range(chunks):
-
-            @pl.when((pl.program_id(0) == index) & (pl.program_id(1) == chunk))
-            def _(index=index, chunk=chunk):
-                tokens_grad[...] = tokens_parts[index][...].astype(wide)
-                block = arrived[chunk][index]
-                output[...] = block[:, rows:, :]
-                memory_grad[...] = block[:, :rows, :].astype(wide)
+        step(3, spot, gradient(1, index), matrix_rate)
 
 
 def swap(value, axis, bit):
@@ -743,7 +761,7 @@
     memory_len = memory_rows * shards
     group_count = tokens.shape[0]
     local = group_count // shards
-    chunks = 2 if local % 2 == 0 else 1
+    chunks = 2
     per_chunk = local // chunks
     bundle = 2 if per_chunk % 2 == 0 else 1
     steps = per_chunk // bundle
@@ -1087,109 +1105,83 @@
     def places_of(index):
         return slot_places(reduce_orders[index], True) if staged else plain_places
 
-    out_shapes = [
-        jax.ShapeDtypeStruct((slot_count // 2, count, 64, 128), narrow) for count in reduce_counts
-    ]
-
-    def gradient_call(kernel, clip, operands, outs, loads, extra, name, work):
-        return pl.pallas_call(
-            kernel,
-            in_specs=[smem, smem] + [anywhere] * len(operands),
-            out_specs=[anywhere] * 4,
-            out_shape=[shape for shape in outs for _ in range(2)],
-            scratch_shapes=extra
-            + [
-                pltpu.SemaphoreType.DMA((loads,)),
-                pltpu.VMEM((local * seq, width), narrow),
-                pltpu.VMEM((2, width, width), narrow),
-                pltpu.VMEM((8, 2, slot_count // 2, 64, 128), narrow),
-                pltpu.SemaphoreType.DMA((16,)),
-            ],
-            compiler_params=pltpu.CompilerParams(vmem_limit_bytes=vmem_bytes),
-            name=name,
-            cost_estimate=work,
-        )(kernel_info, clip, *operands)
-
-    def inner_gradients(clip):
-        kernel = functools.partial(inner_gradient_kernel, (places_of(0), places_of(1)))
-        extra = [
-            pltpu.VMEM((2, local, seq, width), narrow),
-            pltpu.VMEM((8, local, seq, width), narrow),
-        ]
-        operands = [normed_c, d_hidden, d_top, active]
-        return gradient_call(
-            kernel, clip, operands, out_shapes[:2], 10, extra, "inner_gradients", cost(9e9, 14e6)
+    out_shape = jax.ShapeDtypeStruct((slot_count // 2, 4, 64, 128), narrow)
+
+    def gradient_call(kernel, clip, operands, loads, extra, name, work, carried=()):
+        first = 2 + len(operands)
+        return tuple(
+            pl.pallas_call(
+                kernel,
+                in_specs=[smem, smem] + [anywhere] * (len(operands) + len(carried)),
+                out_specs=[anywhere] * (2 + len(carried)),
+                out_shape=[out_shape] * 2
+                + [jax.ShapeDtypeStruct(block.shape, block.dtype) for block in carried],
+                input_output_aliases={first + index: 2 + index for index in range(len(carried))},
+                scratch_shapes=extra
+                + [
+                    pltpu.SemaphoreType.DMA((loads,)),
+                    pltpu.VMEM((local * seq, width), narrow),
+                    pltpu.VMEM((2, width, width), narrow),
+                    pltpu.VMEM((4, 2, slot_count // 2, 64, 128), narrow),
+                    pltpu.SemaphoreType.DMA((8,)),
+                ],
+                compiler_params=pltpu.CompilerParams(vmem_limit_bytes=vmem_bytes),
+                name=name,
+                cost_estimate=work,
+            )(kernel_info, clip, *operands, *carried)
         )
 
-    def attention_gradients(clip):
+    def inner_gradients(index, clip, left, right, parts, carried):
         kernel = functools.partial(
-            attention_gradient_kernel, shards, chunks, (places_of(2), places_of(3))
+            inner_gradient_kernel, places_of(index), shards, local, index * per_chunk
         )
         extra = [
-            pltpu.VMEM((10, local, seq, width), narrow),
+            pltpu.VMEM((5, local, seq, width), narrow),
+            pltpu.VMEM((shards - 1, per_chunk, part_rows, width), narrow),
+            pltpu.VMEM((shards - 1, per_chunk, seq_rows, width), narrow),
+            pltpu.VMEM((shards - 1, per_chunk, memory_rows, width), wide),
+            pltpu.SemaphoreType.DMA((3 * (shards - 1),)),
+        ]
+        return gradient_call(
+            kernel,
+            clip,
+            [left, right, *parts],
+            5,
+            extra,
+            "inner_gradients",
+            cost(5e9, 7e6),
+            carried,
+        )
+
+    def self_gradients(clip, parts, carried):
+        kernel = functools.partial(self_gradient_kernel, places_of(2), shards, local)
+        extra = [
+            pltpu.VMEM((6, local, seq, width), narrow),
+            pltpu.VMEM((shards - 1, local, seq_rows, width), narrow),
+            pltpu.VMEM((shards - 1, local, seq_rows, width), wide),
+            pltpu.SemaphoreType.DMA((2 * (shards - 1),)),
+        ]
+        operands = [normed_a, d_qkv, d_early, mix_a, *parts]
+        return gradient_call(
+            kernel, clip, operands, 6, extra, "self_gradients", cost(5e9, 8e6), carried
+        )
+
+    def cross_gradients(clip):
+        kernel = functools.partial(cross_gradient_kernel, shards, chunks, places_of(3))
+        extra = [
+            pltpu.VMEM((4, local, seq, width), narrow),
             pltpu.VMEM((chunks * shards, per_chunk, memory_rows, width), narrow),
             pltpu.VMEM((2 * chunks, per_chunk, memory_len, width), narrow),
             pltpu.VMEM((chunks, per_chunk * memory_len, width), narrow),
         ]
-        operands = [normed_a, d_qkv, d_early, mix_a, normed_b, d_query_b, d_mid, mix_b]
+        operands = [normed_b, d_query_b, d_mid, mix_b]
         operands += [block for blocks in memory_parts for block in blocks] + [d_pair]
+        loads = 4 + chunks * (shards + 2)
         return gradient_call(
-            kernel,
-            clip,
-            operands,
-            out_shapes[2:],
-            10 + chunks * (shards + 2),
-            extra,
-            "attention_gradients",
-            cost(14e9, 30e6),
+            kernel, clip, operands, loads, extra, "cross_gradients", cost(9e9, 20e6)
         )
 
     tokens_arrived = [swap(block, "tensor", index + 1) for index, block in enumerate(tokens_sent)]
-
-    def by_place(shape, index, chunk=None):
-        def spot(place, step, info):
-            if chunk is not None:
-                return (0, 0, 0)
-            return (jnp.where(place == index, step, jnp.where(place < index, 0, chunks - 1)), 0, 0)
-
-        return pl.BlockSpec((per_chunk,) + shape, spot)
-
-    def to_place(shape):
-        return pl.BlockSpec(
-            (per_chunk,) + shape,
-            lambda place, step, info: ((info[2] ^ (place + 1)) * chunks + step, 0, 0),
-        )
-
-    small_rows, large_rows = (seq_rows, width), (memory_rows, width)
-    operands = [block for blocks in arrived for block in blocks] + tokens_arrived
-    assemble = pl.pallas_call(
-        functools.partial(assemble_kernel, shards, chunks),
-        grid_spec=pltpu.PrefetchScalarGridSpec(
-            num_scalar_prefetch=1,
-            grid=(shards - 1, chunks),
-            in_specs=[
-                by_place((part_rows, width), index, chunk)
-                for chunk in range(chunks)
-                for index in range(shards - 1)
-            ]
-            + [by_place(small_rows, index) for index in range(shards - 1)]
-            + [anywhere] * 3,
-            out_specs=[to_place(small_rows), to_place(small_rows), to_place(large_rows)],
-        ),
-        out_shape=[
-            jax.ShapeDtypeStruct((group_count,) + small_rows, narrow),
-            jax.ShapeDtypeStruct((group_count,) + small_rows, wide),
-            jax.ShapeDtypeStruct((group_count,) + large_rows, wide),
-        ],
-        input_output_aliases={len(operands) + 1 + index: index for index in range(3)},
-        compiler_params=pltpu.CompilerParams(
-            vmem_limit_bytes=vmem_bytes, dimension_semantics=("arbitrary", "arbitrary")
-        ),
-        name="assemble",
-        cost_estimate=cost(1e6, 20e6),
-    )
-    returned = operands + [own_output, own_tokens, own_memory]
-
     pairs = [None] * 4
 
     def travel(index, stage):
@@ -1210,14 +1202,24 @@
     def there(*indices):
         return [block for index in indices for block in pairs[index] if block is not None]
 
-    found = inner_gradients(clip_weights)
-    pairs[:2] = [tuple(found[:2]), tuple(found[2:])]
-    found = attention_gradients(after(clip_weights, *there(0, 1), *tokens_arrived))
-    pairs[2:] = [tuple(found[:2]), tuple(found[2:])]
+    clip_weights = after(clip_weights, *tokens_arrived)
+    carried = (own_output, own_memory)
+    found = inner_gradients(0, clip_weights, normed_c, d_hidden, arrived[0], carried)
+    pairs[0] = found[:2]
+    clip = after(clip_weights, *there(0))
+    found = inner_gradients(1, clip, d_top, active, arrived[1], found[2:])
+    pairs[1] = found[:2]
+    output, memory_grad = found[2:]
+    travel(0)
+    clip = after(clip_weights, *there(0, 1))
+    found = self_gradients(clip, tokens_arrived, (own_tokens,))
+    pairs[2] = found[:2]
+    tokens_grad = found[2]
+    travel(1)
+    clip = after(clip_weights, *there(1, 2))
+    pairs[3] = cross_gradients(clip)
     travel(0, 1)
     travel(2, 3)
-    travel(0, 1, 2, 3)
-    output, tokens_grad, memory_grad = assemble(after(kernel_info, *there(0)), *returned)
 
     def together(*extra):
         held = lax.optimization_barrier((pairs, extra))
@@ -1227,18 +1229,25 @@
     shrink = 1.0 / math.sqrt(group_count * replicas)
     if staged:
         small = small + swap(small, *core)
-        small = after(small, *there(2, 3))
+        (small,) = together(small)
         small = small + swap(small, *side)
-        small, output = together(small, output)
+        travel(0, 1, 2, 3)
+        (small,) = together(small)
         small = small + swap(small, *row)
         travel(0, 1, 2, 3)
         (small,) = together(small)
         small = small + swap(small, *near)
-        travel(0, 1, 2, 3)
-        (small,) = together(small)
+        last = [None] * 4
+        for index in (0, 1):
+            kept, sent = pairs[index]
+            last[index] = (kept[0], swap(sent, *reduce_orders[index][-1])[0])
+        travel(2, 3)
+        small, last = lax.optimization_barrier((small, last))
         small = small + swap(small, *far)
-        last = [swap(sent, *order[-1]) for (kept, sent), order in zip(pairs, reduce_orders)]
-        last = [block[0] for pair, came in zip(pairs, last) for block in (pair[0], came)]
+        for index in (2, 3):
+            kept, sent = pairs[index]
+            last[index] = (kept[0], swap(sent, *reduce_orders[index][-1])[0])
+        last = [block for pair in last for block in pair]
     else:
         reduced = []
         for kept, sent in pairs:
@@ -1282,10 +1291,9 @@
             count, high, across = blocks.shape
             return blocks.transpose(1, 0, 2).reshape(high, count * across)
 
-        inside = jnp.concatenate([reduced[2], reduced[3][1:2], reduced[3][3:]], 0)
-        outward = jnp.stack([reduced[3][0].T, reduced[3][2].T], 0)
-        down = jnp.concatenate([reduced[0][4:], reduced[1]], 0)
-        gradients = [inside, outward, merge(reduced[0][:4]), merge(down).T]
+        inside = jnp.concatenate([reduced[2][:3], reduced[3][:1], reduced[3][2:]], 0)
+        outward = jnp.stack([reduced[2][3].T, reduced[3][1].T], 0)
+        gradients = [inside, outward, merge(reduced[0]), merge(reduced[1]).T]
         stepped = []
         for (weight, momentum, average, rate), gradient in zip(large, gradients):
             stepped += stepper(weight, gradient, momentum, average, rate)

time: 344 us -> 347 us (level)
    pallas_call x3 -> x4, Pallas kernels: 33 us -> 35.1 us  [gradient_call(): pl.pallas_call(kernel, in_specs=[smem, smem] + [anywhere] * (len(operands...]
  transfers between devices with their start and end apart: 64 -> 64, of which waited for: 22 -> 30; matrix products, arithmetic and copies ran while one was open for 5% -> 6% of each run, Pallas kernels for 43% -> 41%
where the time goes in v4:
time: 347 us; the launch traced here: 342 us
  Pallas kernels  150 us (43%)
  waiting for transfers between devices  88.7 us (26%)
  starting transfers between devices  58.8 us (17%)
  between operations  15.8 us (5%)
  other arithmetic  14.9 us (4%)
  local copies, waits for them, and re-layouts  13.4 us (4%)
    ppermute x63, waiting for transfers between devices, swap(): lax.ppermute(value, axis, [(index, index ^ bit) for index in range(size)])  88.7 us
    pallas_call x2, Pallas kernels, cross(): pl.pallas_call(functools.partial(cross_kernel, shards, late_plans, soon_c...  71.6 us
    ppermute x63, starting transfers between devices, swap(): lax.ppermute(value, axis, [(index, index ^ bit) for index in range(size)])  58.7 us
    pallas_call x4, Pallas kernels, gradient_call(): pl.pallas_call(kernel, in_specs=[smem, smem] + [anywhere] * (len(operands...  35.1 us
    pallas_call x1, Pallas kernels, on_device(): pl.pallas_call(functools.partial(self_backward_kernel, shards, self_plans...  27.1 us
    pallas_call x1, Pallas kernels, on_device(): pl.pallas_call(functools.partial(self_forward_kernel, shards, self_plans,...  13.7 us
  transfers between devices with their start and end apart: 64, of which 30 were waited for; matrix products, arithmetic and copies ran while one was open for 6% of the time, Pallas kernels for 41%

profile of v4, /device:TPU:0, one launch (start us, length us, event | category | flops | bytes accessed | tf_op | source)
XLA Modules:
  0.0 341.8 jit_solution(10772766369082681677)
XLA Ops:
  7.3 1.1 convert_bitcast_fusion
  10.8 2.4 collective-permute-start.8
  13.9 2.2 constant_dynamic-slice_fusion.13
  16.1 1.5 collective-permute-start
  17.7 2.7 collective-permute-start.9
  21.3 2.0 constant_dynamic-slice_fusion.11.refs_6_
  25.0 1.3 collective-permute-start.15
  26.4 2.8 collective-permute-start.10
  29.8 2.8 collective-permute-done.15
  33.1 2.1 collective-permute-done.10
  35.2 1.7 collective-permute-start.11
  37.2 9.2 %collective-permute-done.11 = bf16[4,4,64,128]{3,2,1,0:T(8,128)(2,1)S(1)} collective-permute-done((bf16[4,4,64,128]{3,2,1,0:T(8,128)(2,1)S(1)}, bf16[4,4,64,128]{3,2,1,0:T(8,128)(2,1)S(1)}, u32[]{:S(2)}, u32[]{:S(2)}) %collective-permute-start.11) | collective-permute-done | bytes 262176 | tf_op jit(solution)/shard_map/ppermute | solution.py:695
  46.4 1.9 collective-permute-start.12
  48.3 1.5 collective-permute-start.17
  50.9 18.0 %collective-permute-done.17 = bf16[4,4,64,128]{3,2,1,0:T(8,128)(2,1)S(1)} collective-permute-done((bf16[4,4,64,128]{3,2,1,0:T(8,128)(2,1)S(1)}, bf16[4,4,64,128]{3,2,1,0:T(8,128)(2,1)S(1)}, u32[]{:S(2)}, u32[]{:S(2)}) %collective-permute-start.17) | collective-permute-done | bytes 262176 | tf_op jit(solution)/shard_map/ppermute | solution.py:695
  69.0 1.5 collective-permute-start.18
  72.6 2.5 collective-permute-start.2
  75.2 8.3 %collective-permute-done.18.refs_8_ = bf16[8,4,64,128]{3,2,1,0:T(8,128)(2,1)} collective-permute-done((bf16[8,4,64,128]{3,2,1,0:T(8,128)(2,1)S(1)}, bf16[8,4,64,128]{3,2,1,0:T(8,128)(2,1)}, u32[]{:S(2)}, u32[]{:S(2)}) %collective-permute-start.18) | collective-permute-done | bytes 524320 | tf_op jit(solution)/shard_map/ppermute | solution.py:695
  84.2 13.7 %self_forward.1 = (bf16[8,128,512]{2,1,0:T(8,128)(2,1)}, bf16[8,128,512]{2,1,0:T(8,128)(2,1)}, bf16[3,8,128,512]{3,2,1,0:T(8,128)(2,1)}, f32[8,2,128,512]{3,2,1,...) custom-call(s32[3]{0:T(128)} %pad_add_fusion.refs_0_.info, ...), custom_call_target="tpu_custom_call" | custom-call | flops 16000000000 | bytes 16000000 | tf_op jit(solution)/shard_map/self_forward/pallas_call | solution.py:879
  97.9 2.5 collective-permute-start.25
  101.3 35.7 %cross.2 = (bf16[32,32,512]{2,1,0:T(8,128)(2,1)}, f32[32,128,512]{2,1,0:T(8,128)}, bf16[4,160,512]{2,1,0:T(8,128)(2,1)}, bf16[4,160,512]{2,1,0:T(8,128)(2,1)}, b...) custom-call(s32[3]{0:T(128)} %pad_add_fusion.refs_0_.info, ...), custom_call_target="tpu_custom_call" | custom-call | flops 32000000000 | bytes 24000000 | tf_op jit(solution)/shard_map/cross/pallas_call | solution.py:964
  137.3 1.1 collective-permute-start.22
  140.0 36.0 %cross.3 = (bf16[32,32,512]{2,1,0:T(8,128)(2,1)}, f32[32,128,512]{2,1,0:T(8,128)}, bf16[4,160,512]{2,1,0:T(8,128)(2,1)}, bf16[4,160,512]{2,1,0:T(8,128)(2,1)}, b...) custom-call(s32[3]{0:T(128)} %pad_add_fusion.refs_0_.info, ...), custom_call_target="tpu_custom_call", output_to_operand_aliasing={{0}: (12, {}), {1}: (13, {}), {5}: (14, {}), {6}: (15, {}),... | custom-call | flops 32000000000 | bytes 24000000 | tf_op jit(solution)/shard_map/cross/pallas_call | solution.py:964
  176.6 1.1 collective-permute-start.28
  178.1 27.1 %self_backward.1 = (f32[32,32,512]{2,1,0:T(8,128)}, bf16[8,32,512]{2,1,0:T(8,128)(2,1)}, bf16[8,32,512]{2,1,0:T(8,128)(2,1)}, bf16[8,32,512]{2,1,0:T(8,128)(2,1)...) custom-call(s32[3]{0:T(128)} %pad_add_fusion.refs_0_.info, ...), custom_call_target="tpu_custom_call" | custom-call | flops 24000000000 | bytes 24000000 | tf_op jit(solution)/shard_map/self_backward/pallas_call | solution.py:1019
  205.3 1.5 collective-permute-done.29.refs_2_
  209.1 1.1 collective-permute-start.31
  211.0 1.8 collective-permute-done.31
  212.8 1.5 collective-permute-start.32
  214.4 2.1 collective-permute-done.32
  216.6 1.2 collective-permute-start.36
  218.5 1.6 collective-permute-done.33
  221.5 3.1 collective-permute-done.34
  226.4 4.3 %collective-permute-done.37.refs_2_ = bf16[8,32,512]{2,1,0:T(8,128)(2,1)S(1)} collective-permute-done((bf16[8,32,512]{2,1,0:T(8,128)(2,1)}, bf16[8,32,512]{2,1,0:T(8,128)(2,1)S(1)}, u32[]{:S(2)}, u32[]{:S(2)}) %collective-permute-start.37) | collective-permute-done | bytes 262176 | tf_op jit(solution)/shard_map/ppermute | solution.py:695
  230.7 7.7 %inner_gradients.2 = (bf16[16,4,64,128]{3,2,1,0:T(8,128)(2,1)}, bf16[16,4,64,128]{3,2,1,0:T(8,128)(2,1)}, bf16[32,32,512]{2,1,0:T(8,128)(2,1)}, f32[32,128,512]{2,1,0:T(8,128)}) custom-call(s32[3]{0:T(128)} %pad_add_fusion.refs_0_.info, f32[8]{0:T(128)} %divide_minimum_fusion.clip, ...), custom_call_target="tpu_custom_call", output_to_operand_aliasing={{2}: (7, {}), {3}: (8, {})} | custom-call | flops 5000000000 | bytes 7000000 | tf_op jit(solution)/shard_map/inner_gradients/pallas_call | solution.py:1113
  238.8 7.8 %inner_gradients.3 = (bf16[16,4,64,128]{3,2,1,0:T(8,128)(2,1)}, bf16[16,4,64,128]{3,2,1,0:T(8,128)(2,1)}, bf16[32,32,512]{2,1,0:T(8,128)(2,1)}, f32[32,128,512]{2,1,0:T(8,128)}) custom-call(s32[3]{0:T(128)} %pad_add_fusion.refs_0_.info, f32[8]{0:T(128)} %divide_minimum_fusion.clip, ...), custom_call_target="tpu_custom_call", output_to_operand_aliasing={{2}: (7, {}), {3}: (8, {})} | custom-call | flops 5000000000 | bytes 7000000 | tf_op jit(solution)/shard_map/inner_gradients/pallas_call | solution.py:1113
  247.3 1.5 collective-permute-start.39
  250.0 1.2 collective-permute-start.41
  251.2 7.2 %self_gradients.1 = (bf16[16,4,64,128]{3,2,1,0:T(8,128)(2,1)}, bf16[16,4,64,128]{3,2,1,0:T(8,128)(2,1)}, f32[32,32,512]{2,1,0:T(8,128)}) custom-call(s32[3]{0:T(128)} %pad_add_fusion.refs_0_.info, f32[8]{0:T(128)} %divide_minimum_fusion.clip, bf16[8,128,512]{2,1,0:T(8,128)(2,1)} %get-tuple-element.161.refs_3_.normed, ...), custom_call_target="tpu_custom_call", output_to_operand_aliasing={{2}: (9, {})} | custom-call | flops 5000000000 | bytes 8000000 | tf_op jit(solution)/shard_map/self_gradients/pallas_call | solution.py:1113
  258.5 12.4 %cross_gradients.1 = (bf16[16,4,64,128]{3,2,1,0:T(8,128)(2,1)}, bf16[16,4,64,128]{3,2,1,0:T(8,128)(2,1)}) custom-call(s32[3]{0:T(128)} %pad_add_fusion.refs_0_.info, f32[8]{0:T(128)} %divide_minimum_fusion.clip, bf16[8,128,512]{2,1,0:T(8,128)(2,1)} %get-tuple-element.200.refs_0_, bf16[8,128,512]{2,1,0:T(8,128)(2,1)} %get-tuple-element.201.refs_1_, ...), custom_call_target="tpu_custom_call" | custom-call | flops 8999999488 | bytes 20000000 | tf_op jit(solution)/shard_map/cross_gradients/pallas_call | solution.py:1113
  271.7 2.1 collective-permute-done.44
  275.5 2.1 collective-permute-start.45
  278.6 1.4 collective-permute-start.49
  280.6 1.7 collective-permute-done.49
  282.3 2.4 collective-permute-done.45
  284.8 5.3 %collective-permute-done.46 = bf16[4,4,64,128]{3,2,1,0:T(8,128)(2,1)S(1)} collective-permute-done((bf16[4,4,64,128]{3,2,1,0:T(8,128)(2,1)S(1)}, bf16[4,4,64,128]{3,2,1,0:T(8,128)(2,1)S(1)}, u32[]{:S(2)}, u32[]{:S(2)}) %collective-permute-start.46) | collective-permute-done | bytes 262176 | tf_op jit(solution)/shard_map/ppermute | solution.py:695
  290.1 1.4 collective-permute-done.47
  291.7 1.7 collective-permute-done.48
  293.6 1.2 collective-permute-start.50
  296.3 1.7 collective-permute-start.52
  298.0 1.1 collective-permute-start.53
  301.3 1.3 collective-permute-done.52
  302.7 1.6 collective-permute-done.53
  304.4 1.3 collective-permute-start.55
  306.4 2.3 collective-permute-start.57
  308.7 2.9 collective-permute-done.56
  311.6 1.5 collective-permute-done.57
  315.3 2.1 collective-permute-start.58
  318.0 1.3 multiply_add_fusion
  319.2 3.4 %collective-permute-done.58 = bf16[2,4,64,128]{3,2,1,0:T(8,128)(2,1)S(1)} collective-permute-done((bf16[2,4,64,128]{3,2,1,0:T(8,128)(2,1)S(1)}, bf16[2,4,64,128]{3,2,1,0:T(8,128)(2,1)S(1)}, u32[]{:S(2)}, u32[]{:S(2)}) %collective-permute-start.58) | collective-permute-done | bytes 131104 | tf_op jit(solution)/shard_map/ppermute | solution.py:695
  323.3 1.6 collective-permute-start.59
  326.3 1.3 collective-permute-done.59
  327.6 3.7 %collective-permute-done.61 = bf16[1,4,64,128]{3,2,1,0:T(8,128)(2,1)S(1)} collective-permute-done((bf16[1,4,64,128]{3,2,1,0:T(8,128)(2,1)S(1)}, bf16[1,4,64,128]{3,2,1,0:T(8,128)(2,1)S(1)}, u32[]{:S(2)}, u32[]{:S(2)}) %collective-permute-start.61) | collective-permute-done | bytes 65568 | tf_op jit(solution)/shard_map/ppermute | solution.py:695
  331.9 2.8 update.1
  (250 shorter events, 38.3 us)
Async XLA Ops:
  7.2 94.1 %all-gather.3.cloned.1.call-start = ((), (), s32[]{:S(2)}) async-start(), calls=%async_computation | async-start | bytes 4325376 | tf_op jit(solution)/shard_map/all_gather | solution.py:793
  10.8 13.7 %collective-permute-start.8 = (f32[2,128]{1,0:T(2,128)S(1)}, f32[2,128]{1,0:T(2,128)S(1)}, u32[]{:S(2)}, u32[]{:S(2)}) collective-permute-start(f32[2,128]{1,0:T(2,128)S(1)} %pad.4), channel_id=1, source_target_pairs={{0,3},{1,2},{2,1},{3,0},{4,7},{5,6},{6,5},{7,4},{8,11},{9,10},{10,... | collective-permute-start | bytes 3080 | tf_op jit(solution)/shard_map/ppermute | solution.py:695
  13.2 11.8 %collective-permute-start.7 = (f32[2,128]{1,0:T(2,128)S(1)}, f32[2,128]{1,0:T(2,128)S(1)}, u32[]{:S(2)}, u32[]{:S(2)}) collective-permute-start(f32[2,128]{1,0:T(2,128)S(1)} %pad.4), channel_id=1, source_target_pairs={{0,2},{1,3},{2,0},{3,1},{4,6},{5,7},{6,4},{7,5},{8,10},{9,11},{10,... | collective-permute-start | bytes 3080 | tf_op jit(solution)/shard_map/ppermute | solution.py:695
  13.8 12.6 %collective-permute-start.6 = (f32[2,128]{1,0:T(2,128)S(1)}, f32[2,128]{1,0:T(2,128)S(1)}, u32[]{:S(2)}, u32[]{:S(2)}) collective-permute-start(f32[2,128]{1,0:T(2,128)S(1)} %pad.4), channel_id=1, source_target_pairs={{0,1},{1,0},{2,3},{3,2},{4,5},{5,4},{6,7},{7,6},{8,9},{9,8},{10,11... | collective-permute-start | bytes 3080 | tf_op jit(solution)/shard_map/ppermute | solution.py:695
  16.1 20.8 %collective-permute-start = (bf16[8,32,512]{2,1,0:T(8,128)(2,1)}, bf16[8,32,512]{2,1,0:T(8,128)(2,1)}, u32[]{:S(2)}, u32[]{:S(2)}) collective-permute-start(bf16[8,32,512]{2,1,0:T(8,128)(2,1)} %get-tuple-element.292), channel_id=1, source_target_pairs={{0,3},{1,2},{2,1},{3,0},{4,7},{5,6},{6,5},{7,4},{8,11},{9,10},{10,... | collective-permute-start | bytes 786440 | tf_op jit(solution)/shard_map/ppermute | solution.py:695
  17.7 6.8 %collective-permute-start.9 = (bf16[1,4,64,128]{3,2,1,0:T(8,128)(2,1)S(1)}, bf16[1,4,64,128]{3,2,1,0:T(8,128)(2,1)S(1)}, u32[]{:S(2)}, u32[]{:S(2)}) collective-permute-start(bf16[1,4,64,128]{3,2,1,0:T(8,128)(2,1)S(1)} %maximum_bitcast_fusion), channel_id=1, source_target_pairs={{0,16},{4,20},{8,24},{12,28},{16,0},{20,4},{24,8},{28,12},{1,17},{... | collective-permute-start | bytes 196616 | tf_op jit(solution)/shard_map/ppermute | solution.py:695
  24.5 47.8 %collective-permute-start.4 = (bf16[8,32,512]{2,1,0:T(8,128)(2,1)S(1)}, bf16[8,32,512]{2,1,0:T(8,128)(2,1)S(1)}, u32[]{:S(2)}, u32[]{:S(2)}) collective-permute-start(bf16[8,32,512]{2,1,0:T(8,128)(2,1)S(1)} %copy-done.12), channel_id=1, source_target_pairs={{0,1},{1,0},{2,3},{3,2},{4,5},{5,4},{6,7},{7,6},{8,9},{9,8},{10,11... | collective-permute-start | bytes 786440 | tf_op jit(solution)/shard_map/ppermute | solution.py:695
  24.5 48.1 %collective-permute-start.5 = (bf16[8,32,512]{2,1,0:T(8,128)(2,1)S(1)}, bf16[8,32,512]{2,1,0:T(8,128)(2,1)S(1)}, u32[]{:S(2)}, u32[]{:S(2)}) collective-permute-start(bf16[8,32,512]{2,1,0:T(8,128)(2,1)S(1)} %copy-done.11), channel_id=1, source_target_pairs={{0,2},{1,3},{2,0},{3,1},{4,6},{5,7},{6,4},{7,5},{8,10},{9,11},{10,... | collective-permute-start | bytes 786440 | tf_op jit(solution)/shard_map/ppermute | solution.py:695
  25.0 7.6 %collective-permute-start.15 = (bf16[1,4,64,128]{3,2,1,0:T(8,128)(2,1)S(1)}, bf16[1,4,64,128]{3,2,1,0:T(8,128)(2,1)S(1)}, u32[]{:S(2)}, u32[]{:S(2)}) collective-permute-start(bf16[1,4,64,128]{3,2,1,0:T(8,128)(2,1)S(1)} %maximum_bitcast_fusion.1), channel_id=1, source_target_pairs={{0,16},{4,20},{8,24},{12,28},{16,0},{20,4},{24,8},{28,12},{1,17},{... | collective-permute-start | bytes 196616 | tf_op jit(solution)/shard_map/ppermute | solution.py:695
  26.4 8.8 %collective-permute-start.10 = (bf16[2,4,64,128]{3,2,1,0:T(8,128)(2,1)S(1)}, bf16[2,4,64,128]{3,2,1,0:T(8,128)(2,1)S(1)}, u32[]{:S(2)}, u32[]{:S(2)}) collective-permute-start(bf16[2,4,64,128]{3,2,1,0:T(8,128)(2,1)S(1)} %pad_maximum_fusion.12), channel_id=1, source_target_pairs={{0,8},{4,12},{8,0},{12,4},{16,24},{20,28},{24,16},{28,20},{1,9},{5... | collective-permute-start | bytes 393224 | tf_op jit(solution)/shard_map/ppermute | solution.py:695
  32.6 15.7 %collective-permute-start.16 = (bf16[2,4,64,128]{3,2,1,0:T(8,128)(2,1)S(1)}, bf16[2,4,64,128]{3,2,1,0:T(8,128)(2,1)S(1)}, u32[]{:S(2)}, u32[]{:S(2)}) collective-permute-start(bf16[2,4,64,128]{3,2,1,0:T(8,128)(2,1)S(1)} %pad_maximum_fusion.13), channel_id=1, source_target_pairs={{0,8},{4,12},{8,0},{12,4},{16,24},{20,28},{24,16},{28,20},{1,9},{5... | collective-permute-start | bytes 393224 | tf_op jit(solution)/shard_map/ppermute | solution.py:695
  35.2 11.1 %collective-permute-start.11 = (bf16[4,4,64,128]{3,2,1,0:T(8,128)(2,1)S(1)}, bf16[4,4,64,128]{3,2,1,0:T(8,128)(2,1)S(1)}, u32[]{:S(2)}, u32[]{:S(2)}) collective-permute-start(bf16[4,4,64,128]{3,2,1,0:T(8,128)(2,1)S(1)} %pad_maximum_fusion.10), channel_id=1, source_target_pairs={{0,2},{1,3},{2,0},{3,1},{4,6},{5,7},{6,4},{7,5},{8,10},{9,11},{10,... | collective-permute-start | bytes 786440 | tf_op jit(solution)/shard_map/ppermute | solution.py:695
  37.1 31.8 %collective-permute-start.3 = (bf16[4,160,512]{2,1,0:T(8,128)(2,1)S(1)}, bf16[4,160,512]{2,1,0:T(8,128)(2,1)S(1)}, u32[]{:S(2)}, u32[]{:S(2)}) collective-permute-start(bf16[4,160,512]{2,1,0:T(8,128)(2,1)S(1)} %pad_maximum_fusion.3), channel_id=1, source_target_pairs={{0,3},{1,2},{2,1},{3,0},{4,7},{5,6},{6,5},{7,4},{8,11},{9,10},{10,... | collective-permute-start | bytes 1966088 | tf_op jit(solution)/shard_map/ppermute | solution.py:695
  46.4 24.1 %collective-permute-start.12 = (bf16[8,4,64,128]{3,2,1,0:T(8,128)(2,1)S(1)}, bf16[8,4,64,128]{3,2,1,0:T(8,128)(2,1)S(1)}, u32[]{:S(2)}, u32[]{:S(2)}) collective-permute-start(bf16[8,4,64,128]{3,2,1,0:T(8,128)(2,1)S(1)} %pad_maximum_fusion.8.refs_9_.refs_12_), channel_id=1, source_target_pairs={{0,4},{4,0},{8,12},{12,8},{16,20},{20,16},{24,28},{28,24},{1,5},{5... | collective-permute-start | bytes 1572872 | tf_op jit(solution)/shard_map/ppermute | solution.py:695
  48.3 20.5 %collective-permute-start.17 = (bf16[4,4,64,128]{3,2,1,0:T(8,128)(2,1)S(1)}, bf16[4,4,64,128]{3,2,1,0:T(8,128)(2,1)S(1)}, u32[]{:S(2)}, u32[]{:S(2)}) collective-permute-start(bf16[4,4,64,128]{3,2,1,0:T(8,128)(2,1)S(1)} %pad_maximum_fusion.11), channel_id=1, source_target_pairs={{0,2},{1,3},{2,0},{3,1},{4,6},{5,7},{6,4},{7,5},{8,10},{9,11},{10,... | collective-permute-start | bytes 786440 | tf_op jit(solution)/shard_map/ppermute | solution.py:695
  68.9 6.3 %collective-permute-start.13 = (bf16[8,4,64,128]{3,2,1,0:T(8,128)(2,1)S(1)}, bf16[8,4,64,128]{3,2,1,0:T(8,128)(2,1)S(1)}, u32[]{:S(2)}, u32[]{:S(2)}) collective-permute-start(bf16[8,4,64,128]{3,2,1,0:T(8,128)(2,1)S(1)} %pad_maximum_fusion.8.refs_9_.refs_12_), channel_id=1, source_target_pairs={{0,1},{1,0},{2,3},{3,2},{4,5},{5,4},{6,7},{7,6},{8,9},{9,8},{10,11... | collective-permute-start | bytes 1572872 | tf_op jit(solution)/shard_map/ppermute | solution.py:695
  69.0 14.5 %collective-permute-start.18 = (bf16[8,4,64,128]{3,2,1,0:T(8,128)(2,1)S(1)}, bf16[8,4,64,128]{3,2,1,0:T(8,128)(2,1)}, u32[]{:S(2)}, u32[]{:S(2)}) collective-permute-start(bf16[8,4,64,128]{3,2,1,0:T(8,128)(2,1)S(1)} %pad_maximum_fusion.9.refs_7_), channel_id=1, source_target_pairs={{0,4},{4,0},{8,12},{12,8},{16,20},{20,16},{24,28},{28,24},{1,5},{5... | collective-permute-start | bytes 1572872 | tf_op jit(solution)/shard_map/ppermute | solution.py:695
  70.5 13.0 %collective-permute-start.14 = (bf16[8,4,64,128]{3,2,1,0:T(8,128)(2,1)S(1)}, bf16[8,4,64,128]{3,2,1,0:T(8,128)(2,1)S(1)}, u32[]{:S(2)}, u32[]{:S(2)}) collective-permute-start(bf16[8,4,64,128]{3,2,1,0:T(8,128)(2,1)S(1)} %collective-permute-done.12.refs_10_.refs_13_), channel_id=1, source_target_pairs={{0,1},{1,0},{2,3},{3,2},{4,5},{5,4},{6,7},{7,6},{8,9},{9,8},{10,11... | collective-permute-start | bytes 1572872 | tf_op jit(solution)/shard_map/ppermute | solution.py:695
  72.3 25.6 %collective-permute-start.1 = (bf16[4,160,512]{2,1,0:T(8,128)(2,1)S(1)}, bf16[4,160,512]{2,1,0:T(8,128)(2,1)S(1)}, u32[]{:S(2)}, u32[]{:S(2)}) collective-permute-start(bf16[4,160,512]{2,1,0:T(8,128)(2,1)S(1)} %pad_maximum_fusion.1), channel_id=1, source_target_pairs={{0,1},{1,0},{2,3},{3,2},{4,5},{5,4},{6,7},{7,6},{8,9},{9,8},{10,11... | collective-permute-start | bytes 1966088 | tf_op jit(solution)/shard_map/ppermute | solution.py:695
  72.6 27.9 %collective-permute-start.2 = (bf16[4,160,512]{2,1,0:T(8,128)(2,1)S(1)}, bf16[4,160,512]{2,1,0:T(8,128)(2,1)S(1)}, u32[]{:S(2)}, u32[]{:S(2)}) collective-permute-start(bf16[4,160,512]{2,1,0:T(8,128)(2,1)S(1)} %pad_maximum_fusion.2), channel_id=1, source_target_pairs={{0,2},{1,3},{2,0},{3,1},{4,6},{5,7},{6,4},{7,5},{8,10},{9,11},{10,... | collective-permute-start | bytes 1966088 | tf_op jit(solution)/shard_map/ppermute | solution.py:695
  75.1 25.6 %collective-permute-start.19 = (bf16[8,4,64,128]{3,2,1,0:T(8,128)(2,1)S(1)}, bf16[8,4,64,128]{3,2,1,0:T(8,128)(2,1)}, u32[]{:S(2)}, u32[]{:S(2)}) collective-permute-start(bf16[8,4,64,128]{3,2,1,0:T(8,128)(2,1)S(1)} %pad_maximum_fusion.9.refs_7_), channel_id=1, source_target_pairs={{0,1},{1,0},{2,3},{3,2},{4,5},{5,4},{6,7},{7,6},{8,9},{9,8},{10,11... | collective-permute-start | bytes 1572872 | tf_op jit(solution)/shard_map/ppermute | solution.py:695
  83.5 55.0 %collective-permute-start.24 = (bf16[4,160,512]{2,1,0:T(8,128)(2,1)S(1)}, bf16[4,160,512]{2,1,0:T(8,128)(2,1)}, u32[]{:S(2)}, u32[]{:S(2)}) collective-permute-start(bf16[4,160,512]{2,1,0:T(8,128)(2,1)S(1)} %pad_maximum_fusion.5), channel_id=1, source_target_pairs={{0,1},{1,0},{2,3},{3,2},{4,5},{5,4},{6,7},{7,6},{8,9},{9,8},{10,11... | collective-permute-start | bytes 1966088 | tf_op jit(solution)/shard_map/ppermute | solution.py:695
  83.5 17.9 %collective-permute-start.20 = (bf16[8,4,64,128]{3,2,1,0:T(8,128)(2,1)}, bf16[8,4,64,128]{3,2,1,0:T(8,128)(2,1)}, u32[]{:S(2)}, u32[]{:S(2)}) collective-permute-start(bf16[8,4,64,128]{3,2,1,0:T(8,128)(2,1)} %collective-permute-done.18.refs_8_), channel_id=1, source_target_pairs={{0,1},{1,0},{2,3},{3,2},{4,5},{5,4},{6,7},{7,6},{8,9},{9,8},{10,11... | collective-permute-start | bytes 1572872 | tf_op jit(solution)/shard_map/ppermute | solution.py:695
  97.9 41.0 %collective-permute-start.25 = (bf16[4,160,512]{2,1,0:T(8,128)(2,1)S(1)}, bf16[4,160,512]{2,1,0:T(8,128)(2,1)S(1)}, u32[]{:S(2)}, u32[]{:S(2)}) collective-permute-start(bf16[4,160,512]{2,1,0:T(8,128)(2,1)S(1)} %pad_maximum_fusion.6), channel_id=1, source_target_pairs={{0,2},{1,3},{2,0},{3,1},{4,6},{5,7},{6,4},{7,5},{8,10},{9,11},{10,... | collective-permute-start | bytes 1966088 | tf_op jit(solution)/shard_map/ppermute | solution.py:695
  100.5 38.5 %collective-permute-start.26 = (bf16[4,160,512]{2,1,0:T(8,128)(2,1)S(1)}, bf16[4,160,512]{2,1,0:T(8,128)(2,1)S(1)}, u32[]{:S(2)}, u32[]{:S(2)}) collective-permute-start(bf16[4,160,512]{2,1,0:T(8,128)(2,1)S(1)} %pad_maximum_fusion.7), channel_id=1, source_target_pairs={{0,3},{1,2},{2,1},{3,0},{4,7},{5,6},{6,5},{7,4},{8,11},{9,10},{10,... | collective-permute-start | bytes 1966088 | tf_op jit(solution)/shard_map/ppermute | solution.py:695
  137.0 40.7 %collective-permute-start.21 = (bf16[4,160,512]{2,1,0:T(8,128)(2,1)}, bf16[4,160,512]{2,1,0:T(8,128)(2,1)S(1)}, u32[]{:S(2)}, u32[]{:S(2)}) collective-permute-start(bf16[4,160,512]{2,1,0:T(8,128)(2,1)} %get-tuple-element.139), channel_id=1, source_target_pairs={{0,1},{1,0},{2,3},{3,2},{4,5},{5,4},{6,7},{7,6},{8,9},{9,8},{10,11... | collective-permute-start | bytes 1966088 | tf_op jit(solution)/shard_map/ppermute | solution.py:695
  137.3 40.7 %collective-permute-start.22 = (bf16[4,160,512]{2,1,0:T(8,128)(2,1)}, bf16[4,160,512]{2,1,0:T(8,128)(2,1)S(1)}, u32[]{:S(2)}, u32[]{:S(2)}) collective-permute-start(bf16[4,160,512]{2,1,0:T(8,128)(2,1)} %get-tuple-element.140), channel_id=1, source_target_pairs={{0,2},{1,3},{2,0},{3,1},{4,6},{5,7},{6,4},{7,5},{8,10},{9,11},{10,... | collective-permute-start | bytes 1966088 | tf_op jit(solution)/shard_map/ppermute | solution.py:695
  138.5 39.6 %collective-permute-start.23 = (bf16[4,160,512]{2,1,0:T(8,128)(2,1)}, bf16[4,160,512]{2,1,0:T(8,128)(2,1)S(1)}, u32[]{:S(2)}, u32[]{:S(2)}) collective-permute-start(bf16[4,160,512]{2,1,0:T(8,128)(2,1)} %get-tuple-element.141), channel_id=1, source_target_pairs={{0,3},{1,2},{2,1},{3,0},{4,7},{5,6},{6,5},{7,4},{8,11},{9,10},{10,... | collective-permute-start | bytes 1966088 | tf_op jit(solution)/shard_map/ppermute | solution.py:695
  176.0 29.2 %collective-permute-start.27 = (bf16[4,160,512]{2,1,0:T(8,128)(2,1)}, bf16[4,160,512]{2,1,0:T(8,128)(2,1)S(1)}, u32[]{:S(2)}, u32[]{:S(2)}) collective-permute-start(bf16[4,160,512]{2,1,0:T(8,128)(2,1)} %get-tuple-element.169), channel_id=1, source_target_pairs={{0,1},{1,0},{2,3},{3,2},{4,5},{5,4},{6,7},{7,6},{8,9},{9,8},{10,11... | collective-permute-start | bytes 1966088 | tf_op jit(solution)/shard_map/ppermute | solution.py:695
  176.6 28.6 %collective-permute-start.28 = (bf16[4,160,512]{2,1,0:T(8,128)(2,1)}, bf16[4,160,512]{2,1,0:T(8,128)(2,1)S(1)}, u32[]{:S(2)}, u32[]{:S(2)}) collective-permute-start(bf16[4,160,512]{2,1,0:T(8,128)(2,1)} %get-tuple-element.170), channel_id=1, source_target_pairs={{0,2},{1,3},{2,0},{3,1},{4,6},{5,7},{6,4},{7,5},{8,10},{9,11},{10,... | collective-permute-start | bytes 1966088 | tf_op jit(solution)/shard_map/ppermute | solution.py:695
  177.8 29.0 %collective-permute-start.29 = (bf16[4,160,512]{2,1,0:T(8,128)(2,1)}, bf16[4,160,512]{2,1,0:T(8,128)(2,1)S(1)}, u32[]{:S(2)}, u32[]{:S(2)}) collective-permute-start(bf16[4,160,512]{2,1,0:T(8,128)(2,1)} %get-tuple-element.171), channel_id=1, source_target_pairs={{0,3},{1,2},{2,1},{3,0},{4,7},{5,6},{6,5},{7,4},{8,11},{9,10},{10,... | collective-permute-start | bytes 1966088 | tf_op jit(solution)/shard_map/ppermute | solution.py:695
  206.7 1.7 collective-permute-start.30
  209.1 3.7 %collective-permute-start.31 = (f32[16,128]{1,0:T(8,128)S(1)}, f32[16,128]{1,0:T(8,128)S(1)}, u32[]{:S(2)}, u32[]{:S(2)}) collective-permute-start(f32[16,128]{1,0:T(8,128)S(1)} %pad_maximum_fusion.17), channel_id=1, source_target_pairs={{0,2},{1,3},{2,0},{3,1},{4,6},{5,7},{6,4},{7,5},{8,10},{9,11},{10,... | collective-permute-start | bytes 24584 | tf_op jit(solution)/shard_map/ppermute | solution.py:695
  212.8 3.7 %collective-permute-start.32 = (f32[8,128]{1,0:T(8,128)S(1)}, f32[8,128]{1,0:T(8,128)S(1)}, u32[]{:S(2)}, u32[]{:S(2)}) collective-permute-start(f32[8,128]{1,0:T(8,128)S(1)} %broadcast_in_dim.8), channel_id=1, source_target_pairs={{0,4},{4,0},{8,12},{12,8},{16,20},{20,16},{24,28},{28,24},{1,5},{5... | collective-permute-start | bytes 12296 | tf_op jit(solution)/shard_map/ppermute | solution.py:695
  216.5 3.6 %collective-permute-start.33 = (f32[8,128]{1,0:T(8,128)S(1)}, f32[8,128]{1,0:T(8,128)S(1)}, u32[]{:S(2)}, u32[]{:S(2)}) collective-permute-start(f32[8,128]{1,0:T(8,128)S(1)} %broadcast_add_fusion), channel_id=1, source_target_pairs={{0,8},{4,12},{8,0},{12,4},{16,24},{20,28},{24,16},{28,20},{1,9},{5... | collective-permute-start | bytes 12296 | tf_op jit(solution)/shard_map/ppermute | solution.py:695
  216.6 9.8 %collective-permute-start.35 = (bf16[8,32,512]{2,1,0:T(8,128)(2,1)}, bf16[8,32,512]{2,1,0:T(8,128)(2,1)S(1)}, u32[]{:S(2)}, u32[]{:S(2)}) collective-permute-start(bf16[8,32,512]{2,1,0:T(8,128)(2,1)} %get-tuple-element.173), channel_id=1, source_target_pairs={{0,1},{1,0},{2,3},{3,2},{4,5},{5,4},{6,7},{7,6},{8,9},{9,8},{10,11... | collective-permute-start | bytes 786440 | tf_op jit(solution)/shard_map/ppermute | solution.py:695
  216.6 9.8 %collective-permute-start.36 = (bf16[8,32,512]{2,1,0:T(8,128)(2,1)}, bf16[8,32,512]{2,1,0:T(8,128)(2,1)S(1)}, u32[]{:S(2)}, u32[]{:S(2)}) collective-permute-start(bf16[8,32,512]{2,1,0:T(8,128)(2,1)} %get-tuple-element.174), channel_id=1, source_target_pairs={{0,2},{1,3},{2,0},{3,1},{4,6},{5,7},{6,4},{7,5},{8,10},{9,11},{10,... | collective-permute-start | bytes 786440 | tf_op jit(solution)/shard_map/ppermute | solution.py:695
  217.8 12.9 %collective-permute-start.37 = (bf16[8,32,512]{2,1,0:T(8,128)(2,1)}, bf16[8,32,512]{2,1,0:T(8,128)(2,1)S(1)}, u32[]{:S(2)}, u32[]{:S(2)}) collective-permute-start(bf16[8,32,512]{2,1,0:T(8,128)(2,1)} %get-tuple-element.175), channel_id=1, source_target_pairs={{0,3},{1,2},{2,1},{3,0},{4,7},{5,6},{6,5},{7,4},{8,11},{9,10},{10,... | collective-permute-start | bytes 786440 | tf_op jit(solution)/shard_map/ppermute | solution.py:695
  220.1 4.5 %collective-permute-start.34 = (f32[8,128]{1,0:T(8,128)S(1)}, f32[8,128]{1,0:T(8,128)S(1)}, u32[]{:S(2)}, u32[]{:S(2)}) collective-permute-start(f32[8,128]{1,0:T(8,128)S(1)} %fusion.11), channel_id=1, source_target_pairs={{0,16},{4,20},{8,24},{12,28},{16,0},{20,4},{24,8},{28,12},{1,17},{... | collective-permute-start | bytes 12296 | tf_op jit(solution)/shard_map/ppermute | solution.py:695
  238.5 8.5 %collective-permute-start.38 = (bf16[16,4,64,128]{3,2,1,0:T(8,128)(2,1)}, bf16[16,4,64,128]{3,2,1,0:T(8,128)(2,1)S(1)}, u32[]{:S(2)}, u32[]{:S(2)}) collective-permute-start(bf16[16,4,64,128]{3,2,1,0:T(8,128)(2,1)} %get-tuple-element.182), channel_id=1, source_target_pairs={{0,1},{1,0},{2,3},{3,2},{4,5},{5,4},{6,7},{7,6},{8,9},{9,8},{10,11... | collective-permute-start | bytes 3145736 | tf_op jit(solution)/shard_map/ppermute | solution.py:695
  246.6 2.9 collective-permute-start.40
  247.3 26.4 %collective-permute-start.39 = (bf16[8,4,64,128]{3,2,1,0:T(8,128)(2,1)S(1)}, bf16[8,4,64,128]{3,2,1,0:T(8,128)(2,1)S(1)}, u32[]{:S(2)}, u32[]{:S(2)}) collective-permute-start(bf16[8,4,64,128]{3,2,1,0:T(8,128)(2,1)S(1)} %get-tuple-element.272), channel_id=1, source_target_pairs={{0,4},{4,0},{8,12},{12,8},{16,20},{20,16},{24,28},{28,24},{1,5},{5... | collective-permute-start | bytes 1572872 | tf_op jit(solution)/shard_map/ppermute | solution.py:695
  250.0 23.9 %collective-permute-start.41 = (bf16[8,4,64,128]{3,2,1,0:T(8,128)(2,1)S(1)}, bf16[8,4,64,128]{3,2,1,0:T(8,128)(2,1)S(1)}, u32[]{:S(2)}, u32[]{:S(2)}) collective-permute-start(bf16[8,4,64,128]{3,2,1,0:T(8,128)(2,1)S(1)} %get-tuple-element.271), channel_id=1, source_target_pairs={{0,2},{1,3},{2,0},{3,1},{4,6},{5,7},{6,4},{7,5},{8,10},{9,11},{10,... | collective-permute-start | bytes 1572872 | tf_op jit(solution)/shard_map/ppermute | solution.py:695
  258.4 15.7 %collective-permute-start.42 = (bf16[16,4,64,128]{3,2,1,0:T(8,128)(2,1)}, bf16[16,4,64,128]{3,2,1,0:T(8,128)(2,1)S(1)}, u32[]{:S(2)}, u32[]{:S(2)}) collective-permute-start(bf16[16,4,64,128]{3,2,1,0:T(8,128)(2,1)} %get-tuple-element.198), channel_id=1, source_target_pairs={{0,1},{1,0},{2,3},{3,2},{4,5},{5,4},{6,7},{7,6},{8,9},{9,8},{10,11... | collective-permute-start | bytes 3145736 | tf_op jit(solution)/shard_map/ppermute | solution.py:695
  270.9 3.6 %collective-permute-start.43 = (bf16[16,4,64,128]{3,2,1,0:T(8,128)(2,1)}, bf16[16,4,64,128]{3,2,1,0:T(8,128)(2,1)S(1)}, u32[]{:S(2)}, u32[]{:S(2)}) collective-permute-start(bf16[16,4,64,128]{3,2,1,0:T(8,128)(2,1)} %get-tuple-element.206), channel_id=1, source_target_pairs={{0,1},{1,0},{2,3},{3,2},{4,5},{5,4},{6,7},{7,6},{8,9},{9,8},{10,11... | collective-permute-start | bytes 3145736 | tf_op jit(solution)/shard_map/ppermute | solution.py:695
  271.6 2.2 collective-permute-start.44
  275.5 9.2 %collective-permute-start.45 = (bf16[4,4,64,128]{3,2,1,0:T(8,128)(2,1)S(1)}, bf16[4,4,64,128]{3,2,1,0:T(8,128)(2,1)S(1)}, u32[]{:S(2)}, u32[]{:S(2)}) collective-permute-start(bf16[4,4,64,128]{3,2,1,0:T(8,128)(2,1)S(1)} %get-tuple-element.209), channel_id=1, source_target_pairs={{0,8},{4,12},{8,0},{12,4},{16,24},{20,28},{24,16},{28,20},{1,9},{5... | collective-permute-start | bytes 786440 | tf_op jit(solution)/shard_map/ppermute | solution.py:695
  277.6 13.9 %collective-permute-start.47 = (bf16[8,4,64,128]{3,2,1,0:T(8,128)(2,1)S(1)}, bf16[8,4,64,128]{3,2,1,0:T(8,128)(2,1)S(1)}, u32[]{:S(2)}, u32[]{:S(2)}) collective-permute-start(bf16[8,4,64,128]{3,2,1,0:T(8,128)(2,1)S(1)} %get-tuple-element.213), channel_id=1, source_target_pairs={{0,2},{1,3},{2,0},{3,1},{4,6},{5,7},{6,4},{7,5},{8,10},{9,11},{10,... | collective-permute-start | bytes 1572872 | tf_op jit(solution)/shard_map/ppermute | solution.py:695
  278.5 11.5 %collective-permute-start.46 = (bf16[4,4,64,128]{3,2,1,0:T(8,128)(2,1)S(1)}, bf16[4,4,64,128]{3,2,1,0:T(8,128)(2,1)S(1)}, u32[]{:S(2)}, u32[]{:S(2)}) collective-permute-start(bf16[4,4,64,128]{3,2,1,0:T(8,128)(2,1)S(1)} %get-tuple-element.211), channel_id=1, source_target_pairs={{0,8},{4,12},{8,0},{12,4},{16,24},{20,28},{24,16},{28,20},{1,9},{5... | collective-permute-start | bytes 786440 | tf_op jit(solution)/shard_map/ppermute | solution.py:695
  278.6 3.7 %collective-permute-start.49 = (f32[14,128]{1,0:T(8,128)S(1)}, f32[14,128]{1,0:T(8,128)S(1)}, u32[]{:S(2)}, u32[]{:S(2)}) collective-permute-start(f32[14,128]{1,0:T(8,128)S(1)} %bitcast_add_fusion), channel_id=1, source_target_pairs={{0,4},{4,0},{8,12},{12,8},{16,20},{20,16},{24,28},{28,24},{1,5},{5... | collective-permute-start | bytes 21512 | tf_op jit(solution)/shard_map/ppermute | solution.py:695
  280.0 13.4 %collective-permute-start.48 = (bf16[8,4,64,128]{3,2,1,0:T(8,128)(2,1)S(1)}, bf16[8,4,64,128]{3,2,1,0:T(8,128)(2,1)S(1)}, u32[]{:S(2)}, u32[]{:S(2)}) collective-permute-start(bf16[8,4,64,128]{3,2,1,0:T(8,128)(2,1)S(1)} %get-tuple-element.215), channel_id=1, source_target_pairs={{0,4},{4,0},{8,12},{12,8},{16,20},{20,16},{24,28},{28,24},{1,5},{5... | collective-permute-start | bytes 1572872 | tf_op jit(solution)/shard_map/ppermute | solution.py:695
  293.6 6.1 %collective-permute-start.50 = (bf16[2,4,64,128]{3,2,1,0:T(8,128)(2,1)S(1)}, bf16[2,4,64,128]{3,2,1,0:T(8,128)(2,1)S(1)}, u32[]{:S(2)}, u32[]{:S(2)}) collective-permute-start(bf16[2,4,64,128]{3,2,1,0:T(8,128)(2,1)S(1)} %get-tuple-element.218), channel_id=1, source_target_pairs={{0,2},{1,3},{2,0},{3,1},{4,6},{5,7},{6,4},{7,5},{8,10},{9,11},{10,... | collective-permute-start | bytes 393224 | tf_op jit(solution)/shard_map/ppermute | solution.py:695
  294.8 4.9 %collective-permute-start.54 = (f32[14,128]{1,0:T(8,128)S(1)}, f32[14,128]{1,0:T(8,128)S(1)}, u32[]{:S(2)}, u32[]{:S(2)}) collective-permute-start(f32[14,128]{1,0:T(8,128)S(1)} %add.253), channel_id=1, source_target_pairs={{0,2},{1,3},{2,0},{3,1},{4,6},{5,7},{6,4},{7,5},{8,10},{9,11},{10,... | collective-permute-start | bytes 21512 | tf_op jit(solution)/shard_map/ppermute | solution.py:695
  295.7 5.0 %collective-permute-start.51 = (bf16[2,4,64,128]{3,2,1,0:T(8,128)(2,1)S(1)}, bf16[2,4,64,128]{3,2,1,0:T(8,128)(2,1)S(1)}, u32[]{:S(2)}, u32[]{:S(2)}) collective-permute-start(bf16[2,4,64,128]{3,2,1,0:T(8,128)(2,1)S(1)} %get-tuple-element.220), channel_id=1, source_target_pairs={{0,4},{4,0},{8,12},{12,8},{16,20},{20,16},{24,28},{28,24},{1,5},{5... | collective-permute-start | bytes 393224 | tf_op jit(solution)/shard_map/ppermute | solution.py:695
  296.3 6.4 %collective-permute-start.52 = (bf16[4,4,64,128]{3,2,1,0:T(8,128)(2,1)S(1)}, bf16[4,4,64,128]{3,2,1,0:T(8,128)(2,1)S(1)}, u32[]{:S(2)}, u32[]{:S(2)}) collective-permute-start(bf16[4,4,64,128]{3,2,1,0:T(8,128)(2,1)S(1)} %get-tuple-element.222), channel_id=1, source_target_pairs={{0,8},{4,12},{8,0},{12,4},{16,24},{20,28},{24,16},{28,20},{1,9},{5... | collective-permute-start | bytes 786440 | tf_op jit(solution)/shard_map/ppermute | solution.py:695
  298.0 6.4 %collective-permute-start.53 = (bf16[4,4,64,128]{3,2,1,0:T(8,128)(2,1)S(1)}, bf16[4,4,64,128]{3,2,1,0:T(8,128)(2,1)S(1)}, u32[]{:S(2)}, u32[]{:S(2)}) collective-permute-start(bf16[4,4,64,128]{3,2,1,0:T(8,128)(2,1)S(1)} %get-tuple-element.224), channel_id=1, source_target_pairs={{0,2},{1,3},{2,0},{3,1},{4,6},{5,7},{6,4},{7,5},{8,10},{9,11},{10,... | collective-permute-start | bytes 786440 | tf_op jit(solution)/shard_map/ppermute | solution.py:695
  304.4 4.2 %collective-permute-start.55 = (f32[14,128]{1,0:T(8,128)S(1)}, f32[14,128]{1,0:T(8,128)S(1)}, u32[]{:S(2)}, u32[]{:S(2)}) collective-permute-start(f32[14,128]{1,0:T(8,128)S(1)} %add.262), channel_id=1, source_target_pairs={{0,8},{4,12},{8,0},{12,4},{16,24},{20,28},{24,16},{28,20},{1,9},{5... | collective-permute-start | bytes 21512 | tf_op jit(solution)/shard_map/ppermute | solution.py:695
  305.7 5.9 %collective-permute-start.56 = (bf16[1,4,64,128]{3,2,1,0:T(8,128)(2,1)S(1)}, bf16[1,4,64,128]{3,2,1,0:T(8,128)(2,1)S(1)}, u32[]{:S(2)}, u32[]{:S(2)}) collective-permute-start(bf16[1,4,64,128]{3,2,1,0:T(8,128)(2,1)S(1)} %get-tuple-element.228), channel_id=1, source_target_pairs={{0,16},{4,20},{8,24},{12,28},{16,0},{20,4},{24,8},{28,12},{1,17},{... | collective-permute-start | bytes 196616 | tf_op jit(solution)/shard_map/ppermute | solution.py:695
  306.4 6.7 %collective-permute-start.57 = (bf16[1,4,64,128]{3,2,1,0:T(8,128)(2,1)S(1)}, bf16[1,4,64,128]{3,2,1,0:T(8,128)(2,1)S(1)}, u32[]{:S(2)}, u32[]{:S(2)}) collective-permute-start(bf16[1,4,64,128]{3,2,1,0:T(8,128)(2,1)S(1)} %get-tuple-element.230), channel_id=1, source_target_pairs={{0,16},{4,20},{8,24},{12,28},{16,0},{20,4},{24,8},{28,12},{1,17},{... | collective-permute-start | bytes 196616 | tf_op jit(solution)/shard_map/ppermute | solution.py:695
  313.1 4.8 %collective-permute-start.62 = (f32[14,128]{1,0:T(8,128)S(1)}, f32[14,128]{1,0:T(8,128)S(1)}, u32[]{:S(2)}, u32[]{:S(2)}) collective-permute-start(f32[14,128]{1,0:T(8,128)S(1)} %add.263), channel_id=1, source_target_pairs={{0,16},{4,20},{8,24},{12,28},{16,0},{20,4},{24,8},{28,12},{1,17},{... | collective-permute-start | bytes 21512 | tf_op jit(solution)/shard_map/ppermute | solution.py:695
  315.3 7.4 %collective-permute-start.58 = (bf16[2,4,64,128]{3,2,1,0:T(8,128)(2,1)S(1)}, bf16[2,4,64,128]{3,2,1,0:T(8,128)(2,1)S(1)}, u32[]{:S(2)}, u32[]{:S(2)}) collective-permute-start(bf16[2,4,64,128]{3,2,1,0:T(8,128)(2,1)S(1)} %get-tuple-element.236), channel_id=1, source_target_pairs={{0,16},{4,20},{8,24},{12,28},{16,0},{20,4},{24,8},{28,12},{1,17},{... | collective-permute-start | bytes 393224 | tf_op jit(solution)/shard_map/ppermute | solution.py:695
  317.4 7.5 %collective-permute-start.60 = (bf16[2,4,64,128]{3,2,1,0:T(8,128)(2,1)S(1)}, bf16[2,4,64,128]{3,2,1,0:T(8,128)(2,1)S(1)}, u32[]{:S(2)}, u32[]{:S(2)}) collective-permute-start(bf16[2,4,64,128]{3,2,1,0:T(8,128)(2,1)S(1)} %get-tuple-element.238), channel_id=1, source_target_pairs={{0,8},{4,12},{8,0},{12,4},{16,24},{20,28},{24,16},{28,20},{1,9},{5... | collective-permute-start | bytes 393224 | tf_op jit(solution)/shard_map/ppermute | solution.py:695
  323.3 4.3 %collective-permute-start.59 = (bf16[1,4,64,128]{3,2,1,0:T(8,128)(2,1)S(1)}, bf16[1,4,64,128]{3,2,1,0:T(8,128)(2,1)S(1)}, u32[]{:S(2)}, u32[]{:S(2)}) collective-permute-start(bf16[1,4,64,128]{3,2,1,0:T(8,128)(2,1)S(1)} %get-tuple-element.304), channel_id=1, source_target_pairs={{0,4},{4,0},{8,12},{12,8},{16,20},{20,16},{24,28},{28,24},{1,5},{5... | collective-permute-start | bytes 196616 | tf_op jit(solution)/shard_map/ppermute | solution.py:695
  325.6 5.7 %collective-permute-start.61 = (bf16[1,4,64,128]{3,2,1,0:T(8,128)(2,1)S(1)}, bf16[1,4,64,128]{3,2,1,0:T(8,128)(2,1)S(1)}, u32[]{:S(2)}, u32[]{:S(2)}) collective-permute-start(bf16[1,4,64,128]{3,2,1,0:T(8,128)(2,1)S(1)} %get-tuple-element.302), channel_id=1, source_target_pairs={{0,16},{4,20},{8,24},{12,28},{16,0},{20,4},{24,8},{28,12},{1,17},{... | collective-permute-start | bytes 196616 | tf_op jit(solution)/shard_map/ppermute | solution.py:695
  (47 other events, 715.0 us)
Sparse Core Ops, SparseCore 0:
  11.5 68.3 all-gather.2

commit v5 on v4

--- a/solution.py
+++ b/solution.py
@@ -542,72 +542,30 @@
             copy.wait()
 
 
-class Carry:
-    def __init__(self, info, count, first, parts, cuts, outs, low, sems):
-        self.low, self.sems, self.cuts, self.outs = low, sems, cuts, outs
-        self.spots = [
-            (info[2] ^ (index + 1)) * count + first for index in range(len(parts))
-        ]
-        self.loads = [
-            pltpu.make_async_copy(part, low.at[index], sems.at[index])
-            for index, part in enumerate(parts)
-        ]
-        for load in self.loads:
-            load.start()
-
-    def pass_on(self, helds):
-        stores = []
-        size = self.low.shape[1]
-        for index, (load, spot) in enumerate(zip(self.loads, self.spots)):
-            load.wait()
-            for (start, stop), out, held in zip(self.cuts, self.outs, helds):
-                held[index] = self.low[index, :, start:stop, :].astype(held.dtype)
-                sem = self.sems.at[len(self.loads) + len(stores)]
-                store = pltpu.make_async_copy(held.at[index], out.at[pl.ds(spot, size)], sem)
-                store.start()
-                stores.append(store)
-        return stores
-
-
-def inner_gradient_kernel(places, shards, local, first, info, clip, left, right, *refs):
-    parts, refs = refs[: shards - 1], refs[shards + 1 :]
-    outs, carried = refs[:2], refs[2:4]
-    rows_held, low_held, output_held, grad_held, carry_sems = refs[4:9]
-    load_sems, scaled, tile, held, store_sems = refs[9:]
+def inner_gradient_kernel(places, info, clip, left, right, *refs):
+    outs = refs[:2]
+    rows_held, load_sems, scaled, tile, held, store_sems = refs[2:]
     loads = [(left, rows_held.at[0])]
     loads += [(right.at[unit], rows_held.at[1 + unit]) for unit in range(4)]
     work = Gradients(info, clip, loads, load_sems, scaled, tile, held, store_sems)
-    rows = grad_held.shape[2]
-    cuts = ((rows, low_held.shape[2]), (0, rows))
-    carry = Carry(info, local, first, parts, cuts, carried, low_held, carry_sems)
     work.scale(0)
     for unit in range(4):
         work.write(work.product(1 + unit), outs, unit, places)
-    stores = carry.pass_on((output_held, grad_held))
     work.finish()
-    for store in stores:
-        store.wait()
-
-
-def self_gradient_kernel(places, shards, local, info, clip, normed, d_qkv, d_early, mix, *refs):
-    parts, refs = refs[: shards - 1], refs[shards:]
-    outs, carried = refs[:2], refs[2:3]
-    rows_held, low_held, grad_held, carry_sems = refs[3:7]
-    load_sems, scaled, tile, held, store_sems = refs[7:]
+
+
+def self_gradient_kernel(places, info, clip, normed, d_qkv, d_early, mix, *refs):
+    outs = refs[:2]
+    rows_held, load_sems, scaled, tile, held, store_sems = refs[2:]
     sources = [normed, d_qkv.at[0], d_qkv.at[1], d_qkv.at[2], d_early, mix]
     loads = [(source, rows_held.at[index]) for index, source in enumerate(sources)]
     work = Gradients(info, clip, loads, load_sems, scaled, tile, held, store_sems)
-    cuts = ((0, low_held.shape[2]),)
-    carry = Carry(info, local, 0, parts, cuts, carried, low_held, carry_sems)
     work.scale(0)
     for unit in range(3):
         work.write(work.product(1 + unit), outs, unit, places)
     work.scale(4)
     work.write(work.product(5), outs, 3, places)
-    stores = carry.pass_on((grad_held,))
     work.finish()
-    for store in stores:
-        store.wait()
 
 
 def cross_gradient_kernel(shards, chunks, places, info, clip, *refs):
@@ -690,6 +648,30 @@
         step(3, spot, gradient(1, index), matrix_rate)
 
 
+def assemble_kernel(shards, chunks, *refs):
+    refs = list(refs[1:])
+
+    def take(count):
+        taken = refs[:count]
+        del refs[:count]
+        return taken
+
+    arrived = [take(shards - 1) for _ in range(chunks)]
+    tokens_parts = take(shards - 1)
+    take(3)
+    output, tokens_grad, memory_grad = refs
+    rows = memory_grad.shape[1]
+    for index in range(shards - 1):
+        for chunk in range(chunks):
+
+            @pl.when((pl.program_id(0) == index) & (pl.program_id(1) == chunk))
+            def _(index=index, chunk=chunk):
+                tokens_grad[...] = tokens_parts[index][...].astype(wide)
+                block = arrived[chunk][index]
+                output[...] = block[:, rows:, :]
+                memory_grad[...] = block[:, :rows, :].astype(wide)
+
+
 def swap(value, axis, bit):
     size = lax.axis_size(axis)
     return lax.ppermute(value, axis, [(index, index ^ bit) for index in range(size)])
@@ -761,7 +743,7 @@
     memory_len = memory_rows * shards
     group_count = tokens.shape[0]
     local = group_count // shards
-    chunks = 2
+    chunks = 2 if local % 2 == 0 else 1
     per_chunk = local // chunks
     bundle = 2 if per_chunk % 2 == 0 else 1
     steps = per_chunk // bundle
@@ -1107,16 +1089,13 @@
 
     out_shape = jax.ShapeDtypeStruct((slot_count // 2, 4, 64, 128), narrow)
 
-    def gradient_call(kernel, clip, operands, loads, extra, name, work, carried=()):
-        first = 2 + len(operands)
+    def gradient_call(kernel, clip, operands, loads, extra, name, work):
         return tuple(
             pl.pallas_call(
                 kernel,
-                in_specs=[smem, smem] + [anywhere] * (len(operands) + len(carried)),
-                out_specs=[anywhere] * (2 + len(carried)),
-                out_shape=[out_shape] * 2
-                + [jax.ShapeDtypeStruct(block.shape, block.dtype) for block in carried],
-                input_output_aliases={first + index: 2 + index for index in range(len(carried))},
+                in_specs=[smem, smem] + [anywhere] * len(operands),
+                out_specs=[anywhere] * 2,
+                out_shape=[out_shape] * 2,
                 scratch_shapes=extra
                 + [
                     pltpu.SemaphoreType.DMA((loads,)),
@@ -1128,43 +1107,21 @@
                 compiler_params=pltpu.CompilerParams(vmem_limit_bytes=vmem_bytes),
                 name=name,
                 cost_estimate=work,
-            )(kernel_info, clip, *operands, *carried)
+            )(kernel_info, clip, *operands)
         )
 
-    def inner_gradients(index, clip, left, right, parts, carried):
-        kernel = functools.partial(
-            inner_gradient_kernel, places_of(index), shards, local, index * per_chunk
+    def inner_gradients(index, clip, left, right):
+        kernel = functools.partial(inner_gradient_kernel, places_of(index))
+        extra = [pltpu.VMEM((5, local, seq, width), narrow)]
+        return gradient_call(
+            kernel, clip, [left, right], 5, extra, "inner_gradients", cost(5e9, 7e6)
         )
-        extra = [
-            pltpu.VMEM((5, local, seq, width), narrow),
-            pltpu.VMEM((shards - 1, per_chunk, part_rows, width), narrow),
-            pltpu.VMEM((shards - 1, per_chunk, seq_rows, width), narrow),
-            pltpu.VMEM((shards - 1, per_chunk, memory_rows, width), wide),
-            pltpu.SemaphoreType.DMA((3 * (shards - 1),)),
-        ]
-        return gradient_call(
-            kernel,
-            clip,
-            [left, right, *parts],
-            5,
-            extra,
-            "inner_gradients",
-            cost(5e9, 7e6),
-            carried,
-        )
-
-    def self_gradients(clip, parts, carried):
-        kernel = functools.partial(self_gradient_kernel, places_of(2), shards, local)
-        extra = [
-            pltpu.VMEM((6, local, seq, width), narrow),
-            pltpu.VMEM((shards - 1, local, seq_rows, width), narrow),
-            pltpu.VMEM((shards - 1, local, seq_rows, width), wide),
-            pltpu.SemaphoreType.DMA((2 * (shards - 1),)),
-        ]
-        operands = [normed_a, d_qkv, d_early, mix_a, *parts]
-        return gradient_call(
-            kernel, clip, operands, 6, extra, "self_gradients", cost(5e9, 8e6), carried
-        )
+
+    def self_gradients(clip):
+        kernel = functools.partial(self_gradient_kernel, places_of(2))
+        extra = [pltpu.VMEM((6, local, seq, width), narrow)]
+        operands = [normed_a, d_qkv, d_early, mix_a]
+        return gradient_call(kernel, clip, operands, 6, extra, "self_gradients", cost(5e9, 8e6))
 
     def cross_gradients(clip):
         kernel = functools.partial(cross_gradient_kernel, shards, chunks, places_of(3))
@@ -1182,11 +1139,52 @@
         )
 
     tokens_arrived = [swap(block, "tensor", index + 1) for index, block in enumerate(tokens_sent)]
+
+    def by_place(shape, index, chunk=None):
+        def spot(place, step, info):
+            if chunk is not None:
+                return (0, 0, 0)
+            return (jnp.where(place == index, step, jnp.where(place < index, 0, chunks - 1)), 0, 0)
+
+        return pl.BlockSpec((per_chunk,) + shape, spot)
+
+    def to_place(shape):
+        return pl.BlockSpec(
+            (per_chunk,) + shape,
+            lambda place, step, info: ((info[2] ^ (place + 1)) * chunks + step, 0, 0),
+        )
+
+    small_rows, large_rows = (seq_rows, width), (memory_rows, width)
+    operands = [block for blocks in arrived for block in blocks] + tokens_arrived
+    assemble = pl.pallas_call(
+        functools.partial(assemble_kernel, shards, chunks),
+        grid_spec=pltpu.PrefetchScalarGridSpec(
+            num_scalar_prefetch=1,
+            grid=(shards - 1, chunks),
+            in_specs=[
+                by_place((part_rows, width), index, chunk)
+                for chunk in range(chunks)
+                for index in range(shards - 1)
+            ]
+            + [by_place(small_rows, index) for index in range(shards - 1)]
+            + [anywhere] * 3,
+            out_specs=[to_place(small_rows), to_place(small_rows), to_place(large_rows)],
+        ),
+        out_shape=[
+            jax.ShapeDtypeStruct((group_count,) + small_rows, narrow),
+            jax.ShapeDtypeStruct((group_count,) + small_rows, wide),
+            jax.ShapeDtypeStruct((group_count,) + large_rows, wide),
+        ],
+        input_output_aliases={len(operands) + 1 + index: index for index in range(3)},
+        compiler_params=pltpu.CompilerParams(
+            vmem_limit_bytes=vmem_bytes, dimension_semantics=("arbitrary", "arbitrary")
+        ),
+        name="assemble",
+        cost_estimate=cost(1e6, 20e6),
+    )
+    returned = operands + [own_output, own_tokens, own_memory]
+
     pairs = [None] * 4
-
-    def travel(index, stage):
-        kept, sent = pairs[index]
-        pairs[index] = add_stage(kept, swap(sent, *reduce_orders[index][stage]))
 
     last_stage = len(reduce_orders[0]) - 1
     done = [0] * 4
@@ -1199,24 +1197,28 @@
                 pairs[index] = add_stage(kept, swap(sent, *order))
                 done[index] += 1
 
+    def arrive_as_one(*indices):
+        (stage,) = {reduce_orders[index][done[index]] for index in indices}
+        sents = [pairs[index][1] for index in indices]
+        came = swap(jnp.concatenate(sents, 0), *stage)
+        found, start = [], 0
+        for index, sent in zip(indices, sents):
+            found.append(came[start : start + sent.shape[0]])
+            start += sent.shape[0]
+            done[index] += 1
+        return found
+
     def there(*indices):
         return [block for index in indices for block in pairs[index] if block is not None]
 
-    clip_weights = after(clip_weights, *tokens_arrived)
-    carried = (own_output, own_memory)
-    found = inner_gradients(0, clip_weights, normed_c, d_hidden, arrived[0], carried)
-    pairs[0] = found[:2]
+    pairs[0] = inner_gradients(0, clip_weights, normed_c, d_hidden)
     clip = after(clip_weights, *there(0))
-    found = inner_gradients(1, clip, d_top, active, arrived[1], found[2:])
-    pairs[1] = found[:2]
-    output, memory_grad = found[2:]
+    pairs[1] = inner_gradients(1, clip, d_top, active)
     travel(0)
     clip = after(clip_weights, *there(0, 1))
-    found = self_gradients(clip, tokens_arrived, (own_tokens,))
-    pairs[2] = found[:2]
-    tokens_grad = found[2]
+    pairs[2] = self_gradients(clip)
     travel(1)
-    clip = after(clip_weights, *there(1, 2))
+    clip = after(clip_weights, *there(1, 2), *tokens_arrived)
     pairs[3] = cross_gradients(clip)
     travel(0, 1)
     travel(2, 3)
@@ -1225,6 +1227,9 @@
         held = lax.optimization_barrier((pairs, extra))
         pairs[:] = held[0]
         return held[1]
+
+    def assembled():
+        return assemble(after(kernel_info, *there(0)), *returned)
 
     shrink = 1.0 / math.sqrt(group_count * replicas)
     if staged:
@@ -1232,16 +1237,20 @@
         (small,) = together(small)
         small = small + swap(small, *side)
         travel(0, 1, 2, 3)
-        (small,) = together(small)
+        output, tokens_grad, memory_grad = assembled()
+        small, output = together(small, output)
         small = small + swap(small, *row)
-        travel(0, 1, 2, 3)
+        for index, came in zip((0, 3), arrive_as_one(0, 3)):
+            pairs[index] = add_stage(pairs[index][0], came)
+        travel(1, 2)
         (small,) = together(small)
         small = small + swap(small, *near)
         last = [None] * 4
+        came = arrive_as_one(0, 1, 2)
         for index in (0, 1):
-            kept, sent = pairs[index]
-            last[index] = (kept[0], swap(sent, *reduce_orders[index][-1])[0])
-        travel(2, 3)
+            last[index] = (pairs[index][0][0], came[index][0])
+        pairs[2] = add_stage(pairs[2][0], came[2])
+        travel(3)
         small, last = lax.optimization_barrier((small, last))
         small = small + swap(small, *far)
         for index in (2, 3):
@@ -1249,6 +1258,7 @@
             last[index] = (kept[0], swap(sent, *reduce_orders[index][-1])[0])
         last = [block for pair in last for block in pair]
     else:
+        output, tokens_grad, memory_grad = assembled()
         reduced = []
         for kept, sent in pairs:
             whole = jnp.concatenate([kept, sent], 0)

time: 347 us -> 342 us (0.986)
  starting transfers between devices: 58.8 us -> 51.7 us
  Pallas kernels: 150 us -> 155 us
  waiting for transfers between devices: 88.7 us -> 84.8 us
    ppermute x63 -> x60, starting transfers between devices: 58.7 us -> 51.7 us  [swap(): lax.ppermute(value, axis, [(index, index ^ bit) for index in range(size)])]
    pallas_call x4 -> x5, Pallas kernels: 35.1 us -> 39.8 us  [the longest x4 32.1 us: gradient_call(): pl.pallas_call(kernel, in_specs=[smem, smem] + [anywhere] * len(operands)...]
    ppermute x63 -> x60, waiting for transfers between devices: 88.7 us -> 84.8 us  [swap(): lax.ppermute(value, axis, [(index, index ^ bit) for index in range(size)])]
  transfers between devices with their start and end apart: 64 -> 61, of which waited for: 30 -> 24; matrix products, arithmetic and copies ran while one was open for 6% -> 6% of each run, Pallas kernels for 41% -> 43%
where the time goes in v5:
time: 342 us; the launch traced here: 336 us
  Pallas kernels  155 us (45%)
  waiting for transfers between devices  84.8 us (25%)
  starting transfers between devices  51.7 us (15%)
  between operations  15.9 us (5%)
  other arithmetic  15.1 us (4%)
  local copies, waits for them, and re-layouts  13.8 us (4%)
    ppermute x60, waiting for transfers between devices, swap(): lax.ppermute(value, axis, [(index, index ^ bit) for index in range(size)])  84.8 us
    pallas_call x2, Pallas kernels, cross(): pl.pallas_call(functools.partial(cross_kernel, shards, late_plans, soon_c...  71.7 us
    ppermute x60, starting transfers between devices, swap(): lax.ppermute(value, axis, [(index, index ^ bit) for index in range(size)])  51.7 us
    pallas_call x4, Pallas kernels, gradient_call(): pl.pallas_call(kernel, in_specs=[smem, smem] + [anywhere] * len(operands)...  32.1 us
    pallas_call x1, Pallas kernels, on_device(): pl.pallas_call(functools.partial(self_backward_kernel, shards, self_plans...  27.1 us
    pallas_call x1, Pallas kernels, on_device(): pl.pallas_call(functools.partial(self_forward_kernel, shards, self_plans,...  13.7 us
    pallas_call x1, Pallas kernels, assembled(): return assemble(after(kernel_info, *there(0)), *returned)  7.69 us
  transfers between devices with their start and end apart: 61, of which 24 were waited for; matrix products, arithmetic and copies ran while one was open for 6% of the time, Pallas kernels for 43%

profile of v5, /device:TPU:0, one launch (start us, length us, event | category | flops | bytes accessed | tf_op | source)
XLA Modules:
  0.0 336.3 jit_solution(17392882746905351721)
XLA Ops:
  7.3 1.1 convert_bitcast_fusion
  8.4 0.9 convert_element_type.305
  10.8 2.4 collective-permute-start.8
  13.9 2.2 constant_dynamic-slice_fusion.13
  16.1 1.5 collective-permute-start
  17.7 2.7 collective-permute-start.9
  21.2 2.0 constant_dynamic-slice_fusion.11.refs_6_
  25.0 1.3 collective-permute-start.15
  26.4 2.8 collective-permute-start.10
  29.8 2.8 collective-permute-done.15
  33.2 2.0 collective-permute-done.10
  35.2 1.7 collective-permute-start.11
  37.2 9.1 %collective-permute-done.11 = bf16[4,4,64,128]{3,2,1,0:T(8,128)(2,1)S(1)} collective-permute-done((bf16[4,4,64,128]{3,2,1,0:T(8,128)(2,1)S(1)}, bf16[4,4,64,128]{3,2,1,0:T(8,128)(2,1)S(1)}, u32[]{:S(2)}, u32[]{:S(2)}) %collective-permute-start.11) | collective-permute-done | bytes 262176 | tf_op jit(solution)/shard_map/ppermute | solution.py:677
  46.4 1.9 collective-permute-start.12
  48.3 1.5 collective-permute-start.17
  50.9 18.0 %collective-permute-done.17 = bf16[4,4,64,128]{3,2,1,0:T(8,128)(2,1)S(1)} collective-permute-done((bf16[4,4,64,128]{3,2,1,0:T(8,128)(2,1)S(1)}, bf16[4,4,64,128]{3,2,1,0:T(8,128)(2,1)S(1)}, u32[]{:S(2)}, u32[]{:S(2)}) %collective-permute-start.17) | collective-permute-done | bytes 262176 | tf_op jit(solution)/shard_map/ppermute | solution.py:677
  68.9 1.5 collective-permute-start.18
  71.2 0.9 pad_maximum_fusion.4.refs_1_.refs_8_
  72.6 2.5 collective-permute-start.2
  75.2 8.2 %collective-permute-done.18.refs_8_ = bf16[8,4,64,128]{3,2,1,0:T(8,128)(2,1)} collective-permute-done((bf16[8,4,64,128]{3,2,1,0:T(8,128)(2,1)S(1)}, bf16[8,4,64,128]{3,2,1,0:T(8,128)(2,1)}, u32[]{:S(2)}, u32[]{:S(2)}) %collective-permute-start.18) | collective-permute-done | bytes 524320 | tf_op jit(solution)/shard_map/ppermute | solution.py:677
  84.3 13.7 %self_forward.1 = (bf16[8,128,512]{2,1,0:T(8,128)(2,1)}, bf16[8,128,512]{2,1,0:T(8,128)(2,1)}, bf16[3,8,128,512]{3,2,1,0:T(8,128)(2,1)}, f32[8,2,128,512]{3,2,1,...) custom-call(s32[3]{0:T(128)} %pad_add_fusion.refs_0_.info, ...), custom_call_target="tpu_custom_call" | custom-call | flops 16000000000 | bytes 16000000 | tf_op jit(solution)/shard_map/self_forward/pallas_call | solution.py:861
  98.0 2.5 collective-permute-start.25
  102.2 35.7 %cross.2 = (bf16[32,32,512]{2,1,0:T(8,128)(2,1)}, f32[32,128,512]{2,1,0:T(8,128)}, bf16[4,160,512]{2,1,0:T(8,128)(2,1)}, bf16[4,160,512]{2,1,0:T(8,128)(2,1)}, b...) custom-call(s32[3]{0:T(128)} %pad_add_fusion.refs_0_.info, ...), custom_call_target="tpu_custom_call" | custom-call | flops 32000000000 | bytes 24000000 | tf_op jit(solution)/shard_map/cross/pallas_call | solution.py:946
  138.1 1.1 collective-permute-start.22
  139.8 36.0 %cross.3 = (bf16[32,32,512]{2,1,0:T(8,128)(2,1)}, f32[32,128,512]{2,1,0:T(8,128)}, bf16[4,160,512]{2,1,0:T(8,128)(2,1)}, bf16[4,160,512]{2,1,0:T(8,128)(2,1)}, b...) custom-call(s32[3]{0:T(128)} %pad_add_fusion.refs_0_.info, ...), custom_call_target="tpu_custom_call", output_to_operand_aliasing={{0}: (12, {}), {1}: (13, {}), {5}: (14, {}), {6}: (15, {}),... | custom-call | flops 32000000000 | bytes 24000000 | tf_op jit(solution)/shard_map/cross/pallas_call | solution.py:946
  176.4 1.1 collective-permute-start.28
  177.9 27.1 %self_backward.1 = (f32[32,32,512]{2,1,0:T(8,128)}, bf16[8,32,512]{2,1,0:T(8,128)(2,1)}, bf16[8,32,512]{2,1,0:T(8,128)(2,1)}, bf16[8,32,512]{2,1,0:T(8,128)(2,1)...) custom-call(s32[3]{0:T(128)} %pad_add_fusion.refs_0_.info, ...), custom_call_target="tpu_custom_call" | custom-call | flops 24000000000 | bytes 24000000 | tf_op jit(solution)/shard_map/self_backward/pallas_call | solution.py:1001
  205.0 1.6 collective-permute-done.29.refs_6_
  207.3 1.0 collective-permute-done.30
  209.0 1.1 collective-permute-start.31
  210.8 1.9 collective-permute-done.31
  212.7 1.5 collective-permute-start.32
  214.3 2.1 collective-permute-done.32
  216.5 3.5 %collective-permute-done.33 = f32[8,128]{1,0:T(8,128)S(1)} collective-permute-done((f32[8,128]{1,0:T(8,128)S(1)}, f32[8,128]{1,0:T(8,128)S(1)}, u32[]{:S(2)}, u32[]{:S(2)}) %collective-permute-start.33) | collective-permute-done | bytes 4128 | tf_op jit(solution)/shard_map/ppermute | solution.py:677
  221.4 3.1 collective-permute-done.34
  226.2 6.5 %inner_gradients.2 = (bf16[16,4,64,128]{3,2,1,0:T(8,128)(2,1)}, bf16[16,4,64,128]{3,2,1,0:T(8,128)(2,1)}) custom-call(s32[3]{0:T(128)} %pad_add_fusion.refs_0_.info, f32[8]{0:T(128)} %divide_minimum_fusion.clip, bf16[8,128,512]{2,1,0:T(8,128)(2,1)} %get-tuple-element.172.left, bf16[4,8,128,512]{3,2,1,0:T(8,128)(2,1)} %get-tuple-element.173.right), custom_call_target="tpu_custom_call" | custom-call | flops 5000000000 | bytes 7000000 | tf_op jit(solution)/shard_map/inner_gradients/pallas_call | solution.py:1094
  232.8 6.6 %inner_gradients.3 = (bf16[16,4,64,128]{3,2,1,0:T(8,128)(2,1)}, bf16[16,4,64,128]{3,2,1,0:T(8,128)(2,1)}) custom-call(s32[3]{0:T(128)} %pad_add_fusion.refs_0_.info, f32[8]{0:T(128)} %divide_minimum_fusion.clip, bf16[8,128,512]{2,1,0:T(8,128)(2,1)} %get-tuple-element.177.left, bf16[4,8,128,512]{3,2,1,0:T(8,128)(2,1)} %get-tuple-element.178.right), custom_call_target="tpu_custom_call" | custom-call | flops 5000000000 | bytes 7000000 | tf_op jit(solution)/shard_map/inner_gradients/pallas_call | solution.py:1094
  240.1 1.1 collective-permute-start.41
  242.3 1.5 collective-permute-start.36
  244.3 1.1 collective-permute-start.38
  245.4 6.7 %self_gradients.1 = (bf16[16,4,64,128]{3,2,1,0:T(8,128)(2,1)}, bf16[16,4,64,128]{3,2,1,0:T(8,128)(2,1)}) custom-call(s32[3]{0:T(128)} %pad_add_fusion.refs_0_.info, f32[8]{0:T(128)} %divide_minimum_fusion.clip, bf16[8,128,512]{2,1,0:T(8,128)(2,1)} %get-tuple-element.160.refs_3_.normed, bf16[3,8,128,512]{3,2,1,0:T(8,128)(2,1)} %get-tuple-element.182.d_qkv, ...), custom_call_target="tpu_custom_call" | custom-call | flops 5000000000 | bytes 8000000 | tf_op jit(solution)/shard_map/self_gradients/pallas_call | solution.py:1094
  252.2 1.7 collective-permute-done.42.refs_9_
  253.9 12.3 %cross_gradients.1 = (bf16[16,4,64,128]{3,2,1,0:T(8,128)(2,1)}, bf16[16,4,64,128]{3,2,1,0:T(8,128)(2,1)}) custom-call(s32[3]{0:T(128)} %pad_add_fusion.refs_0_.info, f32[8]{0:T(128)} %divide_minimum_fusion.clip, bf16[8,128,512]{2,1,0:T(8,128)(2,1)} %get-tuple-element.190.refs_0_, bf16[8,128,512]{2,1,0:T(8,128)(2,1)} %get-tuple-element.191.refs_1_, ...), custom_call_target="tpu_custom_call" | custom-call | flops 8999999488 | bytes 20000000 | tf_op jit(solution)/shard_map/cross_gradients/pallas_call | solution.py:1094
  266.3 1.1 collective-permute-start.43
  267.6 2.1 collective-permute-done.44
  271.6 1.1 collective-permute-start.47
  272.7 1.9 collective-permute-start.46
  274.7 1.4 collective-permute-start.49
  276.7 1.7 collective-permute-done.49
  278.4 2.3 collective-permute-done.45
  280.8 7.7 %assemble.1 = (bf16[32,32,512]{2,1,0:T(8,128)(2,1)}, f32[32,32,512]{2,1,0:T(8,128)}, f32[32,128,512]{2,1,0:T(8,128)}) custom-call(s32[3]{0:T(128)} %pad_add_fusion.refs_0_.info, bf16[4,160,512]{2,1,0:T(8,128)(2,1)} %copy-done.9, bf16[4,160,512]{2,1,0:T(8,128)(2,1)} %copy-done.10, ...), custom_call_target="tpu_custom_call", output_to_operand_aliasing={{0}: (10, {}), {1}: (11, {}), {2}: (12, {})} | custom-call | flops 1000000 | bytes 20000000 | tf_op jit(solution)/shard_map/assemble/pallas_call | solution.py:1232
  289.5 1.0 collective-permute-start.51
  290.5 1.1 collective-permute-start.53
  291.7 1.0 collective-permute-start.50
  292.7 1.6 collective-permute-done.53
  295.1 2.2 collective-permute-done.52
  297.5 4.0 %collective-permute-done.50 = bf16[6,4,64,128]{3,2,1,0:T(8,128)(2,1)S(1)} collective-permute-done((bf16[6,4,64,128]{3,2,1,0:T(8,128)(2,1)S(1)}, bf16[6,4,64,128]{3,2,1,0:T(8,128)(2,1)S(1)}, u32[]{:S(2)}, u32[]{:S(2)}) %collective-permute-start.50) | collective-permute-done | bytes 393248 | tf_op jit(solution)/shard_map/ppermute | solution.py:677
  302.2 1.6 collective-permute-start.54
  304.3 1.1 collective-permute-start.55
  306.9 3.0 collective-permute-done.57
  310.9 7.7 %collective-permute-done.55 = bf16[4,4,64,128]{3,2,1,0:T(8,128)(2,1)S(1)} collective-permute-done((bf16[4,4,64,128]{3,2,1,0:T(8,128)(2,1)S(1)}, bf16[4,4,64,128]{3,2,1,0:T(8,128)(2,1)S(1)}, u32[]{:S(2)}, u32[]{:S(2)}) %collective-permute-start.55) | collective-permute-done | bytes 262176 | tf_op jit(solution)/shard_map/ppermute | solution.py:677
  319.9 3.9 %collective-permute-done.59 = f32[14,128]{1,0:T(8,128)S(1)} collective-permute-done((f32[14,128]{1,0:T(8,128)S(1)}, f32[14,128]{1,0:T(8,128)S(1)}, u32[]{:S(2)}, u32[]{:S(2)}) %collective-permute-start.59) | collective-permute-done | bytes 7200 | tf_op jit(solution)/shard_map/ppermute | solution.py:677
  323.8 1.3 multiply_add_fusion
  326.4 2.8 update.1
  (246 shorter events, 31.3 us)
Async XLA Ops:
  7.2 94.1 %all-gather.3.cloned.1.call-start = ((), (), s32[]{:S(2)}) async-start(), calls=%async_computation | async-start | bytes 4325376 | tf_op jit(solution)/shard_map/all_gather | solution.py:775
  10.8 13.7 %collective-permute-start.8 = (f32[2,128]{1,0:T(2,128)S(1)}, f32[2,128]{1,0:T(2,128)S(1)}, u32[]{:S(2)}, u32[]{:S(2)}) collective-permute-start(f32[2,128]{1,0:T(2,128)S(1)} %pad.4), channel_id=1, source_target_pairs={{0,3},{1,2},{2,1},{3,0},{4,7},{5,6},{6,5},{7,4},{8,11},{9,10},{10,... | collective-permute-start | bytes 3080 | tf_op jit(solution)/shard_map/ppermute | solution.py:677
  13.2 11.8 %collective-permute-start.7 = (f32[2,128]{1,0:T(2,128)S(1)}, f32[2,128]{1,0:T(2,128)S(1)}, u32[]{:S(2)}, u32[]{:S(2)}) collective-permute-start(f32[2,128]{1,0:T(2,128)S(1)} %pad.4), channel_id=1, source_target_pairs={{0,2},{1,3},{2,0},{3,1},{4,6},{5,7},{6,4},{7,5},{8,10},{9,11},{10,... | collective-permute-start | bytes 3080 | tf_op jit(solution)/shard_map/ppermute | solution.py:677
  13.8 12.6 %collective-permute-start.6 = (f32[2,128]{1,0:T(2,128)S(1)}, f32[2,128]{1,0:T(2,128)S(1)}, u32[]{:S(2)}, u32[]{:S(2)}) collective-permute-start(f32[2,128]{1,0:T(2,128)S(1)} %pad.4), channel_id=1, source_target_pairs={{0,1},{1,0},{2,3},{3,2},{4,5},{5,4},{6,7},{7,6},{8,9},{9,8},{10,11... | collective-permute-start | bytes 3080 | tf_op jit(solution)/shard_map/ppermute | solution.py:677
  16.1 20.8 %collective-permute-start = (bf16[8,32,512]{2,1,0:T(8,128)(2,1)}, bf16[8,32,512]{2,1,0:T(8,128)(2,1)}, u32[]{:S(2)}, u32[]{:S(2)}) collective-permute-start(bf16[8,32,512]{2,1,0:T(8,128)(2,1)} %get-tuple-element.290), channel_id=1, source_target_pairs={{0,3},{1,2},{2,1},{3,0},{4,7},{5,6},{6,5},{7,4},{8,11},{9,10},{10,... | collective-permute-start | bytes 786440 | tf_op jit(solution)/shard_map/ppermute | solution.py:677
  17.7 6.8 %collective-permute-start.9 = (bf16[1,4,64,128]{3,2,1,0:T(8,128)(2,1)S(1)}, bf16[1,4,64,128]{3,2,1,0:T(8,128)(2,1)S(1)}, u32[]{:S(2)}, u32[]{:S(2)}) collective-permute-start(bf16[1,4,64,128]{3,2,1,0:T(8,128)(2,1)S(1)} %maximum_bitcast_fusion), channel_id=1, source_target_pairs={{0,16},{4,20},{8,24},{12,28},{16,0},{20,4},{24,8},{28,12},{1,17},{... | collective-permute-start | bytes 196616 | tf_op jit(solution)/shard_map/ppermute | solution.py:677
  24.5 47.8 %collective-permute-start.4 = (bf16[8,32,512]{2,1,0:T(8,128)(2,1)S(1)}, bf16[8,32,512]{2,1,0:T(8,128)(2,1)S(1)}, u32[]{:S(2)}, u32[]{:S(2)}) collective-permute-start(bf16[8,32,512]{2,1,0:T(8,128)(2,1)S(1)} %copy-done.20), channel_id=1, source_target_pairs={{0,1},{1,0},{2,3},{3,2},{4,5},{5,4},{6,7},{7,6},{8,9},{9,8},{10,11... | collective-permute-start | bytes 786440 | tf_op jit(solution)/shard_map/ppermute | solution.py:677
  24.5 48.1 %collective-permute-start.5 = (bf16[8,32,512]{2,1,0:T(8,128)(2,1)S(1)}, bf16[8,32,512]{2,1,0:T(8,128)(2,1)S(1)}, u32[]{:S(2)}, u32[]{:S(2)}) collective-permute-start(bf16[8,32,512]{2,1,0:T(8,128)(2,1)S(1)} %copy-done.19), channel_id=1, source_target_pairs={{0,2},{1,3},{2,0},{3,1},{4,6},{5,7},{6,4},{7,5},{8,10},{9,11},{10,... | collective-permute-start | bytes 786440 | tf_op jit(solution)/shard_map/ppermute | solution.py:677
  25.0 7.5 %collective-permute-start.15 = (bf16[1,4,64,128]{3,2,1,0:T(8,128)(2,1)S(1)}, bf16[1,4,64,128]{3,2,1,0:T(8,128)(2,1)S(1)}, u32[]{:S(2)}, u32[]{:S(2)}) collective-permute-start(bf16[1,4,64,128]{3,2,1,0:T(8,128)(2,1)S(1)} %maximum_bitcast_fusion.1), channel_id=1, source_target_pairs={{0,16},{4,20},{8,24},{12,28},{16,0},{20,4},{24,8},{28,12},{1,17},{... | collective-permute-start | bytes 196616 | tf_op jit(solution)/shard_map/ppermute | solution.py:677
  26.4 8.8 %collective-permute-start.10 = (bf16[2,4,64,128]{3,2,1,0:T(8,128)(2,1)S(1)}, bf16[2,4,64,128]{3,2,1,0:T(8,128)(2,1)S(1)}, u32[]{:S(2)}, u32[]{:S(2)}) collective-permute-start(bf16[2,4,64,128]{3,2,1,0:T(8,128)(2,1)S(1)} %pad_maximum_fusion.14), channel_id=1, source_target_pairs={{0,8},{4,12},{8,0},{12,4},{16,24},{20,28},{24,16},{28,20},{1,9},{5... | collective-permute-start | bytes 393224 | tf_op jit(solution)/shard_map/ppermute | solution.py:677
  32.6 15.7 %collective-permute-start.16 = (bf16[2,4,64,128]{3,2,1,0:T(8,128)(2,1)S(1)}, bf16[2,4,64,128]{3,2,1,0:T(8,128)(2,1)S(1)}, u32[]{:S(2)}, u32[]{:S(2)}) collective-permute-start(bf16[2,4,64,128]{3,2,1,0:T(8,128)(2,1)S(1)} %pad_maximum_fusion.15), channel_id=1, source_target_pairs={{0,8},{4,12},{8,0},{12,4},{16,24},{20,28},{24,16},{28,20},{1,9},{5... | collective-permute-start | bytes 393224 | tf_op jit(solution)/shard_map/ppermute | solution.py:677
  35.2 11.1 %collective-permute-start.11 = (bf16[4,4,64,128]{3,2,1,0:T(8,128)(2,1)S(1)}, bf16[4,4,64,128]{3,2,1,0:T(8,128)(2,1)S(1)}, u32[]{:S(2)}, u32[]{:S(2)}) collective-permute-start(bf16[4,4,64,128]{3,2,1,0:T(8,128)(2,1)S(1)} %pad_maximum_fusion.11), channel_id=1, source_target_pairs={{0,2},{1,3},{2,0},{3,1},{4,6},{5,7},{6,4},{7,5},{8,10},{9,11},{10,... | collective-permute-start | bytes 786440 | tf_op jit(solution)/shard_map/ppermute | solution.py:677
  37.1 31.8 %collective-permute-start.3 = (bf16[4,160,512]{2,1,0:T(8,128)(2,1)S(1)}, bf16[4,160,512]{2,1,0:T(8,128)(2,1)S(1)}, u32[]{:S(2)}, u32[]{:S(2)}) collective-permute-start(bf16[4,160,512]{2,1,0:T(8,128)(2,1)S(1)} %pad_maximum_fusion.3), channel_id=1, source_target_pairs={{0,3},{1,2},{2,1},{3,0},{4,7},{5,6},{6,5},{7,4},{8,11},{9,10},{10,... | collective-permute-start | bytes 1966088 | tf_op jit(solution)/shard_map/ppermute | solution.py:677
  46.4 24.0 %collective-permute-start.12 = (bf16[8,4,64,128]{3,2,1,0:T(8,128)(2,1)S(1)}, bf16[8,4,64,128]{3,2,1,0:T(8,128)(2,1)S(1)}, u32[]{:S(2)}, u32[]{:S(2)}) collective-permute-start(bf16[8,4,64,128]{3,2,1,0:T(8,128)(2,1)S(1)} %pad_maximum_fusion.8.refs_9_.refs_12_), channel_id=1, source_target_pairs={{0,4},{4,0},{8,12},{12,8},{16,20},{20,16},{24,28},{28,24},{1,5},{5... | collective-permute-start | bytes 1572872 | tf_op jit(solution)/shard_map/ppermute | solution.py:677
  48.3 20.5 %collective-permute-start.17 = (bf16[4,4,64,128]{3,2,1,0:T(8,128)(2,1)S(1)}, bf16[4,4,64,128]{3,2,1,0:T(8,128)(2,1)S(1)}, u32[]{:S(2)}, u32[]{:S(2)}) collective-permute-start(bf16[4,4,64,128]{3,2,1,0:T(8,128)(2,1)S(1)} %pad_maximum_fusion.12), channel_id=1, source_target_pairs={{0,2},{1,3},{2,0},{3,1},{4,6},{5,7},{6,4},{7,5},{8,10},{9,11},{10,... | collective-permute-start | bytes 786440 | tf_op jit(solution)/shard_map/ppermute | solution.py:677
  68.8 6.3 %collective-permute-start.13 = (bf16[8,4,64,128]{3,2,1,0:T(8,128)(2,1)S(1)}, bf16[8,4,64,128]{3,2,1,0:T(8,128)(2,1)S(1)}, u32[]{:S(2)}, u32[]{:S(2)}) collective-permute-start(bf16[8,4,64,128]{3,2,1,0:T(8,128)(2,1)S(1)} %pad_maximum_fusion.8.refs_9_.refs_12_), channel_id=1, source_target_pairs={{0,1},{1,0},{2,3},{3,2},{4,5},{5,4},{6,7},{7,6},{8,9},{9,8},{10,11... | collective-permute-start | bytes 1572872 | tf_op jit(solution)/shard_map/ppermute | solution.py:677
  68.9 14.5 %collective-permute-start.18 = (bf16[8,4,64,128]{3,2,1,0:T(8,128)(2,1)S(1)}, bf16[8,4,64,128]{3,2,1,0:T(8,128)(2,1)}, u32[]{:S(2)}, u32[]{:S(2)}) collective-permute-start(bf16[8,4,64,128]{3,2,1,0:T(8,128)(2,1)S(1)} %pad_maximum_fusion.9.refs_7_), channel_id=1, source_target_pairs={{0,4},{4,0},{8,12},{12,8},{16,20},{20,16},{24,28},{28,24},{1,5},{5... | collective-permute-start | bytes 1572872 | tf_op jit(solution)/shard_map/ppermute | solution.py:677
  70.4 13.0 %collective-permute-start.14 = (bf16[8,4,64,128]{3,2,1,0:T(8,128)(2,1)S(1)}, bf16[8,4,64,128]{3,2,1,0:T(8,128)(2,1)S(1)}, u32[]{:S(2)}, u32[]{:S(2)}) collective-permute-start(bf16[8,4,64,128]{3,2,1,0:T(8,128)(2,1)S(1)} %collective-permute-done.12.refs_10_.refs_13_), channel_id=1, source_target_pairs={{0,1},{1,0},{2,3},{3,2},{4,5},{5,4},{6,7},{7,6},{8,9},{9,8},{10,11... | collective-permute-start | bytes 1572872 | tf_op jit(solution)/shard_map/ppermute | solution.py:677
  72.3 25.6 %collective-permute-start.1 = (bf16[4,160,512]{2,1,0:T(8,128)(2,1)S(1)}, bf16[4,160,512]{2,1,0:T(8,128)(2,1)S(1)}, u32[]{:S(2)}, u32[]{:S(2)}) collective-permute-start(bf16[4,160,512]{2,1,0:T(8,128)(2,1)S(1)} %pad_maximum_fusion.1), channel_id=1, source_target_pairs={{0,1},{1,0},{2,3},{3,2},{4,5},{5,4},{6,7},{7,6},{8,9},{9,8},{10,11... | collective-permute-start | bytes 1966088 | tf_op jit(solution)/shard_map/ppermute | solution.py:677
  72.6 27.9 %collective-permute-start.2 = (bf16[4,160,512]{2,1,0:T(8,128)(2,1)S(1)}, bf16[4,160,512]{2,1,0:T(8,128)(2,1)S(1)}, u32[]{:S(2)}, u32[]{:S(2)}) collective-permute-start(bf16[4,160,512]{2,1,0:T(8,128)(2,1)S(1)} %pad_maximum_fusion.2), channel_id=1, source_target_pairs={{0,2},{1,3},{2,0},{3,1},{4,6},{5,7},{6,4},{7,5},{8,10},{9,11},{10,... | collective-permute-start | bytes 1966088 | tf_op jit(solution)/shard_map/ppermute | solution.py:677
  75.1 25.6 %collective-permute-start.19 = (bf16[8,4,64,128]{3,2,1,0:T(8,128)(2,1)S(1)}, bf16[8,4,64,128]{3,2,1,0:T(8,128)(2,1)S(1)}, u32[]{:S(2)}, u32[]{:S(2)}) collective-permute-start(bf16[8,4,64,128]{3,2,1,0:T(8,128)(2,1)S(1)} %pad_maximum_fusion.9.refs_7_), channel_id=1, source_target_pairs={{0,1},{1,0},{2,3},{3,2},{4,5},{5,4},{6,7},{7,6},{8,9},{9,8},{10,11... | collective-permute-start | bytes 1572872 | tf_op jit(solution)/shard_map/ppermute | solution.py:677
  83.4 55.8 %collective-permute-start.24 = (bf16[4,160,512]{2,1,0:T(8,128)(2,1)S(1)}, bf16[4,160,512]{2,1,0:T(8,128)(2,1)}, u32[]{:S(2)}, u32[]{:S(2)}) collective-permute-start(bf16[4,160,512]{2,1,0:T(8,128)(2,1)S(1)} %pad_maximum_fusion.5), channel_id=1, source_target_pairs={{0,1},{1,0},{2,3},{3,2},{4,5},{5,4},{6,7},{7,6},{8,9},{9,8},{10,11... | collective-permute-start | bytes 1966088 | tf_op jit(solution)/shard_map/ppermute | solution.py:677
  83.4 17.9 %collective-permute-start.20 = (bf16[8,4,64,128]{3,2,1,0:T(8,128)(2,1)}, bf16[8,4,64,128]{3,2,1,0:T(8,128)(2,1)}, u32[]{:S(2)}, u32[]{:S(2)}) collective-permute-start(bf16[8,4,64,128]{3,2,1,0:T(8,128)(2,1)} %collective-permute-done.18.refs_8_), channel_id=1, source_target_pairs={{0,1},{1,0},{2,3},{3,2},{4,5},{5,4},{6,7},{7,6},{8,9},{9,8},{10,11... | collective-permute-start | bytes 1572872 | tf_op jit(solution)/shard_map/ppermute | solution.py:677
  98.0 41.8 %collective-permute-start.25 = (bf16[4,160,512]{2,1,0:T(8,128)(2,1)S(1)}, bf16[4,160,512]{2,1,0:T(8,128)(2,1)}, u32[]{:S(2)}, u32[]{:S(2)}) collective-permute-start(bf16[4,160,512]{2,1,0:T(8,128)(2,1)S(1)} %pad_maximum_fusion.6), channel_id=1, source_target_pairs={{0,2},{1,3},{2,0},{3,1},{4,6},{5,7},{6,4},{7,5},{8,10},{9,11},{10,... | collective-permute-start | bytes 1966088 | tf_op jit(solution)/shard_map/ppermute | solution.py:677
  100.5 39.3 %collective-permute-start.26 = (bf16[4,160,512]{2,1,0:T(8,128)(2,1)S(1)}, bf16[4,160,512]{2,1,0:T(8,128)(2,1)}, u32[]{:S(2)}, u32[]{:S(2)}) collective-permute-start(bf16[4,160,512]{2,1,0:T(8,128)(2,1)S(1)} %pad_maximum_fusion.7), channel_id=1, source_target_pairs={{0,3},{1,2},{2,1},{3,0},{4,7},{5,6},{6,5},{7,4},{8,11},{9,10},{10,... | collective-permute-start | bytes 1966088 | tf_op jit(solution)/shard_map/ppermute | solution.py:677
  137.9 39.6 %collective-permute-start.21 = (bf16[4,160,512]{2,1,0:T(8,128)(2,1)}, bf16[4,160,512]{2,1,0:T(8,128)(2,1)S(1)}, u32[]{:S(2)}, u32[]{:S(2)}) collective-permute-start(bf16[4,160,512]{2,1,0:T(8,128)(2,1)} %get-tuple-element.138), channel_id=1, source_target_pairs={{0,1},{1,0},{2,3},{3,2},{4,5},{5,4},{6,7},{7,6},{8,9},{9,8},{10,11... | collective-permute-start | bytes 1966088 | tf_op jit(solution)/shard_map/ppermute | solution.py:677
  138.1 39.7 %collective-permute-start.22 = (bf16[4,160,512]{2,1,0:T(8,128)(2,1)}, bf16[4,160,512]{2,1,0:T(8,128)(2,1)S(1)}, u32[]{:S(2)}, u32[]{:S(2)}) collective-permute-start(bf16[4,160,512]{2,1,0:T(8,128)(2,1)} %get-tuple-element.139), channel_id=1, source_target_pairs={{0,2},{1,3},{2,0},{3,1},{4,6},{5,7},{6,4},{7,5},{8,10},{9,11},{10,... | collective-permute-start | bytes 1966088 | tf_op jit(solution)/shard_map/ppermute | solution.py:677
  139.2 38.6 %collective-permute-start.23 = (bf16[4,160,512]{2,1,0:T(8,128)(2,1)}, bf16[4,160,512]{2,1,0:T(8,128)(2,1)S(1)}, u32[]{:S(2)}, u32[]{:S(2)}) collective-permute-start(bf16[4,160,512]{2,1,0:T(8,128)(2,1)} %get-tuple-element.140), channel_id=1, source_target_pairs={{0,3},{1,2},{2,1},{3,0},{4,7},{5,6},{6,5},{7,4},{8,11},{9,10},{10,... | collective-permute-start | bytes 1966088 | tf_op jit(solution)/shard_map/ppermute | solution.py:677
  175.8 29.2 %collective-permute-start.27 = (bf16[4,160,512]{2,1,0:T(8,128)(2,1)}, bf16[4,160,512]{2,1,0:T(8,128)(2,1)S(1)}, u32[]{:S(2)}, u32[]{:S(2)}) collective-permute-start(bf16[4,160,512]{2,1,0:T(8,128)(2,1)} %get-tuple-element.168), channel_id=1, source_target_pairs={{0,1},{1,0},{2,3},{3,2},{4,5},{5,4},{6,7},{7,6},{8,9},{9,8},{10,11... | collective-permute-start | bytes 1966088 | tf_op jit(solution)/shard_map/ppermute | solution.py:677
  176.4 28.6 %collective-permute-start.28 = (bf16[4,160,512]{2,1,0:T(8,128)(2,1)}, bf16[4,160,512]{2,1,0:T(8,128)(2,1)S(1)}, u32[]{:S(2)}, u32[]{:S(2)}) collective-permute-start(bf16[4,160,512]{2,1,0:T(8,128)(2,1)} %get-tuple-element.169), channel_id=1, source_target_pairs={{0,2},{1,3},{2,0},{3,1},{4,6},{5,7},{6,4},{7,5},{8,10},{9,11},{10,... | collective-permute-start | bytes 1966088 | tf_op jit(solution)/shard_map/ppermute | solution.py:677
  177.5 29.1 %collective-permute-start.29 = (bf16[4,160,512]{2,1,0:T(8,128)(2,1)}, bf16[4,160,512]{2,1,0:T(8,128)(2,1)}, u32[]{:S(2)}, u32[]{:S(2)}) collective-permute-start(bf16[4,160,512]{2,1,0:T(8,128)(2,1)} %get-tuple-element.170), channel_id=1, source_target_pairs={{0,3},{1,2},{2,1},{3,0},{4,7},{5,6},{6,5},{7,4},{8,11},{9,10},{10,... | collective-permute-start | bytes 1966088 | tf_op jit(solution)/shard_map/ppermute | solution.py:677
  177.8 36.4 %copy-start.44 = (s32[32]{0:T(128)S(1)}, s32[32]{0:T(128)}, u32[]{:S(2)}) copy-start(s32[32]{0:T(128)} %param.30) | copy-start | bytes 388
  177.8 38.5 %copy-start.45 = (f32[4]{0:T(128)S(1)}, f32[4]{0:T(128)}, u32[]{:S(2)}) copy-start(f32[4]{0:T(128)} %constant.62.clone) | copy-start | bytes 52
  206.6 1.7 collective-permute-start.30
  209.0 3.7 %collective-permute-start.31 = (f32[16,128]{1,0:T(8,128)S(1)}, f32[16,128]{1,0:T(8,128)S(1)}, u32[]{:S(2)}, u32[]{:S(2)}) collective-permute-start(f32[16,128]{1,0:T(8,128)S(1)} %pad_maximum_fusion.19), channel_id=1, source_target_pairs={{0,2},{1,3},{2,0},{3,1},{4,6},{5,7},{6,4},{7,5},{8,10},{9,11},{10,... | collective-permute-start | bytes 24584 | tf_op jit(solution)/shard_map/ppermute | solution.py:677
  212.7 3.7 %collective-permute-start.32 = (f32[8,128]{1,0:T(8,128)S(1)}, f32[8,128]{1,0:T(8,128)S(1)}, u32[]{:S(2)}, u32[]{:S(2)}) collective-permute-start(f32[8,128]{1,0:T(8,128)S(1)} %broadcast_in_dim.8), channel_id=1, source_target_pairs={{0,4},{4,0},{8,12},{12,8},{16,20},{20,16},{24,28},{28,24},{1,5},{5... | collective-permute-start | bytes 12296 | tf_op jit(solution)/shard_map/ppermute | solution.py:677
  216.4 3.6 %collective-permute-start.33 = (f32[8,128]{1,0:T(8,128)S(1)}, f32[8,128]{1,0:T(8,128)S(1)}, u32[]{:S(2)}, u32[]{:S(2)}) collective-permute-start(f32[8,128]{1,0:T(8,128)S(1)} %broadcast_add_fusion), channel_id=1, source_target_pairs={{0,8},{4,12},{8,0},{12,4},{16,24},{20,28},{24,16},{28,20},{1,9},{5... | collective-permute-start | bytes 12296 | tf_op jit(solution)/shard_map/ppermute | solution.py:677
  220.0 4.5 %collective-permute-start.34 = (f32[8,128]{1,0:T(8,128)S(1)}, f32[8,128]{1,0:T(8,128)S(1)}, u32[]{:S(2)}, u32[]{:S(2)}) collective-permute-start(f32[8,128]{1,0:T(8,128)S(1)} %fusion.11), channel_id=1, source_target_pairs={{0,16},{4,20},{8,24},{12,28},{16,0},{20,4},{24,8},{28,12},{1,17},{... | collective-permute-start | bytes 12296 | tf_op jit(solution)/shard_map/ppermute | solution.py:677
  232.7 9.2 %collective-permute-start.35 = (bf16[16,4,64,128]{3,2,1,0:T(8,128)(2,1)}, bf16[16,4,64,128]{3,2,1,0:T(8,128)(2,1)S(1)}, u32[]{:S(2)}, u32[]{:S(2)}) collective-permute-start(bf16[16,4,64,128]{3,2,1,0:T(8,128)(2,1)} %get-tuple-element.175), channel_id=1, source_target_pairs={{0,1},{1,0},{2,3},{3,2},{4,5},{5,4},{6,7},{7,6},{8,9},{9,8},{10,11... | collective-permute-start | bytes 3145736 | tf_op jit(solution)/shard_map/ppermute | solution.py:677
  239.5 4.4 %collective-permute-start.37 = (bf16[16,4,64,128]{3,2,1,0:T(8,128)(2,1)}, bf16[16,4,64,128]{3,2,1,0:T(8,128)(2,1)S(1)}, u32[]{:S(2)}, u32[]{:S(2)}) collective-permute-start(bf16[16,4,64,128]{3,2,1,0:T(8,128)(2,1)} %get-tuple-element.180), channel_id=1, source_target_pairs={{0,1},{1,0},{2,3},{3,2},{4,5},{5,4},{6,7},{7,6},{8,9},{9,8},{10,11... | collective-permute-start | bytes 3145736 | tf_op jit(solution)/shard_map/ppermute | solution.py:677
  240.0 12.1 %collective-permute-start.40 = (bf16[8,32,512]{2,1,0:T(8,128)(2,1)S(1)}, bf16[8,32,512]{2,1,0:T(8,128)(2,1)S(1)}, u32[]{:S(2)}, u32[]{:S(2)}) collective-permute-start(bf16[8,32,512]{2,1,0:T(8,128)(2,1)S(1)} %copy-done.43), channel_id=1, source_target_pairs={{0,1},{1,0},{2,3},{3,2},{4,5},{5,4},{6,7},{7,6},{8,9},{9,8},{10,11... | collective-permute-start | bytes 786440 | tf_op jit(solution)/shard_map/ppermute | solution.py:677
  240.1 12.1 %collective-permute-start.41 = (bf16[8,32,512]{2,1,0:T(8,128)(2,1)S(1)}, bf16[8,32,512]{2,1,0:T(8,128)(2,1)S(1)}, u32[]{:S(2)}, u32[]{:S(2)}) collective-permute-start(bf16[8,32,512]{2,1,0:T(8,128)(2,1)S(1)} %copy-done.42), channel_id=1, source_target_pairs={{0,2},{1,3},{2,0},{3,1},{4,6},{5,7},{6,4},{7,5},{8,10},{9,11},{10,... | collective-permute-start | bytes 786440 | tf_op jit(solution)/shard_map/ppermute | solution.py:677
  241.2 12.7 %collective-permute-start.42 = (bf16[8,32,512]{2,1,0:T(8,128)(2,1)S(1)}, bf16[8,32,512]{2,1,0:T(8,128)(2,1)S(1)}, u32[]{:S(2)}, u32[]{:S(2)}) collective-permute-start(bf16[8,32,512]{2,1,0:T(8,128)(2,1)S(1)} %copy-done.41), channel_id=1, source_target_pairs={{0,3},{1,2},{2,1},{3,0},{4,7},{5,6},{6,5},{7,4},{8,11},{9,10},{10,... | collective-permute-start | bytes 786440 | tf_op jit(solution)/shard_map/ppermute | solution.py:677
  242.3 27.3 %collective-permute-start.36 = (bf16[8,4,64,128]{3,2,1,0:T(8,128)(2,1)S(1)}, bf16[8,4,64,128]{3,2,1,0:T(8,128)(2,1)S(1)}, u32[]{:S(2)}, u32[]{:S(2)}) collective-permute-start(bf16[8,4,64,128]{3,2,1,0:T(8,128)(2,1)S(1)} %get-tuple-element.271), channel_id=1, source_target_pairs={{0,4},{4,0},{8,12},{12,8},{16,20},{20,16},{24,28},{28,24},{1,5},{5... | collective-permute-start | bytes 1572872 | tf_op jit(solution)/shard_map/ppermute | solution.py:677
  244.3 25.6 %collective-permute-start.38 = (bf16[8,4,64,128]{3,2,1,0:T(8,128)(2,1)S(1)}, bf16[8,4,64,128]{3,2,1,0:T(8,128)(2,1)S(1)}, u32[]{:S(2)}, u32[]{:S(2)}) collective-permute-start(bf16[8,4,64,128]{3,2,1,0:T(8,128)(2,1)S(1)} %get-tuple-element.269), channel_id=1, source_target_pairs={{0,2},{1,3},{2,0},{3,1},{4,6},{5,7},{6,4},{7,5},{8,10},{9,11},{10,... | collective-permute-start | bytes 1572872 | tf_op jit(solution)/shard_map/ppermute | solution.py:677
  252.1 18.0 %collective-permute-start.39 = (bf16[16,4,64,128]{3,2,1,0:T(8,128)(2,1)}, bf16[16,4,64,128]{3,2,1,0:T(8,128)(2,1)S(1)}, u32[]{:S(2)}, u32[]{:S(2)}) collective-permute-start(bf16[16,4,64,128]{3,2,1,0:T(8,128)(2,1)} %get-tuple-element.185), channel_id=1, source_target_pairs={{0,1},{1,0},{2,3},{3,2},{4,5},{5,4},{6,7},{7,6},{8,9},{9,8},{10,11... | collective-permute-start | bytes 3145736 | tf_op jit(solution)/shard_map/ppermute | solution.py:677
  266.3 4.2 %collective-permute-start.43 = (bf16[16,4,64,128]{3,2,1,0:T(8,128)(2,1)}, bf16[16,4,64,128]{3,2,1,0:T(8,128)(2,1)S(1)}, u32[]{:S(2)}, u32[]{:S(2)}) collective-permute-start(bf16[16,4,64,128]{3,2,1,0:T(8,128)(2,1)} %get-tuple-element.196), channel_id=1, source_target_pairs={{0,1},{1,0},{2,3},{3,2},{4,5},{5,4},{6,7},{7,6},{8,9},{9,8},{10,11... | collective-permute-start | bytes 3145736 | tf_op jit(solution)/shard_map/ppermute | solution.py:677
  267.5 2.2 collective-permute-start.44
  271.5 9.2 %collective-permute-start.45 = (bf16[4,4,64,128]{3,2,1,0:T(8,128)(2,1)S(1)}, bf16[4,4,64,128]{3,2,1,0:T(8,128)(2,1)S(1)}, u32[]{:S(2)}, u32[]{:S(2)}) collective-permute-start(bf16[4,4,64,128]{3,2,1,0:T(8,128)(2,1)S(1)} %get-tuple-element.199), channel_id=1, source_target_pairs={{0,8},{4,12},{8,0},{12,4},{16,24},{20,28},{24,16},{28,20},{1,9},{5... | collective-permute-start | bytes 786440 | tf_op jit(solution)/shard_map/ppermute | solution.py:677
  271.6 17.0 %collective-permute-start.47 = (bf16[8,4,64,128]{3,2,1,0:T(8,128)(2,1)S(1)}, bf16[8,4,64,128]{3,2,1,0:T(8,128)(2,1)S(1)}, u32[]{:S(2)}, u32[]{:S(2)}) collective-permute-start(bf16[8,4,64,128]{3,2,1,0:T(8,128)(2,1)S(1)} %get-tuple-element.203), channel_id=1, source_target_pairs={{0,2},{1,3},{2,0},{3,1},{4,6},{5,7},{6,4},{7,5},{8,10},{9,11},{10,... | collective-permute-start | bytes 1572872 | tf_op jit(solution)/shard_map/ppermute | solution.py:677
  272.7 15.7 %collective-permute-start.46 = (bf16[4,4,64,128]{3,2,1,0:T(8,128)(2,1)S(1)}, bf16[4,4,64,128]{3,2,1,0:T(8,128)(2,1)S(1)}, u32[]{:S(2)}, u32[]{:S(2)}) collective-permute-start(bf16[4,4,64,128]{3,2,1,0:T(8,128)(2,1)S(1)} %get-tuple-element.201), channel_id=1, source_target_pairs={{0,8},{4,12},{8,0},{12,4},{16,24},{20,28},{24,16},{28,20},{1,9},{5... | collective-permute-start | bytes 786440 | tf_op jit(solution)/shard_map/ppermute | solution.py:677
  274.7 3.7 %collective-permute-start.49 = (f32[14,128]{1,0:T(8,128)S(1)}, f32[14,128]{1,0:T(8,128)S(1)}, u32[]{:S(2)}, u32[]{:S(2)}) collective-permute-start(f32[14,128]{1,0:T(8,128)S(1)} %bitcast_add_fusion), channel_id=1, source_target_pairs={{0,4},{4,0},{8,12},{12,8},{16,20},{20,16},{24,28},{28,24},{1,5},{5... | collective-permute-start | bytes 21512 | tf_op jit(solution)/shard_map/ppermute | solution.py:677
  276.1 13.2 %collective-permute-start.48 = (bf16[8,4,64,128]{3,2,1,0:T(8,128)(2,1)S(1)}, bf16[8,4,64,128]{3,2,1,0:T(8,128)(2,1)S(1)}, u32[]{:S(2)}, u32[]{:S(2)}) collective-permute-start(bf16[8,4,64,128]{3,2,1,0:T(8,128)(2,1)S(1)} %get-tuple-element.205), channel_id=1, source_target_pairs={{0,4},{4,0},{8,12},{12,8},{16,20},{20,16},{24,28},{28,24},{1,5},{5... | collective-permute-start | bytes 1572872 | tf_op jit(solution)/shard_map/ppermute | solution.py:677
  289.5 5.0 %collective-permute-start.51 = (bf16[2,4,64,128]{3,2,1,0:T(8,128)(2,1)S(1)}, bf16[2,4,64,128]{3,2,1,0:T(8,128)(2,1)S(1)}, u32[]{:S(2)}, u32[]{:S(2)}) collective-permute-start(bf16[2,4,64,128]{3,2,1,0:T(8,128)(2,1)S(1)} %get-tuple-element.219), channel_id=1, source_target_pairs={{0,4},{4,0},{8,12},{12,8},{16,20},{20,16},{24,28},{28,24},{1,5},{5... | collective-permute-start | bytes 393224 | tf_op jit(solution)/shard_map/ppermute | solution.py:677
  290.5 6.9 %collective-permute-start.52 = (bf16[4,4,64,128]{3,2,1,0:T(8,128)(2,1)S(1)}, bf16[4,4,64,128]{3,2,1,0:T(8,128)(2,1)S(1)}, u32[]{:S(2)}, u32[]{:S(2)}) collective-permute-start(bf16[4,4,64,128]{3,2,1,0:T(8,128)(2,1)S(1)} %get-tuple-element.221), channel_id=1, source_target_pairs={{0,8},{4,12},{8,0},{12,4},{16,24},{20,28},{24,16},{28,20},{1,9},{5... | collective-permute-start | bytes 786440 | tf_op jit(solution)/shard_map/ppermute | solution.py:677
  290.5 3.8 %collective-permute-start.53 = (f32[14,128]{1,0:T(8,128)S(1)}, f32[14,128]{1,0:T(8,128)S(1)}, u32[]{:S(2)}, u32[]{:S(2)}) collective-permute-start(f32[14,128]{1,0:T(8,128)S(1)} %add.252), channel_id=1, source_target_pairs={{0,2},{1,3},{2,0},{3,1},{4,6},{5,7},{6,4},{7,5},{8,10},{9,11},{10,... | collective-permute-start | bytes 21512 | tf_op jit(solution)/shard_map/ppermute | solution.py:677
  291.7 33.5 %copy-start.26 = (f32[32,2]{0,1:T(2,128)S(1)}, f32[32,2]{0,1:T(2,128)}, u32[]{:S(2)}) copy-start(f32[32,2]{0,1:T(2,128)} %param.36) | copy-start | bytes 772
  291.7 9.8 %collective-permute-start.50 = (bf16[6,4,64,128]{3,2,1,0:T(8,128)(2,1)S(1)}, bf16[6,4,64,128]{3,2,1,0:T(8,128)(2,1)S(1)}, u32[]{:S(2)}, u32[]{:S(2)}) collective-permute-start(bf16[6,4,64,128]{3,2,1,0:T(8,128)(2,1)S(1)} %pad_maximum_fusion.10), channel_id=1, source_target_pairs={{0,2},{1,3},{2,0},{3,1},{4,6},{5,7},{6,4},{7,5},{8,10},{9,11},{10,... | collective-permute-start | bytes 1179656 | tf_op jit(solution)/shard_map/ppermute | solution.py:677
  302.2 4.6 %collective-permute-start.54 = (f32[14,128]{1,0:T(8,128)S(1)}, f32[14,128]{1,0:T(8,128)S(1)}, u32[]{:S(2)}, u32[]{:S(2)}) collective-permute-start(f32[14,128]{1,0:T(8,128)S(1)} %add.262), channel_id=1, source_target_pairs={{0,8},{4,12},{8,0},{12,4},{16,24},{20,28},{24,16},{28,20},{1,9},{5... | collective-permute-start | bytes 21512 | tf_op jit(solution)/shard_map/ppermute | solution.py:677
  303.8 6.1 %collective-permute-start.57 = (bf16[2,4,64,128]{3,2,1,0:T(8,128)(2,1)S(1)}, bf16[2,4,64,128]{3,2,1,0:T(8,128)(2,1)S(1)}, u32[]{:S(2)}, u32[]{:S(2)}) collective-permute-start(bf16[2,4,64,128]{3,2,1,0:T(8,128)(2,1)S(1)} %get-tuple-element.236), channel_id=1, source_target_pairs={{0,8},{4,12},{8,0},{12,4},{16,24},{20,28},{24,16},{28,20},{1,9},{5... | collective-permute-start | bytes 393224 | tf_op jit(solution)/shard_map/ppermute | solution.py:677
  304.3 14.2 %collective-permute-start.55 = (bf16[4,4,64,128]{3,2,1,0:T(8,128)(2,1)S(1)}, bf16[4,4,64,128]{3,2,1,0:T(8,128)(2,1)S(1)}, u32[]{:S(2)}, u32[]{:S(2)}) collective-permute-start(bf16[4,4,64,128]{3,2,1,0:T(8,128)(2,1)S(1)} %pad_maximum_fusion.13), channel_id=1, source_target_pairs={{0,16},{4,20},{8,24},{12,28},{16,0},{20,4},{24,8},{28,12},{1,17},{... | collective-permute-start | bytes 786440 | tf_op jit(solution)/shard_map/ppermute | solution.py:677
  310.6 15.2 %collective-permute-start.58 = (bf16[1,4,64,128]{3,2,1,0:T(8,128)(2,1)S(1)}, bf16[1,4,64,128]{3,2,1,0:T(8,128)(2,1)S(1)}, u32[]{:S(2)}, u32[]{:S(2)}) collective-permute-start(bf16[1,4,64,128]{3,2,1,0:T(8,128)(2,1)S(1)} %get-tuple-element.304), channel_id=1, source_target_pairs={{0,16},{4,20},{8,24},{12,28},{16,0},{20,4},{24,8},{28,12},{1,17},{... | collective-permute-start | bytes 196616 | tf_op jit(solution)/shard_map/ppermute | solution.py:677
  319.2 4.5 %collective-permute-start.59 = (f32[14,128]{1,0:T(8,128)S(1)}, f32[14,128]{1,0:T(8,128)S(1)}, u32[]{:S(2)}, u32[]{:S(2)}) collective-permute-start(f32[14,128]{1,0:T(8,128)S(1)} %add.263), channel_id=1, source_target_pairs={{0,16},{4,20},{8,24},{12,28},{16,0},{20,4},{24,8},{28,12},{1,17},{... | collective-permute-start | bytes 21512 | tf_op jit(solution)/shard_map/ppermute | solution.py:677
  319.9 5.9 %collective-permute-start.56 = (bf16[1,4,64,128]{3,2,1,0:T(8,128)(2,1)S(1)}, bf16[1,4,64,128]{3,2,1,0:T(8,128)(2,1)S(1)}, u32[]{:S(2)}, u32[]{:S(2)}) collective-permute-start(bf16[1,4,64,128]{3,2,1,0:T(8,128)(2,1)S(1)} %get-tuple-element.302), channel_id=1, source_target_pairs={{0,4},{4,0},{8,12},{12,8},{16,20},{20,16},{24,28},{28,24},{1,5},{5... | collective-permute-start | bytes 196616 | tf_op jit(solution)/shard_map/ppermute | solution.py:677
  (43 other events, 556.7 us)
Sparse Core Ops, SparseCore 0:
  11.5 68.3 all-gather.2

commit v6 on v5

--- a/solution.py
+++ b/solution.py
@@ -34,7 +34,7 @@
 reduce_orders = (
     (core, side, near, row, far),
     (core, row, near, side, far),
-    (core, row, near, far, side),
+    (core, row, near, side, far),
     (core, side, row, near, far),
 )
 
@@ -1246,16 +1246,14 @@
         (small,) = together(small)
         small = small + swap(small, *near)
         last = [None] * 4
-        came = arrive_as_one(0, 1, 2)
+        came = arrive_as_one(0, 1)
         for index in (0, 1):
             last[index] = (pairs[index][0][0], came[index][0])
-        pairs[2] = add_stage(pairs[2][0], came[2])
-        travel(3)
+        travel(2, 3)
         small, last = lax.optimization_barrier((small, last))
         small = small + swap(small, *far)
-        for index in (2, 3):
-            kept, sent = pairs[index]
-            last[index] = (kept[0], swap(sent, *reduce_orders[index][-1])[0])
+        for index, block in zip((2, 3), arrive_as_one(2, 3)):
+            last[index] = (pairs[index][0][0], block[0])
         last = [block for pair in last for block in pair]
     else:
         output, tokens_grad, memory_grad = assembled()

time: 342 us -> 336 us (0.982)
  waiting for transfers between devices: 84.8 us -> 74.6 us
  starting transfers between devices: 51.7 us -> 56 us
    ppermute x60, waiting for transfers between devices: 84.8 us -> 74.6 us  [swap(): lax.ppermute(value, axis, [(index, index ^ bit) for index in range(size)])]
    ppermute x60, starting transfers between devices: 51.7 us -> 56 us  [swap(): lax.ppermute(value, axis, [(index, index ^ bit) for index in range(size)])]
  transfers between devices with their start and end apart: 61 -> 61, of which waited for: 24 -> 25; matrix products, arithmetic and copies ran while one was open for 6% -> 6% of each run, Pallas kernels for 43% -> 44%
where the time goes in v6:
time: 336 us; the launch traced here: 330 us
  Pallas kernels  155 us (46%)
  waiting for transfers between devices  74.6 us (22%)
  starting transfers between devices  56 us (17%)
  between operations  15.9 us (5%)
  other arithmetic  15.1 us (4%)
  local copies, waits for them, and re-layouts  13.9 us (4%)
    ppermute x60, waiting for transfers between devices, swap(): lax.ppermute(value, axis, [(index, index ^ bit) for index in range(size)])  74.6 us
    pallas_call x2, Pallas kernels, cross(): pl.pallas_call(functools.partial(cross_kernel, shards, late_plans, soon_c...  71.7 us
    ppermute x60, starting transfers between devices, swap(): lax.ppermute(value, axis, [(index, index ^ bit) for index in range(size)])  56 us
    pallas_call x4, Pallas kernels, gradient_call(): pl.pallas_call(kernel, in_specs=[smem, smem] + [anywhere] * len(operands)...  32.1 us
    pallas_call x1, Pallas kernels, on_device(): pl.pallas_call(functools.partial(self_backward_kernel, shards, self_plans...  27.1 us
    pallas_call x1, Pallas kernels, on_device(): pl.pallas_call(functools.partial(self_forward_kernel, shards, self_plans,...  13.7 us
    pallas_call x1, Pallas kernels, assembled(): return assemble(after(kernel_info, *there(0)), *returned)  7.69 us
  transfers between devices with their start and end apart: 61, of which 25 were waited for; matrix products, arithmetic and copies ran while one was open for 6% of the time, Pallas kernels for 44%

profile of v6, /device:TPU:0, one launch (start us, length us, event | category | flops | bytes accessed | tf_op | source)
XLA Modules:
  0.0 330.4 jit_solution(10224727374712611589)
XLA Ops:
  7.3 1.1 convert_bitcast_fusion
  10.8 2.4 collective-permute-start.8
  13.9 2.2 constant_dynamic-slice_fusion.13
  16.1 1.5 collective-permute-start
  17.7 2.7 collective-permute-start.9
  21.2 2.0 constant_dynamic-slice_fusion.11.refs_6_
  25.0 1.3 collective-permute-start.15
  26.4 2.8 collective-permute-start.10
  29.8 2.8 collective-permute-done.15
  33.2 2.0 collective-permute-done.10
  35.2 1.7 collective-permute-start.11
  37.2 9.1 %collective-permute-done.11 = bf16[4,4,64,128]{3,2,1,0:T(8,128)(2,1)S(1)} collective-permute-done((bf16[4,4,64,128]{3,2,1,0:T(8,128)(2,1)S(1)}, bf16[4,4,64,128]{3,2,1,0:T(8,128)(2,1)S(1)}, u32[]{:S(2)}, u32[]{:S(2)}) %collective-permute-start.11) | collective-permute-done | bytes 262176 | tf_op jit(solution)/shard_map/ppermute | solution.py:677
  46.4 1.9 collective-permute-start.12
  48.3 1.5 collective-permute-start.17
  49.9 0.9 pad_maximum_fusion.refs_1_.refs_4_
  50.9 17.9 %collective-permute-done.17 = bf16[4,4,64,128]{3,2,1,0:T(8,128)(2,1)S(1)} collective-permute-done((bf16[4,4,64,128]{3,2,1,0:T(8,128)(2,1)S(1)}, bf16[4,4,64,128]{3,2,1,0:T(8,128)(2,1)S(1)}, u32[]{:S(2)}, u32[]{:S(2)}) %collective-permute-start.17) | collective-permute-done | bytes 262176 | tf_op jit(solution)/shard_map/ppermute | solution.py:677
  68.9 1.5 collective-permute-start.18
  72.6 2.5 collective-permute-start.2
  75.2 8.3 %collective-permute-done.18.refs_8_ = bf16[8,4,64,128]{3,2,1,0:T(8,128)(2,1)} collective-permute-done((bf16[8,4,64,128]{3,2,1,0:T(8,128)(2,1)S(1)}, bf16[8,4,64,128]{3,2,1,0:T(8,128)(2,1)}, u32[]{:S(2)}, u32[]{:S(2)}) %collective-permute-start.18) | collective-permute-done | bytes 524320 | tf_op jit(solution)/shard_map/ppermute | solution.py:677
  84.3 13.7 %self_forward.1 = (bf16[8,128,512]{2,1,0:T(8,128)(2,1)}, bf16[8,128,512]{2,1,0:T(8,128)(2,1)}, bf16[3,8,128,512]{3,2,1,0:T(8,128)(2,1)}, f32[8,2,128,512]{3,2,1,...) custom-call(s32[3]{0:T(128)} %pad_add_fusion.refs_0_.info, ...), custom_call_target="tpu_custom_call" | custom-call | flops 16000000000 | bytes 16000000 | tf_op jit(solution)/shard_map/self_forward/pallas_call | solution.py:861
  98.0 2.6 collective-permute-start.25
  102.2 35.7 %cross.2 = (bf16[32,32,512]{2,1,0:T(8,128)(2,1)}, f32[32,128,512]{2,1,0:T(8,128)}, bf16[4,160,512]{2,1,0:T(8,128)(2,1)}, bf16[4,160,512]{2,1,0:T(8,128)(2,1)}, b...) custom-call(s32[3]{0:T(128)} %pad_add_fusion.refs_0_.info, ...), custom_call_target="tpu_custom_call" | custom-call | flops 32000000000 | bytes 24000000 | tf_op jit(solution)/shard_map/cross/pallas_call | solution.py:946
  138.2 1.1 collective-permute-start.22
  139.8 36.0 %cross.3 = (bf16[32,32,512]{2,1,0:T(8,128)(2,1)}, f32[32,128,512]{2,1,0:T(8,128)}, bf16[4,160,512]{2,1,0:T(8,128)(2,1)}, bf16[4,160,512]{2,1,0:T(8,128)(2,1)}, b...) custom-call(s32[3]{0:T(128)} %pad_add_fusion.refs_0_.info, ...), custom_call_target="tpu_custom_call", output_to_operand_aliasing={{0}: (12, {}), {1}: (13, {}), {5}: (14, {}), {6}: (15, {}),... | custom-call | flops 32000000000 | bytes 24000000 | tf_op jit(solution)/shard_map/cross/pallas_call | solution.py:946
  176.4 1.1 collective-permute-start.28
  177.9 27.1 %self_backward.1 = (f32[32,32,512]{2,1,0:T(8,128)}, bf16[8,32,512]{2,1,0:T(8,128)(2,1)}, bf16[8,32,512]{2,1,0:T(8,128)(2,1)}, bf16[8,32,512]{2,1,0:T(8,128)(2,1)...) custom-call(s32[3]{0:T(128)} %pad_add_fusion.refs_0_.info, ...), custom_call_target="tpu_custom_call" | custom-call | flops 24000000000 | bytes 24000000 | tf_op jit(solution)/shard_map/self_backward/pallas_call | solution.py:1001
  205.0 1.6 collective-permute-done.29.refs_6_
  207.3 1.0 collective-permute-done.30
  209.0 1.1 collective-permute-start.31
  210.8 1.9 collective-permute-done.31
  212.7 1.5 collective-permute-start.32
  214.3 2.1 collective-permute-done.32
  216.5 3.5 %collective-permute-done.33 = f32[8,128]{1,0:T(8,128)S(1)} collective-permute-done((f32[8,128]{1,0:T(8,128)S(1)}, f32[8,128]{1,0:T(8,128)S(1)}, u32[]{:S(2)}, u32[]{:S(2)}) %collective-permute-start.33) | collective-permute-done | bytes 4128 | tf_op jit(solution)/shard_map/ppermute | solution.py:677
  221.4 3.1 collective-permute-done.34
  226.2 6.5 %inner_gradients.2 = (bf16[16,4,64,128]{3,2,1,0:T(8,128)(2,1)}, bf16[16,4,64,128]{3,2,1,0:T(8,128)(2,1)}) custom-call(s32[3]{0:T(128)} %pad_add_fusion.refs_0_.info, f32[8]{0:T(128)} %divide_minimum_fusion.clip, bf16[8,128,512]{2,1,0:T(8,128)(2,1)} %get-tuple-element.172.left, bf16[4,8,128,512]{3,2,1,0:T(8,128)(2,1)} %get-tuple-element.173.right), custom_call_target="tpu_custom_call" | custom-call | flops 5000000000 | bytes 7000000 | tf_op jit(solution)/shard_map/inner_gradients/pallas_call | solution.py:1094
  232.9 6.6 %inner_gradients.3 = (bf16[16,4,64,128]{3,2,1,0:T(8,128)(2,1)}, bf16[16,4,64,128]{3,2,1,0:T(8,128)(2,1)}) custom-call(s32[3]{0:T(128)} %pad_add_fusion.refs_0_.info, f32[8]{0:T(128)} %divide_minimum_fusion.clip, bf16[8,128,512]{2,1,0:T(8,128)(2,1)} %get-tuple-element.177.left, bf16[4,8,128,512]{3,2,1,0:T(8,128)(2,1)} %get-tuple-element.178.right), custom_call_target="tpu_custom_call" | custom-call | flops 5000000000 | bytes 7000000 | tf_op jit(solution)/shard_map/inner_gradients/pallas_call | solution.py:1094
  240.1 1.1 collective-permute-start.41
  242.3 1.5 collective-permute-start.36
  244.2 1.1 collective-permute-start.38
  245.4 6.7 %self_gradients.1 = (bf16[16,4,64,128]{3,2,1,0:T(8,128)(2,1)}, bf16[16,4,64,128]{3,2,1,0:T(8,128)(2,1)}) custom-call(s32[3]{0:T(128)} %pad_add_fusion.refs_0_.info, f32[8]{0:T(128)} %divide_minimum_fusion.clip, bf16[8,128,512]{2,1,0:T(8,128)(2,1)} %get-tuple-element.160.refs_3_.normed, bf16[3,8,128,512]{3,2,1,0:T(8,128)(2,1)} %get-tuple-element.182.d_qkv, ...), custom_call_target="tpu_custom_call" | custom-call | flops 5000000000 | bytes 8000000 | tf_op jit(solution)/shard_map/self_gradients/pallas_call | solution.py:1094
  252.2 1.7 collective-permute-done.42.refs_9_
  253.9 12.3 %cross_gradients.1 = (bf16[16,4,64,128]{3,2,1,0:T(8,128)(2,1)}, bf16[16,4,64,128]{3,2,1,0:T(8,128)(2,1)}) custom-call(s32[3]{0:T(128)} %pad_add_fusion.refs_0_.info, f32[8]{0:T(128)} %divide_minimum_fusion.clip, bf16[8,128,512]{2,1,0:T(8,128)(2,1)} %get-tuple-element.190.refs_0_, bf16[8,128,512]{2,1,0:T(8,128)(2,1)} %get-tuple-element.191.refs_1_, ...), custom_call_target="tpu_custom_call" | custom-call | flops 8999999488 | bytes 20000000 | tf_op jit(solution)/shard_map/cross_gradients/pallas_call | solution.py:1094
  266.3 1.1 collective-permute-start.43
  267.6 2.1 collective-permute-done.44
  271.5 1.1 collective-permute-start.47
  272.7 1.9 collective-permute-start.46
  274.6 1.4 collective-permute-start.49
  276.7 1.7 collective-permute-done.49
  278.4 2.3 collective-permute-done.45
  280.7 7.7 %assemble.1 = (bf16[32,32,512]{2,1,0:T(8,128)(2,1)}, f32[32,32,512]{2,1,0:T(8,128)}, f32[32,128,512]{2,1,0:T(8,128)}) custom-call(s32[3]{0:T(128)} %pad_add_fusion.refs_0_.info, bf16[4,160,512]{2,1,0:T(8,128)(2,1)} %copy-done.9, bf16[4,160,512]{2,1,0:T(8,128)(2,1)} %copy-done.10, ...), custom_call_target="tpu_custom_call", output_to_operand_aliasing={{0}: (10, {}), {1}: (11, {}), {2}: (12, {})} | custom-call | flops 1000000 | bytes 20000000 | tf_op jit(solution)/shard_map/assemble/pallas_call | solution.py:1232
  289.4 1.0 collective-permute-start.51
  290.5 1.1 collective-permute-start.53
  291.6 1.0 collective-permute-start.50
  292.7 1.6 collective-permute-done.53
  295.1 2.2 collective-permute-done.52
  297.4 4.0 %collective-permute-done.50 = bf16[6,4,64,128]{3,2,1,0:T(8,128)(2,1)S(1)} collective-permute-done((bf16[6,4,64,128]{3,2,1,0:T(8,128)(2,1)S(1)}, bf16[6,4,64,128]{3,2,1,0:T(8,128)(2,1)S(1)}, u32[]{:S(2)}, u32[]{:S(2)}) %collective-permute-start.50) | collective-permute-done | bytes 393248 | tf_op jit(solution)/shard_map/ppermute | solution.py:677
  302.2 1.1 collective-permute-start.55
  305.2 1.1 collective-permute-start.56
  306.4 1.3 collective-permute-start.57
  309.3 1.8 collective-permute-start.59
  312.5 2.0 collective-permute-start.58
  314.8 1.3 multiply_add_fusion
  316.7 3.2 collective-permute-done.58
  320.5 2.8 update.1
  (244 shorter events, 33.2 us)
Async XLA Ops:
  7.2 94.1 %all-gather.3.cloned.1.call-start = ((), (), s32[]{:S(2)}) async-start(), calls=%async_computation | async-start | bytes 4325376 | tf_op jit(solution)/shard_map/all_gather | solution.py:775
  10.8 13.7 %collective-permute-start.8 = (f32[2,128]{1,0:T(2,128)S(1)}, f32[2,128]{1,0:T(2,128)S(1)}, u32[]{:S(2)}, u32[]{:S(2)}) collective-permute-start(f32[2,128]{1,0:T(2,128)S(1)} %pad.4), channel_id=1, source_target_pairs={{0,3},{1,2},{2,1},{3,0},{4,7},{5,6},{6,5},{7,4},{8,11},{9,10},{10,... | collective-permute-start | bytes 3080 | tf_op jit(solution)/shard_map/ppermute | solution.py:677
  13.2 11.8 %collective-permute-start.7 = (f32[2,128]{1,0:T(2,128)S(1)}, f32[2,128]{1,0:T(2,128)S(1)}, u32[]{:S(2)}, u32[]{:S(2)}) collective-permute-start(f32[2,128]{1,0:T(2,128)S(1)} %pad.4), channel_id=1, source_target_pairs={{0,2},{1,3},{2,0},{3,1},{4,6},{5,7},{6,4},{7,5},{8,10},{9,11},{10,... | collective-permute-start | bytes 3080 | tf_op jit(solution)/shard_map/ppermute | solution.py:677
  13.8 12.6 %collective-permute-start.6 = (f32[2,128]{1,0:T(2,128)S(1)}, f32[2,128]{1,0:T(2,128)S(1)}, u32[]{:S(2)}, u32[]{:S(2)}) collective-permute-start(f32[2,128]{1,0:T(2,128)S(1)} %pad.4), channel_id=1, source_target_pairs={{0,1},{1,0},{2,3},{3,2},{4,5},{5,4},{6,7},{7,6},{8,9},{9,8},{10,11... | collective-permute-start | bytes 3080 | tf_op jit(solution)/shard_map/ppermute | solution.py:677
  16.1 20.8 %collective-permute-start = (bf16[8,32,512]{2,1,0:T(8,128)(2,1)}, bf16[8,32,512]{2,1,0:T(8,128)(2,1)}, u32[]{:S(2)}, u32[]{:S(2)}) collective-permute-start(bf16[8,32,512]{2,1,0:T(8,128)(2,1)} %get-tuple-element.290), channel_id=1, source_target_pairs={{0,3},{1,2},{2,1},{3,0},{4,7},{5,6},{6,5},{7,4},{8,11},{9,10},{10,... | collective-permute-start | bytes 786440 | tf_op jit(solution)/shard_map/ppermute | solution.py:677
  17.7 6.8 %collective-permute-start.9 = (bf16[1,4,64,128]{3,2,1,0:T(8,128)(2,1)S(1)}, bf16[1,4,64,128]{3,2,1,0:T(8,128)(2,1)S(1)}, u32[]{:S(2)}, u32[]{:S(2)}) collective-permute-start(bf16[1,4,64,128]{3,2,1,0:T(8,128)(2,1)S(1)} %maximum_bitcast_fusion), channel_id=1, source_target_pairs={{0,16},{4,20},{8,24},{12,28},{16,0},{20,4},{24,8},{28,12},{1,17},{... | collective-permute-start | bytes 196616 | tf_op jit(solution)/shard_map/ppermute | solution.py:677
  24.5 47.8 %collective-permute-start.4 = (bf16[8,32,512]{2,1,0:T(8,128)(2,1)S(1)}, bf16[8,32,512]{2,1,0:T(8,128)(2,1)S(1)}, u32[]{:S(2)}, u32[]{:S(2)}) collective-permute-start(bf16[8,32,512]{2,1,0:T(8,128)(2,1)S(1)} %copy-done.20), channel_id=1, source_target_pairs={{0,1},{1,0},{2,3},{3,2},{4,5},{5,4},{6,7},{7,6},{8,9},{9,8},{10,11... | collective-permute-start | bytes 786440 | tf_op jit(solution)/shard_map/ppermute | solution.py:677
  24.5 48.1 %collective-permute-start.5 = (bf16[8,32,512]{2,1,0:T(8,128)(2,1)S(1)}, bf16[8,32,512]{2,1,0:T(8,128)(2,1)S(1)}, u32[]{:S(2)}, u32[]{:S(2)}) collective-permute-start(bf16[8,32,512]{2,1,0:T(8,128)(2,1)S(1)} %copy-done.19), channel_id=1, source_target_pairs={{0,2},{1,3},{2,0},{3,1},{4,6},{5,7},{6,4},{7,5},{8,10},{9,11},{10,... | collective-permute-start | bytes 786440 | tf_op jit(solution)/shard_map/ppermute | solution.py:677
  25.0 7.6 %collective-permute-start.15 = (bf16[1,4,64,128]{3,2,1,0:T(8,128)(2,1)S(1)}, bf16[1,4,64,128]{3,2,1,0:T(8,128)(2,1)S(1)}, u32[]{:S(2)}, u32[]{:S(2)}) collective-permute-start(bf16[1,4,64,128]{3,2,1,0:T(8,128)(2,1)S(1)} %maximum_bitcast_fusion.1), channel_id=1, source_target_pairs={{0,16},{4,20},{8,24},{12,28},{16,0},{20,4},{24,8},{28,12},{1,17},{... | collective-permute-start | bytes 196616 | tf_op jit(solution)/shard_map/ppermute | solution.py:677
  26.4 8.8 %collective-permute-start.10 = (bf16[2,4,64,128]{3,2,1,0:T(8,128)(2,1)S(1)}, bf16[2,4,64,128]{3,2,1,0:T(8,128)(2,1)S(1)}, u32[]{:S(2)}, u32[]{:S(2)}) collective-permute-start(bf16[2,4,64,128]{3,2,1,0:T(8,128)(2,1)S(1)} %pad_maximum_fusion.13), channel_id=1, source_target_pairs={{0,8},{4,12},{8,0},{12,4},{16,24},{20,28},{24,16},{28,20},{1,9},{5... | collective-permute-start | bytes 393224 | tf_op jit(solution)/shard_map/ppermute | solution.py:677
  32.6 15.7 %collective-permute-start.16 = (bf16[2,4,64,128]{3,2,1,0:T(8,128)(2,1)S(1)}, bf16[2,4,64,128]{3,2,1,0:T(8,128)(2,1)S(1)}, u32[]{:S(2)}, u32[]{:S(2)}) collective-permute-start(bf16[2,4,64,128]{3,2,1,0:T(8,128)(2,1)S(1)} %pad_maximum_fusion.14), channel_id=1, source_target_pairs={{0,8},{4,12},{8,0},{12,4},{16,24},{20,28},{24,16},{28,20},{1,9},{5... | collective-permute-start | bytes 393224 | tf_op jit(solution)/shard_map/ppermute | solution.py:677
  35.2 11.1 %collective-permute-start.11 = (bf16[4,4,64,128]{3,2,1,0:T(8,128)(2,1)S(1)}, bf16[4,4,64,128]{3,2,1,0:T(8,128)(2,1)S(1)}, u32[]{:S(2)}, u32[]{:S(2)}) collective-permute-start(bf16[4,4,64,128]{3,2,1,0:T(8,128)(2,1)S(1)} %pad_maximum_fusion.11), channel_id=1, source_target_pairs={{0,2},{1,3},{2,0},{3,1},{4,6},{5,7},{6,4},{7,5},{8,10},{9,11},{10,... | collective-permute-start | bytes 786440 | tf_op jit(solution)/shard_map/ppermute | solution.py:677
  37.1 31.8 %collective-permute-start.3 = (bf16[4,160,512]{2,1,0:T(8,128)(2,1)S(1)}, bf16[4,160,512]{2,1,0:T(8,128)(2,1)S(1)}, u32[]{:S(2)}, u32[]{:S(2)}) collective-permute-start(bf16[4,160,512]{2,1,0:T(8,128)(2,1)S(1)} %pad_maximum_fusion.3), channel_id=1, source_target_pairs={{0,3},{1,2},{2,1},{3,0},{4,7},{5,6},{6,5},{7,4},{8,11},{9,10},{10,... | collective-permute-start | bytes 1966088 | tf_op jit(solution)/shard_map/ppermute | solution.py:677
  46.4 24.0 %collective-permute-start.12 = (bf16[8,4,64,128]{3,2,1,0:T(8,128)(2,1)S(1)}, bf16[8,4,64,128]{3,2,1,0:T(8,128)(2,1)S(1)}, u32[]{:S(2)}, u32[]{:S(2)}) collective-permute-start(bf16[8,4,64,128]{3,2,1,0:T(8,128)(2,1)S(1)} %pad_maximum_fusion.8.refs_9_.refs_12_), channel_id=1, source_target_pairs={{0,4},{4,0},{8,12},{12,8},{16,20},{20,16},{24,28},{28,24},{1,5},{5... | collective-permute-start | bytes 1572872 | tf_op jit(solution)/shard_map/ppermute | solution.py:677
  48.3 20.5 %collective-permute-start.17 = (bf16[4,4,64,128]{3,2,1,0:T(8,128)(2,1)S(1)}, bf16[4,4,64,128]{3,2,1,0:T(8,128)(2,1)S(1)}, u32[]{:S(2)}, u32[]{:S(2)}) collective-permute-start(bf16[4,4,64,128]{3,2,1,0:T(8,128)(2,1)S(1)} %pad_maximum_fusion.12), channel_id=1, source_target_pairs={{0,2},{1,3},{2,0},{3,1},{4,6},{5,7},{6,4},{7,5},{8,10},{9,11},{10,... | collective-permute-start | bytes 786440 | tf_op jit(solution)/shard_map/ppermute | solution.py:677
  68.8 6.3 %collective-permute-start.13 = (bf16[8,4,64,128]{3,2,1,0:T(8,128)(2,1)S(1)}, bf16[8,4,64,128]{3,2,1,0:T(8,128)(2,1)S(1)}, u32[]{:S(2)}, u32[]{:S(2)}) collective-permute-start(bf16[8,4,64,128]{3,2,1,0:T(8,128)(2,1)S(1)} %pad_maximum_fusion.8.refs_9_.refs_12_), channel_id=1, source_target_pairs={{0,1},{1,0},{2,3},{3,2},{4,5},{5,4},{6,7},{7,6},{8,9},{9,8},{10,11... | collective-permute-start | bytes 1572872 | tf_op jit(solution)/shard_map/ppermute | solution.py:677
  68.9 14.5 %collective-permute-start.18 = (bf16[8,4,64,128]{3,2,1,0:T(8,128)(2,1)S(1)}, bf16[8,4,64,128]{3,2,1,0:T(8,128)(2,1)}, u32[]{:S(2)}, u32[]{:S(2)}) collective-permute-start(bf16[8,4,64,128]{3,2,1,0:T(8,128)(2,1)S(1)} %pad_maximum_fusion.9.refs_7_), channel_id=1, source_target_pairs={{0,4},{4,0},{8,12},{12,8},{16,20},{20,16},{24,28},{28,24},{1,5},{5... | collective-permute-start | bytes 1572872 | tf_op jit(solution)/shard_map/ppermute | solution.py:677
  70.4 13.0 %collective-permute-start.14 = (bf16[8,4,64,128]{3,2,1,0:T(8,128)(2,1)S(1)}, bf16[8,4,64,128]{3,2,1,0:T(8,128)(2,1)S(1)}, u32[]{:S(2)}, u32[]{:S(2)}) collective-permute-start(bf16[8,4,64,128]{3,2,1,0:T(8,128)(2,1)S(1)} %collective-permute-done.12.refs_10_.refs_13_), channel_id=1, source_target_pairs={{0,1},{1,0},{2,3},{3,2},{4,5},{5,4},{6,7},{7,6},{8,9},{9,8},{10,11... | collective-permute-start | bytes 1572872 | tf_op jit(solution)/shard_map/ppermute | solution.py:677
  72.3 25.6 %collective-permute-start.1 = (bf16[4,160,512]{2,1,0:T(8,128)(2,1)S(1)}, bf16[4,160,512]{2,1,0:T(8,128)(2,1)S(1)}, u32[]{:S(2)}, u32[]{:S(2)}) collective-permute-start(bf16[4,160,512]{2,1,0:T(8,128)(2,1)S(1)} %pad_maximum_fusion.1), channel_id=1, source_target_pairs={{0,1},{1,0},{2,3},{3,2},{4,5},{5,4},{6,7},{7,6},{8,9},{9,8},{10,11... | collective-permute-start | bytes 1966088 | tf_op jit(solution)/shard_map/ppermute | solution.py:677
  72.6 27.9 %collective-permute-start.2 = (bf16[4,160,512]{2,1,0:T(8,128)(2,1)S(1)}, bf16[4,160,512]{2,1,0:T(8,128)(2,1)S(1)}, u32[]{:S(2)}, u32[]{:S(2)}) collective-permute-start(bf16[4,160,512]{2,1,0:T(8,128)(2,1)S(1)} %pad_maximum_fusion.2), channel_id=1, source_target_pairs={{0,2},{1,3},{2,0},{3,1},{4,6},{5,7},{6,4},{7,5},{8,10},{9,11},{10,... | collective-permute-start | bytes 1966088 | tf_op jit(solution)/shard_map/ppermute | solution.py:677
  75.1 25.6 %collective-permute-start.19 = (bf16[8,4,64,128]{3,2,1,0:T(8,128)(2,1)S(1)}, bf16[8,4,64,128]{3,2,1,0:T(8,128)(2,1)S(1)}, u32[]{:S(2)}, u32[]{:S(2)}) collective-permute-start(bf16[8,4,64,128]{3,2,1,0:T(8,128)(2,1)S(1)} %pad_maximum_fusion.9.refs_7_), channel_id=1, source_target_pairs={{0,1},{1,0},{2,3},{3,2},{4,5},{5,4},{6,7},{7,6},{8,9},{9,8},{10,11... | collective-permute-start | bytes 1572872 | tf_op jit(solution)/shard_map/ppermute | solution.py:677
  83.4 55.8 %collective-permute-start.24 = (bf16[4,160,512]{2,1,0:T(8,128)(2,1)S(1)}, bf16[4,160,512]{2,1,0:T(8,128)(2,1)}, u32[]{:S(2)}, u32[]{:S(2)}) collective-permute-start(bf16[4,160,512]{2,1,0:T(8,128)(2,1)S(1)} %pad_maximum_fusion.5), channel_id=1, source_target_pairs={{0,1},{1,0},{2,3},{3,2},{4,5},{5,4},{6,7},{7,6},{8,9},{9,8},{10,11... | collective-permute-start | bytes 1966088 | tf_op jit(solution)/shard_map/ppermute | solution.py:677
  83.4 17.9 %collective-permute-start.20 = (bf16[8,4,64,128]{3,2,1,0:T(8,128)(2,1)}, bf16[8,4,64,128]{3,2,1,0:T(8,128)(2,1)}, u32[]{:S(2)}, u32[]{:S(2)}) collective-permute-start(bf16[8,4,64,128]{3,2,1,0:T(8,128)(2,1)} %collective-permute-done.18.refs_8_), channel_id=1, source_target_pairs={{0,1},{1,0},{2,3},{3,2},{4,5},{5,4},{6,7},{7,6},{8,9},{9,8},{10,11... | collective-permute-start | bytes 1572872 | tf_op jit(solution)/shard_map/ppermute | solution.py:677
  98.0 41.8 %collective-permute-start.25 = (bf16[4,160,512]{2,1,0:T(8,128)(2,1)S(1)}, bf16[4,160,512]{2,1,0:T(8,128)(2,1)}, u32[]{:S(2)}, u32[]{:S(2)}) collective-permute-start(bf16[4,160,512]{2,1,0:T(8,128)(2,1)S(1)} %pad_maximum_fusion.6), channel_id=1, source_target_pairs={{0,2},{1,3},{2,0},{3,1},{4,6},{5,7},{6,4},{7,5},{8,10},{9,11},{10,... | collective-permute-start | bytes 1966088 | tf_op jit(solution)/shard_map/ppermute | solution.py:677
  100.5 39.3 %collective-permute-start.26 = (bf16[4,160,512]{2,1,0:T(8,128)(2,1)S(1)}, bf16[4,160,512]{2,1,0:T(8,128)(2,1)}, u32[]{:S(2)}, u32[]{:S(2)}) collective-permute-start(bf16[4,160,512]{2,1,0:T(8,128)(2,1)S(1)} %pad_maximum_fusion.7), channel_id=1, source_target_pairs={{0,3},{1,2},{2,1},{3,0},{4,7},{5,6},{6,5},{7,4},{8,11},{9,10},{10,... | collective-permute-start | bytes 1966088 | tf_op jit(solution)/shard_map/ppermute | solution.py:677
  137.9 39.6 %collective-permute-start.21 = (bf16[4,160,512]{2,1,0:T(8,128)(2,1)}, bf16[4,160,512]{2,1,0:T(8,128)(2,1)S(1)}, u32[]{:S(2)}, u32[]{:S(2)}) collective-permute-start(bf16[4,160,512]{2,1,0:T(8,128)(2,1)} %get-tuple-element.138), channel_id=1, source_target_pairs={{0,1},{1,0},{2,3},{3,2},{4,5},{5,4},{6,7},{7,6},{8,9},{9,8},{10,11... | collective-permute-start | bytes 1966088 | tf_op jit(solution)/shard_map/ppermute | solution.py:677
  138.2 39.6 %collective-permute-start.22 = (bf16[4,160,512]{2,1,0:T(8,128)(2,1)}, bf16[4,160,512]{2,1,0:T(8,128)(2,1)S(1)}, u32[]{:S(2)}, u32[]{:S(2)}) collective-permute-start(bf16[4,160,512]{2,1,0:T(8,128)(2,1)} %get-tuple-element.139), channel_id=1, source_target_pairs={{0,2},{1,3},{2,0},{3,1},{4,6},{5,7},{6,4},{7,5},{8,10},{9,11},{10,... | collective-permute-start | bytes 1966088 | tf_op jit(solution)/shard_map/ppermute | solution.py:677
  139.2 38.6 %collective-permute-start.23 = (bf16[4,160,512]{2,1,0:T(8,128)(2,1)}, bf16[4,160,512]{2,1,0:T(8,128)(2,1)S(1)}, u32[]{:S(2)}, u32[]{:S(2)}) collective-permute-start(bf16[4,160,512]{2,1,0:T(8,128)(2,1)} %get-tuple-element.140), channel_id=1, source_target_pairs={{0,3},{1,2},{2,1},{3,0},{4,7},{5,6},{6,5},{7,4},{8,11},{9,10},{10,... | collective-permute-start | bytes 1966088 | tf_op jit(solution)/shard_map/ppermute | solution.py:677
  175.8 29.2 %collective-permute-start.27 = (bf16[4,160,512]{2,1,0:T(8,128)(2,1)}, bf16[4,160,512]{2,1,0:T(8,128)(2,1)S(1)}, u32[]{:S(2)}, u32[]{:S(2)}) collective-permute-start(bf16[4,160,512]{2,1,0:T(8,128)(2,1)} %get-tuple-element.168), channel_id=1, source_target_pairs={{0,1},{1,0},{2,3},{3,2},{4,5},{5,4},{6,7},{7,6},{8,9},{9,8},{10,11... | collective-permute-start | bytes 1966088 | tf_op jit(solution)/shard_map/ppermute | solution.py:677
  176.4 28.6 %collective-permute-start.28 = (bf16[4,160,512]{2,1,0:T(8,128)(2,1)}, bf16[4,160,512]{2,1,0:T(8,128)(2,1)S(1)}, u32[]{:S(2)}, u32[]{:S(2)}) collective-permute-start(bf16[4,160,512]{2,1,0:T(8,128)(2,1)} %get-tuple-element.169), channel_id=1, source_target_pairs={{0,2},{1,3},{2,0},{3,1},{4,6},{5,7},{6,4},{7,5},{8,10},{9,11},{10,... | collective-permute-start | bytes 1966088 | tf_op jit(solution)/shard_map/ppermute | solution.py:677
  177.5 29.1 %collective-permute-start.29 = (bf16[4,160,512]{2,1,0:T(8,128)(2,1)}, bf16[4,160,512]{2,1,0:T(8,128)(2,1)}, u32[]{:S(2)}, u32[]{:S(2)}) collective-permute-start(bf16[4,160,512]{2,1,0:T(8,128)(2,1)} %get-tuple-element.170), channel_id=1, source_target_pairs={{0,3},{1,2},{2,1},{3,0},{4,7},{5,6},{6,5},{7,4},{8,11},{9,10},{10,... | collective-permute-start | bytes 1966088 | tf_op jit(solution)/shard_map/ppermute | solution.py:677
  177.8 36.4 %copy-start.42 = (s32[32]{0:T(128)S(1)}, s32[32]{0:T(128)}, u32[]{:S(2)}) copy-start(s32[32]{0:T(128)} %param.30) | copy-start | bytes 388
  177.9 38.5 %copy-start.43 = (f32[4]{0:T(128)S(1)}, f32[4]{0:T(128)}, u32[]{:S(2)}) copy-start(f32[4]{0:T(128)} %constant.62.clone) | copy-start | bytes 52
  205.0 27.7 %copy-start.12 = (bf16[4,160,512]{2,1,0:T(8,128)(2,1)}, bf16[4,160,512]{2,1,0:T(8,128)(2,1)S(1)}, u32[]{:S(2)}) copy-start(bf16[4,160,512]{2,1,0:T(8,128)(2,1)S(1)} %collective-permute-done.27.refs_4_) | copy-start | bytes 1966084
  206.6 1.7 collective-permute-start.30
  209.0 3.7 %collective-permute-start.31 = (f32[16,128]{1,0:T(8,128)S(1)}, f32[16,128]{1,0:T(8,128)S(1)}, u32[]{:S(2)}, u32[]{:S(2)}) collective-permute-start(f32[16,128]{1,0:T(8,128)S(1)} %pad_maximum_fusion.20), channel_id=1, source_target_pairs={{0,2},{1,3},{2,0},{3,1},{4,6},{5,7},{6,4},{7,5},{8,10},{9,11},{10,... | collective-permute-start | bytes 24584 | tf_op jit(solution)/shard_map/ppermute | solution.py:677
  212.7 3.7 %collective-permute-start.32 = (f32[8,128]{1,0:T(8,128)S(1)}, f32[8,128]{1,0:T(8,128)S(1)}, u32[]{:S(2)}, u32[]{:S(2)}) collective-permute-start(f32[8,128]{1,0:T(8,128)S(1)} %broadcast_in_dim.8), channel_id=1, source_target_pairs={{0,4},{4,0},{8,12},{12,8},{16,20},{20,16},{24,28},{28,24},{1,5},{5... | collective-permute-start | bytes 12296 | tf_op jit(solution)/shard_map/ppermute | solution.py:677
  216.4 3.6 %collective-permute-start.33 = (f32[8,128]{1,0:T(8,128)S(1)}, f32[8,128]{1,0:T(8,128)S(1)}, u32[]{:S(2)}, u32[]{:S(2)}) collective-permute-start(f32[8,128]{1,0:T(8,128)S(1)} %broadcast_add_fusion), channel_id=1, source_target_pairs={{0,8},{4,12},{8,0},{12,4},{16,24},{20,28},{24,16},{28,20},{1,9},{5... | collective-permute-start | bytes 12296 | tf_op jit(solution)/shard_map/ppermute | solution.py:677
  220.0 4.5 %collective-permute-start.34 = (f32[8,128]{1,0:T(8,128)S(1)}, f32[8,128]{1,0:T(8,128)S(1)}, u32[]{:S(2)}, u32[]{:S(2)}) collective-permute-start(f32[8,128]{1,0:T(8,128)S(1)} %fusion.11), channel_id=1, source_target_pairs={{0,16},{4,20},{8,24},{12,28},{16,0},{20,4},{24,8},{28,12},{1,17},{... | collective-permute-start | bytes 12296 | tf_op jit(solution)/shard_map/ppermute | solution.py:677
  232.7 9.2 %collective-permute-start.35 = (bf16[16,4,64,128]{3,2,1,0:T(8,128)(2,1)}, bf16[16,4,64,128]{3,2,1,0:T(8,128)(2,1)S(1)}, u32[]{:S(2)}, u32[]{:S(2)}) collective-permute-start(bf16[16,4,64,128]{3,2,1,0:T(8,128)(2,1)} %get-tuple-element.175), channel_id=1, source_target_pairs={{0,1},{1,0},{2,3},{3,2},{4,5},{5,4},{6,7},{7,6},{8,9},{9,8},{10,11... | collective-permute-start | bytes 3145736 | tf_op jit(solution)/shard_map/ppermute | solution.py:677
  239.5 4.4 %collective-permute-start.37 = (bf16[16,4,64,128]{3,2,1,0:T(8,128)(2,1)}, bf16[16,4,64,128]{3,2,1,0:T(8,128)(2,1)S(1)}, u32[]{:S(2)}, u32[]{:S(2)}) collective-permute-start(bf16[16,4,64,128]{3,2,1,0:T(8,128)(2,1)} %get-tuple-element.180), channel_id=1, source_target_pairs={{0,1},{1,0},{2,3},{3,2},{4,5},{5,4},{6,7},{7,6},{8,9},{9,8},{10,11... | collective-permute-start | bytes 3145736 | tf_op jit(solution)/shard_map/ppermute | solution.py:677
  240.0 12.1 %collective-permute-start.40 = (bf16[8,32,512]{2,1,0:T(8,128)(2,1)S(1)}, bf16[8,32,512]{2,1,0:T(8,128)(2,1)S(1)}, u32[]{:S(2)}, u32[]{:S(2)}) collective-permute-start(bf16[8,32,512]{2,1,0:T(8,128)(2,1)S(1)} %copy-done.41), channel_id=1, source_target_pairs={{0,1},{1,0},{2,3},{3,2},{4,5},{5,4},{6,7},{7,6},{8,9},{9,8},{10,11... | collective-permute-start | bytes 786440 | tf_op jit(solution)/shard_map/ppermute | solution.py:677
  240.1 12.1 %collective-permute-start.41 = (bf16[8,32,512]{2,1,0:T(8,128)(2,1)S(1)}, bf16[8,32,512]{2,1,0:T(8,128)(2,1)S(1)}, u32[]{:S(2)}, u32[]{:S(2)}) collective-permute-start(bf16[8,32,512]{2,1,0:T(8,128)(2,1)S(1)} %copy-done.40), channel_id=1, source_target_pairs={{0,2},{1,3},{2,0},{3,1},{4,6},{5,7},{6,4},{7,5},{8,10},{9,11},{10,... | collective-permute-start | bytes 786440 | tf_op jit(solution)/shard_map/ppermute | solution.py:677
  241.2 12.7 %collective-permute-start.42 = (bf16[8,32,512]{2,1,0:T(8,128)(2,1)S(1)}, bf16[8,32,512]{2,1,0:T(8,128)(2,1)S(1)}, u32[]{:S(2)}, u32[]{:S(2)}) collective-permute-start(bf16[8,32,512]{2,1,0:T(8,128)(2,1)S(1)} %copy-done.39), channel_id=1, source_target_pairs={{0,3},{1,2},{2,1},{3,0},{4,7},{5,6},{6,5},{7,4},{8,11},{9,10},{10,... | collective-permute-start | bytes 786440 | tf_op jit(solution)/shard_map/ppermute | solution.py:677
  242.3 27.3 %collective-permute-start.36 = (bf16[8,4,64,128]{3,2,1,0:T(8,128)(2,1)S(1)}, bf16[8,4,64,128]{3,2,1,0:T(8,128)(2,1)S(1)}, u32[]{:S(2)}, u32[]{:S(2)}) collective-permute-start(bf16[8,4,64,128]{3,2,1,0:T(8,128)(2,1)S(1)} %get-tuple-element.271), channel_id=1, source_target_pairs={{0,4},{4,0},{8,12},{12,8},{16,20},{20,16},{24,28},{28,24},{1,5},{5... | collective-permute-start | bytes 1572872 | tf_op jit(solution)/shard_map/ppermute | solution.py:677
  244.2 25.6 %collective-permute-start.38 = (bf16[8,4,64,128]{3,2,1,0:T(8,128)(2,1)S(1)}, bf16[8,4,64,128]{3,2,1,0:T(8,128)(2,1)S(1)}, u32[]{:S(2)}, u32[]{:S(2)}) collective-permute-start(bf16[8,4,64,128]{3,2,1,0:T(8,128)(2,1)S(1)} %get-tuple-element.269), channel_id=1, source_target_pairs={{0,2},{1,3},{2,0},{3,1},{4,6},{5,7},{6,4},{7,5},{8,10},{9,11},{10,... | collective-permute-start | bytes 1572872 | tf_op jit(solution)/shard_map/ppermute | solution.py:677
  252.1 18.0 %collective-permute-start.39 = (bf16[16,4,64,128]{3,2,1,0:T(8,128)(2,1)}, bf16[16,4,64,128]{3,2,1,0:T(8,128)(2,1)S(1)}, u32[]{:S(2)}, u32[]{:S(2)}) collective-permute-start(bf16[16,4,64,128]{3,2,1,0:T(8,128)(2,1)} %get-tuple-element.185), channel_id=1, source_target_pairs={{0,1},{1,0},{2,3},{3,2},{4,5},{5,4},{6,7},{7,6},{8,9},{9,8},{10,11... | collective-permute-start | bytes 3145736 | tf_op jit(solution)/shard_map/ppermute | solution.py:677
  266.3 4.2 %collective-permute-start.43 = (bf16[16,4,64,128]{3,2,1,0:T(8,128)(2,1)}, bf16[16,4,64,128]{3,2,1,0:T(8,128)(2,1)S(1)}, u32[]{:S(2)}, u32[]{:S(2)}) collective-permute-start(bf16[16,4,64,128]{3,2,1,0:T(8,128)(2,1)} %get-tuple-element.196), channel_id=1, source_target_pairs={{0,1},{1,0},{2,3},{3,2},{4,5},{5,4},{6,7},{7,6},{8,9},{9,8},{10,11... | collective-permute-start | bytes 3145736 | tf_op jit(solution)/shard_map/ppermute | solution.py:677
  267.5 2.2 collective-permute-start.44
  271.5 9.2 %collective-permute-start.45 = (bf16[4,4,64,128]{3,2,1,0:T(8,128)(2,1)S(1)}, bf16[4,4,64,128]{3,2,1,0:T(8,128)(2,1)S(1)}, u32[]{:S(2)}, u32[]{:S(2)}) collective-permute-start(bf16[4,4,64,128]{3,2,1,0:T(8,128)(2,1)S(1)} %get-tuple-element.199), channel_id=1, source_target_pairs={{0,8},{4,12},{8,0},{12,4},{16,24},{20,28},{24,16},{28,20},{1,9},{5... | collective-permute-start | bytes 786440 | tf_op jit(solution)/shard_map/ppermute | solution.py:677
  271.5 17.0 %collective-permute-start.47 = (bf16[8,4,64,128]{3,2,1,0:T(8,128)(2,1)S(1)}, bf16[8,4,64,128]{3,2,1,0:T(8,128)(2,1)S(1)}, u32[]{:S(2)}, u32[]{:S(2)}) collective-permute-start(bf16[8,4,64,128]{3,2,1,0:T(8,128)(2,1)S(1)} %get-tuple-element.203), channel_id=1, source_target_pairs={{0,2},{1,3},{2,0},{3,1},{4,6},{5,7},{6,4},{7,5},{8,10},{9,11},{10,... | collective-permute-start | bytes 1572872 | tf_op jit(solution)/shard_map/ppermute | solution.py:677
  272.7 15.8 %collective-permute-start.46 = (bf16[4,4,64,128]{3,2,1,0:T(8,128)(2,1)S(1)}, bf16[4,4,64,128]{3,2,1,0:T(8,128)(2,1)S(1)}, u32[]{:S(2)}, u32[]{:S(2)}) collective-permute-start(bf16[4,4,64,128]{3,2,1,0:T(8,128)(2,1)S(1)} %get-tuple-element.201), channel_id=1, source_target_pairs={{0,8},{4,12},{8,0},{12,4},{16,24},{20,28},{24,16},{28,20},{1,9},{5... | collective-permute-start | bytes 786440 | tf_op jit(solution)/shard_map/ppermute | solution.py:677
  274.6 3.7 %collective-permute-start.49 = (f32[14,128]{1,0:T(8,128)S(1)}, f32[14,128]{1,0:T(8,128)S(1)}, u32[]{:S(2)}, u32[]{:S(2)}) collective-permute-start(f32[14,128]{1,0:T(8,128)S(1)} %bitcast_add_fusion), channel_id=1, source_target_pairs={{0,4},{4,0},{8,12},{12,8},{16,20},{20,16},{24,28},{28,24},{1,5},{5... | collective-permute-start | bytes 21512 | tf_op jit(solution)/shard_map/ppermute | solution.py:677
  276.1 13.2 %collective-permute-start.48 = (bf16[8,4,64,128]{3,2,1,0:T(8,128)(2,1)S(1)}, bf16[8,4,64,128]{3,2,1,0:T(8,128)(2,1)S(1)}, u32[]{:S(2)}, u32[]{:S(2)}) collective-permute-start(bf16[8,4,64,128]{3,2,1,0:T(8,128)(2,1)S(1)} %get-tuple-element.205), channel_id=1, source_target_pairs={{0,4},{4,0},{8,12},{12,8},{16,20},{20,16},{24,28},{28,24},{1,5},{5... | collective-permute-start | bytes 1572872 | tf_op jit(solution)/shard_map/ppermute | solution.py:677
  289.4 5.0 %collective-permute-start.51 = (bf16[2,4,64,128]{3,2,1,0:T(8,128)(2,1)S(1)}, bf16[2,4,64,128]{3,2,1,0:T(8,128)(2,1)S(1)}, u32[]{:S(2)}, u32[]{:S(2)}) collective-permute-start(bf16[2,4,64,128]{3,2,1,0:T(8,128)(2,1)S(1)} %get-tuple-element.219), channel_id=1, source_target_pairs={{0,4},{4,0},{8,12},{12,8},{16,20},{20,16},{24,28},{28,24},{1,5},{5... | collective-permute-start | bytes 393224 | tf_op jit(solution)/shard_map/ppermute | solution.py:677
  290.4 6.9 %collective-permute-start.52 = (bf16[4,4,64,128]{3,2,1,0:T(8,128)(2,1)S(1)}, bf16[4,4,64,128]{3,2,1,0:T(8,128)(2,1)S(1)}, u32[]{:S(2)}, u32[]{:S(2)}) collective-permute-start(bf16[4,4,64,128]{3,2,1,0:T(8,128)(2,1)S(1)} %get-tuple-element.221), channel_id=1, source_target_pairs={{0,8},{4,12},{8,0},{12,4},{16,24},{20,28},{24,16},{28,20},{1,9},{5... | collective-permute-start | bytes 786440 | tf_op jit(solution)/shard_map/ppermute | solution.py:677
  290.5 3.8 %collective-permute-start.53 = (f32[14,128]{1,0:T(8,128)S(1)}, f32[14,128]{1,0:T(8,128)S(1)}, u32[]{:S(2)}, u32[]{:S(2)}) collective-permute-start(f32[14,128]{1,0:T(8,128)S(1)} %add.252), channel_id=1, source_target_pairs={{0,2},{1,3},{2,0},{3,1},{4,6},{5,7},{6,4},{7,5},{8,10},{9,11},{10,... | collective-permute-start | bytes 21512 | tf_op jit(solution)/shard_map/ppermute | solution.py:677
  291.6 9.8 %collective-permute-start.50 = (bf16[6,4,64,128]{3,2,1,0:T(8,128)(2,1)S(1)}, bf16[6,4,64,128]{3,2,1,0:T(8,128)(2,1)S(1)}, u32[]{:S(2)}, u32[]{:S(2)}) collective-permute-start(bf16[6,4,64,128]{3,2,1,0:T(8,128)(2,1)S(1)} %pad_maximum_fusion.10), channel_id=1, source_target_pairs={{0,2},{1,3},{2,0},{3,1},{4,6},{5,7},{6,4},{7,5},{8,10},{9,11},{10,... | collective-permute-start | bytes 1179656 | tf_op jit(solution)/shard_map/ppermute | solution.py:677
  302.2 6.4 %collective-permute-start.55 = (bf16[2,4,64,128]{3,2,1,0:T(8,128)(2,1)S(1)}, bf16[2,4,64,128]{3,2,1,0:T(8,128)(2,1)S(1)}, u32[]{:S(2)}, u32[]{:S(2)}) collective-permute-start(bf16[2,4,64,128]{3,2,1,0:T(8,128)(2,1)S(1)} %pad_maximum_fusion.16), channel_id=1, source_target_pairs={{0,16},{4,20},{8,24},{12,28},{16,0},{20,4},{24,8},{28,12},{1,17},{... | collective-permute-start | bytes 393224 | tf_op jit(solution)/shard_map/ppermute | solution.py:677
  303.4 4.8 %collective-permute-start.54 = (f32[14,128]{1,0:T(8,128)S(1)}, f32[14,128]{1,0:T(8,128)S(1)}, u32[]{:S(2)}, u32[]{:S(2)}) collective-permute-start(f32[14,128]{1,0:T(8,128)S(1)} %add.262), channel_id=1, source_target_pairs={{0,8},{4,12},{8,0},{12,4},{16,24},{20,28},{24,16},{28,20},{1,9},{5... | collective-permute-start | bytes 21512 | tf_op jit(solution)/shard_map/ppermute | solution.py:677
  305.2 5.9 %collective-permute-start.56 = (bf16[2,4,64,128]{3,2,1,0:T(8,128)(2,1)S(1)}, bf16[2,4,64,128]{3,2,1,0:T(8,128)(2,1)S(1)}, u32[]{:S(2)}, u32[]{:S(2)}) collective-permute-start(bf16[2,4,64,128]{3,2,1,0:T(8,128)(2,1)S(1)} %get-tuple-element.234), channel_id=1, source_target_pairs={{0,4},{4,0},{8,12},{12,8},{16,20},{20,16},{24,28},{28,24},{1,5},{5... | collective-permute-start | bytes 393224 | tf_op jit(solution)/shard_map/ppermute | solution.py:677
  306.4 5.4 %collective-permute-start.57 = (bf16[2,4,64,128]{3,2,1,0:T(8,128)(2,1)S(1)}, bf16[2,4,64,128]{3,2,1,0:T(8,128)(2,1)S(1)}, u32[]{:S(2)}, u32[]{:S(2)}) collective-permute-start(bf16[2,4,64,128]{3,2,1,0:T(8,128)(2,1)S(1)} %get-tuple-element.236), channel_id=1, source_target_pairs={{0,8},{4,12},{8,0},{12,4},{16,24},{20,28},{24,16},{28,20},{1,9},{5... | collective-permute-start | bytes 393224 | tf_op jit(solution)/shard_map/ppermute | solution.py:677
  309.3 5.4 %collective-permute-start.59 = (f32[14,128]{1,0:T(8,128)S(1)}, f32[14,128]{1,0:T(8,128)S(1)}, u32[]{:S(2)}, u32[]{:S(2)}) collective-permute-start(f32[14,128]{1,0:T(8,128)S(1)} %add.263), channel_id=1, source_target_pairs={{0,16},{4,20},{8,24},{12,28},{16,0},{20,4},{24,8},{28,12},{1,17},{... | collective-permute-start | bytes 21512 | tf_op jit(solution)/shard_map/ppermute | solution.py:677
  312.5 7.3 %collective-permute-start.58 = (bf16[2,4,64,128]{3,2,1,0:T(8,128)(2,1)S(1)}, bf16[2,4,64,128]{3,2,1,0:T(8,128)(2,1)S(1)}, u32[]{:S(2)}, u32[]{:S(2)}) collective-permute-start(bf16[2,4,64,128]{3,2,1,0:T(8,128)(2,1)S(1)} %pad_maximum_fusion.17), channel_id=1, source_target_pairs={{0,16},{4,20},{8,24},{12,28},{16,0},{20,4},{24,8},{28,12},{1,17},{... | collective-permute-start | bytes 393224 | tf_op jit(solution)/shard_map/ppermute | solution.py:677
  (41 other events, 508.7 us)
Sparse Core Ops, SparseCore 0:
  11.5 68.3 all-gather.2
